TPU v7x, 32 devices: a whole 2x2x4 slice. The times are simulated.
32 devices in a mesh: groups: 1, pts: 32 (over z, y, x, core).
Axes of the slice: x: 2, y: 2, z: 4, core: 2. Of those that a mesh axis runs over, the one named last changes fastest.
Arguments:
- residual_cols: bfloat16 [16384, 256], P(('groups', 'pts')), may hold values from -6 to 6
- leaf_inverse: bfloat16 [16384, 128], P(('groups', 'pts'))
- basis_left: float32 [7, 16384, 128], P(None, ('groups', 'pts')), may hold values from -0.15625 to 0.15625
- basis_right: float32 [7, 16384, 128], P(None, ('groups', 'pts'))
- point_pos: float32 [16384], replicated, may hold values from 0 to 16, as said below
- map_pos: float32 [2048], P('pts'), may hold values from 0 to 16, as said below
- prior_map: bfloat16 [2048, 256], P(('groups', 'pts')), may hold values from -6 to 6
- block_first: int32 [32, 32], replicated, may hold values from 0 to 2, as said below
- block_count: int32 [32, 32], replicated, may hold values from 0 to 2, as said below
Outputs:
- solved_cols: float32 [16384, 256], P(('groups', 'pts'))
- sample_map: float32 [2048, 256], P(('groups', 'pts'))
Inputs may be any that keep to these rules, and one draw needn't show every extreme that they name: `block_count`: at most 2; the listed blocks of tile d from source s include every block of s that has a point within distance 1 of some map point of tile d; in every draw some tile owner receives 2 blocks from every source; the totals per owner differ strongly between owners. `block_first`: listed blocks stay inside the source's 4 blocks. `point_pos`: points of one leaf block lie in increasing order within an interval of length 1. `map_pos`: the map points of one tile lie within an interval of length at most 6.
All inputs are finite; a program needn't handle non-finite values.
Results may differ from a plain program's by a relative error of at most 0.003.
Values may be sent and summed in bfloat16 or wider, within the bound.
No kernel may reach another device: no remote copies, remote signals or barrier semaphores. Data moves between devices by JAX's collectives and lax.ppermute only.
A program may use at most 128 MiB of HBM per device.

v0:
```python
import jax
import jax.numpy as jnp
from jax import lax
from jax.sharding import PartitionSpec as P

LEAF = 128
CAP = 2


amplitude = 0.2
highest = lax.Precision.HIGHEST


def swapped(value, axis, bit):
    mask = 2**bit
    pairs = [(source, source ^ mask) for source in range(lax.axis_size(axis))]
    return lax.ppermute(value, axis, pairs)


def wendland(distance):
    scaled = jnp.minimum(jnp.abs(distance) * (2.0 * LEAF), 1.0)
    return (1.0 - scaled) ** 4 * (1.0 + 4.0 * scaled)


def sibling_sum(projected, depth_bits):
    current = projected
    for bit_index in range(depth_bits):
        current = current + swapped(current, "pts", bit_index)
    received = swapped(current, "pts", depth_bits)
    return received


def body(
    residual_cols,
    leaf_inverse,
    basis_left,
    basis_right,
    point_pos,
    map_pos,
    prior_map,
    block_first,
    block_count,
):
    row_count, samples = residual_cols.shape
    leaf_size = leaf_inverse.shape[1]
    block_local = row_count // leaf_size
    devices = lax.axis_size("pts")
    my_index = lax.axis_index("pts")
    inverses = leaf_inverse.reshape(block_local, leaf_size, leaf_size)
    right_side = residual_cols.reshape(block_local, leaf_size, samples)
    solved = jnp.einsum(
        "bij,bjs->bis", inverses, right_side, preferred_element_type=jnp.float32
    ).reshape(row_count, samples)
    level_total = basis_left.shape[0]
    total_rows = row_count * devices
    for level_index in reversed(range(level_total)):
        half_size = total_rows // 2 ** (level_index + 1)
        left_basis = basis_left[level_index]
        right_basis = basis_right[level_index]
        if half_size < row_count:
            node_count = row_count // (2 * half_size)
            coeff_view = solved.reshape(node_count, 2, half_size, samples)
            right_view = right_basis.reshape(node_count, 2, half_size, -1)
            left_view = left_basis.reshape(node_count, 2, half_size, -1)
            projected = jnp.einsum("nhpr,nhps->nhrs", right_view, coeff_view, precision=highest)
            update = jnp.einsum("nhpr,nhrs->nhps", left_view, projected[:, ::-1], precision=highest)
            solved = solved + update.reshape(row_count, samples)
        else:
            span_devices = half_size // row_count
            depth_bits = span_devices.bit_length() - 1
            projected = jnp.dot(right_basis.T, solved, precision=highest)
            sibling = sibling_sum(projected, depth_bits)
            solved = solved + jnp.dot(left_basis, sibling, precision=highest)
    coeffs = solved.astype(jnp.bfloat16)
    coeff_blocks = coeffs.reshape(block_local, leaf_size, samples)
    map_rows = map_pos.shape[0]
    slot_range = jnp.arange(CAP)[None, :]
    send_first = block_first[:, my_index]
    send_count = block_count[:, my_index]
    send_index = send_first[:, None] + slot_range
    send_live = slot_range < send_count[:, None]
    outgoing = jnp.where(
        send_live[:, :, None, None], coeff_blocks[send_index], jnp.zeros((), jnp.bfloat16)
    )
    sources = jnp.arange(devices)[:, None]
    slot_index = block_first[my_index][:, None] + slot_range
    live = slot_range < block_count[my_index][:, None]
    point_index = (sources * block_local + slot_index)[:, :, None] * leaf_size + jnp.arange(
        leaf_size
    )
    positions = point_pos[point_index]
    kernel = amplitude * wendland(map_pos[:, None, None, None] - positions[None])
    weights = (
        jnp.where(live[None, :, :, None], kernel, 0.0).astype(jnp.bfloat16).reshape(map_rows, -1)
    )
    mapped = jnp.dot(
        weights,
        lax.all_to_all(outgoing, "pts", split_axis=0, concat_axis=0, tiled=True).reshape(
            weights.shape[1], -1
        ),
        preferred_element_type=jnp.float32,
    )
    sample_map = prior_map.astype(jnp.float32) + mapped
    return (solved, sample_map)


def solution(mesh):
    in_specs = (
        P(("groups", "pts"), None),
        P(("groups", "pts"), None),
        P(None, ("groups", "pts"), None),
        P(None, ("groups", "pts"), None),
        P(),
        P("pts"),
        P(("groups", "pts"), None),
        P(),
        P(),
    )
    out_specs = (P(("groups", "pts"), None), P(("groups", "pts"), None))
    return jax.shard_map(body, mesh=mesh, in_specs=in_specs, out_specs=out_specs, check_vma=False)
```

profile of v0, /device:TPU:0, one launch (start us, length us, event | category | flops | bytes accessed | tf_op | source)
XLA Modules:
  0.0 193.8 jit_solution(8209846204342725354)
XLA Ops:
  0.6 1.1 fusion.42
  1.8 1.1 fusion.44
  2.9 0.7 convolution_bitcast_fusion.5
  3.6 1.1 fusion.41
  4.7 0.6 fusion.45
  5.4 0.6 convolution_bitcast_fusion.6
  6.0 0.6 bitcast_add_fusion.1
  6.7 2.0 %convolution_bitcast_fusion.11 = f32[128,256]{0,1:T(8,128)S(1)} fusion(f32[512,256]{1,0:T(8,128)S(1)} %bitcast.132, f32[7,512,128]{2,1,0:T(8,128)} %param.12), kind=kOutput, calls=%fused_computation.20 | convolution fusion | flops 201326592 | bytes 917504 | tf_op jit(solution)/shard_map/dot_general | solution.py:71
  8.6 0.5 collective-permute-start
  9.1 0.2 copy.18
  9.3 0.2 copy.16
  9.5 0.2 copy.17
  9.8 0.4 collective-permute-done
  10.1 1.8 fusion
  11.9 0.6 convolution_bitcast_fusion.10
  12.5 0.2 collective-permute-start.1
  12.7 1.2 collective-permute-done.1
  13.9 2.7 %collective-permute-start.2 = (f32[128,256]{0,1:T(8,128)S(1)}, f32[128,256]{0,1:T(8,128)S(1)}, u32[]{:S(2)}, u32[]{:S(2)}) collective-permute-start(f32[128,256]{0,1:T(8,128)S(1)} %add.174), channel_id=1, source_target_pairs={{0,2},{1,3},{2,0},{3,1},{4,6},{5,7},{6,4},{7,5},{8,10},{9,11},{10,... | collective-permute-start | bytes 393224 | tf_op jit(solution)/shard_map/ppermute | solution.py:17
  16.7 4.0 %collective-permute-done.2 = f32[128,256]{0,1:T(8,128)S(1)} collective-permute-done((f32[128,256]{0,1:T(8,128)S(1)}, f32[128,256]{0,1:T(8,128)S(1)}, u32[]{:S(2)}, u32[]{:S(2)}) %collective-permute-start.2) | collective-permute-done | bytes 131104 | tf_op jit(solution)/shard_map/ppermute | solution.py:17
  20.6 1.5 fusion.1
  22.2 0.6 convolution_bitcast_fusion.9
  22.9 1.3 collective-permute-done.3
  24.2 1.8 collective-permute-start.4
  26.0 3.8 %collective-permute-done.4 = f32[128,256]{0,1:T(8,128)S(1)} collective-permute-done((f32[128,256]{0,1:T(8,128)S(1)}, f32[128,256]{0,1:T(8,128)S(1)}, u32[]{:S(2)}, u32[]{:S(2)}) %collective-permute-start.4) | collective-permute-done | bytes 131104 | tf_op jit(solution)/shard_map/ppermute | solution.py:17
  29.8 1.8 collective-permute-start.5
  31.7 3.2 %collective-permute-done.5 = f32[128,256]{0,1:T(8,128)S(1)} collective-permute-done((f32[128,256]{0,1:T(8,128)S(1)}, f32[128,256]{0,1:T(8,128)S(1)}, u32[]{:S(2)}, u32[]{:S(2)}) %collective-permute-start.5) | collective-permute-done | bytes 131104 | tf_op jit(solution)/shard_map/ppermute | solution.py:17
  34.9 1.5 fusion.2
  36.4 0.6 convolution_bitcast_fusion.8
  37.0 0.1 collective-permute-start.6
  37.1 1.3 collective-permute-done.6
  38.5 1.8 collective-permute-start.7
  40.3 3.8 %collective-permute-done.7 = f32[128,256]{0,1:T(8,128)S(1)} collective-permute-done((f32[128,256]{0,1:T(8,128)S(1)}, f32[128,256]{0,1:T(8,128)S(1)}, u32[]{:S(2)}, u32[]{:S(2)}) %collective-permute-start.7) | collective-permute-done | bytes 131104 | tf_op jit(solution)/shard_map/ppermute | solution.py:17
  44.1 1.8 collective-permute-start.8
  45.9 3.2 %collective-permute-done.8 = f32[128,256]{0,1:T(8,128)S(1)} collective-permute-done((f32[128,256]{0,1:T(8,128)S(1)}, f32[128,256]{0,1:T(8,128)S(1)}, u32[]{:S(2)}, u32[]{:S(2)}) %collective-permute-start.8) | collective-permute-done | bytes 131104 | tf_op jit(solution)/shard_map/ppermute | solution.py:17
  49.2 1.9 collective-permute-start.9
  51.1 3.1 %collective-permute-done.9 = f32[128,256]{0,1:T(8,128)S(1)} collective-permute-done((f32[128,256]{0,1:T(8,128)S(1)}, f32[128,256]{0,1:T(8,128)S(1)}, u32[]{:S(2)}, u32[]{:S(2)}) %collective-permute-start.9) | collective-permute-done | bytes 131104 | tf_op jit(solution)/shard_map/ppermute | solution.py:17
  54.2 1.5 fusion.3
  55.7 0.6 convolution_bitcast_fusion.7
  56.4 1.3 collective-permute-done.10
  57.8 1.8 collective-permute-start.11
  59.6 3.8 %collective-permute-done.11 = f32[128,256]{0,1:T(8,128)S(1)} collective-permute-done((f32[128,256]{0,1:T(8,128)S(1)}, f32[128,256]{0,1:T(8,128)S(1)}, u32[]{:S(2)}, u32[]{:S(2)}) %collective-permute-start.11) | collective-permute-done | bytes 131104 | tf_op jit(solution)/shard_map/ppermute | solution.py:17
  63.4 1.8 collective-permute-start.12
  65.2 0.2 dynamic-slice_reduce_fusion
  65.4 3.0 %collective-permute-done.12 = f32[128,256]{0,1:T(8,128)S(1)} collective-permute-done((f32[128,256]{0,1:T(8,128)S(1)}, f32[128,256]{0,1:T(8,128)S(1)}, u32[]{:S(2)}, u32[]{:S(2)}) %collective-permute-start.12) | collective-permute-done | bytes 131104 | tf_op jit(solution)/shard_map/ppermute | solution.py:17
  68.4 1.9 collective-permute-start.13
  70.3 0.1 compare_select_fusion.1
  70.4 3.1 %collective-permute-done.13 = f32[128,256]{0,1:T(8,128)S(1)} collective-permute-done((f32[128,256]{0,1:T(8,128)S(1)}, f32[128,256]{0,1:T(8,128)S(1)}, u32[]{:S(2)}, u32[]{:S(2)}) %collective-permute-start.13) | collective-permute-done | bytes 131104 | tf_op jit(solution)/shard_map/ppermute | solution.py:17
  73.5 3.3 %collective-permute-start.14 = (f32[128,256]{0,1:T(8,128)S(1)}, f32[128,256]{0,1:T(8,128)S(1)}, u32[]{:S(2)}, u32[]{:S(2)}) collective-permute-start(f32[128,256]{0,1:T(8,128)S(1)} %add.186), channel_id=1, source_target_pairs={{0,16},{1,17},{2,18},{3,19},{4,20},{5,21},{6,22},{7,23},{8,24},{9,... | collective-permute-start | bytes 393224 | tf_op jit(solution)/shard_map/ppermute | solution.py:17
  76.8 0.1 iota_compare_fusion
  76.9 0.1 reshape.221
  77.0 4.2 %collective-permute-done.14 = f32[128,256]{0,1:T(8,128)S(1)} collective-permute-done((f32[128,256]{0,1:T(8,128)S(1)}, f32[128,256]{0,1:T(8,128)S(1)}, u32[]{:S(2)}, u32[]{:S(2)}) %collective-permute-start.14) | collective-permute-done | bytes 131104 | tf_op jit(solution)/shard_map/ppermute | solution.py:17
  81.2 1.5 fusion.43
  82.7 0.1 copy.22
  82.9 2.8 %gather_fusion.1 = bf16[64,128,256]{2,1,0:T(8,128)(2,1)} fusion(bf16[4,128,256]{2,1,0:T(8,128)(2,1)S(1)} %bitcast.126, s32[1024]{0:T(1024)S(1)} %pad_clamp_fusion), kind=kCustom, calls=%fused_computation.1 | custom fusion | bytes 8388864 | tf_op jit(solution)/shard_map/gather | solution.py:83
  85.7 4.5 %broadcast_select_fusion = bf16[32,2,128,256]{3,2,1,0:T(8,128)(2,1)} fusion(bf16[32,2,128,256]{3,2,1,0:T(8,128)(2,1)} %bitcast.127, pred[32,2]{1,0:T(8,128)(4,1)S(1)} %iota_compare_fusion), kind=kLoop, calls=%fused_computation.2 | loop fusion | flops 2097152 | bytes 8388672 | tf_op jit(solution)/shard_map/jit(_where)/select_n | solution.py:82
  90.1 5.9 %all-to-all-start = ((bf16[32,2,128,256]{3,2,1,0:T(8,128)(2,1)}), bf16[32,2,128,256]{3,2,1,0:T(8,128)(2,1)}, u32[]{:S(2)}, u32[]{:S(2)}) async-start(bf16[32,2,128,256]{3,2,1,0:T(8,128)(2,1)} %broadcast_select_fusion), calls=%async_computation | async-start | bytes 8388608 | tf_op jit(solution)/shard_map/all_to_all | solution.py:98
  96.1 0.1 add_multiply_fusion
  96.2 0.1 compare_select_fusion
  96.3 0.6 copy-done.1
  96.9 45.5 %gather_fusion = f32[8192]{0:T(1024)S(1)} fusion(f32[16384]{0:T(1024)S(1)} %copy-done.1, s32[8192]{0:T(1024)S(1)} %broadcast_clamp_fusion), kind=kCustom, calls=%fused_computation | custom fusion | bytes 98304 | tf_op jit(solution)/shard_map/gather | solution.py:91
  142.4 0.1 iota_compare_fusion.1
  142.5 1.0 copy.20
  143.5 46.4 %all-to-all-done = bf16[32,2,128,256]{3,2,1,0:T(8,128)(2,1)} async-done(((bf16[32,2,128,256]{3,2,1,0:T(8,128)(2,1)}), bf16[32,2,128,256]{3,2,1,0:T(8,128)(2,1)}, u32[]{:S(2)}, u32[]{:S(2)}) %all-to-all-start) | async-done | bytes 4194336 | tf_op jit(solution)/shard_map/all_to_all | solution.py:98
  189.9 3.8 %fusion.5 = f32[64,256]{1,0:T(8,128)} fusion(bf16[32,2,128,256]{3,2,1,0:T(8,128)(2,1)} %all-to-all-done, f32[32,2,128]{2,1,0:T(2,128)S(1)} %bitcast.140, f32[64]{0:T(128)S(1)} %copy-done.6, pred[32,2]{1,0:T(8,128)(4,1)S(1)} %iota_compare_fusion.1, bf16[64,256]{1,0:T(8,128)(2,1)S(1)} %copy-done.5), kind=kOutput, calls=%fused_computation.22 | convolution fusion | flops 275283968 | bytes 4325696 | tf_op jit(solution)/shard_map/dot_general | solution.py:96
  (33 shorter events, 0.5 us)
Async XLA Ops:
  0.6 1.1 copy-start
  8.6 1.5 collective-permute-start
  9.7 2.1 %copy-start.2 = (f32[7,512,128]{2,1,0:T(8,128)S(1)}, f32[7,512,128]{2,1,0:T(8,128)}, u32[]{:S(2)}) copy-start(f32[7,512,128]{2,1,0:T(8,128)} %param.12) | copy-start | bytes 5505028
  12.5 1.4 collective-permute-start.1
  13.9 6.7 %collective-permute-start.2 = (f32[128,256]{0,1:T(8,128)S(1)}, f32[128,256]{0,1:T(8,128)S(1)}, u32[]{:S(2)}, u32[]{:S(2)}) collective-permute-start(f32[128,256]{0,1:T(8,128)S(1)} %add.174), channel_id=1, source_target_pairs={{0,2},{1,3},{2,0},{3,1},{4,6},{5,7},{6,4},{7,5},{8,10},{9,11},{10,... | collective-permute-start | bytes 393224 | tf_op jit(solution)/shard_map/ppermute | solution.py:17
  22.8 1.4 collective-permute-start.3
  24.2 5.6 %collective-permute-start.4 = (f32[128,256]{0,1:T(8,128)S(1)}, f32[128,256]{0,1:T(8,128)S(1)}, u32[]{:S(2)}, u32[]{:S(2)}) collective-permute-start(f32[128,256]{0,1:T(8,128)S(1)} %add.176), channel_id=1, source_target_pairs={{0,2},{1,3},{2,0},{3,1},{4,6},{5,7},{6,4},{7,5},{8,10},{9,11},{10,... | collective-permute-start | bytes 393224 | tf_op jit(solution)/shard_map/ppermute | solution.py:17
  29.8 5.0 %collective-permute-start.5 = (f32[128,256]{0,1:T(8,128)S(1)}, f32[128,256]{0,1:T(8,128)S(1)}, u32[]{:S(2)}, u32[]{:S(2)}) collective-permute-start(f32[128,256]{0,1:T(8,128)S(1)} %add.177), channel_id=1, source_target_pairs={{0,4},{1,5},{2,6},{3,7},{4,0},{5,1},{6,2},{7,3},{8,12},{9,13},{10,... | collective-permute-start | bytes 393224 | tf_op jit(solution)/shard_map/ppermute | solution.py:17
  37.0 28.2 %copy-start.3 = (s32[32,32]{1,0:T(8,128)S(1)}, s32[32,32]{1,0:T(8,128)}, u32[]{:S(2)}) copy-start(s32[32,32]{1,0:T(8,128)} %param.16) | copy-start | bytes 12292
  37.0 28.2 %copy-start.4 = (s32[32,32]{1,0:T(8,128)S(1)}, s32[32,32]{1,0:T(8,128)}, u32[]{:S(2)}) copy-start(s32[32,32]{1,0:T(8,128)} %param.17) | copy-start | bytes 12292
  37.0 1.4 collective-permute-start.6
  38.5 5.6 %collective-permute-start.7 = (f32[128,256]{0,1:T(8,128)S(1)}, f32[128,256]{0,1:T(8,128)S(1)}, u32[]{:S(2)}, u32[]{:S(2)}) collective-permute-start(f32[128,256]{0,1:T(8,128)S(1)} %add.179), channel_id=1, source_target_pairs={{0,2},{1,3},{2,0},{3,1},{4,6},{5,7},{6,4},{7,5},{8,10},{9,11},{10,... | collective-permute-start | bytes 393224 | tf_op jit(solution)/shard_map/ppermute | solution.py:17
  44.1 5.0 %collective-permute-start.8 = (f32[128,256]{0,1:T(8,128)S(1)}, f32[128,256]{0,1:T(8,128)S(1)}, u32[]{:S(2)}, u32[]{:S(2)}) collective-permute-start(f32[128,256]{0,1:T(8,128)S(1)} %add.180), channel_id=1, source_target_pairs={{0,4},{1,5},{2,6},{3,7},{4,0},{5,1},{6,2},{7,3},{8,12},{9,13},{10,... | collective-permute-start | bytes 393224 | tf_op jit(solution)/shard_map/ppermute | solution.py:17
  49.2 5.0 %collective-permute-start.9 = (f32[128,256]{0,1:T(8,128)S(1)}, f32[128,256]{0,1:T(8,128)S(1)}, u32[]{:S(2)}, u32[]{:S(2)}) collective-permute-start(f32[128,256]{0,1:T(8,128)S(1)} %add.181), channel_id=1, source_target_pairs={{0,8},{1,9},{2,10},{3,11},{4,12},{5,13},{6,14},{7,15},{8,0},{9,1},... | collective-permute-start | bytes 393224 | tf_op jit(solution)/shard_map/ppermute | solution.py:17
  56.3 1.4 collective-permute-start.10
  57.8 5.6 %collective-permute-start.11 = (f32[128,256]{0,1:T(8,128)S(1)}, f32[128,256]{0,1:T(8,128)S(1)}, u32[]{:S(2)}, u32[]{:S(2)}) collective-permute-start(f32[128,256]{0,1:T(8,128)S(1)} %add.183), channel_id=1, source_target_pairs={{0,2},{1,3},{2,0},{3,1},{4,6},{5,7},{6,4},{7,5},{8,10},{9,11},{10,... | collective-permute-start | bytes 393224 | tf_op jit(solution)/shard_map/ppermute | solution.py:17
  63.4 5.0 %collective-permute-start.12 = (f32[128,256]{0,1:T(8,128)S(1)}, f32[128,256]{0,1:T(8,128)S(1)}, u32[]{:S(2)}, u32[]{:S(2)}) collective-permute-start(f32[128,256]{0,1:T(8,128)S(1)} %add.184), channel_id=1, source_target_pairs={{0,4},{1,5},{2,6},{3,7},{4,0},{5,1},{6,2},{7,3},{8,12},{9,13},{10,... | collective-permute-start | bytes 393224 | tf_op jit(solution)/shard_map/ppermute | solution.py:17
  68.4 5.0 %collective-permute-start.13 = (f32[128,256]{0,1:T(8,128)S(1)}, f32[128,256]{0,1:T(8,128)S(1)}, u32[]{:S(2)}, u32[]{:S(2)}) collective-permute-start(f32[128,256]{0,1:T(8,128)S(1)} %add.185), channel_id=1, source_target_pairs={{0,8},{1,9},{2,10},{3,11},{4,12},{5,13},{6,14},{7,15},{8,0},{9,1},... | collective-permute-start | bytes 393224 | tf_op jit(solution)/shard_map/ppermute | solution.py:17
  73.5 7.7 %collective-permute-start.14 = (f32[128,256]{0,1:T(8,128)S(1)}, f32[128,256]{0,1:T(8,128)S(1)}, u32[]{:S(2)}, u32[]{:S(2)}) collective-permute-start(f32[128,256]{0,1:T(8,128)S(1)} %add.186), channel_id=1, source_target_pairs={{0,16},{1,17},{2,18},{3,19},{4,20},{5,21},{6,22},{7,23},{8,24},{9,... | collective-permute-start | bytes 393224 | tf_op jit(solution)/shard_map/ppermute | solution.py:17
  90.1 99.8 %all-to-all-start = ((bf16[32,2,128,256]{3,2,1,0:T(8,128)(2,1)}), bf16[32,2,128,256]{3,2,1,0:T(8,128)(2,1)}, u32[]{:S(2)}, u32[]{:S(2)}) async-start(bf16[32,2,128,256]{3,2,1,0:T(8,128)(2,1)} %broadcast_select_fusion), calls=%async_computation | async-start | bytes 8388608 | tf_op jit(solution)/shard_map/all_to_all | solution.py:98
  96.0 0.8 copy-start.1
  96.9 93.0 %copy-start.5 = (bf16[64,256]{1,0:T(8,128)(2,1)S(1)}, bf16[64,256]{1,0:T(8,128)(2,1)}, u32[]{:S(2)}) copy-start(bf16[64,256]{1,0:T(8,128)(2,1)} %param.15) | copy-start | bytes 98308
  96.9 93.0 %copy-start.6 = (f32[64]{0:T(128)S(1)}, f32[64]{0:T(128)}, u32[]{:S(2)}) copy-start(f32[64]{0:T(128)} %param.14) | copy-start | bytes 772
where the time goes:
time: 194 us
  waiting for transfers between devices  87.1 us (45%)
  local copies, waits for them, and re-layouts  53.2 us (27%)
  starting transfers between devices  27.6 us (14%)
  matrix products  19.7 us (10%)
  other arithmetic  5.1 us (3%)
    all_to_all x1, waiting for transfers between devices, body(): lax.all_to_all(outgoing, 'pts', split_axis=0, concat_axis=0, tiled=True)  46.4 us
    gather x1, local copies, waits for them, and re-layouts, body(): positions = point_pos[point_index]  45.5 us
    ppermute x15, waiting for transfers between devices, swapped(): return lax.ppermute(value, axis, pairs)  40.7 us
    ppermute x15, starting transfers between devices, swapped(): return lax.ppermute(value, axis, pairs)  21.8 us
    dot_general x5, matrix products, body(): solved = solved + jnp.dot(left_basis, sibling, precision=highest)  7.89 us
    all_to_all x1, starting transfers between devices, body(): lax.all_to_all(outgoing, 'pts', split_axis=0, concat_axis=0, tiled=True)  5.89 us
    select_n x1, other arithmetic, body(): jnp.where(send_live[:, :, None, None], coeff_blocks[send_index], jnp.zero...  4.46 us
    dot_general x5, matrix products, body(): projected = jnp.dot(right_basis.T, solved, precision=highest)  4.3 us
  transfers between devices with their start and end apart: 16, of which 16 were waited for; matrix products, arithmetic and copies ran while one was open for 25% of the time, Pallas kernels for 0%

commit v1 on v0

v1 whole, which is shorter than its diff:
```python
import jax
import jax.numpy as jnp
from jax import lax
from jax.sharding import PartitionSpec as P

CAP = 2
amplitude = 0.2
bf16 = jnp.bfloat16
f32 = jnp.float32
HIGH = lax.Precision.HIGH


def swapped(value, mask):
    pairs = [(source, source ^ mask) for source in range(lax.axis_size("pts"))]
    return lax.ppermute(value, "pts", pairs)


def dot16(a, b):
    return jnp.dot(a.astype(bf16), b.astype(bf16), preferred_element_type=f32)


def halves(value, core):
    width = value.shape[-1] // 2
    low, high = value[..., :width], value[..., width:]
    return jnp.where(core == 0, low, high), jnp.where(core == 0, high, low)


def split3(value):
    one = lax.reduce_precision(value, 8, 7)
    two = lax.reduce_precision(value - one, 8, 7)
    return jnp.concatenate([one, two, value - one - two], 0).astype(bf16)


def body(
    residual_cols,
    leaf_inverse,
    basis_left,
    basis_right,
    point_pos,
    map_pos,
    prior_map,
    block_first,
    block_count,
):
    rows, samples = residual_cols.shape
    leaf = leaf_inverse.shape[1]
    rank = basis_left.shape[2]
    blocks = rows // leaf
    devices = lax.axis_size("pts")
    bits = devices.bit_length() - 1
    me = lax.axis_index("pts")
    core = me % 2
    levels = basis_left.shape[0]
    tile = map_pos.shape[0]
    half = samples // 2

    left16 = basis_left[:bits].astype(bf16)
    right16 = basis_right[:bits].astype(bf16)
    pairs = [(i, j) for j in range(bits) for i in range(j)]
    small = {
        (i, j): lax.dot_general(
            right16[i], left16[j], (((0,), (0,)), ((), ())), preferred_element_type=f32
        )
        for i, j in pairs
    }
    left_other = swapped(left16, 1)

    inverses = leaf_inverse.reshape(blocks, leaf, leaf)
    solved = jnp.einsum(
        "bij,bjs->bis",
        inverses,
        residual_cols.reshape(blocks, leaf, samples),
        preferred_element_type=f32,
    ).reshape(rows, samples)
    for level in reversed(range(bits, levels)):
        size = rows * devices // 2 ** (level + 1)
        nodes = rows // (2 * size)
        view = solved.reshape(nodes, 2, size, samples)
        right = basis_right[level].reshape(nodes, 2, size, rank)
        left = basis_left[level].reshape(nodes, 2, size, rank)
        projected = jnp.einsum("nhpr,nhps->nhrs", right, view, precision=HIGH)
        update = jnp.einsum("nhpr,nhrs->nhps", left, projected[:, ::-1], precision=HIGH)
        solved = solved + update.reshape(rows, samples)
    solved_mine, solved_send = halves(solved, core)
    solved_other = swapped(solved_send, 1)
    projections = jnp.einsum("lpr,ps->lrs", basis_right[:bits], solved, precision=HIGH)
    mine, send = halves(projections, core)

    gathered = map_pos
    shares = [None] * bits
    current = mine
    for bit in range(bits):
        level = bits - 1 - bit
        inner = [(i, j) for i, j in pairs if j <= level]
        outgoing = send if bit == 0 else current
        parts = [outgoing.astype(bf16).reshape(-1, half)]
        parts += [small[p].astype(bf16) for p in inner]
        spots = split3(gathered)
        pad = -spots.size % (16 * half)
        parts.append(jnp.pad(spots, (0, pad)).reshape(-1, half))
        arrived = swapped(jnp.concatenate(parts, 0), 1 << bit)
        theirs = arrived[: (level + 1) * rank].reshape(level + 1, rank, half)
        at = (level + 1) * rank
        small_theirs = {}
        for p in inner:
            small_theirs[p] = arrived[at : at + rank]
            at += rank
        spots = arrived[at:].reshape(-1)[: 3 * gathered.size].reshape(3, -1).astype(f32)
        gathered = jnp.concatenate([gathered, spots[0] + spots[1] + spots[2]], 0)
        shares[level] = theirs[level]
        if level:
            both = jnp.concatenate(
                [
                    jnp.concatenate([small[i, level].astype(bf16) for i in range(level)], 0),
                    jnp.concatenate([small_theirs[i, level] for i in range(level)], 0),
                ],
                1,
            )
            pair = jnp.concatenate([theirs[level], current[level].astype(bf16)], 0)
            step = jnp.dot(both, pair, preferred_element_type=f32).reshape(level, rank, half)
            if bit == 0:
                last_mine = current[level].astype(bf16)
            current = current[:level] + theirs[:level].astype(f32) + step
            small = {
                p: small[p] + small_theirs[p].astype(f32) for p in inner if p[1] < level
            }
        elif bit == 0:
            last_mine = current[level].astype(bf16)

    top = bits - 1
    share = jnp.stack(shares)
    passed = jnp.stack(shares[:top] + [last_mine])
    share_other = swapped(passed, 1)

    def update(left, part):
        return jnp.einsum("lpr,lrs->ps", left, part.astype(left.dtype), precision=HIGH, preferred_element_type=f32)

    final_mine = solved_mine + update(basis_left[:bits], share)
    solved_rest = solved_send + update(basis_left[:bits], share_other)
    final_other = solved_other + update(left_other, passed)
    solved_out = jnp.where(
        core == 0,
        jnp.concatenate([final_mine, solved_rest], 1),
        jnp.concatenate([solved_rest, final_mine], 1),
    )
    coeffs = jnp.concatenate([final_mine, final_other], 0).astype(bf16)

    order = jnp.arange(devices) ^ me
    pick = order[:, None] == jnp.arange(devices)[None, :]
    live = []
    points = []
    for source in (me, me ^ 1):
        first = lax.dynamic_index_in_dim(block_first, source, 1, keepdims=False)
        count = lax.dynamic_index_in_dim(block_count, source, 1, keepdims=False)
        first = jnp.sum(jnp.where(pick, first[None, :], 0), 1)
        count = jnp.sum(jnp.where(pick, count[None, :], 0), 1)
        at = jnp.arange(blocks)[None, :]
        live.append((at >= first[:, None]) & (at < (first + count)[:, None]))
        points.append(lax.dynamic_slice_in_dim(point_pos, source * rows, rows))
    live = jnp.concatenate(live, 1)
    points = jnp.concatenate(points).reshape(2 * blocks, leaf)
    plane = 4
    far = devices // (2 * plane)
    spot_view = gathered.reshape(far, plane, 2 * tile)
    live_view = live.reshape(far, plane, 2, 2 * blocks)
    total = None
    for mask in range(plane):
        spots = spot_view[:, mask].reshape(far, 2, tile)
        r = jnp.minimum(jnp.abs(spots[..., None, None] - points) * (2.0 * leaf), 1.0)
        weight = amplitude * ((1.0 - r) ** 4 * (1.0 + 4.0 * r))
        weight = jnp.where(live_view[:, mask][:, :, None, :, None], weight, 0.0)
        weight = weight.astype(bf16).reshape(far * 2 * tile, 2 * rows)
        partial = jnp.dot(weight, coeffs, preferred_element_type=f32)
        if mask:
            partial = swapped(partial.astype(bf16), mask << 1).astype(f32)
        total = partial if total is None else total + partial
    total = total.reshape(far, 2 * tile, half)
    result = total[0]
    for mask in range(1, far):
        result = result + swapped(total[mask].astype(bf16), mask << 3).astype(f32)
    rest = swapped(result[tile:], 1)
    mapped = jnp.where(
        core == 0,
        jnp.concatenate([result[:tile], rest], 1),
        jnp.concatenate([rest, result[:tile]], 1),
    )
    return (solved_out, prior_map.astype(f32) + mapped)


def solution(mesh):
    in_specs = (
        P(("groups", "pts"), None),
        P(("groups", "pts"), None),
        P(None, ("groups", "pts"), None),
        P(None, ("groups", "pts"), None),
        P(),
        P("pts"),
        P(("groups", "pts"), None),
        P(),
        P(),
    )
    out_specs = (P(("groups", "pts"), None), P(("groups", "pts"), None))
    return jax.shard_map(body, mesh=mesh, in_specs=in_specs, out_specs=out_specs, check_vma=False)
```

time: 194 us -> 98 us (0.51)
  waiting for transfers between devices: 87.1 us -> 26.3 us
  local copies, waits for them, and re-layouts: 53.2 us -> 19.6 us
  starting transfers between devices: 27.6 us -> 18.2 us
  matrix products: 19.7 us -> 25.2 us
    gather x2 -> x0, local copies, waits for them, and re-layouts: 48.3 us -> none  [the longest x1 45.5 us: body(): positions = point_pos[point_index]]
    all_to_all x1 -> x0, waiting for transfers between devices: 46.4 us -> none  [body(): lax.all_to_all(outgoing, 'pts', split_axis=0, concat_axis=0, tiled=True)]
    ppermute x15, waiting for transfers between devices: 40.7 us -> 26.3 us  [swapped(): return lax.ppermute(value, 'pts', pairs)]
    all_to_all x1 -> x0, starting transfers between devices: 5.89 us -> none  [body(): lax.all_to_all(outgoing, 'pts', split_axis=0, concat_axis=0, tiled=True)]
    dot_general x16 -> x26, matrix products: 19.7 us -> 24.5 us  [the longest x10 12.8 us: body(): lax.dot_general(right16[i], left16[j], (((0,), (0,)), ((), ())), preferre...]
    select_n x3, other arithmetic: 4.64 us -> 0.12 us  [the longest x2 0.07 us: halves(): return (jnp.where(core == 0, low, high), jnp.where(core == 0, high, low))]
    ppermute x15, starting transfers between devices: 21.8 us -> 18.2 us  [swapped(): return lax.ppermute(value, 'pts', pairs)]
    slice x2 -> x17, local copies, waits for them, and re-layouts: 2.18 us -> 5.16 us  [the longest x1 2.4 us: body(): final_mine = solved_mine + update(basis_left[:bits], share)]
  transfers between devices with their start and end apart: 16 -> 15, of which waited for: 16 -> 8; matrix products, arithmetic and copies ran while one was open for 25% -> 43% of each run, Pallas kernels for 0% -> 0%
where the time goes in v1:
time: 98 us; the launch traced here: 97 us
  waiting for transfers between devices  26.3 us (27%)
  matrix products  25.2 us (26%)
  local copies, waits for them, and re-layouts  19.6 us (20%)
  starting transfers between devices  18.2 us (19%)
  other arithmetic  6.06 us (6%)
  between operations  1.66 us (2%)
    ppermute x15, waiting for transfers between devices, swapped(): return lax.ppermute(value, 'pts', pairs)  26.3 us
    ppermute x15, starting transfers between devices, swapped(): return lax.ppermute(value, 'pts', pairs)  18.2 us
    dot_general x10, matrix products, body(): lax.dot_general(right16[i], left16[j], (((0,), (0,)), ((), ())), preferre...  12.8 us
    unnamed x62, local copies, waits for them, and re-layouts  4.56 us
    dot_general x4, matrix products, body(): partial = jnp.dot(weight, coeffs, preferred_element_type=f32)  4.51 us
    dot_general x3, matrix products, update(): jnp.einsum('lpr,lrs->ps', left, part.astype(left.dtype), precision=HIGH,...  2.63 us
    slice x1, local copies, waits for them, and re-layouts, body(): final_mine = solved_mine + update(basis_left[:bits], share)  2.4 us
    reshape x3, local copies, waits for them, and re-layouts, body(): solved = solved + update.reshape(rows, samples)  2.2 us
  transfers between devices with their start and end apart: 15, of which 8 were waited for; matrix products, arithmetic and copies ran while one was open for 43% of the time, Pallas kernels for 0%

profile of v1, /device:TPU:0, one launch (start us, length us, event | category | flops | bytes accessed | tf_op | source)
XLA Modules:
  0.0 97.0 jit_solution(12330367925903409040)
XLA Ops:
  0.7 2.4 %slice.640 = bf16[5,512,128]{2,1,0:T(8,128)(2,1)} slice(f32[7,512,128]{2,1,0:T(8,128)} %param.11), slice={[0:5], [0:512], [0:128]} | slice | bytes 1310720 | tf_op jit(solution)/shard_map/slice | solution.py:138
  3.1 0.5 collective-permute-start.7
  3.5 1.9 %fusion.147 = (f32[1,512,128]{2,1,0:T(8,128)}, f32[1,512,128]{2,1,0:T(8,128)}) fusion(f32[7,512,128]{2,1,0:T(8,128)} %param.11), kind=kLoop, calls=%fused_computation.291 | loop fusion | bytes 1048576 | tf_op jit(solution)/shard_map/slice | solution.py:80
  5.4 0.7 fusion.148
  6.5 0.6 convolution_bitcast_fusion
  7.2 0.4 fusion.160
  8.1 0.4 convolution_bitcast_fusion.2
  8.5 1.3 %fusion.161 = f32[2,256,256]{1,2,0:T(8,128)S(1)} fusion(f32[2,128,256]{1,2,0:T(8,128)S(1)} %reverse.3, f32[2,256,128]{2,1,0:T(8,128)} %bitcast.262), kind=kOutput, calls=%fused_computation.305 | convolution fusion | flops 100663296 | bytes 1048576 | tf_op jit(solution)/shard_map/nhpr,nhrs->nhps/dot_general | solution.py:82
  9.9 1.0 %copy.52 = f32[512,256]{0,1:T(8,128)} copy(f32[512,256]{1,0:T(8,128)S(1)} %bitcast.259) | data formatting | bytes 1048576 | tf_op jit(solution)/shard_map/reshape | solution.py:83
  10.9 1.0 %copy.48 = f32[512,256]{0,1:T(8,128)} copy(f32[512,256]{1,0:T(8,128)S(1)} %bitcast.256) | data formatting | bytes 1048576 | tf_op jit(solution)/shard_map/reshape | solution.py:83
  11.9 1.0 %copy.47 = f32[512,256]{0,1:T(8,128)} copy(f32[512,256]{1,0:T(8,128)S(1)} %bitcast.254) | data formatting | bytes 1048576 | tf_op jit(solution)/shard_map/reshape | solution.py:74
  12.9 0.4 copy.74
  13.4 0.5 copy-done.3
  13.9 0.4 copy-done.4
  14.7 0.7 fusion.162
  15.5 1.1 %constant_dynamic-update-slice_fusion.10 = (bf16[1936,128]{1,0:T(8,128)(2,1)S(1)}, f32[128,128]{1,0:T(8,128)S(1)}) fusion(bf16[1936,128]{1,0:T(8,128)(2,1)S(1)} %constant_dynamic-update-slice_fusion.11, bf16[5,512,128]{2,1,0:T(8,128)(2,1)} %slice.640, bf16[5,512,128]{1,2,0:T(8,128)(2,1)S(1)} %convert_element_type.251), kind=kOutput, calls=%fused_computation.95 | convolution fusion | flops 16793600 | bytes 360448 | tf_op jit(solution)/shard_map/dot_general | solution.py:61
  16.6 1.1 %constant_dynamic-update-slice_fusion.9 = (bf16[1936,128]{1,0:T(8,128)(2,1)S(1)}, f32[128,128]{1,0:T(8,128)S(1)}) fusion(bf16[1936,128]{1,0:T(8,128)(2,1)S(1)} %get-tuple-element.76, bf16[5,512,128]{2,1,0:T(8,128)(2,1)} %slice.640, bf16[5,512,128]{1,2,0:T(8,128)(2,1)S(1)} %convert_element_type.251), kind=kOutput, calls=%fused_computation.94 | convolution fusion | flops 16793600 | bytes 360448 | tf_op jit(solution)/shard_map/dot_general | solution.py:61
  17.7 1.1 %constant_dynamic-update-slice_fusion.8 = (bf16[1936,128]{1,0:T(8,128)(2,1)S(1)}, f32[128,128]{1,0:T(8,128)S(1)}) fusion(bf16[1936,128]{1,0:T(8,128)(2,1)S(1)} %get-tuple-element.78, bf16[5,512,128]{2,1,0:T(8,128)(2,1)} %slice.640, bf16[5,512,128]{1,2,0:T(8,128)(2,1)S(1)} %convert_element_type.251), kind=kOutput, calls=%fused_computation.93 | convolution fusion | flops 16793600 | bytes 360448 | tf_op jit(solution)/shard_map/dot_general | solution.py:61
  18.9 1.1 %constant_dynamic-update-slice_fusion.7 = (bf16[1936,128]{1,0:T(8,128)(2,1)S(1)}, f32[128,128]{1,0:T(8,128)S(1)}) fusion(bf16[1936,128]{1,0:T(8,128)(2,1)S(1)} %get-tuple-element.80, bf16[5,512,128]{2,1,0:T(8,128)(2,1)} %slice.640, bf16[5,512,128]{1,2,0:T(8,128)(2,1)S(1)} %convert_element_type.251), kind=kOutput, calls=%fused_computation.92 | convolution fusion | flops 16793600 | bytes 360448 | tf_op jit(solution)/shard_map/dot_general | solution.py:61
  20.0 1.1 %constant_dynamic-update-slice_fusion.6 = (bf16[1936,128]{1,0:T(8,128)(2,1)S(1)}, f32[128,128]{1,0:T(8,128)S(1)}) fusion(bf16[1936,128]{1,0:T(8,128)(2,1)S(1)} %get-tuple-element.82, bf16[5,512,128]{2,1,0:T(8,128)(2,1)} %slice.640, bf16[5,512,128]{1,2,0:T(8,128)(2,1)S(1)} %convert_element_type.251), kind=kOutput, calls=%fused_computation.91 | convolution fusion | flops 16793600 | bytes 360448 | tf_op jit(solution)/shard_map/dot_general | solution.py:61
  21.1 1.1 %constant_dynamic-update-slice_fusion.5 = (bf16[1936,128]{1,0:T(8,128)(2,1)S(1)}, f32[128,128]{1,0:T(8,128)S(1)}) fusion(bf16[1936,128]{1,0:T(8,128)(2,1)S(1)} %get-tuple-element.84, bf16[5,512,128]{2,1,0:T(8,128)(2,1)} %slice.640, bf16[5,512,128]{1,2,0:T(8,128)(2,1)S(1)} %convert_element_type.251), kind=kOutput, calls=%fused_computation.90 | convolution fusion | flops 16793600 | bytes 360448 | tf_op jit(solution)/shard_map/dot_general | solution.py:61
  22.2 1.1 %constant_dynamic-update-slice_fusion.4 = (bf16[1936,128]{1,0:T(8,128)(2,1)S(1)}, bf16[128,128]{1,0:T(8,128)(2,1)S(1)}) fusion(bf16[1936,128]{1,0:T(8,128)(2,1)S(1)} %get-tuple-element.86, bf16[5,512,128]{2,1,0:T(8,128)(2,1)} %slice.640, bf16[5,512,128]{1,2,0:T(8,128)(2,1)S(1)} %convert_element_type.251), kind=kOutput, calls=%fused_computation.89 | convolution fusion | flops 16793600 | bytes 327680 | tf_op jit(solution)/shard_map/dot_general | solution.py:61
  23.3 1.7 %constant_dynamic-update-slice_fusion.3 = (bf16[1936,128]{1,0:T(8,128)(2,1)S(1)}, bf16[128,128]{1,0:T(8,128)(2,1)}) fusion(bf16[1936,128]{1,0:T(8,128)(2,1)S(1)} %get-tuple-element.88, bf16[5,512,128]{2,1,0:T(8,128)(2,1)} %slice.640, bf16[5,512,128]{1,2,0:T(8,128)(2,1)S(1)} %convert_element_type.251), kind=kOutput, calls=%fused_computation.88 | convolution fusion | flops 16793600 | bytes 327680 | tf_op jit(solution)/shard_map/dot_general | solution.py:61
  25.0 1.7 %constant_dynamic-update-slice_fusion.2 = (bf16[1936,128]{1,0:T(8,128)(2,1)S(1)}, bf16[128,128]{1,0:T(8,128)(2,1)}) fusion(bf16[1936,128]{1,0:T(8,128)(2,1)S(1)} %get-tuple-element.90, bf16[5,512,128]{2,1,0:T(8,128)(2,1)} %slice.640, bf16[5,512,128]{1,2,0:T(8,128)(2,1)S(1)} %convert_element_type.251), kind=kOutput, calls=%fused_computation.87 | convolution fusion | flops 16793600 | bytes 327680 | tf_op jit(solution)/shard_map/dot_general | solution.py:61
  26.7 1.7 %constant_dynamic-update-slice_fusion.1 = (bf16[1936,128]{1,0:T(8,128)(2,1)S(1)}, bf16[128,128]{1,0:T(8,128)(2,1)}) fusion(bf16[1936,128]{1,0:T(8,128)(2,1)S(1)} %get-tuple-element.92, bf16[5,512,128]{2,1,0:T(8,128)(2,1)} %slice.640, bf16[5,512,128]{1,2,0:T(8,128)(2,1)S(1)} %convert_element_type.251), kind=kOutput, calls=%fused_computation.86 | convolution fusion | flops 16793600 | bytes 327680 | tf_op jit(solution)/shard_map/dot_general | solution.py:61
  28.6 0.5 collective-permute-start.6
  30.6 0.7 add_bitcast_fusion.1
  31.4 1.1 %fusion.16 = f32[512,128]{1,0:T(8,128)S(1)} fusion(bf16[512,128]{1,0:T(8,128)(2,1)S(1)} %get-tuple-element.41, bf16[128,128]{1,0:T(8,128)(2,1)} %get-tuple-element.95, bf16[128,128]{1,0:T(8,128)(2,1)} %get-tuple-element.93, bf16[128,128]{1,0:T(8,128)(2,1)} %get-tuple-element.91, bf16[128,128]{1,0:T(8,128)(2,1)S(1)} %get-tuple-element.89, ...), kind=kOutput, calls=%fused_computation.40 | convolution fusion | flops 34996224 | bytes 589824 | tf_op jit(solution)/shard_map/dot_general | solution.py:120
  33.0 2.6 %collective-permute-start.1 = (bf16[1296,128]{1,0:T(8,128)(2,1)S(1)}, bf16[1296,128]{1,0:T(8,128)(2,1)S(1)}, u32[]{:S(2)}, u32[]{:S(2)}) collective-permute-start(bf16[1296,128]{1,0:T(8,128)(2,1)S(1)} %constant_dynamic-update-slice_fusion.12), channel_id=1, source_target_pairs={{0,2},{1,3},{2,0},{3,1},{4,6},{5,7},{6,4},{7,5},{8,10},{9,11},{10,... | collective-permute-start | bytes 995336 | tf_op jit(solution)/shard_map/ppermute | solution.py:15
  35.6 1.4 %fusion.155 = (f32[512]{0:T(512)S(1)}, f32[512]{0:T(512)}) fusion(f32[16384]{0:T(1024)} %param.13, s32[]{:T(128)S(6)} %select_n.108, s32[]{:T(128)S(6)} %select_n.109), kind=kLoop, calls=%fused_computation.299 | loop fusion | bytes 8200 | tf_op jit(solution)/shard_map/dynamic_slice | solution.py:159
  37.0 7.0 %collective-permute-done.1 = bf16[1296,128]{1,0:T(8,128)(2,1)S(1)} collective-permute-done((bf16[1296,128]{1,0:T(8,128)(2,1)S(1)}, bf16[1296,128]{1,0:T(8,128)(2,1)S(1)}, u32[]{:S(2)}, u32[]{:S(2)}) %collective-permute-start.1) | collective-permute-done | bytes 331808 | tf_op jit(solution)/shard_map/ppermute | solution.py:15
  44.5 0.9 constant_dynamic-update-slice_fusion.22
  45.4 0.8 constant_dynamic-update-slice_fusion.21
  46.2 1.8 %collective-permute-start.2 = (bf16[784,128]{1,0:T(8,128)(2,1)S(1)}, bf16[784,128]{1,0:T(8,128)(2,1)S(1)}, u32[]{:S(2)}, u32[]{:S(2)}) collective-permute-start(bf16[784,128]{1,0:T(8,128)(2,1)S(1)} %constant_dynamic-update-slice_fusion.20), channel_id=1, source_target_pairs={{0,4},{1,5},{2,6},{3,7},{4,0},{5,1},{6,2},{7,3},{8,12},{9,13},{10,... | collective-permute-start | bytes 602120 | tf_op jit(solution)/shard_map/ppermute | solution.py:15
  48.1 5.0 %collective-permute-done.2 = bf16[784,128]{1,0:T(8,128)(2,1)S(1)} collective-permute-done((bf16[784,128]{1,0:T(8,128)(2,1)S(1)}, bf16[784,128]{1,0:T(8,128)(2,1)S(1)}, u32[]{:S(2)}, u32[]{:S(2)}) %collective-permute-start.2) | collective-permute-done | bytes 200736 | tf_op jit(solution)/shard_map/ppermute | solution.py:15
  53.4 0.9 add_convert_fusion
  54.3 1.7 %collective-permute-start.3 = (bf16[400,128]{1,0:T(8,128)(2,1)S(1)}, bf16[400,128]{1,0:T(8,128)(2,1)S(1)}, u32[]{:S(2)}, u32[]{:S(2)}) collective-permute-start(bf16[400,128]{1,0:T(8,128)(2,1)S(1)} %pad_maximum_fusion.1), channel_id=1, source_target_pairs={{0,8},{1,9},{2,10},{3,11},{4,12},{5,13},{6,14},{7,15},{8,0},{9,1},... | collective-permute-start | bytes 307208 | tf_op jit(solution)/shard_map/ppermute | solution.py:15
  56.0 3.0 %collective-permute-done.3 = bf16[400,128]{1,0:T(8,128)(2,1)S(1)} collective-permute-done((bf16[400,128]{1,0:T(8,128)(2,1)S(1)}, bf16[400,128]{1,0:T(8,128)(2,1)S(1)}, u32[]{:S(2)}, u32[]{:S(2)}) %collective-permute-start.3) | collective-permute-done | bytes 102432 | tf_op jit(solution)/shard_map/ppermute | solution.py:15
  59.3 2.7 %collective-permute-start.4 = (bf16[160,128]{1,0:T(8,128)(2,1)S(1)}, bf16[160,128]{1,0:T(8,128)(2,1)S(1)}, u32[]{:S(2)}, u32[]{:S(2)}) collective-permute-start(bf16[160,128]{1,0:T(8,128)(2,1)S(1)} %pad_maximum_fusion.2), channel_id=1, source_target_pairs={{0,16},{1,17},{2,18},{3,19},{4,20},{5,21},{6,22},{7,23},{8,24},{9,... | collective-permute-start | bytes 122888 | tf_op jit(solution)/shard_map/ppermute | solution.py:15
  62.0 0.6 pad_maximum_fusion.3
  62.6 0.7 copy.63
  63.3 0.7 copy.64
  64.3 0.8 constant_dynamic-update-slice_fusion.33
  65.1 0.8 constant_dynamic-update-slice_fusion.31
  66.0 0.8 constant_dynamic-update-slice_fusion.25
  66.7 0.9 constant_dynamic-update-slice_fusion.30
  67.6 0.6 fusion.157
  68.2 1.5 %fusion.7 = bf16[512,128]{0,1:T(8,128)(2,1)S(1)} fusion(f32[512,128]{0,1:T(8,128)} %collective-permute-done.6, bf16[5,128,128]{2,1,0:T(8,128)(2,1)S(1)} %constant_dynamic-update-slice_fusion.30, bf16[5,512,128]{2,1,0:T(8,128)(2,1)} %collective-permute-done.7), kind=kOutput, calls=%fused_computation.18 | convolution fusion | flops 84017152 | bytes 1212416 | tf_op jit(solution)/shard_map/lpr,lrs->ps/dot_general | solution.py:136
  69.9 1.1 %convolution_convert_fusion.2 = bf16[512,128]{1,0:T(8,128)(2,1)S(1)} fusion(pred[64,8,8,128]{3,2,1,0:T(8,128)(4,1)S(1)} %bitcast.268, f32[512]{0:T(512)S(1)} %bitcast.283, f32[1024]{0:T(1024)S(1)} %copy-done.25, bf16[512,128]{0,1:T(8,128)(2,1)S(1)} %fusion.7, bf16[512,128]{0,1:T(8,128)(2,1)S(1)} %get-tuple-element.96), kind=kOutput, calls=%fused_computation.21 | convolution fusion | flops 141623296 | bytes 923648 | tf_op jit(solution)/shard_map/dot_general | solution.py:173
  71.1 1.6 %collective-permute-start.8 = (bf16[512,128]{1,0:T(8,128)(2,1)S(1)}, bf16[512,128]{1,0:T(8,128)(2,1)S(1)}, u32[]{:S(2)}, u32[]{:S(2)}) collective-permute-start(bf16[512,128]{1,0:T(8,128)(2,1)S(1)} %convolution_convert_fusion.2), channel_id=1, source_target_pairs={{0,2},{1,3},{2,0},{3,1},{4,6},{5,7},{6,4},{7,5},{8,10},{9,11},{10,... | collective-permute-start | bytes 393224 | tf_op jit(solution)/shard_map/ppermute | solution.py:15
  72.9 1.1 %convolution_convert_fusion.1 = bf16[512,128]{1,0:T(8,128)(2,1)S(1)} fusion(pred[64,8,8,128]{3,2,1,0:T(8,128)(4,1)S(1)} %bitcast.269, f32[512]{0:T(512)S(1)} %bitcast.282, f32[1024]{0:T(1024)S(1)} %copy-done.25, bf16[512,128]{0,1:T(8,128)(2,1)S(1)} %fusion.7, bf16[512,128]{0,1:T(8,128)(2,1)S(1)} %get-tuple-element.96), kind=kOutput, calls=%fused_computation.20 | convolution fusion | flops 141623296 | bytes 923648 | tf_op jit(solution)/shard_map/dot_general | solution.py:173
  74.0 1.6 %collective-permute-start.9 = (bf16[512,128]{1,0:T(8,128)(2,1)S(1)}, bf16[512,128]{1,0:T(8,128)(2,1)S(1)}, u32[]{:S(2)}, u32[]{:S(2)}) collective-permute-start(bf16[512,128]{1,0:T(8,128)(2,1)S(1)} %convolution_convert_fusion.1), channel_id=1, source_target_pairs={{0,4},{1,5},{2,6},{3,7},{4,0},{5,1},{6,2},{7,3},{8,12},{9,13},{10,... | collective-permute-start | bytes 393224 | tf_op jit(solution)/shard_map/ppermute | solution.py:15
  75.8 1.1 %convolution_convert_fusion = bf16[512,128]{1,0:T(8,128)(2,1)S(1)} fusion(pred[64,8,8,128]{3,2,1,0:T(8,128)(4,1)S(1)} %bitcast.270, f32[512]{0:T(512)S(1)} %bitcast.281, f32[1024]{0:T(1024)S(1)} %copy-done.25, bf16[512,128]{0,1:T(8,128)(2,1)S(1)} %fusion.7, bf16[512,128]{0,1:T(8,128)(2,1)S(1)} %get-tuple-element.96), kind=kOutput, calls=%fused_computation.19 | convolution fusion | flops 141623296 | bytes 923648 | tf_op jit(solution)/shard_map/dot_general | solution.py:173
  76.9 0.5 collective-permute-start.10
  77.6 2.3 %collective-permute-done.9 = bf16[512,128]{1,0:T(8,128)(2,1)S(1)} collective-permute-done((bf16[512,128]{1,0:T(8,128)(2,1)S(1)}, bf16[512,128]{1,0:T(8,128)(2,1)S(1)}, u32[]{:S(2)}, u32[]{:S(2)}) %collective-permute-start.9) | collective-permute-done | bytes 131104 | tf_op jit(solution)/shard_map/ppermute | solution.py:15
  79.9 2.9 %collective-permute-done.10 = bf16[512,128]{1,0:T(8,128)(2,1)S(1)} collective-permute-done((bf16[512,128]{1,0:T(8,128)(2,1)S(1)}, bf16[512,128]{1,0:T(8,128)(2,1)S(1)}, u32[]{:S(2)}, u32[]{:S(2)}) %collective-permute-start.10) | collective-permute-done | bytes 131104 | tf_op jit(solution)/shard_map/ppermute | solution.py:15
  83.1 1.2 %fusion.158 = (bf16[512,128]{1,0:T(8,128)(2,1)S(1)}, f32[512,128]{1,0:T(8,128)S(1)}) fusion(bf16[512,128]{1,0:T(8,128)(2,1)S(1)} %collective-permute-done.10, bf16[512,128]{1,0:T(8,128)(2,1)S(1)} %collective-permute-done.9, bf16[512,128]{1,0:T(8,128)(2,1)S(1)} %collective-permute-done.8, bf16[512,128]{0,1:T(8,128)(2,1)S(1)} %fusion.7, ...), kind=kOutput, calls=%fused_computation.302 | convolution fusion | flops 142016512 | bytes 1579008 | tf_op jit(solution)/shard_map/dot_general | solution.py:173
  84.3 1.6 %collective-permute-start.11 = (bf16[128,128]{1,0:T(8,128)(2,1)S(1)}, bf16[128,128]{1,0:T(8,128)(2,1)S(1)}, u32[]{:S(2)}, u32[]{:S(2)}) collective-permute-start(bf16[128,128]{1,0:T(8,128)(2,1)S(1)} %get-tuple-element.46), channel_id=1, source_target_pairs={{0,8},{1,9},{2,10},{3,11},{4,12},{5,13},{6,14},{7,15},{8,0},{9,1},... | collective-permute-start | bytes 98312 | tf_op jit(solution)/shard_map/ppermute | solution.py:15
  85.9 2.9 %collective-permute-start.12 = (bf16[128,128]{1,0:T(8,128)(2,1)S(1)}, bf16[128,128]{1,0:T(8,128)(2,1)S(1)}, u32[]{:S(2)}, u32[]{:S(2)}) collective-permute-start(bf16[128,128]{1,0:T(8,128)(2,1)S(1)} %get-tuple-element.48), channel_id=1, source_target_pairs={{0,16},{1,17},{2,18},{3,19},{4,20},{5,21},{6,22},{7,23},{8,24},{9,... | collective-permute-start | bytes 98312 | tf_op jit(solution)/shard_map/ppermute | solution.py:15
  88.8 2.2 %collective-permute-done.12 = bf16[128,128]{1,0:T(8,128)(2,1)S(1)} collective-permute-done((bf16[128,128]{1,0:T(8,128)(2,1)S(1)}, bf16[128,128]{1,0:T(8,128)(2,1)S(1)}, u32[]{:S(2)}, u32[]{:S(2)}) %collective-permute-start.12) | collective-permute-done | bytes 32800 | tf_op jit(solution)/shard_map/ppermute | solution.py:15
  91.0 3.5 %collective-permute-done.13 = bf16[128,128]{1,0:T(8,128)(2,1)S(1)} collective-permute-done((bf16[128,128]{1,0:T(8,128)(2,1)S(1)}, bf16[128,128]{1,0:T(8,128)(2,1)S(1)}, u32[]{:S(2)}, u32[]{:S(2)}) %collective-permute-start.13) | collective-permute-done | bytes 32800 | tf_op jit(solution)/shard_map/ppermute | solution.py:15
  94.7 0.6 fusion.4
  95.3 1.0 %copy.66 = f32[512,256]{1,0:T(8,128)} copy(f32[512,256]{0,1:T(8,128)S(1)} %maximum_select_fusion) | data formatting | bytes 1048576
  96.3 0.6 fusion.72
  (158 shorter events, 6.1 us)
Async XLA Ops:
  0.6 5.5 %copy-start = (bf16[512,256]{1,0:T(8,128)(2,1)S(1)}, bf16[512,256]{1,0:T(8,128)(2,1)}, u32[]{:S(2)}) copy-start(bf16[512,256]{1,0:T(8,128)(2,1)} %param.9) | copy-start | bytes 786436
  0.6 4.7 %copy-start.2 = (f32[7,512,128]{2,1,0:T(8,128)S(1)}, f32[7,512,128]{2,1,0:T(8,128)}, u32[]{:S(2)}) copy-start(f32[7,512,128]{2,1,0:T(8,128)} %param.12) | copy-start | bytes 5505028
  3.1 65.2 %collective-permute-start.7 = (bf16[5,512,128]{2,1,0:T(8,128)(2,1)}, bf16[5,512,128]{2,1,0:T(8,128)(2,1)}, u32[]{:S(2)}, u32[]{:S(2)}) collective-permute-start(bf16[5,512,128]{2,1,0:T(8,128)(2,1)} %slice.640), channel_id=1, source_target_pairs={{0,1},{1,0},{2,3},{3,2},{4,5},{5,4},{6,7},{7,6},{8,9},{9,8},{10,11... | collective-permute-start | bytes 1966088 | tf_op jit(solution)/shard_map/ppermute | solution.py:15
  5.4 0.9 copy-start.16
  6.1 1.1 %copy-start.7 = (f32[1,512,128]{2,1,0:T(8,128)S(1)}, f32[1,512,128]{2,1,0:T(8,128)}, u32[]{:S(2)}) copy-start(f32[1,512,128]{2,1,0:T(8,128)} %get-tuple-element.37) | copy-start | bytes 786436
  7.2 1.0 copy-start.9
  9.9 3.0 %slice-start = ((f32[7,512,128]{2,1,0:T(8,128)}), f32[5,512,128]{2,1,0:T(8,128)S(1)}, s32[]{:S(2)}) async-start(f32[7,512,128]{2,1,0:T(8,128)} %param.12), calls=%async_computation | async-start | bytes 2621440 | tf_op jit(solution)/shard_map/slice | solution.py:86
  12.9 1.0 %copy-start.3 = (f32[512,256]{0,1:T(8,128)S(1)}, f32[512,256]{0,1:T(8,128)}, u32[]{:S(2)}) copy-start(f32[512,256]{0,1:T(8,128)} %copy.52) | copy-start | bytes 1572868
  13.3 1.1 %copy-start.4 = (f32[512,256]{0,1:T(8,128)S(1)}, f32[512,256]{0,1:T(8,128)}, u32[]{:S(2)}) copy-start(f32[512,256]{0,1:T(8,128)} %copy.48) | copy-start | bytes 1572868
  13.3 1.2 %copy-start.5 = (f32[512,256]{0,1:T(8,128)S(1)}, f32[512,256]{0,1:T(8,128)}, u32[]{:S(2)}) copy-start(f32[512,256]{0,1:T(8,128)} %copy.47) | copy-start | bytes 1572868
  15.5 12.9 %copy-start.21 = (f32[64]{0:T(128)S(1)}, f32[64]{0:T(128)}, u32[]{:S(2)}) copy-start(f32[64]{0:T(128)} %param.14) | copy-start | bytes 772
  16.6 27.9 %copy-start.8 = (f32[128,128]{1,0:T(8,128)}, f32[128,128]{1,0:T(8,128)S(1)}, u32[]{:S(2)}) copy-start(f32[128,128]{1,0:T(8,128)S(1)} %get-tuple-element.77) | copy-start | bytes 196612
  17.7 15.1 %copy-start.13 = (f32[128,128]{1,0:T(8,128)}, f32[128,128]{1,0:T(8,128)S(1)}, u32[]{:S(2)}) copy-start(f32[128,128]{1,0:T(8,128)S(1)} %get-tuple-element.79) | copy-start | bytes 196612
  17.7 11.4 %copy-start.18 = (s32[32,32]{1,0:T(8,128)S(1)}, s32[32,32]{1,0:T(8,128)}, u32[]{:S(2)}) copy-start(s32[32,32]{1,0:T(8,128)} %param.17) | copy-start | bytes 12292
  17.7 11.4 %copy-start.19 = (s32[32,32]{1,0:T(8,128)S(1)}, s32[32,32]{1,0:T(8,128)}, u32[]{:S(2)}) copy-start(s32[32,32]{1,0:T(8,128)} %param.16) | copy-start | bytes 12292
  18.9 14.0 %copy-start.11 = (f32[128,128]{1,0:T(8,128)}, f32[128,128]{1,0:T(8,128)S(1)}, u32[]{:S(2)}) copy-start(f32[128,128]{1,0:T(8,128)S(1)} %get-tuple-element.81) | copy-start | bytes 196612
  28.5 2.9 %collective-permute-start = (bf16[1936,128]{1,0:T(8,128)(2,1)S(1)}, bf16[1936,128]{1,0:T(8,128)(2,1)S(1)}, u32[]{:S(2)}, u32[]{:S(2)}) collective-permute-start(bf16[1936,128]{1,0:T(8,128)(2,1)S(1)} %constant_dynamic-update-slice_fusion), channel_id=1, source_target_pairs={{0,1},{1,0},{2,3},{3,2},{4,5},{5,4},{6,7},{7,6},{8,9},{9,8},{10,11... | collective-permute-start | bytes 1486856 | tf_op jit(solution)/shard_map/ppermute | solution.py:15
  28.6 39.6 %collective-permute-start.6 = (f32[512,128]{0,1:T(8,128)S(1)}, f32[512,128]{0,1:T(8,128)}, u32[]{:S(2)}, u32[]{:S(2)}) collective-permute-start(f32[512,128]{0,1:T(8,128)S(1)} %slice_select_fusion.1), channel_id=1, source_target_pairs={{0,1},{1,0},{2,3},{3,2},{4,5},{5,4},{6,7},{7,6},{8,9},{9,8},{10,11... | collective-permute-start | bytes 786440 | tf_op jit(solution)/shard_map/ppermute | solution.py:15
  31.3 1.6 %copy-start.6 = (f32[5,128,128]{2,1,0:T(8,128)}, f32[5,128,128]{2,1,0:T(8,128)S(1)}, u32[]{:S(2)}) copy-start(f32[5,128,128]{2,1,0:T(8,128)S(1)} %slice_select_fusion) | copy-start | bytes 983044
  31.3 13.1 %copy-start.10 = (bf16[1936,128]{1,0:T(8,128)(2,1)}, bf16[1936,128]{1,0:T(8,128)(2,1)S(1)}, u32[]{:S(2)}) copy-start(bf16[1936,128]{1,0:T(8,128)(2,1)S(1)} %collective-permute-done) | copy-start | bytes 1486852
  32.8 11.6 %copy-start.14 = (f32[128,128]{1,0:T(8,128)S(1)}, f32[128,128]{1,0:T(8,128)}, u32[]{:S(2)}) copy-start(f32[128,128]{1,0:T(8,128)} %copy-done.13) | copy-start | bytes 196612
  32.9 12.5 %copy-start.12 = (f32[128,128]{1,0:T(8,128)S(1)}, f32[128,128]{1,0:T(8,128)}, u32[]{:S(2)}) copy-start(f32[128,128]{1,0:T(8,128)} %copy-done.11) | copy-start | bytes 196612
  33.0 11.0 %collective-permute-start.1 = (bf16[1296,128]{1,0:T(8,128)(2,1)S(1)}, bf16[1296,128]{1,0:T(8,128)(2,1)S(1)}, u32[]{:S(2)}, u32[]{:S(2)}) collective-permute-start(bf16[1296,128]{1,0:T(8,128)(2,1)S(1)} %constant_dynamic-update-slice_fusion.12), channel_id=1, source_target_pairs={{0,2},{1,3},{2,0},{3,1},{4,6},{5,7},{6,4},{7,5},{8,10},{9,11},{10,... | collective-permute-start | bytes 995336 | tf_op jit(solution)/shard_map/ppermute | solution.py:15
  44.0 9.4 %copy-start.15 = (bf16[1296,128]{1,0:T(8,128)(2,1)}, bf16[1296,128]{1,0:T(8,128)(2,1)S(1)}, u32[]{:S(2)}) copy-start(bf16[1296,128]{1,0:T(8,128)(2,1)S(1)} %collective-permute-done.1) | copy-start | bytes 995332
  44.4 17.7 %copy-start.22 = (f32[512]{0:T(512)S(1)}, f32[512]{0:T(512)}, u32[]{:S(2)}) copy-start(f32[512]{0:T(512)} %get-tuple-element.54) | copy-start | bytes 6148
  44.4 19.6 %copy-start.24 = (pred[4,2,8]{2,0,1:T(4,128)(4,1)S(1)}, pred[4,2,8]{2,0,1:T(4,128)(4,1)}, u32[]{:S(2)}) copy-start(pred[4,2,8]{2,0,1:T(4,128)(4,1)} %get-tuple-element.61) | copy-start | bytes 196
  44.5 23.1 %copy-start.1 = (f32[7,512,128]{2,1,0:T(8,128)S(1)}, f32[7,512,128]{2,1,0:T(8,128)}, u32[]{:S(2)}) copy-start(f32[7,512,128]{2,1,0:T(8,128)} %param.11) | copy-start | bytes 5505028
  46.2 6.8 %collective-permute-start.2 = (bf16[784,128]{1,0:T(8,128)(2,1)S(1)}, bf16[784,128]{1,0:T(8,128)(2,1)S(1)}, u32[]{:S(2)}, u32[]{:S(2)}) collective-permute-start(bf16[784,128]{1,0:T(8,128)(2,1)S(1)} %constant_dynamic-update-slice_fusion.20), channel_id=1, source_target_pairs={{0,4},{1,5},{2,6},{3,7},{4,0},{5,1},{6,2},{7,3},{8,12},{9,13},{10,... | collective-permute-start | bytes 602120 | tf_op jit(solution)/shard_map/ppermute | solution.py:15
  54.3 4.7 %collective-permute-start.3 = (bf16[400,128]{1,0:T(8,128)(2,1)S(1)}, bf16[400,128]{1,0:T(8,128)(2,1)S(1)}, u32[]{:S(2)}, u32[]{:S(2)}) collective-permute-start(bf16[400,128]{1,0:T(8,128)(2,1)S(1)} %pad_maximum_fusion.1), channel_id=1, source_target_pairs={{0,8},{1,9},{2,10},{3,11},{4,12},{5,13},{6,14},{7,15},{8,0},{9,1},... | collective-permute-start | bytes 307208 | tf_op jit(solution)/shard_map/ppermute | solution.py:15
  59.1 4.9 %copy-start.17 = (bf16[400,128]{1,0:T(8,128)(2,1)}, bf16[400,128]{1,0:T(8,128)(2,1)S(1)}, u32[]{:S(2)}) copy-start(bf16[400,128]{1,0:T(8,128)(2,1)S(1)} %collective-permute-done.3) | copy-start | bytes 307204
  59.3 5.0 %collective-permute-start.4 = (bf16[160,128]{1,0:T(8,128)(2,1)S(1)}, bf16[160,128]{1,0:T(8,128)(2,1)S(1)}, u32[]{:S(2)}, u32[]{:S(2)}) collective-permute-start(bf16[160,128]{1,0:T(8,128)(2,1)S(1)} %pad_maximum_fusion.2), channel_id=1, source_target_pairs={{0,16},{1,17},{2,18},{3,19},{4,20},{5,21},{6,22},{7,23},{8,24},{9,... | collective-permute-start | bytes 122888 | tf_op jit(solution)/shard_map/ppermute | solution.py:15
  67.6 2.3 %copy-start.25 = (f32[1024]{0:T(1024)S(1)}, f32[1024]{0:T(1024)}, u32[]{:S(2)}) copy-start(f32[1024]{0:T(1024)} %pad_maximum_fusion.3) | copy-start | bytes 12292
  71.1 6.4 %collective-permute-start.8 = (bf16[512,128]{1,0:T(8,128)(2,1)S(1)}, bf16[512,128]{1,0:T(8,128)(2,1)S(1)}, u32[]{:S(2)}, u32[]{:S(2)}) collective-permute-start(bf16[512,128]{1,0:T(8,128)(2,1)S(1)} %convolution_convert_fusion.2), channel_id=1, source_target_pairs={{0,2},{1,3},{2,0},{3,1},{4,6},{5,7},{6,4},{7,5},{8,10},{9,11},{10,... | collective-permute-start | bytes 393224 | tf_op jit(solution)/shard_map/ppermute | solution.py:15
  74.0 5.9 %collective-permute-start.9 = (bf16[512,128]{1,0:T(8,128)(2,1)S(1)}, bf16[512,128]{1,0:T(8,128)(2,1)S(1)}, u32[]{:S(2)}, u32[]{:S(2)}) collective-permute-start(bf16[512,128]{1,0:T(8,128)(2,1)S(1)} %convolution_convert_fusion.1), channel_id=1, source_target_pairs={{0,4},{1,5},{2,6},{3,7},{4,0},{5,1},{6,2},{7,3},{8,12},{9,13},{10,... | collective-permute-start | bytes 393224 | tf_op jit(solution)/shard_map/ppermute | solution.py:15
  75.8 1.6 %copy-start.23 = (pred[4,2,8]{2,0,1:T(4,128)(4,1)S(1)}, pred[4,2,8]{2,0,1:T(4,128)(4,1)}, u32[]{:S(2)}) copy-start(pred[4,2,8]{2,0,1:T(4,128)(4,1)} %get-tuple-element.60) | copy-start | bytes 196
  76.9 5.9 %collective-permute-start.10 = (bf16[512,128]{1,0:T(8,128)(2,1)S(1)}, bf16[512,128]{1,0:T(8,128)(2,1)S(1)}, u32[]{:S(2)}, u32[]{:S(2)}) collective-permute-start(bf16[512,128]{1,0:T(8,128)(2,1)S(1)} %convolution_convert_fusion), channel_id=1, source_target_pairs={{0,6},{1,7},{2,4},{3,5},{4,2},{5,3},{6,0},{7,1},{8,14},{9,15},{10,... | collective-permute-start | bytes 393224 | tf_op jit(solution)/shard_map/ppermute | solution.py:15
  84.3 4.6 %collective-permute-start.11 = (bf16[128,128]{1,0:T(8,128)(2,1)S(1)}, bf16[128,128]{1,0:T(8,128)(2,1)S(1)}, u32[]{:S(2)}, u32[]{:S(2)}) collective-permute-start(bf16[128,128]{1,0:T(8,128)(2,1)S(1)} %get-tuple-element.46), channel_id=1, source_target_pairs={{0,8},{1,9},{2,10},{3,11},{4,12},{5,13},{6,14},{7,15},{8,0},{9,1},... | collective-permute-start | bytes 98312 | tf_op jit(solution)/shard_map/ppermute | solution.py:15
  85.9 5.1 %collective-permute-start.12 = (bf16[128,128]{1,0:T(8,128)(2,1)S(1)}, bf16[128,128]{1,0:T(8,128)(2,1)S(1)}, u32[]{:S(2)}, u32[]{:S(2)}) collective-permute-start(bf16[128,128]{1,0:T(8,128)(2,1)S(1)} %get-tuple-element.48), channel_id=1, source_target_pairs={{0,16},{1,17},{2,18},{3,19},{4,20},{5,21},{6,22},{7,23},{8,24},{9,... | collective-permute-start | bytes 98312 | tf_op jit(solution)/shard_map/ppermute | solution.py:15
  88.8 5.7 %collective-permute-start.13 = (bf16[128,128]{1,0:T(8,128)(2,1)S(1)}, bf16[128,128]{1,0:T(8,128)(2,1)S(1)}, u32[]{:S(2)}, u32[]{:S(2)}) collective-permute-start(bf16[128,128]{1,0:T(8,128)(2,1)S(1)} %get-tuple-element.47), channel_id=1, source_target_pairs={{0,24},{1,25},{2,26},{3,27},{4,28},{5,29},{6,30},{7,31},{8,16},{9,... | collective-permute-start | bytes 98312 | tf_op jit(solution)/shard_map/ppermute | solution.py:15
  88.8 5.8 %collective-permute-start.5 = (bf16[5,128,128]{2,1,0:T(8,128)(2,1)S(1)}, bf16[5,128,128]{2,1,0:T(8,128)(2,1)S(1)}, u32[]{:S(2)}, u32[]{:S(2)}) collective-permute-start(bf16[5,128,128]{2,1,0:T(8,128)(2,1)S(1)} %constant_dynamic-update-slice_fusion.30), channel_id=1, source_target_pairs={{0,1},{1,0},{2,3},{3,2},{4,5},{5,4},{6,7},{7,6},{8,9},{9,8},{10,11... | collective-permute-start | bytes 491528 | tf_op jit(solution)/shard_map/ppermute | solution.py:15
  94.6 1.7 %copy-start.20 = (bf16[64,256]{1,0:T(8,128)(2,1)S(1)}, bf16[64,256]{1,0:T(8,128)(2,1)}, u32[]{:S(2)}) copy-start(bf16[64,256]{1,0:T(8,128)(2,1)} %param.15) | copy-start | bytes 98308
  94.6 1.7 %collective-permute-start.14 = (f32[64,128]{1,0:T(8,128)S(1)}, f32[64,128]{1,0:T(8,128)S(1)}, u32[]{:S(2)}, u32[]{:S(2)}) collective-permute-start(f32[64,128]{1,0:T(8,128)S(1)} %get-tuple-element.52), channel_id=1, source_target_pairs={{0,1},{1,0},{2,3},{3,2},{4,5},{5,4},{6,7},{7,6},{8,9},{9,8},{10,11... | collective-permute-start | bytes 98312 | tf_op jit(solution)/shard_map/ppermute | solution.py:15

commit v2 on v0

v2 whole, which is shorter than its diff:
```python
import functools

import jax
import jax.numpy as jnp
from jax import lax
from jax.experimental import pallas as pl
from jax.experimental.pallas import tpu as pltpu
from jax.sharding import PartitionSpec as P

CAP = 2
amplitude = 0.2
bf16 = jnp.bfloat16
f32 = jnp.float32
ROOM = 32 * 2**20
VMEM = pl.BlockSpec(memory_space=pltpu.VMEM)
SMEM = pl.BlockSpec(memory_space=pltpu.SMEM)


def swapped(value, mask):
    pairs = [(source, source ^ mask) for source in range(lax.axis_size("pts"))]
    return lax.ppermute(value, "pts", pairs)


def call(kernel, outs, name, flops, moved, ins=None, grid=None, out_specs=None):
    more = {} if grid is None else {"grid": grid, "in_specs": ins, "out_specs": out_specs}
    return pl.pallas_call(
        kernel,
        out_shape=outs,
        name=name,
        compiler_params=pltpu.CompilerParams(vmem_limit_bytes=ROOM),
        cost_estimate=pl.CostEstimate(flops=flops, bytes_accessed=moved, transcendentals=0),
        **more,
    )


def dot(a, b):
    return jnp.dot(a, b, preferred_element_type=f32)


def two(value):
    high = value.astype(bf16)
    return high, (value - high.astype(f32)).astype(bf16)


def dot3(a, b):
    (ah, al), (bh, bl) = a, b
    return dot(ah, bh) + (dot(ah, bl) + dot(al, bh))


def out(shape, kind):
    return jax.ShapeDtypeStruct(shape, kind)


def small_kernel(bits, rank, left_ref, right_ref, small_ref, left16_ref, high_ref, low_ref):
    for i in range(bits):
        high, low = two(right_ref[i].T)
        high_ref[i * rank : (i + 1) * rank, :] = high
        low_ref[i * rank : (i + 1) * rank, :] = low
        left16_ref[i] = left_ref[i].astype(bf16)
    for j in range(1, bits):
        at = j * (j - 1) // 2 * rank
        small_ref[at : at + j * rank, :] = dot(high_ref[: j * rank, :], left16_ref[j]).astype(bf16)


def front_kernel(rows, leaf, sizes, half, core_ref, residual_ref, inverse_ref, high_ref, low_ref, *rest):
    count = 2 * len(sizes)
    bases, (mine_ref, other_ref, keep_ref, send_ref) = rest[:count], rest[count:]
    x = [
        dot(inverse_ref[b * leaf : (b + 1) * leaf, :], residual_ref[b * leaf : (b + 1) * leaf, :])
        for b in range(rows // leaf)
    ]
    x = jnp.concatenate(x, 0)
    for k, size in enumerate(sizes):
        right_ref, left_ref = bases[2 * k], bases[2 * k + 1]
        projected = [
            dot3(two(right_ref[0, a : a + size, :].T), two(x[a : a + size, :]))
            for a in range(0, rows, size)
        ]
        x = jnp.concatenate(
            [
                x[a * size : (a + 1) * size, :]
                + dot3(two(left_ref[0, a * size : (a + 1) * size, :]), two(projected[a ^ 1]))
                for a in range(rows // size)
            ],
            0,
        )
    xh, xl = two(x)
    a = dot(high_ref[...], xh) + (dot(high_ref[...], xl) + dot(low_ref[...], xh))
    first = core_ref[0] == 0
    mine_ref[...] = jnp.where(first, x[:, :half], x[:, half:])
    other_ref[...] = jnp.where(first, x[:, half:], x[:, :half])
    keep_ref[...] = jnp.where(first, a[:, :half], a[:, half:])
    send_ref[...] = jnp.where(first, a[:, half:], a[:, :half]).astype(bf16)


def spread(value, depth):
    value = jnp.concatenate([value, jnp.zeros((depth - value.shape[0], value.shape[1]), f32)], 0) if depth > value.shape[0] else value
    one = value.astype(bf16)
    rest = value - one.astype(f32)
    second = rest.astype(bf16)
    return one, second, (rest - second.astype(f32)).astype(bf16)


def gathered(ref, at, depth):
    a = ref[at : at + depth, :].astype(f32)
    b = ref[at + depth : at + 2 * depth, :].astype(f32)
    return a + b + ref[at + 2 * depth : at + 3 * depth, :].astype(f32)


def put_spots(ref, at, depth, value):
    for k, part in enumerate(spread(value, depth)):
        ref[at + k * depth : at + (k + 1) * depth, :] = part


def linked(level, rank, own, theirs, own_small, their_small):
    cut = level * rank
    mine16, theirs16 = own[cut : cut + rank, :].astype(bf16), theirs[cut : cut + rank, :]
    return own[:cut, :] + theirs[:cut, :].astype(f32) + (dot(own_small, theirs16) + dot(their_small, mine16))


def small_at(level, rank):
    at = level * (level - 1) // 2 * rank
    return slice(at, at + level * rank)


def first_merge(level, rank, depth, keep_ref, got_ref, small_ref, their_ref, spot_ref, y_ref, message_ref, last_ref):
    at = small_at(level, rank)
    y = linked(level, rank, keep_ref[...], got_ref[...], small_ref[at, :], their_ref[at, :])
    y_ref[...] = y
    cut = level * rank
    message_ref[:cut, :] = y.astype(bf16)
    put_spots(message_ref, cut, depth, spot_ref[...])
    last_ref[...] = keep_ref[cut : cut + rank, :].astype(bf16)


def merge(level, rank, apart, counts, depths, y_in, own_ref, got_ref, *rest):
    if apart:
        own_small_ref, their_small_ref, y_ref, message_ref = rest
        base = 0
        spots_at = (level + 1) * rank
    else:
        own_small_ref, their_small_ref = own_ref, got_ref
        y_ref, message_ref = rest
        base = (level + 1) * rank
        spots_at = base + level * (level + 1) // 2 * rank
    at = small_at(level, rank)
    at = slice(base + at.start, base + at.stop)
    y = linked(level, rank, y_in[...], got_ref[...], own_small_ref[at, :], their_small_ref[at, :])
    y_ref[...] = y
    cut = level * rank
    message_ref[:cut, :] = y.astype(bf16)
    inner = level * (level - 1) // 2 * rank
    if inner:
        total = own_small_ref[base : base + inner, :].astype(f32) + their_small_ref[base : base + inner, :].astype(f32)
        message_ref[cut : cut + inner, :] = total.astype(bf16)
    n = counts[0]
    spots = jnp.concatenate(
        [gathered(own_ref, spots_at, depths[0])[:n, :], gathered(got_ref, spots_at, depths[0])[:n, :]], 0
    )
    put_spots(message_ref, cut + inner, depths[1], spots)


def coeff_kernel(bits, rank, mine_ref, other_ref, left_ref, left_other_ref, last_ref, *rest):
    shares, coeff_ref = rest[:bits], rest[bits]
    rows = mine_ref.shape[0]
    for k, (x_ref, l_ref) in enumerate(((mine_ref, left_ref), (other_ref, left_other_ref))):
        x = x_ref[...]
        for level in range(bits):
            share = last_ref if k and level == bits - 1 else shares[level]
            x = x + dot(l_ref[level], share[...])
        coeff_ref[k * rows : (k + 1) * rows, :] = x.astype(bf16)


def weigh_kernel(mask, plane, far, tile, leaf, blocks, n, depth, rank, me_ref, first_ref, count_ref, own_ref, got_ref, point_ref, coeff_ref, out_ref, weight_ref):
    me = me_ref[0]
    scale = 2.0 * leaf
    spots = jnp.concatenate([gathered(own_ref, rank, depth)[:n, :], gathered(got_ref, rank, depth)[:n, :]], 0) * scale
    spots = spots.T
    for z in range(far):
        q = mask + plane * z
        for r in range(2):
            column = jnp.broadcast_to(spots[r * tile : (r + 1) * tile, q : q + 1], (tile, leaf))
            target = me ^ (2 * q + r)
            for b in range(2 * blocks):
                source = me ^ (b // blocks)
                first = first_ref[target, source]
                there = (b % blocks >= first) & (b % blocks < first + count_ref[target, source])
                level = jnp.where(there, amplitude, 0.0)
                distance = jnp.minimum(jnp.abs(column - point_ref[b : b + 1, :] * scale), 1.0)
                left = 1.0 - distance
                left = left * left
                value = (left * left) * (1.0 + 4.0 * distance) * level
                at = (2 * z + r) * tile
                weight_ref[at : at + tile, b * leaf : (b + 1) * leaf] = value.astype(bf16)
    out_ref[...] = dot(weight_ref[...], coeff_ref[...]).astype(out_ref.dtype)


def solved_kernel(bits, core_ref, mine_ref, other_ref, left_ref, *rest):
    shares, others, out_ref = rest[:bits], rest[bits : 2 * bits], rest[2 * bits]
    half = mine_ref.shape[1]
    x, y = mine_ref[...], other_ref[...]
    for level in range(bits):
        high, low = two(left_ref[level])
        a, b = shares[level][...], others[level][...]
        x = x + (dot(high, a) + dot(low, a))
        y = y + (dot(high, b) + dot(low, b))
    first = core_ref[0] == 0
    out_ref[:, :half] = jnp.where(first, x, y)
    out_ref[:, half:] = jnp.where(first, y, x)


def body(
    residual_cols,
    leaf_inverse,
    basis_left,
    basis_right,
    point_pos,
    map_pos,
    prior_map,
    block_first,
    block_count,
):
    rows, samples = residual_cols.shape
    leaf = leaf_inverse.shape[1]
    rank = basis_left.shape[2]
    blocks = rows // leaf
    devices = lax.axis_size("pts")
    bits = devices.bit_length() - 1
    me = lax.axis_index("pts").astype(jnp.int32)
    core = me % 2
    me_s, core_s = me.reshape(1), core.reshape(1)
    levels = basis_left.shape[0]
    tile = map_pos.shape[0]
    half = samples // 2
    pair_count = bits * (bits - 1) // 2

    spot_other = swapped(map_pos, 1)
    top_levels = pl.BlockSpec((bits, rows, rank), lambda g: (0, 0, 0))
    whole = lambda *shape: pl.BlockSpec(shape, lambda g: (0,) * len(shape))
    small, left16, high, low = call(
        functools.partial(small_kernel, bits, rank),
        [
            out((pair_count * rank, rank), bf16),
            out((bits, rows, rank), bf16),
            out((bits * rank, rows), bf16),
            out((bits * rank, rows), bf16),
        ],
        "small",
        2 * pair_count * rank * rank * rows,
        12 * bits * rows * rank,
        ins=[top_levels, top_levels],
        grid=(1,),
        out_specs=[
            whole(pair_count * rank, rank),
            whole(bits, rows, rank),
            whole(bits * rank, rows),
            whole(bits * rank, rows),
        ],
    )(basis_left, basis_right)
    small_other = swapped(small, 1)
    left_other = swapped(left16, 1)

    inner = list(reversed(range(bits, levels)))
    sizes = [rows * devices // 2 ** (level + 1) for level in inner]
    one_level = lambda level: pl.BlockSpec((1, rows, rank), lambda g: (level, 0, 0))
    solved_mine, solved_send, keep, send = call(
        functools.partial(front_kernel, rows, leaf, sizes, half),
        [
            out((rows, half), f32),
            out((rows, half), f32),
            out((bits * rank, half), f32),
            out((bits * rank, half), bf16),
        ],
        "front",
        6 * bits * rank * rows * samples,
        4 * bits * rows * rank,
        ins=[SMEM, whole(rows, samples), whole(rows, leaf), whole(bits * rank, rows), whole(bits * rank, rows)]
        + [one_level(level) for level in inner for _ in range(2)],
        grid=(1,),
        out_specs=[whole(rows, half), whole(rows, half), whole(bits * rank, half), whole(bits * rank, half)],
    )(core_s, residual_cols, leaf_inverse, high, low, *[b for _ in inner for b in (basis_right, basis_left)])
    got = swapped(send, 1)
    solved_other = swapped(solved_send, 1)

    shares, others = [None] * bits, [None] * bits
    top = bits - 1
    depth_of = lambda bit: max(16, 1 << (bit - 1))
    held = top * (top - 1) // 2 * rank
    small_own = (small[:held].astype(f32) + small_other[:held].astype(f32)).astype(bf16)
    small_theirs = swapped(small_own, 2)
    spot_rows = jnp.concatenate([map_pos, spot_other]).reshape(1, 2 * tile)
    y, message, last = call(
        functools.partial(first_merge, top, rank, depth_of(1)),
        [
            out((top * rank, half), f32),
            out((top * rank + 3 * depth_of(1), half), bf16),
            out((rank, half), bf16),
        ],
        "merge0",
        4 * top * rank * rank * half,
        8 * top * rank * half,
    )(keep, got, small, small_other, spot_rows)
    shares[top] = got[top * rank :]
    others[top] = swapped(last, 1)
    for bit in range(1, bits):
        level = top - bit
        arrived = swapped(message, 1 << bit)
        share = arrived[level * rank : (level + 1) * rank]
        shares[level] = share
        others[level] = swapped(share, 1)
        if level:
            inner_rows = level * (level - 1) // 2 * rank
            apart = bit == 1
            y, message = call(
                functools.partial(
                    merge, level, rank, apart, (1 << (bit - 1),), (depth_of(bit), depth_of(bit + 1))
                ),
                [
                    out((level * rank, half), f32),
                    out((level * rank + inner_rows + 3 * depth_of(bit + 1), half), bf16),
                ],
                f"merge{bit}",
                4 * level * rank * rank * half,
                8 * level * rank * half,
            )(y, message, arrived, *((small_own, small_theirs) if apart else ()))

    coeffs = call(
        functools.partial(coeff_kernel, bits, rank),
        out((2 * rows, half), bf16),
        "coeffs",
        4 * bits * rows * rank * half,
        16 * rows * half,
    )(solved_mine, solved_other, left16, left_other, last, *shares)

    points = [lax.dynamic_slice_in_dim(point_pos, s * rows, rows).reshape(blocks, leaf) for s in (me, me ^ 1)]
    points = jnp.concatenate(points, 0)
    plane = 4
    far = devices // (2 * plane)
    depth = depth_of(bits - 1)

    def weighed(mask):
        return pl.pallas_call(
            functools.partial(
                weigh_kernel, mask, plane, far, tile, leaf, blocks, 1 << (bits - 2), depth, rank
            ),
            out_shape=out((far * 2 * tile, half), bf16 if mask else f32),
            in_specs=[SMEM, SMEM, SMEM, VMEM, VMEM, VMEM, VMEM],
            out_specs=VMEM,
            scratch_shapes=[pltpu.VMEM((far * 2 * tile, 2 * rows), bf16)],
            name=f"weigh{mask}",
            compiler_params=pltpu.CompilerParams(vmem_limit_bytes=ROOM),
            cost_estimate=pl.CostEstimate(
                flops=16 * far * tile * rows * half, bytes_accessed=16 * far * tile * half, transcendentals=0
            ),
        )(me_s, block_first, block_count, message, arrived, points, coeffs)

    sent = [swapped(weighed(mask), mask << 1) for mask in (3, 1, 2)]
    total = weighed(0)
    for partial in sent:
        total = total + partial.astype(f32)
    total = total.reshape(far, 2 * tile, half)
    result = total[0]
    for mask in reversed(range(1, far)):
        result = result + swapped(total[mask].astype(bf16), mask << 3).astype(f32)
    rest = swapped(result[tile:], 1)

    solved_out = call(
        functools.partial(solved_kernel, bits),
        out((rows, samples), f32),
        "solved",
        8 * bits * rows * rank * half,
        16 * rows * samples,
        ins=[SMEM, whole(rows, half), whole(rows, half), top_levels] + [whole(rank, half)] * (2 * bits),
        grid=(1,),
        out_specs=whole(rows, samples),
    )(core_s, solved_mine, solved_send, basis_left, *shares, *others)

    mapped = jnp.where(
        core == 0,
        jnp.concatenate([result[:tile], rest], 1),
        jnp.concatenate([rest, result[:tile]], 1),
    )
    return (solved_out, prior_map.astype(f32) + mapped)


def solution(mesh):
    in_specs = (
        P(("groups", "pts"), None),
        P(("groups", "pts"), None),
        P(None, ("groups", "pts"), None),
        P(None, ("groups", "pts"), None),
        P(),
        P("pts"),
        P(("groups", "pts"), None),
        P(),
        P(),
    )
    out_specs = (P(("groups", "pts"), None), P(("groups", "pts"), None))
    return jax.shard_map(body, mesh=mesh, in_specs=in_specs, out_specs=out_specs, check_vma=False)
```

time: 194 us -> 77 us (0.40)
  waiting for transfers between devices: 87.1 us -> 22.4 us
  local copies, waits for them, and re-layouts: 53.2 us -> 12.7 us
  matrix products: 19.7 us -> 0 us
  Pallas kernels: 0 us -> 19.7 us
  starting transfers between devices: 27.6 us -> 19.8 us
  other arithmetic: 5.1 us -> 0.86 us
    gather x2 -> x0, local copies, waits for them, and re-layouts: 48.3 us -> none  [the longest x1 45.5 us: body(): positions = point_pos[point_index]]
    all_to_all x1 -> x0, waiting for transfers between devices: 46.4 us -> none  [body(): lax.all_to_all(outgoing, 'pts', split_axis=0, concat_axis=0, tiled=True)]
    pallas_call x0 -> x12, Pallas kernels: none -> 19.7 us  [the longest x4 9.16 us: weighed(): pl.pallas_call(functools.partial(weigh_kernel, mask, plane, far, tile, le...]
    dot_general x16 -> x0, matrix products: 19.7 us -> none  [the longest x5 7.89 us: body(): solved = solved + jnp.dot(left_basis, sibling, precision=highest)]
    ppermute x15 -> x22, waiting for transfers between devices: 40.7 us -> 22.4 us  [swapped(): return lax.ppermute(value, 'pts', pairs)]
    unnamed x15 -> x34, local copies, waits for them, and re-layouts: 1.63 us -> 11.1 us
    all_to_all x1 -> x0, starting transfers between devices: 5.89 us -> none  [body(): lax.all_to_all(outgoing, 'pts', split_axis=0, concat_axis=0, tiled=True)]
    select_n x3 -> x0, other arithmetic: 4.64 us -> none  [the longest x1 4.46 us: body(): jnp.where(send_live[:, :, None, None], coeff_blocks[send_index], jnp.zero...]
  transfers between devices with their start and end apart: 16 -> 22, of which waited for: 16 -> 9; matrix products, arithmetic and copies ran while one was open for 25% -> 2% of each run, Pallas kernels for 0% -> 19%
where the time goes in v2:
time: 77 us; the launch traced here: 76.4 us
  waiting for transfers between devices  22.4 us (29%)
  starting transfers between devices  19.8 us (26%)
  Pallas kernels  19.7 us (26%)
  local copies, waits for them, and re-layouts  12.7 us (16%)
  other arithmetic  0.86 us (1%)
  between operations  0.86 us (1%)
    ppermute x22, waiting for transfers between devices, swapped(): return lax.ppermute(value, 'pts', pairs)  22.4 us
    ppermute x22, starting transfers between devices, swapped(): return lax.ppermute(value, 'pts', pairs)  19.8 us
    unnamed x34, local copies, waits for them, and re-layouts  11.1 us
    pallas_call x4, Pallas kernels, weighed(): pl.pallas_call(functools.partial(weigh_kernel, mask, plane, far, tile, le...  9.16 us
    pallas_call x3, Pallas kernels, body(): call(functools.partial(merge, level, rank, apart, (1 << bit - 1,), (depth...  2.79 us
    pallas_call x1, Pallas kernels, body(): call(functools.partial(solved_kernel, bits), out((rows, samples), f32), '...  2.57 us
    pallas_call x1, Pallas kernels, body(): call(functools.partial(front_kernel, rows, leaf, sizes, half), [out((rows...  2.01 us
    pallas_call x1, Pallas kernels, body(): call(functools.partial(coeff_kernel, bits, rank), out((2 * rows, half), b...  1.57 us
  transfers between devices with their start and end apart: 22, of which 9 were waited for; matrix products, arithmetic and copies ran while one was open for 2% of the time, Pallas kernels for 19%

profile of v2, /device:TPU:0, one launch (start us, length us, event | category | flops | bytes accessed | tf_op | source)
XLA Modules:
  0.0 76.4 jit_solution(13858617191834207449)
XLA Ops:
  0.6 1.5 %copy-done = f32[7,512,128]{2,1,0:T(8,128)S(1)} copy-done((f32[7,512,128]{2,1,0:T(8,128)S(1)}, f32[7,512,128]{2,1,0:T(8,128)}, u32[]{:S(2)}) %copy-start) | copy-done | bytes 1835032
  2.1 1.5 %copy-done.2 = f32[7,512,128]{2,1,0:T(8,128)S(1)} copy-done((f32[7,512,128]{2,1,0:T(8,128)S(1)}, f32[7,512,128]{2,1,0:T(8,128)}, u32[]{:S(2)}) %copy-start.2) | copy-done | bytes 1835032
  3.6 1.4 %small.1 = (bf16[1280,128]{1,0:T(8,128)(2,1)S(1)}, bf16[5,512,128]{2,1,0:T(8,128)(2,1)}, bf16[640,512]{1,0:T(8,128)(2,1)S(1)}, bf16[640,512]{1,0:T(8,128)(2,1)S(1)}) custom-call(f32[7,512,128]{2,1,0:T(8,128)S(1)} %copy-done, f32[7,512,128]{2,1,0:T(8,128)S(1)} %copy-done.2), custom_call_target="tpu_custom_call" | custom-call | flops 167772160 | bytes 3932160 | tf_op jit(solution)/shard_map/small/pallas_call | solution.py:240
  5.0 0.9 %copy-done.4 = bf16[640,512]{1,0:T(8,128)(2,1)} copy-done((bf16[640,512]{1,0:T(8,128)(2,1)}, bf16[640,512]{1,0:T(8,128)(2,1)S(1)}, u32[]{:S(2)}) %copy-start.4) | copy-done | bytes 655384
  5.9 0.5 collective-permute-start.1
  6.3 1.5 %copy-done.3 = f32[7,512,128]{2,1,0:T(8,128)S(1)} copy-done((f32[7,512,128]{2,1,0:T(8,128)S(1)}, f32[7,512,128]{2,1,0:T(8,128)}, u32[]{:S(2)}) %copy-start.3) | copy-done | bytes 1835032
  7.8 1.1 %copy-done.5 = bf16[640,512]{1,0:T(8,128)(2,1)S(1)} copy-done((bf16[640,512]{1,0:T(8,128)(2,1)S(1)}, bf16[640,512]{1,0:T(8,128)(2,1)}, u32[]{:S(2)}) %copy-start.5) | copy-done | bytes 655384
  8.9 0.9 %copy-done.6 = bf16[512,256]{1,0:T(8,128)(2,1)S(1)} copy-done((bf16[512,256]{1,0:T(8,128)(2,1)S(1)}, bf16[512,256]{1,0:T(8,128)(2,1)}, u32[]{:S(2)}) %copy-start.6) | copy-done | bytes 262168
  9.9 2.0 %front.1 = (f32[512,128]{1,0:T(8,128)S(1)}, f32[512,128]{1,0:T(8,128)}, f32[640,128]{1,0:T(8,128)S(1)}, bf16[640,128]{1,0:T(8,128)(2,1)S(1)}) custom-call(s32[1]{0:T(128)} %bitcast.core_ref, bf16[512,256]{1,0:T(8,128)(2,1)S(1)} %copy-done.6, bf16[512,128]{1,0:T(8,128)(2,1)S(1)} %copy-done.10, bf16[640,512]{1,0:T(8,128)(2,1)S(1)} %get-tuple-element.18.high_ref, ...), custom_call_target="tpu_custom_call" | custom-call | flops 503316480 | bytes 1310720 | tf_op jit(solution)/shard_map/front/pallas_call | solution.py:266
  11.9 0.1 collective-permute-start
  12.0 0.5 collective-permute-start.2
  12.4 0.1 collective-permute-start.14
  12.5 0.1 add_convert_fusion.rest_0_
  12.6 3.0 %collective-permute-start.4 = (bf16[768,128]{1,0:T(8,128)(2,1)S(1)}, bf16[768,128]{1,0:T(8,128)(2,1)S(1)}, u32[]{:S(2)}, u32[]{:S(2)}) collective-permute-start(bf16[768,128]{1,0:T(8,128)(2,1)S(1)} %add_convert_fusion.rest_0_), channel_id=1, source_target_pairs={{0,2},{1,3},{2,0},{3,1},{4,6},{5,7},{6,4},{7,5},{8,10},{9,11},{10,... | collective-permute-start | bytes 589832 | tf_op jit(solution)/shard_map/ppermute | solution.py:21
  15.5 0.1 maximum_bitcast_fusion.spot_ref
  15.6 0.2 merge0.1
  15.8 0.6 copy-done.11
  16.4 0.5 collective-permute-start.3
  16.9 6.8 %collective-permute-done.3.got_ref = bf16[560,128]{1,0:T(8,128)(2,1)S(1)} collective-permute-done((bf16[560,128]{1,0:T(8,128)(2,1)S(1)}, bf16[560,128]{1,0:T(8,128)(2,1)S(1)}, u32[]{:S(2)}, u32[]{:S(2)}) %collective-permute-start.3) | collective-permute-done | bytes 143392 | tf_op jit(solution)/shard_map/ppermute | solution.py:21
  23.8 0.0 collective-permute-done.4.rest_1_
  23.8 0.9 %merge1.1 = (f32[384,128]{1,0:T(8,128)S(1)}, bf16[816,128]{1,0:T(8,128)(2,1)}) custom-call(f32[512,128]{1,0:T(8,128)S(1)} %get-tuple-element.25.y_in, bf16[560,128]{1,0:T(8,128)(2,1)S(1)} %get-tuple-element.26.own_ref, bf16[560,128]{1,0:T(8,128)(2,1)S(1)} %collective-permute-done.3.got_ref, bf16[768,128]{1,0:T(8,128)(2,1)S(1)} %add_convert_fusion.rest_0_, ...), custom_call_target="tpu_custom_call" | custom-call | flops 25165824 | bytes 393216 | tf_op jit(solution)/shard_map/merge1/pallas_call | solution.py:314
  24.6 0.7 copy-done.8
  25.3 1.8 %collective-permute-start.5 = (bf16[816,128]{1,0:T(8,128)(2,1)}, bf16[816,128]{1,0:T(8,128)(2,1)S(1)}, u32[]{:S(2)}, u32[]{:S(2)}) collective-permute-start(bf16[816,128]{1,0:T(8,128)(2,1)} %get-tuple-element.28.own_ref), channel_id=1, source_target_pairs={{0,4},{1,5},{2,6},{3,7},{4,0},{5,1},{6,2},{7,3},{8,12},{9,13},{10,... | collective-permute-start | bytes 626696 | tf_op jit(solution)/shard_map/ppermute | solution.py:21
  27.1 0.0 collective-permute-start.13
  27.1 5.1 %collective-permute-done.5.got_ref = bf16[816,128]{1,0:T(8,128)(2,1)S(1)} collective-permute-done((bf16[816,128]{1,0:T(8,128)(2,1)}, bf16[816,128]{1,0:T(8,128)(2,1)S(1)}, u32[]{:S(2)}, u32[]{:S(2)}) %collective-permute-start.5) | collective-permute-done | bytes 208928 | tf_op jit(solution)/shard_map/ppermute | solution.py:21
  32.2 0.9 %copy-done.9 = f32[384,128]{1,0:T(8,128)S(1)} copy-done((f32[384,128]{1,0:T(8,128)S(1)}, f32[384,128]{1,0:T(8,128)}, u32[]{:S(2)}) %copy-start.9) | copy-done | bytes 196632
  33.1 1.1 %merge2.1 = (f32[256,128]{1,0:T(8,128)S(1)}, bf16[432,128]{1,0:T(8,128)(2,1)S(1)}) custom-call(f32[384,128]{1,0:T(8,128)S(1)} %copy-done.9, bf16[816,128]{1,0:T(8,128)(2,1)} %get-tuple-element.28.own_ref, bf16[816,128]{1,0:T(8,128)(2,1)S(1)} %collective-permute-done.5.got_ref), custom_call_target="tpu_custom_call" | custom-call | flops 16777216 | bytes 262144 | tf_op jit(solution)/shard_map/merge2/pallas_call | solution.py:314
  34.2 1.6 %collective-permute-start.6 = (bf16[432,128]{1,0:T(8,128)(2,1)S(1)}, bf16[432,128]{1,0:T(8,128)(2,1)S(1)}, u32[]{:S(2)}, u32[]{:S(2)}) collective-permute-start(bf16[432,128]{1,0:T(8,128)(2,1)S(1)} %get-tuple-element.30.own_ref), channel_id=1, source_target_pairs={{0,8},{1,9},{2,10},{3,11},{4,12},{5,13},{6,14},{7,15},{8,0},{9,1},... | collective-permute-start | bytes 331784 | tf_op jit(solution)/shard_map/ppermute | solution.py:21
  35.8 0.8 %dynamic-slice_bitcast_fusion.1 = (f32[4,128]{1,0:T(4,128)S(1)}, f32[4,128]{1,0:T(4,128)S(1)}) fusion(f32[16384]{0:T(1024)} %param.13, s32[]{:T(128)S(6)} %select_n.23, s32[]{:T(128)S(6)} %select_n.24), kind=kLoop, calls=%fused_computation.9 | loop fusion | bytes 8200 | tf_op jit(solution)/shard_map/reshape | solution.py:335
  36.6 2.4 %collective-permute-done.6.got_ref = bf16[432,128]{1,0:T(8,128)(2,1)S(1)} collective-permute-done((bf16[432,128]{1,0:T(8,128)(2,1)S(1)}, bf16[432,128]{1,0:T(8,128)(2,1)S(1)}, u32[]{:S(2)}, u32[]{:S(2)}) %collective-permute-start.6) | collective-permute-done | bytes 110624 | tf_op jit(solution)/shard_map/ppermute | solution.py:21
  39.0 0.8 %merge3.1 = (f32[128,128]{1,0:T(8,128)}, bf16[176,128]{1,0:T(8,128)(2,1)S(1)}) custom-call(f32[256,128]{1,0:T(8,128)S(1)} %get-tuple-element.29.y_in, bf16[432,128]{1,0:T(8,128)(2,1)S(1)} %get-tuple-element.30.own_ref, bf16[432,128]{1,0:T(8,128)(2,1)S(1)} %collective-permute-done.6.got_ref), custom_call_target="tpu_custom_call" | custom-call | flops 8388608 | bytes 131072 | tf_op jit(solution)/shard_map/merge3/pallas_call | solution.py:314
  39.8 2.5 %collective-permute-start.7 = (bf16[176,128]{1,0:T(8,128)(2,1)S(1)}, bf16[176,128]{1,0:T(8,128)(2,1)S(1)}, u32[]{:S(2)}, u32[]{:S(2)}) collective-permute-start(bf16[176,128]{1,0:T(8,128)(2,1)S(1)} %get-tuple-element.31.own_ref), channel_id=1, source_target_pairs={{0,16},{1,17},{2,18},{3,19},{4,20},{5,21},{6,22},{7,23},{8,24},{9,... | collective-permute-start | bytes 135176 | tf_op jit(solution)/shard_map/ppermute | solution.py:21
  42.4 0.8 slice.65.rest_4_
  43.1 1.6 %collective-permute-done.7.got_ref = bf16[176,128]{1,0:T(8,128)(2,1)S(1)} collective-permute-done((bf16[176,128]{1,0:T(8,128)(2,1)S(1)}, bf16[176,128]{1,0:T(8,128)(2,1)S(1)}, u32[]{:S(2)}, u32[]{:S(2)}) %collective-permute-start.7) | collective-permute-done | bytes 45088 | tf_op jit(solution)/shard_map/ppermute | solution.py:21
  44.8 0.0 collective-permute-done.13.other_ref
  44.8 0.0 collective-permute-done.14.left_other_ref
  44.8 0.7 copy-done.12
  45.5 1.6 %coeffs.1.coeff_ref = bf16[1024,128]{1,0:T(8,128)(2,1)S(1)} custom-call(f32[512,128]{1,0:T(8,128)S(1)} %get-tuple-element.20.mine_ref, f32[512,128]{1,0:T(8,128)S(1)} %collective-permute-done.13.other_ref, bf16[5,512,128]{2,1,0:T(8,128)(2,1)} %get-tuple-element.33.left_ref, bf16[5,512,128]{2,1,0:T(8,128)(2,1)S(1)} %collective-permute-done.14.left_other_ref, ...), custom_call_target="tpu_custom_call" | custom-call | flops 167772160 | bytes 1048576 | tf_op jit(solution)/shard_map/coeffs/pallas_call | solution.py:327
  47.1 0.0 copy-start.14
  47.2 0.7 copy-done.14
  47.9 2.3 %weigh3.1 = bf16[512,128]{1,0:T(8,128)(2,1)S(1)} custom-call(s32[1]{0:T(128)} %bitcast.2.me_ref, s32[32,32]{1,0:T(8,128)S(1)} %copy-done.13, s32[32,32]{1,0:T(8,128)S(1)} %copy-done.14, bf16[176,128]{1,0:T(8,128)(2,1)S(1)} %get-tuple-element.31.own_ref, bf16[176,128]{1,0:T(8,128)(2,1)S(1)} %collective-permute-done.7.got_ref, ...), custom_call_target="tpu_custom_call" | custom-call | flops 268435456 | bytes 524288 | tf_op jit(solution)/shard_map/weigh3/pallas_call | solution.py:342
  50.2 2.4 %collective-permute-start.15 = (bf16[512,128]{1,0:T(8,128)(2,1)S(1)}, bf16[512,128]{1,0:T(8,128)(2,1)S(1)}, u32[]{:S(2)}, u32[]{:S(2)}) collective-permute-start(bf16[512,128]{1,0:T(8,128)(2,1)S(1)} %weigh3.1), channel_id=1, source_target_pairs={{0,6},{1,7},{2,4},{3,5},{4,2},{5,3},{6,0},{7,1},{8,14},{9,15},{10,... | collective-permute-start | bytes 393224 | tf_op jit(solution)/shard_map/ppermute | solution.py:21
  52.6 2.3 %weigh1.1 = bf16[512,128]{1,0:T(8,128)(2,1)S(1)} custom-call(s32[1]{0:T(128)} %bitcast.2.me_ref, s32[32,32]{1,0:T(8,128)S(1)} %copy-done.13, s32[32,32]{1,0:T(8,128)S(1)} %copy-done.14, bf16[176,128]{1,0:T(8,128)(2,1)S(1)} %get-tuple-element.31.own_ref, bf16[176,128]{1,0:T(8,128)(2,1)S(1)} %collective-permute-done.7.got_ref, ...), custom_call_target="tpu_custom_call" | custom-call | flops 268435456 | bytes 524288 | tf_op jit(solution)/shard_map/weigh1/pallas_call | solution.py:342
  54.9 0.6 collective-permute-start.16
  55.5 2.3 %weigh2.1 = bf16[512,128]{1,0:T(8,128)(2,1)S(1)} custom-call(s32[1]{0:T(128)} %bitcast.2.me_ref, s32[32,32]{1,0:T(8,128)S(1)} %copy-done.13, s32[32,32]{1,0:T(8,128)S(1)} %copy-done.14, bf16[176,128]{1,0:T(8,128)(2,1)S(1)} %get-tuple-element.31.own_ref, bf16[176,128]{1,0:T(8,128)(2,1)S(1)} %collective-permute-done.7.got_ref, ...), custom_call_target="tpu_custom_call" | custom-call | flops 268435456 | bytes 524288 | tf_op jit(solution)/shard_map/weigh2/pallas_call | solution.py:342
  57.8 0.6 collective-permute-start.17
  58.4 2.3 %weigh0.1 = f32[512,128]{1,0:T(8,128)S(1)} custom-call(s32[1]{0:T(128)} %bitcast.2.me_ref, s32[32,32]{1,0:T(8,128)S(1)} %copy-done.13, s32[32,32]{1,0:T(8,128)S(1)} %copy-done.14, bf16[176,128]{1,0:T(8,128)(2,1)S(1)} %get-tuple-element.31.own_ref, bf16[176,128]{1,0:T(8,128)(2,1)S(1)} %collective-permute-done.7.got_ref, ...), custom_call_target="tpu_custom_call" | custom-call | flops 268435456 | bytes 524288 | tf_op jit(solution)/shard_map/weigh0/pallas_call | solution.py:342
  60.7 0.0 collective-permute-done.15
  60.8 2.1 %collective-permute-done.17 = bf16[512,128]{1,0:T(8,128)(2,1)S(1)} collective-permute-done((bf16[512,128]{1,0:T(8,128)(2,1)S(1)}, bf16[512,128]{1,0:T(8,128)(2,1)S(1)}, u32[]{:S(2)}, u32[]{:S(2)}) %collective-permute-start.17) | collective-permute-done | bytes 131104 | tf_op jit(solution)/shard_map/ppermute | solution.py:21
  62.8 0.1 fusion.3
  62.9 0.0 copy-start.15
  62.9 4.0 %collective-permute-start.18 = (bf16[128,128]{1,0:T(8,128)(2,1)S(1)}, bf16[128,128]{1,0:T(8,128)(2,1)S(1)}, u32[]{:S(2)}, u32[]{:S(2)}) collective-permute-start(bf16[128,128]{1,0:T(8,128)(2,1)S(1)} %get-tuple-element.36), channel_id=1, source_target_pairs={{0,24},{1,25},{2,26},{3,27},{4,28},{5,29},{6,30},{7,31},{8,16},{9,... | collective-permute-start | bytes 98312 | tf_op jit(solution)/shard_map/ppermute | solution.py:21
  67.0 0.6 collective-permute-start.20
  67.6 0.5 collective-permute-start.11
  68.1 0.7 collective-permute-done.18
  68.9 2.9 %collective-permute-done.19 = bf16[128,128]{1,0:T(8,128)(2,1)S(1)} collective-permute-done((bf16[128,128]{1,0:T(8,128)(2,1)S(1)}, bf16[128,128]{1,0:T(8,128)(2,1)S(1)}, u32[]{:S(2)}, u32[]{:S(2)}) %collective-permute-start.19) | collective-permute-done | bytes 32800 | tf_op jit(solution)/shard_map/ppermute | solution.py:21
  71.8 0.0 collective-permute-start.9
  71.8 0.0 collective-permute-done.20
  71.8 0.5 collective-permute-start.8
  72.3 0.1 collective-permute-start.21
  72.4 0.5 collective-permute-done.9.rest_6_
  73.0 0.2 collective-permute-done.8.rest_5_
  73.1 2.6 %solved.1 = f32[512,256]{1,0:T(8,128)} custom-call(s32[1]{0:T(128)} %bitcast.core_ref, f32[512,128]{1,0:T(8,128)S(1)} %get-tuple-element.20.mine_ref, f32[512,128]{1,0:T(8,128)} %get-tuple-element.21.other_ref, f32[7,512,128]{2,1,0:T(8,128)S(1)} %copy-done.1, bf16[128,128]{1,0:T(8,128)(2,1)S(1)} %slice.61.rest_0_, bf16[128,128]{1,0:T(8,128)(2,1)S(1)} %slice.62.rest_1_, ...), custom_call_target="tpu_custom_call" | custom-call | flops 335544320 | bytes 2097152 | tf_op jit(solution)/shard_map/solved/pallas_call | solution.py:367
  75.7 0.6 fusion.2
  (40 shorter events, 0.1 us)
Async XLA Ops:
  0.6 1.5 %copy-start = (f32[7,512,128]{2,1,0:T(8,128)S(1)}, f32[7,512,128]{2,1,0:T(8,128)}, u32[]{:S(2)}) copy-start(f32[7,512,128]{2,1,0:T(8,128)} %left_ref.3) | copy-start | bytes 5505028
  2.1 1.5 %copy-start.2 = (f32[7,512,128]{2,1,0:T(8,128)S(1)}, f32[7,512,128]{2,1,0:T(8,128)}, u32[]{:S(2)}) copy-start(f32[7,512,128]{2,1,0:T(8,128)} %rest_2_.1) | copy-start | bytes 5505028
  3.6 2.7 %copy-start.1 = (f32[7,512,128]{2,1,0:T(8,128)S(1)}, f32[7,512,128]{2,1,0:T(8,128)}, u32[]{:S(2)}) copy-start(f32[7,512,128]{2,1,0:T(8,128)} %left_ref.3) | copy-start | bytes 5505028
  3.6 2.7 %copy-start.10 = (bf16[512,128]{1,0:T(8,128)(2,1)S(1)}, bf16[512,128]{1,0:T(8,128)(2,1)}, u32[]{:S(2)}) copy-start(bf16[512,128]{1,0:T(8,128)(2,1)} %inverse_ref.1) | copy-start | bytes 393220
  5.0 0.9 %copy-start.4 = (bf16[640,512]{1,0:T(8,128)(2,1)}, bf16[640,512]{1,0:T(8,128)(2,1)S(1)}, u32[]{:S(2)}) copy-start(bf16[640,512]{1,0:T(8,128)(2,1)S(1)} %get-tuple-element.19.low_ref) | copy-start | bytes 1966084
  5.9 6.6 %collective-permute-start.1 = (bf16[1280,128]{1,0:T(8,128)(2,1)S(1)}, bf16[1280,128]{1,0:T(8,128)(2,1)S(1)}, u32[]{:S(2)}, u32[]{:S(2)}) collective-permute-start(bf16[1280,128]{1,0:T(8,128)(2,1)S(1)} %get-tuple-element.24.small_ref), channel_id=1, source_target_pairs={{0,1},{1,0},{2,3},{3,2},{4,5},{5,4},{6,7},{7,6},{8,9},{9,8},{10,11... | collective-permute-start | bytes 983048 | tf_op jit(solution)/shard_map/ppermute | solution.py:21
  6.3 1.5 %copy-start.3 = (f32[7,512,128]{2,1,0:T(8,128)S(1)}, f32[7,512,128]{2,1,0:T(8,128)}, u32[]{:S(2)}) copy-start(f32[7,512,128]{2,1,0:T(8,128)} %rest_2_.1) | copy-start | bytes 5505028
  7.8 1.1 %copy-start.5 = (bf16[640,512]{1,0:T(8,128)(2,1)S(1)}, bf16[640,512]{1,0:T(8,128)(2,1)}, u32[]{:S(2)}) copy-start(bf16[640,512]{1,0:T(8,128)(2,1)} %copy-done.4) | copy-start | bytes 1966084
  8.9 0.9 %copy-start.6 = (bf16[512,256]{1,0:T(8,128)(2,1)S(1)}, bf16[512,256]{1,0:T(8,128)(2,1)}, u32[]{:S(2)}) copy-start(bf16[512,256]{1,0:T(8,128)(2,1)} %residual_ref.1) | copy-start | bytes 786436
  9.9 2.1 %copy-start.16 = (f32[64]{0:T(128)S(1)}, f32[64]{0:T(128)}, u32[]{:S(2)}) copy-start(f32[64]{0:T(128)} %param.14) | copy-start | bytes 772
  11.9 3.7 %collective-permute-start = (bf16[640,128]{1,0:T(8,128)(2,1)S(1)}, bf16[640,128]{1,0:T(8,128)(2,1)S(1)}, u32[]{:S(2)}, u32[]{:S(2)}) collective-permute-start(bf16[640,128]{1,0:T(8,128)(2,1)S(1)} %get-tuple-element.23), channel_id=1, source_target_pairs={{0,1},{1,0},{2,3},{3,2},{4,5},{5,4},{6,7},{7,6},{8,9},{9,8},{10,11... | collective-permute-start | bytes 491528 | tf_op jit(solution)/shard_map/ppermute | solution.py:21
  12.0 3.6 %collective-permute-start.2 = (f32[64]{0:T(128)S(1)}, f32[64]{0:T(128)S(1)}, u32[]{:S(2)}, u32[]{:S(2)}) collective-permute-start(f32[64]{0:T(128)S(1)} %copy-done.16), channel_id=1, source_target_pairs={{0,1},{1,0},{2,3},{3,2},{4,5},{5,4},{6,7},{7,6},{8,9},{9,8},{10,11... | collective-permute-start | bytes 776 | tf_op jit(solution)/shard_map/ppermute | solution.py:21
  12.4 32.4 %collective-permute-start.14 = (bf16[5,512,128]{2,1,0:T(8,128)(2,1)}, bf16[5,512,128]{2,1,0:T(8,128)(2,1)S(1)}, u32[]{:S(2)}, u32[]{:S(2)}) collective-permute-start(bf16[5,512,128]{2,1,0:T(8,128)(2,1)} %get-tuple-element.33.left_ref), channel_id=1, source_target_pairs={{0,1},{1,0},{2,3},{3,2},{4,5},{5,4},{6,7},{7,6},{8,9},{9,8},{10,11... | collective-permute-start | bytes 1966088 | tf_op jit(solution)/shard_map/ppermute | solution.py:21
  12.6 11.2 %collective-permute-start.4 = (bf16[768,128]{1,0:T(8,128)(2,1)S(1)}, bf16[768,128]{1,0:T(8,128)(2,1)S(1)}, u32[]{:S(2)}, u32[]{:S(2)}) collective-permute-start(bf16[768,128]{1,0:T(8,128)(2,1)S(1)} %add_convert_fusion.rest_0_), channel_id=1, source_target_pairs={{0,2},{1,3},{2,0},{3,1},{4,6},{5,7},{6,4},{7,5},{8,10},{9,11},{10,... | collective-permute-start | bytes 589832 | tf_op jit(solution)/shard_map/ppermute | solution.py:21
  15.6 8.1 %copy-start.7 = (bf16[640,128]{1,0:T(8,128)(2,1)}, bf16[640,128]{1,0:T(8,128)(2,1)S(1)}, u32[]{:S(2)}) copy-start(bf16[640,128]{1,0:T(8,128)(2,1)S(1)} %collective-permute-done.got_ref) | copy-start | bytes 491524
  15.8 0.6 copy-start.11
  16.4 7.3 %collective-permute-start.3 = (bf16[560,128]{1,0:T(8,128)(2,1)S(1)}, bf16[560,128]{1,0:T(8,128)(2,1)S(1)}, u32[]{:S(2)}, u32[]{:S(2)}) collective-permute-start(bf16[560,128]{1,0:T(8,128)(2,1)S(1)} %get-tuple-element.26.own_ref), channel_id=1, source_target_pairs={{0,2},{1,3},{2,0},{3,1},{4,6},{5,7},{6,4},{7,5},{8,10},{9,11},{10,... | collective-permute-start | bytes 430088 | tf_op jit(solution)/shard_map/ppermute | solution.py:21
  24.6 0.7 copy-start.8
  25.3 21.8 %copy-start.13 = (s32[32,32]{1,0:T(8,128)S(1)}, s32[32,32]{1,0:T(8,128)}, u32[]{:S(2)}) copy-start(s32[32,32]{1,0:T(8,128)} %first_ref.7) | copy-start | bytes 12292
  25.3 6.8 %collective-permute-start.5 = (bf16[816,128]{1,0:T(8,128)(2,1)}, bf16[816,128]{1,0:T(8,128)(2,1)S(1)}, u32[]{:S(2)}, u32[]{:S(2)}) collective-permute-start(bf16[816,128]{1,0:T(8,128)(2,1)} %get-tuple-element.28.own_ref), channel_id=1, source_target_pairs={{0,4},{1,5},{2,6},{3,7},{4,0},{5,1},{6,2},{7,3},{8,12},{9,13},{10,... | collective-permute-start | bytes 626696 | tf_op jit(solution)/shard_map/ppermute | solution.py:21
  27.1 17.7 %collective-permute-start.13 = (f32[512,128]{1,0:T(8,128)}, f32[512,128]{1,0:T(8,128)S(1)}, u32[]{:S(2)}, u32[]{:S(2)}) collective-permute-start(f32[512,128]{1,0:T(8,128)} %get-tuple-element.21.other_ref), channel_id=1, source_target_pairs={{0,1},{1,0},{2,3},{3,2},{4,5},{5,4},{6,7},{7,6},{8,9},{9,8},{10,11... | collective-permute-start | bytes 786440 | tf_op jit(solution)/shard_map/ppermute | solution.py:21
  32.2 0.9 %copy-start.9 = (f32[384,128]{1,0:T(8,128)S(1)}, f32[384,128]{1,0:T(8,128)}, u32[]{:S(2)}) copy-start(f32[384,128]{1,0:T(8,128)} %copy-done.8) | copy-start | bytes 589828
  34.2 4.8 %collective-permute-start.6 = (bf16[432,128]{1,0:T(8,128)(2,1)S(1)}, bf16[432,128]{1,0:T(8,128)(2,1)S(1)}, u32[]{:S(2)}, u32[]{:S(2)}) collective-permute-start(bf16[432,128]{1,0:T(8,128)(2,1)S(1)} %get-tuple-element.30.own_ref), channel_id=1, source_target_pairs={{0,8},{1,9},{2,10},{3,11},{4,12},{5,13},{6,14},{7,15},{8,0},{9,1},... | collective-permute-start | bytes 331784 | tf_op jit(solution)/shard_map/ppermute | solution.py:21
  39.8 4.9 %collective-permute-start.7 = (bf16[176,128]{1,0:T(8,128)(2,1)S(1)}, bf16[176,128]{1,0:T(8,128)(2,1)S(1)}, u32[]{:S(2)}, u32[]{:S(2)}) collective-permute-start(bf16[176,128]{1,0:T(8,128)(2,1)S(1)} %get-tuple-element.31.own_ref), channel_id=1, source_target_pairs={{0,16},{1,17},{2,18},{3,19},{4,20},{5,21},{6,22},{7,23},{8,24},{9,... | collective-permute-start | bytes 135176 | tf_op jit(solution)/shard_map/ppermute | solution.py:21
  44.8 0.8 copy-start.12
  47.1 0.7 copy-start.14
  50.2 10.6 %collective-permute-start.15 = (bf16[512,128]{1,0:T(8,128)(2,1)S(1)}, bf16[512,128]{1,0:T(8,128)(2,1)S(1)}, u32[]{:S(2)}, u32[]{:S(2)}) collective-permute-start(bf16[512,128]{1,0:T(8,128)(2,1)S(1)} %weigh3.1), channel_id=1, source_target_pairs={{0,6},{1,7},{2,4},{3,5},{4,2},{5,3},{6,0},{7,1},{8,14},{9,15},{10,... | collective-permute-start | bytes 393224 | tf_op jit(solution)/shard_map/ppermute | solution.py:21
  54.9 5.9 %collective-permute-start.16 = (bf16[512,128]{1,0:T(8,128)(2,1)S(1)}, bf16[512,128]{1,0:T(8,128)(2,1)S(1)}, u32[]{:S(2)}, u32[]{:S(2)}) collective-permute-start(bf16[512,128]{1,0:T(8,128)(2,1)S(1)} %weigh1.1), channel_id=1, source_target_pairs={{0,2},{1,3},{2,0},{3,1},{4,6},{5,7},{6,4},{7,5},{8,10},{9,11},{10,... | collective-permute-start | bytes 393224 | tf_op jit(solution)/shard_map/ppermute | solution.py:21
  57.8 5.0 %collective-permute-start.17 = (bf16[512,128]{1,0:T(8,128)(2,1)S(1)}, bf16[512,128]{1,0:T(8,128)(2,1)S(1)}, u32[]{:S(2)}, u32[]{:S(2)}) collective-permute-start(bf16[512,128]{1,0:T(8,128)(2,1)S(1)} %weigh2.1), channel_id=1, source_target_pairs={{0,4},{1,5},{2,6},{3,7},{4,0},{5,1},{6,2},{7,3},{8,12},{9,13},{10,... | collective-permute-start | bytes 393224 | tf_op jit(solution)/shard_map/ppermute | solution.py:21
  62.9 12.8 %copy-start.15 = (bf16[64,256]{1,0:T(8,128)(2,1)S(1)}, bf16[64,256]{1,0:T(8,128)(2,1)}, u32[]{:S(2)}) copy-start(bf16[64,256]{1,0:T(8,128)(2,1)} %param.15) | copy-start | bytes 98308
  62.9 5.9 %collective-permute-start.18 = (bf16[128,128]{1,0:T(8,128)(2,1)S(1)}, bf16[128,128]{1,0:T(8,128)(2,1)S(1)}, u32[]{:S(2)}, u32[]{:S(2)}) collective-permute-start(bf16[128,128]{1,0:T(8,128)(2,1)S(1)} %get-tuple-element.36), channel_id=1, source_target_pairs={{0,24},{1,25},{2,26},{3,27},{4,28},{5,29},{6,30},{7,31},{8,16},{9,... | collective-permute-start | bytes 98312 | tf_op jit(solution)/shard_map/ppermute | solution.py:21
  67.0 4.8 %collective-permute-start.19 = (bf16[128,128]{1,0:T(8,128)(2,1)S(1)}, bf16[128,128]{1,0:T(8,128)(2,1)S(1)}, u32[]{:S(2)}, u32[]{:S(2)}) collective-permute-start(bf16[128,128]{1,0:T(8,128)(2,1)S(1)} %get-tuple-element.38), channel_id=1, source_target_pairs={{0,16},{1,17},{2,18},{3,19},{4,20},{5,21},{6,22},{7,23},{8,24},{9,... | collective-permute-start | bytes 98312 | tf_op jit(solution)/shard_map/ppermute | solution.py:21
  67.0 4.8 %collective-permute-start.20 = (bf16[128,128]{1,0:T(8,128)(2,1)S(1)}, bf16[128,128]{1,0:T(8,128)(2,1)S(1)}, u32[]{:S(2)}, u32[]{:S(2)}) collective-permute-start(bf16[128,128]{1,0:T(8,128)(2,1)S(1)} %get-tuple-element.37), channel_id=1, source_target_pairs={{0,8},{1,9},{2,10},{3,11},{4,12},{5,13},{6,14},{7,15},{8,0},{9,1},... | collective-permute-start | bytes 98312 | tf_op jit(solution)/shard_map/ppermute | solution.py:21
  67.6 4.7 %collective-permute-start.12 = (bf16[128,128]{1,0:T(8,128)(2,1)S(1)}, bf16[128,128]{1,0:T(8,128)(2,1)S(1)}, u32[]{:S(2)}, u32[]{:S(2)}) collective-permute-start(bf16[128,128]{1,0:T(8,128)(2,1)S(1)} %copy-done.12), channel_id=1, source_target_pairs={{0,1},{1,0},{2,3},{3,2},{4,5},{5,4},{6,7},{7,6},{8,9},{9,8},{10,11... | collective-permute-start | bytes 98312 | tf_op jit(solution)/shard_map/ppermute | solution.py:21
  67.6 4.8 %collective-permute-start.11 = (bf16[128,128]{1,0:T(8,128)(2,1)S(1)}, bf16[128,128]{1,0:T(8,128)(2,1)S(1)}, u32[]{:S(2)}, u32[]{:S(2)}) collective-permute-start(bf16[128,128]{1,0:T(8,128)(2,1)S(1)} %slice.64.rest_3_), channel_id=1, source_target_pairs={{0,1},{1,0},{2,3},{3,2},{4,5},{5,4},{6,7},{7,6},{8,9},{9,8},{10,11... | collective-permute-start | bytes 98312 | tf_op jit(solution)/shard_map/ppermute | solution.py:21
  68.9 3.6 %collective-permute-start.10 = (bf16[128,128]{1,0:T(8,128)(2,1)S(1)}, bf16[128,128]{1,0:T(8,128)(2,1)S(1)}, u32[]{:S(2)}, u32[]{:S(2)}) collective-permute-start(bf16[128,128]{1,0:T(8,128)(2,1)S(1)} %slice.63.rest_2_), channel_id=1, source_target_pairs={{0,1},{1,0},{2,3},{3,2},{4,5},{5,4},{6,7},{7,6},{8,9},{9,8},{10,11... | collective-permute-start | bytes 98312 | tf_op jit(solution)/shard_map/ppermute | solution.py:21
  71.8 1.2 %collective-permute-start.9 = (bf16[128,128]{1,0:T(8,128)(2,1)S(1)}, bf16[128,128]{1,0:T(8,128)(2,1)S(1)}, u32[]{:S(2)}, u32[]{:S(2)}) collective-permute-start(bf16[128,128]{1,0:T(8,128)(2,1)S(1)} %slice.62.rest_1_), channel_id=1, source_target_pairs={{0,1},{1,0},{2,3},{3,2},{4,5},{5,4},{6,7},{7,6},{8,9},{9,8},{10,11... | collective-permute-start | bytes 98312 | tf_op jit(solution)/shard_map/ppermute | solution.py:21
  71.8 1.4 %collective-permute-start.8 = (bf16[128,128]{1,0:T(8,128)(2,1)S(1)}, bf16[128,128]{1,0:T(8,128)(2,1)S(1)}, u32[]{:S(2)}, u32[]{:S(2)}) collective-permute-start(bf16[128,128]{1,0:T(8,128)(2,1)S(1)} %slice.61.rest_0_), channel_id=1, source_target_pairs={{0,1},{1,0},{2,3},{3,2},{4,5},{5,4},{6,7},{7,6},{8,9},{9,8},{10,11... | collective-permute-start | bytes 98312 | tf_op jit(solution)/shard_map/ppermute | solution.py:21
  72.3 3.4 %collective-permute-start.21 = (f32[64,128]{1,0:T(8,128)S(1)}, f32[64,128]{1,0:T(8,128)S(1)}, u32[]{:S(2)}, u32[]{:S(2)}) collective-permute-start(f32[64,128]{1,0:T(8,128)S(1)} %get-tuple-element.40), channel_id=1, source_target_pairs={{0,1},{1,0},{2,3},{3,2},{4,5},{5,4},{6,7},{7,6},{8,9},{9,8},{10,11... | collective-permute-start | bytes 98312 | tf_op jit(solution)/shard_map/ppermute | solution.py:21

commit v3 on v2

v3 whole, which is shorter than its diff:
```python
import functools

import jax
import jax.numpy as jnp
from jax import lax
from jax.experimental import pallas as pl
from jax.experimental.pallas import tpu as pltpu
from jax.sharding import PartitionSpec as P

CAP = 2
amplitude = 0.2
bf16 = jnp.bfloat16
f32 = jnp.float32
MIB = 2**20
FRONT = 52
VMEM = pl.BlockSpec(memory_space=pltpu.VMEM)
SMEM = pl.BlockSpec(memory_space=pltpu.SMEM)
HBM = pl.BlockSpec(memory_space=pltpu.HBM)


def swapped(value, mask):
    pairs = [(source, source ^ mask) for source in range(lax.axis_size("pts"))]
    return lax.ppermute(value, "pts", pairs)


def call(kernel, outs, name, flops, moved, room=6, ins=None, scratch=()):
    more = {} if ins is None else {"in_specs": ins}
    return pl.pallas_call(
        kernel,
        out_shape=outs,
        name=name,
        compiler_params=pltpu.CompilerParams(vmem_limit_bytes=room * MIB),
        scratch_shapes=list(scratch),
        cost_estimate=pl.CostEstimate(flops=flops, bytes_accessed=moved, transcendentals=0),
        **more,
    )


def dot(a, b):
    return jnp.dot(a, b, preferred_element_type=f32)


def two(value):
    high = value.astype(bf16)
    return high, (value - high.astype(f32)).astype(bf16)


def dot3(a, b):
    (ah, al), (bh, bl) = a, b
    return dot(ah, bh) + (dot(ah, bl) + dot(al, bh))


def out(shape, kind):
    return jax.ShapeDtypeStruct(shape, kind)


def front_kernel(
    rows, leaf, bits, rank, levels, sizes, half, core_ref, residual_ref, inverse_ref, right_ref, left_ref,
    mine_ref, other_ref, keep_ref, send_ref, small_ref, left16_ref,
    residual_got, inverse_got, right_got, left_got, high_ref, low_ref, sems,
):
    places = [(residual_ref, residual_got), (inverse_ref, inverse_got)]
    order = levels + list(range(bits))
    for level in order:
        places.append((right_ref.at[level], right_got.at[level]))
        places.append((left_ref.at[level], left_got.at[level]))
    copies = [pltpu.make_async_copy(a, b, sems.at[k]) for k, (a, b) in enumerate(places)]
    for copy in copies:
        copy.start()
    right_copy = {level: copies[2 + 2 * k] for k, level in enumerate(order)}
    left_copy = {level: copies[3 + 2 * k] for k, level in enumerate(order)}
    copies[0].wait()
    copies[1].wait()
    x = [
        dot(inverse_got[b * leaf : (b + 1) * leaf, :], residual_got[b * leaf : (b + 1) * leaf, :])
        for b in range(rows // leaf)
    ]
    x = jnp.concatenate(x, 0)
    for level, size in zip(levels, sizes):
        right_copy[level].wait()
        projected = [
            dot3(two(right_got[level, a : a + size, :].T), two(x[a : a + size, :]))
            for a in range(0, rows, size)
        ]
        left_copy[level].wait()
        x = jnp.concatenate(
            [
                x[a * size : (a + 1) * size, :]
                + dot3(two(left_got[level, a * size : (a + 1) * size, :]), two(projected[a ^ 1]))
                for a in range(rows // size)
            ],
            0,
        )
    first = core_ref[0] == 0
    mine_ref[...] = jnp.where(first, x[:, :half], x[:, half:])
    other_ref[...] = jnp.where(first, x[:, half:], x[:, :half])
    xh, xl = two(x)
    for i in range(bits):
        right_copy[i].wait()
        at = slice(i * rank, (i + 1) * rank)
        high, low = two(right_got[i].T)
        high_ref[at, :] = high
        low_ref[at, :] = low
        left_copy[i].wait()
        left16_ref[:, at] = left_got[i].astype(bf16)
        if i:
            small_ref[small_at(i, rank), :] = dot(high_ref[: i * rank, :], left16_ref[:, at]).astype(bf16)
    a = dot(high_ref[...], xh) + (dot(high_ref[...], xl) + dot(low_ref[...], xh))
    keep_ref[...] = jnp.where(first, a[:, :half], a[:, half:])
    send_ref[...] = jnp.where(first, a[:, half:], a[:, :half]).astype(bf16)


def spread(value, depth):
    value = jnp.concatenate([value, jnp.zeros((depth - value.shape[0], value.shape[1]), f32)], 0) if depth > value.shape[0] else value
    one = value.astype(bf16)
    rest = value - one.astype(f32)
    second = rest.astype(bf16)
    return one, second, (rest - second.astype(f32)).astype(bf16)


def gathered(ref, at, depth):
    a = ref[at : at + depth, :].astype(f32)
    b = ref[at + depth : at + 2 * depth, :].astype(f32)
    return a + b + ref[at + 2 * depth : at + 3 * depth, :].astype(f32)


def put_spots(ref, at, depth, value):
    for k, part in enumerate(spread(value, depth)):
        ref[at + k * depth : at + (k + 1) * depth, :] = part


def linked(level, rank, own, theirs, own_small, their_small):
    cut = level * rank
    mine16, theirs16 = own[cut : cut + rank, :].astype(bf16), theirs[cut : cut + rank, :]
    return own[:cut, :] + theirs[:cut, :].astype(f32) + (dot(own_small, theirs16) + dot(their_small, mine16))


def small_at(level, rank):
    at = level * (level - 1) // 2 * rank
    return slice(at, at + level * rank)


def first_merge(level, rank, depth, keep_ref, got_ref, small_ref, their_ref, spot_ref, y_ref, message_ref, last_ref):
    at = small_at(level, rank)
    y = linked(level, rank, keep_ref[...], got_ref[...], small_ref[at, :], their_ref[at, :])
    y_ref[...] = y
    cut = level * rank
    message_ref[:cut, :] = y.astype(bf16)
    put_spots(message_ref, cut, depth, spot_ref[...])
    last_ref[...] = keep_ref[cut : cut + rank, :].astype(bf16)


def merge(level, rank, apart, along, n, depths, y_in, own_ref, got_ref, *rest):
    own_small_ref, their_small_ref = rest[:2] if apart else (own_ref, got_ref)
    y_ref, message_ref = rest[2:] if apart else rest
    base = 0 if apart else (level + 1) * rank
    spots_at = (level + 1) * rank + (0 if apart else level * (level + 1) // 2 * rank)
    at = small_at(level, rank)
    at = slice(base + at.start, base + at.stop)
    y = linked(level, rank, y_in[...], got_ref[...], own_small_ref[at, :], their_small_ref[at, :])
    y_ref[...] = y
    cut = level * rank
    message_ref[:cut, :] = y.astype(bf16)
    inner = level * (level - 1) // 2 * rank if along else 0
    if inner:
        total = own_small_ref[base : base + inner, :].astype(f32) + their_small_ref[base : base + inner, :].astype(f32)
        message_ref[cut : cut + inner, :] = total.astype(bf16)
    spots = jnp.concatenate(
        [gathered(own_ref, spots_at, depths[0])[:n, :], gathered(got_ref, spots_at, depths[0])[:n, :]], 0
    )
    put_spots(message_ref, cut + inner, depths[1], spots)


def partial_kernel(bits, rank, mine_ref, rest_ref, other_ref, left_ref, left_other_ref, last_ref, *refs):
    shares, others, outs = refs[: bits - 1], refs[bits - 1 : 2 * bits - 2], refs[2 * bits - 2 :]
    top = [s[...] for s in shares[:-1]]
    left = left_ref[:, rank:]
    outs[0][...] = mine_ref[...] + dot(left, jnp.concatenate([s[...] for s in shares], 0))
    outs[1][...] = rest_ref[...] + dot(left, jnp.concatenate([s[...] for s in others], 0))
    outs[2][...] = other_ref[...] + dot(left_other_ref[:, rank:], jnp.concatenate(top + [last_ref[...]], 0))


def coeff_kernel(rank, mine_ref, other_ref, left_ref, left_other_ref, got_ref, final_ref, coeff_ref):
    rows = mine_ref.shape[0]
    share = got_ref[:rank, :]
    x = mine_ref[...] + dot(left_ref[:, :rank], share)
    final_ref[...] = x
    coeff_ref[:rows, :] = x.astype(bf16)
    coeff_ref[rows:, :] = (other_ref[...] + dot(left_other_ref[:, :rank], share)).astype(bf16)


def weigh_kernel(mask, plane, far, tile, leaf, blocks, n, depth, rank, me_ref, first_ref, count_ref, own_ref, got_ref, point_ref, coeff_ref, out_ref, weight_ref):
    me = me_ref[0]
    scale = 2.0 * leaf
    spots = jnp.concatenate([gathered(own_ref, rank, depth)[:n, :], gathered(got_ref, rank, depth)[:n, :]], 0) * scale
    spots = spots.T
    weight_ref[...] = jnp.zeros_like(weight_ref)
    for z in range(far):
        q = mask + plane * z
        for r in range(2):
            column = jnp.broadcast_to(spots[r * tile : (r + 1) * tile, q : q + 1], (tile, leaf))
            target = me ^ (2 * q + r)
            at = (2 * z + r) * tile
            for s in range(2):
                first = first_ref[target, me ^ s]
                count = count_ref[target, me ^ s]
                for k in range(CAP):
                    block = s * blocks + first + k
                    level = jnp.where(k < count, amplitude, 0.0)
                    distance = jnp.minimum(jnp.abs(column - point_ref[pl.ds(block, 1), :] * scale), 1.0)
                    left = 1.0 - distance
                    left = left * left
                    value = (left * left) * (1.0 + 4.0 * distance) * level
                    lanes = pl.ds(pl.multiple_of(block * leaf, leaf), leaf)
                    weight_ref[at : at + tile, lanes] = value.astype(bf16)
    out_ref[...] = dot(weight_ref[...], coeff_ref[...]).astype(out_ref.dtype)


def solved_kernel(rank, core_ref, mine_ref, rest_ref, left_ref, share_ref, out_ref):
    half = mine_ref.shape[1]
    x, y = mine_ref[...], rest_ref[...] + dot(left_ref[:, :rank], share_ref[...])
    first = core_ref[0] == 0
    out_ref[:, :half] = jnp.where(first, x, y)
    out_ref[:, half:] = jnp.where(first, y, x)


def body(
    residual_cols,
    leaf_inverse,
    basis_left,
    basis_right,
    point_pos,
    map_pos,
    prior_map,
    block_first,
    block_count,
):
    rows, samples = residual_cols.shape
    leaf = leaf_inverse.shape[1]
    rank = basis_left.shape[2]
    blocks = rows // leaf
    devices = lax.axis_size("pts")
    bits = devices.bit_length() - 1
    me = lax.axis_index("pts").astype(jnp.int32)
    core = me % 2
    me_s, core_s = me.reshape(1), core.reshape(1)
    levels = basis_left.shape[0]
    tile = map_pos.shape[0]
    half = samples // 2
    pair_count = bits * (bits - 1) // 2

    spot_other = swapped(map_pos, 1)
    inner = list(reversed(range(bits, levels)))
    sizes = [rows * devices // 2 ** (level + 1) for level in inner]
    solved_mine, solved_send, keep, send, small, left16 = call(
        functools.partial(front_kernel, rows, leaf, bits, rank, inner, sizes, half),
        [
            out((rows, half), f32),
            out((rows, half), f32),
            out((bits * rank, half), f32),
            out((bits * rank, half), bf16),
            out((pair_count * rank, rank), bf16),
            out((rows, bits * rank), bf16),
        ],
        "front",
        6 * bits * rank * rows * samples,
        8 * levels * rows * rank,
        room=FRONT,
        ins=[SMEM, HBM, HBM, HBM, HBM],
        scratch=[
            pltpu.VMEM((rows, samples), bf16),
            pltpu.VMEM((rows, leaf), bf16),
            pltpu.VMEM((levels, rows, rank), f32),
            pltpu.VMEM((levels, rows, rank), f32),
            pltpu.VMEM((bits * rank, rows), bf16),
            pltpu.VMEM((bits * rank, rows), bf16),
            pltpu.SemaphoreType.DMA((2 + 2 * levels,)),
        ],
    )(core_s, residual_cols, leaf_inverse, basis_right, basis_left)
    small_other = swapped(small, 1)
    left_other = swapped(left16, 1)
    got = swapped(send, 1)
    solved_other = swapped(solved_send, 1)

    shares, others = [None] * bits, [None] * bits
    top = bits - 1
    depth_of = lambda bit: max(16, 1 << (bit - 1))
    pairs_below = lambda level: level * (level - 1) // 2 * rank
    ahead = (1, 2)
    small_own, small_theirs = {}, {}
    previous = small, small_other
    for bit in ahead:
        kept = pairs_below(top - bit + 1)
        small_own[bit] = (previous[0][:kept].astype(f32) + previous[1][:kept].astype(f32)).astype(bf16)
        small_theirs[bit] = swapped(small_own[bit], 1 << bit)
        previous = small_own[bit], small_theirs[bit]
    spot_rows = jnp.concatenate([map_pos, spot_other]).reshape(1, 2 * tile)
    y, message, last = call(
        functools.partial(first_merge, top, rank, depth_of(1)),
        [
            out((top * rank, half), f32),
            out((top * rank + 3 * depth_of(1), half), bf16),
            out((rank, half), bf16),
        ],
        "merge0",
        4 * top * rank * rank * half,
        8 * top * rank * half,
    )(keep, got, small, small_other, spot_rows)
    shares[top] = got[top * rank :]
    others[top] = swapped(last, 1)
    for bit in range(1, bits):
        level = top - bit
        arrived = swapped(message, 1 << bit)
        share = arrived[level * rank : (level + 1) * rank]
        shares[level] = share
        others[level] = swapped(share, 1)
        if level:
            apart, along = bit in ahead, bit + 1 not in ahead
            inner_rows = pairs_below(level) if along else 0
            y, message = call(
                functools.partial(
                    merge, level, rank, apart, along, 1 << (bit - 1), (depth_of(bit), depth_of(bit + 1))
                ),
                [
                    out((level * rank, half), f32),
                    out((level * rank + inner_rows + 3 * depth_of(bit + 1), half), bf16),
                ],
                f"merge{bit}",
                4 * level * rank * rank * half,
                8 * level * rank * half,
            )(y, message, arrived, *((small_own[bit], small_theirs[bit]) if apart else ()))

    part_mine, part_rest, part_other = call(
        functools.partial(partial_kernel, bits, rank),
        [out((rows, half), f32)] * 3,
        "partial",
        6 * bits * rows * rank * half,
        24 * rows * half,
    )(solved_mine, solved_send, solved_other, left16, left_other, last, *shares[1:], *others[1:])
    final_mine, coeffs = call(
        functools.partial(coeff_kernel, rank),
        [out((rows, half), f32), out((2 * rows, half), bf16)],
        "coeffs",
        4 * rows * rank * half,
        16 * rows * half,
    )(part_mine, part_other, left16, left_other, arrived)

    points = [lax.dynamic_slice_in_dim(point_pos, s * rows, rows).reshape(blocks, leaf) for s in (me, me ^ 1)]
    points = jnp.concatenate(points, 0)
    plane = 4
    far = devices // (2 * plane)
    depth = depth_of(bits - 1)

    def weighed(mask, coeffs):
        return call(
            functools.partial(
                weigh_kernel, mask, plane, far, tile, leaf, blocks, 1 << (bits - 2), depth, rank
            ),
            out((far * 2 * tile, half), bf16 if mask else f32),
            f"weigh{mask}",
            16 * far * tile * rows * half,
            16 * far * tile * half,
            room=8 if far <= 4 else 16,
            ins=[SMEM, SMEM, SMEM, VMEM, VMEM, VMEM, VMEM],
            scratch=[pltpu.VMEM((far * 2 * tile, 2 * rows), bf16)],
        )(me_s, block_first, block_count, message, arrived, points, coeffs)

    sent = [swapped(weighed(mask, coeffs), mask << 1) for mask in (3, 1, 2)]
    solved_out = call(
        functools.partial(solved_kernel, rank),
        out((rows, samples), f32),
        "solved",
        2 * rows * rank * half,
        16 * rows * samples,
        ins=[SMEM, VMEM, VMEM, VMEM, VMEM],
    )(core_s, final_mine, part_rest, left16, others[0])
    coeffs, solved_out = lax.optimization_barrier((coeffs, solved_out))
    total = weighed(0, coeffs)
    for partial in sent:
        total = total + partial.astype(f32)
    total = total.reshape(far, 2 * tile, half)
    result = total[0]
    for mask in reversed(range(1, far)):
        result = result + swapped(total[mask].astype(bf16), mask << 3).astype(f32)
    rest = swapped(result[tile:], 1)

    mapped = jnp.where(
        core == 0,
        jnp.concatenate([result[:tile], rest], 1),
        jnp.concatenate([rest, result[:tile]], 1),
    )
    return (solved_out, prior_map.astype(f32) + mapped)


def solution(mesh):
    in_specs = (
        P(("groups", "pts"), None),
        P(("groups", "pts"), None),
        P(None, ("groups", "pts"), None),
        P(None, ("groups", "pts"), None),
        P(),
        P("pts"),
        P(("groups", "pts"), None),
        P(),
        P(),
    )
    out_specs = (P(("groups", "pts"), None), P(("groups", "pts"), None))
    return jax.shard_map(body, mesh=mesh, in_specs=in_specs, out_specs=out_specs, check_vma=False)
```

time: 77 us -> 65.2 us (0.85)
  local copies, waits for them, and re-layouts: 12.7 us -> 2.74 us
  Pallas kernels: 19.7 us -> 16.7 us
  waiting for transfers between devices: 22.4 us -> 24 us
    unnamed x34 -> x14, local copies, waits for them, and re-layouts: 11.1 us -> 1.87 us
    pallas_call x11, Pallas kernels: 19.5 us -> 16.5 us  [the longest x4 8.3 us: weighed(): call(functools.partial(weigh_kernel, mask, plane, far, tile, leaf, blocks...]
    ppermute x22 -> x23, waiting for transfers between devices: 22.4 us -> 24 us  [swapped(): return lax.ppermute(value, 'pts', pairs)]
    ppermute x22 -> x23, starting transfers between devices: 19.8 us -> 19.7 us  [swapped(): return lax.ppermute(value, 'pts', pairs)]
  transfers between devices with their start and end apart: 22 -> 23, of which waited for: 9 -> 11; matrix products, arithmetic and copies ran while one was open for 2% -> 2% of each run, Pallas kernels for 19% -> 14%
where the time goes in v3:
time: 65.2 us; the launch traced here: 65 us
  waiting for transfers between devices  24 us (37%)
  starting transfers between devices  19.7 us (30%)
  Pallas kernels  16.7 us (26%)
  local copies, waits for them, and re-layouts  2.74 us (4%)
  other arithmetic  0.9 us (1%)
  between operations  0.9 us (1%)
    ppermute x23, waiting for transfers between devices, swapped(): return lax.ppermute(value, 'pts', pairs)  24 us
    ppermute x23, starting transfers between devices, swapped(): return lax.ppermute(value, 'pts', pairs)  19.7 us
    pallas_call x4, Pallas kernels, weighed(): call(functools.partial(weigh_kernel, mask, plane, far, tile, leaf, blocks...  8.3 us
    pallas_call x1, Pallas kernels, body(): call(functools.partial(front_kernel, rows, leaf, bits, rank, inner, sizes...  5.28 us
    unnamed x14, local copies, waits for them, and re-layouts  1.87 us
  transfers between devices with their start and end apart: 23, of which 11 were waited for; matrix products, arithmetic and copies ran while one was open for 2% of the time, Pallas kernels for 14%

profile of v3, /device:TPU:0, one launch (start us, length us, event | category | flops | bytes accessed | tf_op | source)
XLA Modules:
  0.0 65.0 jit_solution(9742835193088902476)
XLA Ops:
  0.7 0.9 %copy-done.1 = bf16[512,256]{1,0:T(8,128)(2,1)S(1)} copy-done((bf16[512,256]{1,0:T(8,128)(2,1)S(1)}, bf16[512,256]{1,0:T(8,128)(2,1)}, u32[]{:S(2)}) %copy-start.1) | copy-done | bytes 262168
  1.6 0.9 %copy-done.2 = bf16[512,128]{1,0:T(8,128)(2,1)S(1)} copy-done((bf16[512,128]{1,0:T(8,128)(2,1)S(1)}, bf16[512,128]{1,0:T(8,128)(2,1)}, u32[]{:S(2)}) %copy-start.2) | copy-done | bytes 131096
  2.5 5.3 %front.1 = (f32[512,128]{1,0:T(8,128)S(1)}, f32[512,128]{1,0:T(8,128)S(1)}, f32[640,128]{1,0:T(8,128)S(1)}, bf16[640,128]{1,0:T(8,128)(2,1)S(1)}, bf16[1280,128]...) custom-call(s32[1]{0:T(128)} %bitcast.core_ref, bf16[512,256]{1,0:T(8,128)(2,1)S(1)} %copy-done.1, ...), custom_call_target="tpu_custom_call" | custom-call | flops 503316480 | bytes 3670016 | tf_op jit(solution)/shard_map/front/pallas_call | solution.py:255
  7.8 0.5 collective-permute-start.3
  8.3 0.1 collective-permute-start.4
  8.4 0.4 collective-permute-start.2
  8.8 0.7 %collective-permute-done.3.their_ref = bf16[1280,128]{1,0:T(8,128)(2,1)S(1)} collective-permute-done((bf16[1280,128]{1,0:T(8,128)(2,1)S(1)}, bf16[1280,128]{1,0:T(8,128)(2,1)S(1)}, u32[]{:S(2)}, u32[]{:S(2)}) %collective-permute-start.3) | collective-permute-done | bytes 327712 | tf_op jit(solution)/shard_map/ppermute | solution.py:23
  9.6 0.1 add_convert_fusion.rest_0_
  9.6 2.9 %collective-permute-start.6 = (bf16[768,128]{1,0:T(8,128)(2,1)S(1)}, bf16[768,128]{1,0:T(8,128)(2,1)S(1)}, u32[]{:S(2)}, u32[]{:S(2)}) collective-permute-start(bf16[768,128]{1,0:T(8,128)(2,1)S(1)} %add_convert_fusion.rest_0_), channel_id=1, source_target_pairs={{0,2},{1,3},{2,0},{3,1},{4,6},{5,7},{6,4},{7,5},{8,10},{9,11},{10,... | collective-permute-start | bytes 589832 | tf_op jit(solution)/shard_map/ppermute | solution.py:23
  12.5 0.0 collective-permute-done.4
  12.5 0.1 maximum_bitcast_fusion.spot_ref
  12.6 0.0 collective-permute-done.2.got_ref
  12.6 0.2 merge0.1
  12.9 0.1 collective-permute-start.5
  13.0 0.0 collective-permute-start.1
  13.0 0.5 collective-permute-start
  13.5 7.3 %collective-permute-done.5.got_ref = bf16[560,128]{1,0:T(8,128)(2,1)S(1)} collective-permute-done((bf16[560,128]{1,0:T(8,128)(2,1)S(1)}, bf16[560,128]{1,0:T(8,128)(2,1)S(1)}, u32[]{:S(2)}, u32[]{:S(2)}) %collective-permute-start.5) | collective-permute-done | bytes 143392 | tf_op jit(solution)/shard_map/ppermute | solution.py:23
  20.8 0.0 collective-permute-done.6.rest_1_
  20.8 0.2 merge1.1
  21.0 1.8 %collective-permute-start.7 = (bf16[432,128]{1,0:T(8,128)(2,1)S(1)}, bf16[432,128]{1,0:T(8,128)(2,1)S(1)}, u32[]{:S(2)}, u32[]{:S(2)}) collective-permute-start(bf16[432,128]{1,0:T(8,128)(2,1)S(1)} %get-tuple-element.33.own_ref), channel_id=1, source_target_pairs={{0,4},{1,5},{2,6},{3,7},{4,0},{5,1},{6,2},{7,3},{8,12},{9,13},{10,... | collective-permute-start | bytes 331784 | tf_op jit(solution)/shard_map/ppermute | solution.py:23
  22.9 0.3 collective-permute-start.8
  23.2 0.0 collective-permute-start.13
  23.2 4.7 %collective-permute-done.8.rest_1_ = bf16[384,128]{1,0:T(8,128)(2,1)S(1)} collective-permute-done((bf16[384,128]{1,0:T(8,128)(2,1)S(1)}, bf16[384,128]{1,0:T(8,128)(2,1)S(1)}, u32[]{:S(2)}, u32[]{:S(2)}) %collective-permute-start.8) | collective-permute-done | bytes 98336 | tf_op jit(solution)/shard_map/ppermute | solution.py:23
  27.9 0.0 collective-permute-done.7.got_ref
  27.9 0.2 merge2.1
  28.1 1.6 %collective-permute-start.9 = (bf16[432,128]{1,0:T(8,128)(2,1)S(1)}, bf16[432,128]{1,0:T(8,128)(2,1)S(1)}, u32[]{:S(2)}, u32[]{:S(2)}) collective-permute-start(bf16[432,128]{1,0:T(8,128)(2,1)S(1)} %get-tuple-element.34.own_ref), channel_id=1, source_target_pairs={{0,8},{1,9},{2,10},{3,11},{4,12},{5,13},{6,14},{7,15},{8,0},{9,1},... | collective-permute-start | bytes 331784 | tf_op jit(solution)/shard_map/ppermute | solution.py:23
  29.7 0.8 %dynamic-slice_bitcast_fusion.1 = (f32[4,128]{1,0:T(4,128)S(1)}, f32[4,128]{1,0:T(4,128)S(1)}) fusion(f32[16384]{0:T(1024)} %param.13, s32[]{:T(128)S(6)} %select_n.23, s32[]{:T(128)S(6)} %select_n.24), kind=kLoop, calls=%fused_computation.10 | loop fusion | bytes 8200 | tf_op jit(solution)/shard_map/reshape | solution.py:348
  30.5 0.0 collective-permute-start.12
  30.6 2.3 %collective-permute-done.9.got_ref = bf16[432,128]{1,0:T(8,128)(2,1)S(1)} collective-permute-done((bf16[432,128]{1,0:T(8,128)(2,1)S(1)}, bf16[432,128]{1,0:T(8,128)(2,1)S(1)}, u32[]{:S(2)}, u32[]{:S(2)}) %collective-permute-start.9) | collective-permute-done | bytes 110624 | tf_op jit(solution)/shard_map/ppermute | solution.py:23
  32.9 0.0 collective-permute-start.11
  32.9 0.8 %merge3.1 = (f32[128,128]{1,0:T(8,128)}, bf16[176,128]{1,0:T(8,128)(2,1)S(1)}) custom-call(f32[256,128]{1,0:T(8,128)S(1)} %get-tuple-element.37.y_in, bf16[432,128]{1,0:T(8,128)(2,1)S(1)} %get-tuple-element.34.own_ref, bf16[432,128]{1,0:T(8,128)(2,1)S(1)} %collective-permute-done.9.got_ref), custom_call_target="tpu_custom_call" | custom-call | flops 8388608 | bytes 131072 | tf_op jit(solution)/shard_map/merge3/pallas_call | solution.py:320
  33.7 0.0 collective-permute-done.other_ref
  33.7 0.5 collective-permute-start.10
  34.2 2.6 %collective-permute-start.14 = (bf16[176,128]{1,0:T(8,128)(2,1)S(1)}, bf16[176,128]{1,0:T(8,128)(2,1)S(1)}, u32[]{:S(2)}, u32[]{:S(2)}) collective-permute-start(bf16[176,128]{1,0:T(8,128)(2,1)S(1)} %get-tuple-element.38.own_ref), channel_id=1, source_target_pairs={{0,16},{1,17},{2,18},{3,19},{4,20},{5,21},{6,22},{7,23},{8,24},{9,... | collective-permute-start | bytes 135176 | tf_op jit(solution)/shard_map/ppermute | solution.py:23
  36.8 0.0 collective-permute-done.12.refs_6_
  36.8 0.0 collective-permute-done.1.left_other_ref
  36.8 0.0 collective-permute-done.10.refs_4_
  36.8 0.0 copy-start.3
  36.9 0.0 copy-start.4
  36.9 0.6 partial.1
  37.5 2.2 %collective-permute-done.14.got_ref = bf16[176,128]{1,0:T(8,128)(2,1)S(1)} collective-permute-done((bf16[176,128]{1,0:T(8,128)(2,1)S(1)}, bf16[176,128]{1,0:T(8,128)(2,1)S(1)}, u32[]{:S(2)}, u32[]{:S(2)}) %collective-permute-start.14) | collective-permute-done | bytes 45088 | tf_op jit(solution)/shard_map/ppermute | solution.py:23
  39.6 0.2 coeffs.1
  39.9 2.1 %weigh3.1 = bf16[512,128]{1,0:T(8,128)(2,1)S(1)} custom-call(s32[1]{0:T(128)} %bitcast.2.me_ref, s32[32,32]{1,0:T(8,128)S(1)} %copy-done.3, s32[32,32]{1,0:T(8,128)S(1)} %copy-done.4, bf16[176,128]{1,0:T(8,128)(2,1)S(1)} %get-tuple-element.38.own_ref, bf16[176,128]{1,0:T(8,128)(2,1)S(1)} %collective-permute-done.14.got_ref, ...), custom_call_target="tpu_custom_call" | custom-call | flops 268435456 | bytes 524288 | tf_op jit(solution)/shard_map/weigh3/pallas_call | solution.py:355
  42.0 2.4 %collective-permute-start.16 = (bf16[512,128]{1,0:T(8,128)(2,1)S(1)}, bf16[512,128]{1,0:T(8,128)(2,1)S(1)}, u32[]{:S(2)}, u32[]{:S(2)}) collective-permute-start(bf16[512,128]{1,0:T(8,128)(2,1)S(1)} %weigh3.1), channel_id=1, source_target_pairs={{0,6},{1,7},{2,4},{3,5},{4,2},{5,3},{6,0},{7,1},{8,14},{9,15},{10,... | collective-permute-start | bytes 393224 | tf_op jit(solution)/shard_map/ppermute | solution.py:23
  44.3 2.1 %weigh1.1 = bf16[512,128]{1,0:T(8,128)(2,1)S(1)} custom-call(s32[1]{0:T(128)} %bitcast.2.me_ref, s32[32,32]{1,0:T(8,128)S(1)} %copy-done.3, s32[32,32]{1,0:T(8,128)S(1)} %copy-done.4, bf16[176,128]{1,0:T(8,128)(2,1)S(1)} %get-tuple-element.38.own_ref, bf16[176,128]{1,0:T(8,128)(2,1)S(1)} %collective-permute-done.14.got_ref, ...), custom_call_target="tpu_custom_call" | custom-call | flops 268435456 | bytes 524288 | tf_op jit(solution)/shard_map/weigh1/pallas_call | solution.py:355
  46.4 0.6 collective-permute-start.17
  47.0 2.1 %weigh2.1 = bf16[512,128]{1,0:T(8,128)(2,1)S(1)} custom-call(s32[1]{0:T(128)} %bitcast.2.me_ref, s32[32,32]{1,0:T(8,128)S(1)} %copy-done.3, s32[32,32]{1,0:T(8,128)S(1)} %copy-done.4, bf16[176,128]{1,0:T(8,128)(2,1)S(1)} %get-tuple-element.38.own_ref, bf16[176,128]{1,0:T(8,128)(2,1)S(1)} %collective-permute-done.14.got_ref, ...), custom_call_target="tpu_custom_call" | custom-call | flops 268435456 | bytes 524288 | tf_op jit(solution)/shard_map/weigh2/pallas_call | solution.py:355
  49.1 0.7 %collective-permute-start.18 = (bf16[512,128]{1,0:T(8,128)(2,1)S(1)}, bf16[512,128]{1,0:T(8,128)(2,1)S(1)}, u32[]{:S(2)}, u32[]{:S(2)}) collective-permute-start(bf16[512,128]{1,0:T(8,128)(2,1)S(1)} %weigh2.1), channel_id=1, source_target_pairs={{0,4},{1,5},{2,6},{3,7},{4,0},{5,1},{6,2},{7,3},{8,12},{9,13},{10,... | collective-permute-start | bytes 393224 | tf_op jit(solution)/shard_map/ppermute | solution.py:23
  49.8 0.0 collective-permute-start.15
  49.8 1.2 %collective-permute-done.15.share_ref = bf16[128,128]{1,0:T(8,128)(2,1)S(1)} collective-permute-done((bf16[128,128]{1,0:T(8,128)(2,1)S(1)}, bf16[128,128]{1,0:T(8,128)(2,1)S(1)}, u32[]{:S(2)}, u32[]{:S(2)}) %collective-permute-start.15) | collective-permute-done | bytes 32800 | tf_op jit(solution)/shard_map/ppermute | solution.py:23
  51.0 1.0 %solved.1 = f32[512,256]{1,0:T(8,128)} custom-call(s32[1]{0:T(128)} %bitcast.core_ref, f32[512,128]{1,0:T(8,128)S(1)} %get-tuple-element.40.mine_ref, f32[512,128]{1,0:T(8,128)S(1)} %get-tuple-element.41.rest_ref, bf16[512,640]{1,0:T(8,128)(2,1)S(1)} %copy-done, bf16[128,128]{1,0:T(8,128)(2,1)S(1)} %collective-permute-done.15.share_ref), custom_call_target="tpu_custom_call" | custom-call | flops 16777216 | bytes 2097152 | tf_op jit(solution)/shard_map/solved/pallas_call | solution.py:369
  52.0 2.0 %weigh0.1 = f32[512,128]{1,0:T(8,128)S(1)} custom-call(s32[1]{0:T(128)} %bitcast.2.me_ref, s32[32,32]{1,0:T(8,128)S(1)} %copy-done.3, s32[32,32]{1,0:T(8,128)S(1)} %copy-done.4, bf16[176,128]{1,0:T(8,128)(2,1)S(1)} %get-tuple-element.38.own_ref, bf16[176,128]{1,0:T(8,128)(2,1)S(1)} %collective-permute-done.14.got_ref, ...), custom_call_target="tpu_custom_call" | custom-call | flops 268435456 | bytes 524288 | tf_op jit(solution)/shard_map/weigh0/pallas_call | solution.py:355
  54.1 0.0 collective-permute-done.16
  54.1 0.1 collective-permute-done.18
  54.1 0.1 fusion.3
  54.2 3.6 %collective-permute-start.19 = (bf16[128,128]{1,0:T(8,128)(2,1)S(1)}, bf16[128,128]{1,0:T(8,128)(2,1)S(1)}, u32[]{:S(2)}, u32[]{:S(2)}) collective-permute-start(bf16[128,128]{1,0:T(8,128)(2,1)S(1)} %get-tuple-element.46), channel_id=1, source_target_pairs={{0,24},{1,25},{2,26},{3,27},{4,28},{5,29},{6,30},{7,31},{8,16},{9,... | collective-permute-start | bytes 98312 | tf_op jit(solution)/shard_map/ppermute | solution.py:23
  57.8 0.0 collective-permute-start.21
  57.8 0.8 %collective-permute-start.20 = (bf16[128,128]{1,0:T(8,128)(2,1)S(1)}, bf16[128,128]{1,0:T(8,128)(2,1)S(1)}, u32[]{:S(2)}, u32[]{:S(2)}) collective-permute-start(bf16[128,128]{1,0:T(8,128)(2,1)S(1)} %get-tuple-element.48), channel_id=1, source_target_pairs={{0,16},{1,17},{2,18},{3,19},{4,20},{5,21},{6,22},{7,23},{8,24},{9,... | collective-permute-start | bytes 98312 | tf_op jit(solution)/shard_map/ppermute | solution.py:23
  58.7 1.3 %collective-permute-done.19 = bf16[128,128]{1,0:T(8,128)(2,1)S(1)} collective-permute-done((bf16[128,128]{1,0:T(8,128)(2,1)S(1)}, bf16[128,128]{1,0:T(8,128)(2,1)S(1)}, u32[]{:S(2)}, u32[]{:S(2)}) %collective-permute-start.19) | collective-permute-done | bytes 32800 | tf_op jit(solution)/shard_map/ppermute | solution.py:23
  60.0 1.9 %collective-permute-done.21 = bf16[128,128]{1,0:T(8,128)(2,1)S(1)} collective-permute-done((bf16[128,128]{1,0:T(8,128)(2,1)S(1)}, bf16[128,128]{1,0:T(8,128)(2,1)S(1)}, u32[]{:S(2)}, u32[]{:S(2)}) %collective-permute-start.21) | collective-permute-done | bytes 32800 | tf_op jit(solution)/shard_map/ppermute | solution.py:23
  61.9 1.1 %collective-permute-done.20 = bf16[128,128]{1,0:T(8,128)(2,1)S(1)} collective-permute-done((bf16[128,128]{1,0:T(8,128)(2,1)S(1)}, bf16[128,128]{1,0:T(8,128)(2,1)S(1)}, u32[]{:S(2)}, u32[]{:S(2)}) %collective-permute-start.20) | collective-permute-done | bytes 32800 | tf_op jit(solution)/shard_map/ppermute | solution.py:23
  63.0 0.1 collective-permute-start.22
  63.1 1.2 %collective-permute-done.22 = f32[64,128]{1,0:T(8,128)S(1)} collective-permute-done((f32[64,128]{1,0:T(8,128)S(1)}, f32[64,128]{1,0:T(8,128)S(1)}, u32[]{:S(2)}, u32[]{:S(2)}) %collective-permute-start.22) | collective-permute-done | bytes 32800 | tf_op jit(solution)/shard_map/ppermute | solution.py:23
  64.3 0.6 fusion.2
  (23 shorter events, 0.1 us)
Async XLA Ops:
  0.6 1.0 %copy-start.1 = (bf16[512,256]{1,0:T(8,128)(2,1)S(1)}, bf16[512,256]{1,0:T(8,128)(2,1)}, u32[]{:S(2)}) copy-start(bf16[512,256]{1,0:T(8,128)(2,1)} %residual_ref.1) | copy-start | bytes 786436
  1.6 0.9 %copy-start.2 = (bf16[512,128]{1,0:T(8,128)(2,1)S(1)}, bf16[512,128]{1,0:T(8,128)(2,1)}, u32[]{:S(2)}) copy-start(bf16[512,128]{1,0:T(8,128)(2,1)} %inverse_ref.1) | copy-start | bytes 393220
  2.5 5.8 %copy-start.6 = (f32[64]{0:T(128)S(1)}, f32[64]{0:T(128)}, u32[]{:S(2)}) copy-start(f32[64]{0:T(128)} %param.14) | copy-start | bytes 772
  7.8 1.8 %collective-permute-start.3 = (bf16[1280,128]{1,0:T(8,128)(2,1)S(1)}, bf16[1280,128]{1,0:T(8,128)(2,1)S(1)}, u32[]{:S(2)}, u32[]{:S(2)}) collective-permute-start(bf16[1280,128]{1,0:T(8,128)(2,1)S(1)} %get-tuple-element.28.small_ref), channel_id=1, source_target_pairs={{0,1},{1,0},{2,3},{3,2},{4,5},{5,4},{6,7},{7,6},{8,9},{9,8},{10,11... | collective-permute-start | bytes 983048 | tf_op jit(solution)/shard_map/ppermute | solution.py:23
  8.3 4.2 %collective-permute-start.4 = (f32[64]{0:T(128)S(1)}, f32[64]{0:T(128)S(1)}, u32[]{:S(2)}, u32[]{:S(2)}) collective-permute-start(f32[64]{0:T(128)S(1)} %copy-done.6), channel_id=1, source_target_pairs={{0,1},{1,0},{2,3},{3,2},{4,5},{5,4},{6,7},{7,6},{8,9},{9,8},{10,11... | collective-permute-start | bytes 776 | tf_op jit(solution)/shard_map/ppermute | solution.py:23
  8.4 4.2 %collective-permute-start.2 = (bf16[640,128]{1,0:T(8,128)(2,1)S(1)}, bf16[640,128]{1,0:T(8,128)(2,1)S(1)}, u32[]{:S(2)}, u32[]{:S(2)}) collective-permute-start(bf16[640,128]{1,0:T(8,128)(2,1)S(1)} %get-tuple-element.27), channel_id=1, source_target_pairs={{0,1},{1,0},{2,3},{3,2},{4,5},{5,4},{6,7},{7,6},{8,9},{9,8},{10,11... | collective-permute-start | bytes 491528 | tf_op jit(solution)/shard_map/ppermute | solution.py:23
  9.6 11.2 %collective-permute-start.6 = (bf16[768,128]{1,0:T(8,128)(2,1)S(1)}, bf16[768,128]{1,0:T(8,128)(2,1)S(1)}, u32[]{:S(2)}, u32[]{:S(2)}) collective-permute-start(bf16[768,128]{1,0:T(8,128)(2,1)S(1)} %add_convert_fusion.rest_0_), channel_id=1, source_target_pairs={{0,2},{1,3},{2,0},{3,1},{4,6},{5,7},{6,4},{7,5},{8,10},{9,11},{10,... | collective-permute-start | bytes 589832 | tf_op jit(solution)/shard_map/ppermute | solution.py:23
  12.6 24.2 %copy-start = (bf16[512,640]{1,0:T(8,128)(2,1)S(1)}, bf16[512,640]{1,0:T(8,128)(2,1)}, u32[]{:S(2)}) copy-start(bf16[512,640]{1,0:T(8,128)(2,1)} %get-tuple-element.25.left_ref) | copy-start | bytes 1966084
  12.9 8.0 %collective-permute-start.5 = (bf16[560,128]{1,0:T(8,128)(2,1)S(1)}, bf16[560,128]{1,0:T(8,128)(2,1)S(1)}, u32[]{:S(2)}, u32[]{:S(2)}) collective-permute-start(bf16[560,128]{1,0:T(8,128)(2,1)S(1)} %get-tuple-element.31.own_ref), channel_id=1, source_target_pairs={{0,2},{1,3},{2,0},{3,1},{4,6},{5,7},{6,4},{7,5},{8,10},{9,11},{10,... | collective-permute-start | bytes 430088 | tf_op jit(solution)/shard_map/ppermute | solution.py:23
  13.0 23.8 %collective-permute-start.1 = (bf16[512,640]{1,0:T(8,128)(2,1)}, bf16[512,640]{1,0:T(8,128)(2,1)S(1)}, u32[]{:S(2)}, u32[]{:S(2)}) collective-permute-start(bf16[512,640]{1,0:T(8,128)(2,1)} %get-tuple-element.25.left_ref), channel_id=1, source_target_pairs={{0,1},{1,0},{2,3},{3,2},{4,5},{5,4},{6,7},{7,6},{8,9},{9,8},{10,11... | collective-permute-start | bytes 1966088 | tf_op jit(solution)/shard_map/ppermute | solution.py:23
  13.0 20.7 %collective-permute-start = (f32[512,128]{1,0:T(8,128)S(1)}, f32[512,128]{1,0:T(8,128)S(1)}, u32[]{:S(2)}, u32[]{:S(2)}) collective-permute-start(f32[512,128]{1,0:T(8,128)S(1)} %get-tuple-element.24.rest_ref), channel_id=1, source_target_pairs={{0,1},{1,0},{2,3},{3,2},{4,5},{5,4},{6,7},{7,6},{8,9},{9,8},{10,11... | collective-permute-start | bytes 786440 | tf_op jit(solution)/shard_map/ppermute | solution.py:23
  21.0 6.9 %collective-permute-start.7 = (bf16[432,128]{1,0:T(8,128)(2,1)S(1)}, bf16[432,128]{1,0:T(8,128)(2,1)S(1)}, u32[]{:S(2)}, u32[]{:S(2)}) collective-permute-start(bf16[432,128]{1,0:T(8,128)(2,1)S(1)} %get-tuple-element.33.own_ref), channel_id=1, source_target_pairs={{0,4},{1,5},{2,6},{3,7},{4,0},{5,1},{6,2},{7,3},{8,12},{9,13},{10,... | collective-permute-start | bytes 331784 | tf_op jit(solution)/shard_map/ppermute | solution.py:23
  22.9 5.0 %collective-permute-start.8 = (bf16[384,128]{1,0:T(8,128)(2,1)S(1)}, bf16[384,128]{1,0:T(8,128)(2,1)S(1)}, u32[]{:S(2)}, u32[]{:S(2)}) collective-permute-start(bf16[384,128]{1,0:T(8,128)(2,1)S(1)} %add_convert_fusion.1.rest_0_), channel_id=1, source_target_pairs={{0,4},{1,5},{2,6},{3,7},{4,0},{5,1},{6,2},{7,3},{8,12},{9,13},{10,... | collective-permute-start | bytes 294920 | tf_op jit(solution)/shard_map/ppermute | solution.py:23
  23.2 11.0 %collective-permute-start.13 = (bf16[128,128]{1,0:T(8,128)(2,1)S(1)}, bf16[128,128]{1,0:T(8,128)(2,1)S(1)}, u32[]{:S(2)}, u32[]{:S(2)}) collective-permute-start(bf16[128,128]{1,0:T(8,128)(2,1)S(1)} %get-tuple-element.29.last_ref), channel_id=1, source_target_pairs={{0,1},{1,0},{2,3},{3,2},{4,5},{5,4},{6,7},{7,6},{8,9},{9,8},{10,11... | collective-permute-start | bytes 98312 | tf_op jit(solution)/shard_map/ppermute | solution.py:23
  28.1 4.8 %collective-permute-start.9 = (bf16[432,128]{1,0:T(8,128)(2,1)S(1)}, bf16[432,128]{1,0:T(8,128)(2,1)S(1)}, u32[]{:S(2)}, u32[]{:S(2)}) collective-permute-start(bf16[432,128]{1,0:T(8,128)(2,1)S(1)} %get-tuple-element.34.own_ref), channel_id=1, source_target_pairs={{0,8},{1,9},{2,10},{3,11},{4,12},{5,13},{6,14},{7,15},{8,0},{9,1},... | collective-permute-start | bytes 331784 | tf_op jit(solution)/shard_map/ppermute | solution.py:23
  30.5 6.3 %collective-permute-start.12 = (bf16[128,128]{1,0:T(8,128)(2,1)S(1)}, bf16[128,128]{1,0:T(8,128)(2,1)S(1)}, u32[]{:S(2)}, u32[]{:S(2)}) collective-permute-start(bf16[128,128]{1,0:T(8,128)(2,1)S(1)} %slice.73.refs_2_), channel_id=1, source_target_pairs={{0,1},{1,0},{2,3},{3,2},{4,5},{5,4},{6,7},{7,6},{8,9},{9,8},{10,11... | collective-permute-start | bytes 98312 | tf_op jit(solution)/shard_map/ppermute | solution.py:23
  32.9 3.9 %collective-permute-start.11 = (bf16[128,128]{1,0:T(8,128)(2,1)S(1)}, bf16[128,128]{1,0:T(8,128)(2,1)S(1)}, u32[]{:S(2)}, u32[]{:S(2)}) collective-permute-start(bf16[128,128]{1,0:T(8,128)(2,1)S(1)} %slice.72.refs_1_), channel_id=1, source_target_pairs={{0,1},{1,0},{2,3},{3,2},{4,5},{5,4},{6,7},{7,6},{8,9},{9,8},{10,11... | collective-permute-start | bytes 98312 | tf_op jit(solution)/shard_map/ppermute | solution.py:23
  33.7 3.1 %collective-permute-start.10 = (bf16[128,128]{1,0:T(8,128)(2,1)S(1)}, bf16[128,128]{1,0:T(8,128)(2,1)S(1)}, u32[]{:S(2)}, u32[]{:S(2)}) collective-permute-start(bf16[128,128]{1,0:T(8,128)(2,1)S(1)} %slice.71.refs_0_), channel_id=1, source_target_pairs={{0,1},{1,0},{2,3},{3,2},{4,5},{5,4},{6,7},{7,6},{8,9},{9,8},{10,11... | collective-permute-start | bytes 98312 | tf_op jit(solution)/shard_map/ppermute | solution.py:23
  34.2 5.4 %collective-permute-start.14 = (bf16[176,128]{1,0:T(8,128)(2,1)S(1)}, bf16[176,128]{1,0:T(8,128)(2,1)S(1)}, u32[]{:S(2)}, u32[]{:S(2)}) collective-permute-start(bf16[176,128]{1,0:T(8,128)(2,1)S(1)} %get-tuple-element.38.own_ref), channel_id=1, source_target_pairs={{0,16},{1,17},{2,18},{3,19},{4,20},{5,21},{6,22},{7,23},{8,24},{9,... | collective-permute-start | bytes 135176 | tf_op jit(solution)/shard_map/ppermute | solution.py:23
  36.8 3.0 %copy-start.3 = (s32[32,32]{1,0:T(8,128)S(1)}, s32[32,32]{1,0:T(8,128)}, u32[]{:S(2)}) copy-start(s32[32,32]{1,0:T(8,128)} %first_ref.7) | copy-start | bytes 12292
  36.9 3.0 %copy-start.4 = (s32[32,32]{1,0:T(8,128)S(1)}, s32[32,32]{1,0:T(8,128)}, u32[]{:S(2)}) copy-start(s32[32,32]{1,0:T(8,128)} %count_ref.7) | copy-start | bytes 12292
  42.0 12.1 %collective-permute-start.16 = (bf16[512,128]{1,0:T(8,128)(2,1)S(1)}, bf16[512,128]{1,0:T(8,128)(2,1)S(1)}, u32[]{:S(2)}, u32[]{:S(2)}) collective-permute-start(bf16[512,128]{1,0:T(8,128)(2,1)S(1)} %weigh3.1), channel_id=1, source_target_pairs={{0,6},{1,7},{2,4},{3,5},{4,2},{5,3},{6,0},{7,1},{8,14},{9,15},{10,... | collective-permute-start | bytes 393224 | tf_op jit(solution)/shard_map/ppermute | solution.py:23
  46.4 7.7 %collective-permute-start.17 = (bf16[512,128]{1,0:T(8,128)(2,1)S(1)}, bf16[512,128]{1,0:T(8,128)(2,1)S(1)}, u32[]{:S(2)}, u32[]{:S(2)}) collective-permute-start(bf16[512,128]{1,0:T(8,128)(2,1)S(1)} %weigh1.1), channel_id=1, source_target_pairs={{0,2},{1,3},{2,0},{3,1},{4,6},{5,7},{6,4},{7,5},{8,10},{9,11},{10,... | collective-permute-start | bytes 393224 | tf_op jit(solution)/shard_map/ppermute | solution.py:23
  49.1 5.0 %collective-permute-start.18 = (bf16[512,128]{1,0:T(8,128)(2,1)S(1)}, bf16[512,128]{1,0:T(8,128)(2,1)S(1)}, u32[]{:S(2)}, u32[]{:S(2)}) collective-permute-start(bf16[512,128]{1,0:T(8,128)(2,1)S(1)} %weigh2.1), channel_id=1, source_target_pairs={{0,4},{1,5},{2,6},{3,7},{4,0},{5,1},{6,2},{7,3},{8,12},{9,13},{10,... | collective-permute-start | bytes 393224 | tf_op jit(solution)/shard_map/ppermute | solution.py:23
  49.8 1.2 %collective-permute-start.15 = (bf16[128,128]{1,0:T(8,128)(2,1)S(1)}, bf16[128,128]{1,0:T(8,128)(2,1)S(1)}, u32[]{:S(2)}, u32[]{:S(2)}) collective-permute-start(bf16[128,128]{1,0:T(8,128)(2,1)S(1)} %slice.75), channel_id=1, source_target_pairs={{0,1},{1,0},{2,3},{3,2},{4,5},{5,4},{6,7},{7,6},{8,9},{9,8},{10,11... | collective-permute-start | bytes 98312 | tf_op jit(solution)/shard_map/ppermute | solution.py:23
  51.0 13.3 %copy-start.5 = (bf16[64,256]{1,0:T(8,128)(2,1)S(1)}, bf16[64,256]{1,0:T(8,128)(2,1)}, u32[]{:S(2)}) copy-start(bf16[64,256]{1,0:T(8,128)(2,1)} %param.15) | copy-start | bytes 98308
  54.2 5.8 %collective-permute-start.19 = (bf16[128,128]{1,0:T(8,128)(2,1)S(1)}, bf16[128,128]{1,0:T(8,128)(2,1)S(1)}, u32[]{:S(2)}, u32[]{:S(2)}) collective-permute-start(bf16[128,128]{1,0:T(8,128)(2,1)S(1)} %get-tuple-element.46), channel_id=1, source_target_pairs={{0,24},{1,25},{2,26},{3,27},{4,28},{5,29},{6,30},{7,31},{8,16},{9,... | collective-permute-start | bytes 98312 | tf_op jit(solution)/shard_map/ppermute | solution.py:23
  57.8 4.0 %collective-permute-start.21 = (bf16[128,128]{1,0:T(8,128)(2,1)S(1)}, bf16[128,128]{1,0:T(8,128)(2,1)S(1)}, u32[]{:S(2)}, u32[]{:S(2)}) collective-permute-start(bf16[128,128]{1,0:T(8,128)(2,1)S(1)} %get-tuple-element.47), channel_id=1, source_target_pairs={{0,8},{1,9},{2,10},{3,11},{4,12},{5,13},{6,14},{7,15},{8,0},{9,1},... | collective-permute-start | bytes 98312 | tf_op jit(solution)/shard_map/ppermute | solution.py:23
  57.8 5.2 %collective-permute-start.20 = (bf16[128,128]{1,0:T(8,128)(2,1)S(1)}, bf16[128,128]{1,0:T(8,128)(2,1)S(1)}, u32[]{:S(2)}, u32[]{:S(2)}) collective-permute-start(bf16[128,128]{1,0:T(8,128)(2,1)S(1)} %get-tuple-element.48), channel_id=1, source_target_pairs={{0,16},{1,17},{2,18},{3,19},{4,20},{5,21},{6,22},{7,23},{8,24},{9,... | collective-permute-start | bytes 98312 | tf_op jit(solution)/shard_map/ppermute | solution.py:23
  63.0 1.3 %collective-permute-start.22 = (f32[64,128]{1,0:T(8,128)S(1)}, f32[64,128]{1,0:T(8,128)S(1)}, u32[]{:S(2)}, u32[]{:S(2)}) collective-permute-start(f32[64,128]{1,0:T(8,128)S(1)} %get-tuple-element.50), channel_id=1, source_target_pairs={{0,1},{1,0},{2,3},{3,2},{4,5},{5,4},{6,7},{7,6},{8,9},{9,8},{10,11... | collective-permute-start | bytes 98312 | tf_op jit(solution)/shard_map/ppermute | solution.py:23

commit v4 on v3

--- a/solution.py
+++ b/solution.py
@@ -12,7 +12,7 @@
 bf16 = jnp.bfloat16
 f32 = jnp.float32
 MIB = 2**20
-FRONT = 52
+FRONT = 52.25
 VMEM = pl.BlockSpec(memory_space=pltpu.VMEM)
 SMEM = pl.BlockSpec(memory_space=pltpu.SMEM)
 HBM = pl.BlockSpec(memory_space=pltpu.HBM)
@@ -29,7 +29,7 @@
         kernel,
         out_shape=outs,
         name=name,
-        compiler_params=pltpu.CompilerParams(vmem_limit_bytes=room * MIB),
+        compiler_params=pltpu.CompilerParams(vmem_limit_bytes=int(room * MIB)),
         scratch_shapes=list(scratch),
         cost_estimate=pl.CostEstimate(flops=flops, bytes_accessed=moved, transcendentals=0),
         **more,
@@ -54,21 +54,47 @@
     return jax.ShapeDtypeStruct(shape, kind)
 
 
+def small_kernel(bits, rank, right_ref, left_ref, small_ref, right_got, left_got, high_ref, sems):
+    copies = []
+    for i in range(bits - 1):
+        copies.append(pltpu.make_async_copy(right_ref.at[i], right_got.at[i], sems.at[2 * i]))
+        copies.append(pltpu.make_async_copy(left_ref.at[i + 1], left_got.at[i], sems.at[2 * i + 1]))
+    for copy in copies:
+        copy.start()
+    for i in range(bits - 1):
+        copies[2 * i].wait()
+        high_ref[i * rank : (i + 1) * rank, :] = right_got[i].astype(bf16).T
+        copies[2 * i + 1].wait()
+        small_ref[small_at(i + 1, rank), :] = dot(
+            high_ref[: (i + 1) * rank, :], left_got[i].astype(bf16)
+        ).astype(bf16)
+
+
+def left_kernel(bits, rank, left_ref, left16_ref, left_got, sems):
+    copies = [pltpu.make_async_copy(left_ref.at[i], left_got.at[i], sems.at[i]) for i in range(bits)]
+    for copy in copies:
+        copy.start()
+    for i in range(bits):
+        copies[i].wait()
+        left16_ref[:, i * rank : (i + 1) * rank] = left_got[i].astype(bf16)
+
+
 def front_kernel(
     rows, leaf, bits, rank, levels, sizes, half, core_ref, residual_ref, inverse_ref, right_ref, left_ref,
-    mine_ref, other_ref, keep_ref, send_ref, small_ref, left16_ref,
+    mine_ref, other_ref, keep_ref, message_ref,
     residual_got, inverse_got, right_got, left_got, high_ref, low_ref, sems,
 ):
     places = [(residual_ref, residual_got), (inverse_ref, inverse_got)]
     order = levels + list(range(bits))
     for level in order:
         places.append((right_ref.at[level], right_got.at[level]))
-        places.append((left_ref.at[level], left_got.at[level]))
+    for k, level in enumerate(levels):
+        places.append((left_ref.at[level], left_got.at[k]))
     copies = [pltpu.make_async_copy(a, b, sems.at[k]) for k, (a, b) in enumerate(places)]
-    for copy in copies:
-        copy.start()
-    right_copy = {level: copies[2 + 2 * k] for k, level in enumerate(order)}
-    left_copy = {level: copies[3 + 2 * k] for k, level in enumerate(order)}
+    for k in (0, 1, *range(2, 2 + len(levels)), *range(2 + len(order), len(places)), *range(2 + len(levels), 2 + len(order))):
+        copies[k].start()
+    right_copy = {level: copies[2 + k] for k, level in enumerate(order)}
+    left_copy = copies[2 + len(order) :]
     copies[0].wait()
     copies[1].wait()
     x = [
@@ -76,17 +102,17 @@
         for b in range(rows // leaf)
     ]
     x = jnp.concatenate(x, 0)
-    for level, size in zip(levels, sizes):
+    for k, (level, size) in enumerate(zip(levels, sizes)):
         right_copy[level].wait()
         projected = [
             dot3(two(right_got[level, a : a + size, :].T), two(x[a : a + size, :]))
             for a in range(0, rows, size)
         ]
-        left_copy[level].wait()
+        left_copy[k].wait()
         x = jnp.concatenate(
             [
                 x[a * size : (a + 1) * size, :]
-                + dot3(two(left_got[level, a * size : (a + 1) * size, :]), two(projected[a ^ 1]))
+                + dot3(two(left_got[k, a * size : (a + 1) * size, :]), two(projected[a ^ 1]))
                 for a in range(rows // size)
             ],
             0,
@@ -101,13 +127,9 @@
         high, low = two(right_got[i].T)
         high_ref[at, :] = high
         low_ref[at, :] = low
-        left_copy[i].wait()
-        left16_ref[:, at] = left_got[i].astype(bf16)
-        if i:
-            small_ref[small_at(i, rank), :] = dot(high_ref[: i * rank, :], left16_ref[:, at]).astype(bf16)
     a = dot(high_ref[...], xh) + (dot(high_ref[...], xl) + dot(low_ref[...], xh))
     keep_ref[...] = jnp.where(first, a[:, :half], a[:, half:])
-    send_ref[...] = jnp.where(first, a[:, half:], a[:, :half]).astype(bf16)
+    message_ref[...] = jnp.where(first, a[:, half:], a[:, :half]).astype(bf16)
 
 
 def spread(value, depth):
@@ -152,13 +174,14 @@
 
 def merge(level, rank, apart, along, n, depths, y_in, own_ref, got_ref, *rest):
     own_small_ref, their_small_ref = rest[:2] if apart else (own_ref, got_ref)
-    y_ref, message_ref = rest[2:] if apart else rest
+    *y_ref, message_ref = rest[2:] if apart else rest
     base = 0 if apart else (level + 1) * rank
     spots_at = (level + 1) * rank + (0 if apart else level * (level + 1) // 2 * rank)
     at = small_at(level, rank)
     at = slice(base + at.start, base + at.stop)
     y = linked(level, rank, y_in[...], got_ref[...], own_small_ref[at, :], their_small_ref[at, :])
-    y_ref[...] = y
+    if y_ref:
+        y_ref[0][...] = y
     cut = level * rank
     message_ref[:cut, :] = y.astype(bf16)
     inner = level * (level - 1) // 2 * rank if along else 0
@@ -180,40 +203,56 @@
     outs[2][...] = other_ref[...] + dot(left_other_ref[:, rank:], jnp.concatenate(top + [last_ref[...]], 0))
 
 
-def coeff_kernel(rank, mine_ref, other_ref, left_ref, left_other_ref, got_ref, final_ref, coeff_ref):
+def coeff_kernel(rank, n, depth, scale, mine_ref, other_ref, left_ref, left_other_ref, got_ref, final_ref, coeff_ref, spot_ref):
     rows = mine_ref.shape[0]
     share = got_ref[:rank, :]
     x = mine_ref[...] + dot(left_ref[:, :rank], share)
     final_ref[...] = x
     coeff_ref[:rows, :] = x.astype(bf16)
     coeff_ref[rows:, :] = (other_ref[...] + dot(left_other_ref[:, :rank], share)).astype(bf16)
-
-
-def weigh_kernel(mask, plane, far, tile, leaf, blocks, n, depth, rank, me_ref, first_ref, count_ref, own_ref, got_ref, point_ref, coeff_ref, out_ref, weight_ref):
-    me = me_ref[0]
+    spot_ref[...] = (gathered(got_ref, rank, depth)[:n, :] * scale).T
+
+
+def weigh(tile, leaf, blocks, devices, info_ref, spots, point_ref, weight_ref, q, column_at, at):
     scale = 2.0 * leaf
-    spots = jnp.concatenate([gathered(own_ref, rank, depth)[:n, :], gathered(got_ref, rank, depth)[:n, :]], 0) * scale
-    spots = spots.T
+    for r in range(2):
+        column = jnp.broadcast_to(spots[r * tile : (r + 1) * tile, column_at : column_at + 1], (tile, leaf))
+        target = info_ref[0] ^ (2 * q + r)
+        for s in range(2):
+            first = info_ref[1 + s * devices + target]
+            count = info_ref[1 + (2 + s) * devices + target]
+            for k in range(CAP):
+                block = s * blocks + first + k
+                level = jnp.where(k < count, amplitude, 0.0)
+                distance = jnp.minimum(jnp.abs(column - point_ref[pl.ds(block, 1), :] * scale), 1.0)
+                left = 1.0 - distance
+                left = left * left
+                value = (left * left) * (1.0 + 4.0 * distance) * level
+                lanes = pl.ds(pl.multiple_of(block * leaf, leaf), leaf)
+                weight_ref[at + r * tile : at + (r + 1) * tile, lanes] = value.astype(bf16)
+
+
+def near_kernel(plane, near, tile, leaf, blocks, devices, n, depth, rank, info_ref, own_ref, point_ref, *weight_refs):
+    spots = (gathered(own_ref, rank, depth)[:n, :] * (2.0 * leaf)).T
+    for mask in range(plane):
+        weight_refs[mask][...] = jnp.zeros_like(weight_refs[mask])
+        for z in range(near):
+            q = mask + plane * z
+            weigh(tile, leaf, blocks, devices, info_ref, spots, point_ref, weight_refs[mask], q, q, 2 * z * tile)
+
+
+def far_kernel(mask, plane, near, tile, leaf, blocks, devices, info_ref, spot_ref, near_ref, point_ref, coeff_ref, out_ref, weight_ref):
+    spots = spot_ref[...]
     weight_ref[...] = jnp.zeros_like(weight_ref)
-    for z in range(far):
-        q = mask + plane * z
-        for r in range(2):
-            column = jnp.broadcast_to(spots[r * tile : (r + 1) * tile, q : q + 1], (tile, leaf))
-            target = me ^ (2 * q + r)
-            at = (2 * z + r) * tile
-            for s in range(2):
-                first = first_ref[target, me ^ s]
-                count = count_ref[target, me ^ s]
-                for k in range(CAP):
-                    block = s * blocks + first + k
-                    level = jnp.where(k < count, amplitude, 0.0)
-                    distance = jnp.minimum(jnp.abs(column - point_ref[pl.ds(block, 1), :] * scale), 1.0)
-                    left = 1.0 - distance
-                    left = left * left
-                    value = (left * left) * (1.0 + 4.0 * distance) * level
-                    lanes = pl.ds(pl.multiple_of(block * leaf, leaf), leaf)
-                    weight_ref[at : at + tile, lanes] = value.astype(bf16)
-    out_ref[...] = dot(weight_ref[...], coeff_ref[...]).astype(out_ref.dtype)
+    for z in range(near):
+        column = mask + plane * z
+        weigh(
+            tile, leaf, blocks, devices, info_ref, spots, point_ref, weight_ref,
+            column + plane * near, column, 2 * z * tile,
+        )
+    half = 2 * near * tile
+    out_ref[:half, :] = dot(near_ref[...], coeff_ref[...]).astype(out_ref.dtype)
+    out_ref[half:, :] = dot(weight_ref[...], coeff_ref[...]).astype(out_ref.dtype)
 
 
 def solved_kernel(rank, core_ref, mine_ref, rest_ref, left_ref, share_ref, out_ref):
@@ -243,7 +282,7 @@
     bits = devices.bit_length() - 1
     me = lax.axis_index("pts").astype(jnp.int32)
     core = me % 2
-    me_s, core_s = me.reshape(1), core.reshape(1)
+    core_s = core.reshape(1)
     levels = basis_left.shape[0]
     tile = map_pos.shape[0]
     half = samples // 2
@@ -252,15 +291,29 @@
     spot_other = swapped(map_pos, 1)
     inner = list(reversed(range(bits, levels)))
     sizes = [rows * devices // 2 ** (level + 1) for level in inner]
-    solved_mine, solved_send, keep, send, small, left16 = call(
+    small = call(
+        functools.partial(small_kernel, bits, rank),
+        out((pair_count * rank, rank), bf16),
+        "small",
+        2 * pair_count * rank * rank * rows,
+        8 * bits * rows * rank,
+        room=FRONT,
+        ins=[HBM, HBM],
+        scratch=[
+            pltpu.VMEM((bits - 1, rows, rank), f32),
+            pltpu.VMEM((bits - 1, rows, rank), f32),
+            pltpu.VMEM(((bits - 1) * rank, rows), bf16),
+            pltpu.SemaphoreType.DMA((2 * bits - 2,)),
+        ],
+    )(basis_right, basis_left)
+    small_other = swapped(small, 1)
+    solved_mine, solved_send, keep, send = call(
         functools.partial(front_kernel, rows, leaf, bits, rank, inner, sizes, half),
         [
             out((rows, half), f32),
             out((rows, half), f32),
             out((bits * rank, half), f32),
             out((bits * rank, half), bf16),
-            out((pair_count * rank, rank), bf16),
-            out((rows, bits * rank), bf16),
         ],
         "front",
         6 * bits * rank * rows * samples,
@@ -271,29 +324,30 @@
             pltpu.VMEM((rows, samples), bf16),
             pltpu.VMEM((rows, leaf), bf16),
             pltpu.VMEM((levels, rows, rank), f32),
-            pltpu.VMEM((levels, rows, rank), f32),
+            pltpu.VMEM((max(1, len(inner)), rows, rank), f32),
             pltpu.VMEM((bits * rank, rows), bf16),
             pltpu.VMEM((bits * rank, rows), bf16),
-            pltpu.SemaphoreType.DMA((2 + 2 * levels,)),
+            pltpu.SemaphoreType.DMA((2 + levels + max(1, len(inner)),)),
         ],
     )(core_s, residual_cols, leaf_inverse, basis_right, basis_left)
-    small_other = swapped(small, 1)
-    left_other = swapped(left16, 1)
     got = swapped(send, 1)
     solved_other = swapped(solved_send, 1)
+    left16 = call(
+        functools.partial(left_kernel, bits, rank),
+        out((rows, bits * rank), bf16),
+        "left16",
+        bits * rows * rank,
+        6 * bits * rows * rank,
+        room=24,
+        ins=[HBM],
+        scratch=[pltpu.VMEM((bits, rows, rank), f32), pltpu.SemaphoreType.DMA((bits,))],
+    )(basis_left)
+    left_other = swapped(left16, 1)
 
     shares, others = [None] * bits, [None] * bits
     top = bits - 1
     depth_of = lambda bit: max(16, 1 << (bit - 1))
     pairs_below = lambda level: level * (level - 1) // 2 * rank
-    ahead = (1, 2)
-    small_own, small_theirs = {}, {}
-    previous = small, small_other
-    for bit in ahead:
-        kept = pairs_below(top - bit + 1)
-        small_own[bit] = (previous[0][:kept].astype(f32) + previous[1][:kept].astype(f32)).astype(bf16)
-        small_theirs[bit] = swapped(small_own[bit], 1 << bit)
-        previous = small_own[bit], small_theirs[bit]
     spot_rows = jnp.concatenate([map_pos, spot_other]).reshape(1, 2 * tile)
     y, message, last = call(
         functools.partial(first_merge, top, rank, depth_of(1)),
@@ -306,6 +360,15 @@
         4 * top * rank * rank * half,
         8 * top * rank * half,
     )(keep, got, small, small_other, spot_rows)
+    ahead = (1, 2)
+    small_own, small_theirs = {}, {}
+    previous = small, small_other
+    for bit in ahead:
+        kept = pairs_below(top - bit + 1)
+        both = (previous[0][:kept].astype(f32) + previous[1][:kept].astype(f32)).astype(bf16)
+        small_own[bit] = both
+        small_theirs[bit] = swapped(both, 1 << bit)
+        previous = small_own[bit], small_theirs[bit]
     shares[top] = got[top * rank :]
     others[top] = swapped(last, 1)
     for bit in range(1, bits):
@@ -317,18 +380,17 @@
         if level:
             apart, along = bit in ahead, bit + 1 not in ahead
             inner_rows = pairs_below(level) if along else 0
-            y, message = call(
+            *kept_y, message = call(
                 functools.partial(
                     merge, level, rank, apart, along, 1 << (bit - 1), (depth_of(bit), depth_of(bit + 1))
                 ),
-                [
-                    out((level * rank, half), f32),
-                    out((level * rank + inner_rows + 3 * depth_of(bit + 1), half), bf16),
-                ],
+                [out((level * rank, half), f32)] * (level > 1)
+                + [out((level * rank + inner_rows + 3 * depth_of(bit + 1), half), bf16)],
                 f"merge{bit}",
                 4 * level * rank * rank * half,
                 8 * level * rank * half,
             )(y, message, arrived, *((small_own[bit], small_theirs[bit]) if apart else ()))
+            y = kept_y[0] if kept_y else None
 
     part_mine, part_rest, part_other = call(
         functools.partial(partial_kernel, bits, rank),
@@ -337,35 +399,52 @@
         6 * bits * rows * rank * half,
         24 * rows * half,
     )(solved_mine, solved_send, solved_other, left16, left_other, last, *shares[1:], *others[1:])
-    final_mine, coeffs = call(
-        functools.partial(coeff_kernel, rank),
-        [out((rows, half), f32), out((2 * rows, half), bf16)],
+    plane = 4
+    near = devices // (4 * plane)
+    depth = depth_of(bits - 1)
+    chips = 1 << (bits - 2)
+    points = [lax.dynamic_slice_in_dim(point_pos, s * rows, rows).reshape(blocks, leaf) for s in (me, me ^ 1)]
+    points = jnp.concatenate(points, 0)
+    info = jnp.concatenate(
+        [me.reshape(1)]
+        + [lax.dynamic_index_in_dim(t, s, 1, keepdims=False) for t in (block_first, block_count) for s in (me, me ^ 1)]
+    )
+    near_weights = call(
+        functools.partial(near_kernel, plane, near, tile, leaf, blocks, devices, chips, depth, rank),
+        [out((2 * near * tile, 2 * rows), bf16)] * plane,
+        "near",
+        40 * plane * near * tile * rows,
+        8 * plane * near * tile * rows,
+        room=8 if near <= 4 else 24,
+        ins=[SMEM, VMEM, VMEM],
+    )(info, message, points)
+    final_mine, coeffs, spots = call(
+        functools.partial(coeff_kernel, rank, chips, depth, 2.0 * leaf),
+        [out((rows, half), f32), out((2 * rows, half), bf16), out((2 * tile, chips), f32)],
         "coeffs",
         4 * rows * rank * half,
         16 * rows * half,
     )(part_mine, part_other, left16, left_other, arrived)
 
-    points = [lax.dynamic_slice_in_dim(point_pos, s * rows, rows).reshape(blocks, leaf) for s in (me, me ^ 1)]
-    points = jnp.concatenate(points, 0)
-    plane = 4
-    far = devices // (2 * plane)
-    depth = depth_of(bits - 1)
-
     def weighed(mask, coeffs):
         return call(
-            functools.partial(
-                weigh_kernel, mask, plane, far, tile, leaf, blocks, 1 << (bits - 2), depth, rank
-            ),
-            out((far * 2 * tile, half), bf16 if mask else f32),
+            functools.partial(far_kernel, mask, plane, near, tile, leaf, blocks, devices),
+            out((4 * near * tile, half), bf16 if mask else f32),
             f"weigh{mask}",
-            16 * far * tile * rows * half,
-            16 * far * tile * half,
-            room=8 if far <= 4 else 16,
-            ins=[SMEM, SMEM, SMEM, VMEM, VMEM, VMEM, VMEM],
-            scratch=[pltpu.VMEM((far * 2 * tile, 2 * rows), bf16)],
-        )(me_s, block_first, block_count, message, arrived, points, coeffs)
-
-    sent = [swapped(weighed(mask, coeffs), mask << 1) for mask in (3, 1, 2)]
+            32 * near * tile * rows * half,
+            32 * near * tile * half,
+            room=8 if near <= 4 else 16,
+            ins=[SMEM, VMEM, VMEM, VMEM, VMEM],
+            scratch=[pltpu.VMEM((2 * near * tile, 2 * rows), bf16)],
+        )(info, spots, near_weights[mask], points, coeffs)
+
+    sent = []
+    for mask in (3, 2, 1):
+        if mask == 1:
+            coeffs, others[0] = lax.optimization_barrier((coeffs, others[0]))
+        partial = weighed(mask, coeffs)
+        coeffs, partial = lax.optimization_barrier((coeffs, partial))
+        sent.append(swapped(partial, mask << 1))
     solved_out = call(
         functools.partial(solved_kernel, rank),
         out((rows, samples), f32),
@@ -378,9 +457,10 @@
     total = weighed(0, coeffs)
     for partial in sent:
         total = total + partial.astype(f32)
+    far = 2 * near
     total = total.reshape(far, 2 * tile, half)
     result = total[0]
-    for mask in reversed(range(1, far)):
+    for mask in range(1, far):
         result = result + swapped(total[mask].astype(bf16), mask << 3).astype(f32)
     rest = swapped(result[tile:], 1)
 

time: 65.2 us -> 61.7 us (0.946)
  waiting for transfers between devices: 24 us -> 21.9 us
  local copies, waits for them, and re-layouts: 2.74 us -> 1.21 us
  starting transfers between devices: 19.7 us -> 20.9 us
  Pallas kernels: 16.7 us -> 15.8 us
    ppermute x23, waiting for transfers between devices: 24 us -> 21.9 us  [swapped(): return lax.ppermute(value, 'pts', pairs)]
    unnamed x14, local copies, waits for them, and re-layouts: 1.87 us -> 0.03 us
    pallas_call x1, Pallas kernels: 5.28 us -> 4.11 us  [body(): call(functools.partial(front_kernel, rows, leaf, bits, rank, inner, sizes...]
    ppermute x23, starting transfers between devices: 19.7 us -> 20.9 us  [swapped(): return lax.ppermute(value, 'pts', pairs)]
    pallas_call x5 -> x8, Pallas kernels: 8.5 us -> 9.35 us  [the longest x4 4.77 us: weighed(): call(functools.partial(far_kernel, mask, plane, near, tile, leaf, blocks,...]
  transfers between devices with their start and end apart: 23 -> 23, of which waited for: 11 -> 9; matrix products, arithmetic and copies ran while one was open for 2% -> 2% of each run, Pallas kernels for 14% -> 21%
where the time goes in v4:
time: 61.7 us; the launch traced here: 61.5 us
  waiting for transfers between devices  21.9 us (35%)
  starting transfers between devices  20.9 us (34%)
  Pallas kernels  15.8 us (26%)
  local copies, waits for them, and re-layouts  1.21 us (2%)
  between operations  0.9 us (1%)
  other arithmetic  0.89 us (1%)
    ppermute x23, waiting for transfers between devices, swapped(): return lax.ppermute(value, 'pts', pairs)  21.9 us
    ppermute x23, starting transfers between devices, swapped(): return lax.ppermute(value, 'pts', pairs)  20.9 us
    pallas_call x4, Pallas kernels, weighed(): call(functools.partial(far_kernel, mask, plane, near, tile, leaf, blocks,...  4.77 us
    pallas_call x1, Pallas kernels, body(): call(functools.partial(front_kernel, rows, leaf, bits, rank, inner, sizes...  4.11 us
    pallas_call x1, Pallas kernels, body(): call(functools.partial(small_kernel, bits, rank), out((pair_count * rank,...  2.62 us
    pallas_call x1, Pallas kernels, body(): call(functools.partial(near_kernel, plane, near, tile, leaf, blocks, devi...  1.51 us
  transfers between devices with their start and end apart: 23, of which 9 were waited for; matrix products, arithmetic and copies ran while one was open for 2% of the time, Pallas kernels for 21%

profile of v4, /device:TPU:0, one launch (start us, length us, event | category | flops | bytes accessed | tf_op | source)
XLA Modules:
  0.0 61.5 jit_solution(1433641944543200743)
XLA Ops:
  0.6 2.6 %small.1.small_ref = bf16[1280,128]{1,0:T(8,128)(2,1)S(1)} custom-call(f32[7,512,128]{2,1,0:T(8,128)} %right_ref.3, f32[7,512,128]{2,1,0:T(8,128)} %left_ref.5), custom_call_target="tpu_custom_call" | custom-call | flops 167772160 | bytes 2621440 | tf_op jit(solution)/shard_map/small/pallas_call | solution.py:294
  3.3 0.5 collective-permute-start.3
  3.8 4.1 %front.1 = (f32[512,128]{1,0:T(8,128)S(1)}, f32[512,128]{1,0:T(8,128)S(1)}, f32[640,128]{1,0:T(8,128)S(1)}, bf16[640,128]{1,0:T(8,128)(2,1)S(1)}) custom-call(s32[1]{0:T(128)} %bitcast.core_ref, bf16[512,256]{1,0:T(8,128)(2,1)S(1)} %copy-done.1, bf16[512,128]{1,0:T(8,128)(2,1)S(1)} %copy-done.2, f32[7,512,128]{2,1,0:T(8,128)} %right_ref.3, ...), custom_call_target="tpu_custom_call" | custom-call | flops 503316480 | bytes 3670016 | tf_op jit(solution)/shard_map/front/pallas_call | solution.py:310
  7.9 0.1 collective-permute-start.2
  8.0 0.5 collective-permute-start.4
  8.5 0.1 add_convert_fusion.rest_0_
  8.6 2.6 %collective-permute-start.6 = (bf16[768,128]{1,0:T(8,128)(2,1)S(1)}, bf16[768,128]{1,0:T(8,128)(2,1)S(1)}, u32[]{:S(2)}, u32[]{:S(2)}) collective-permute-start(bf16[768,128]{1,0:T(8,128)(2,1)S(1)} %add_convert_fusion.rest_0_), channel_id=1, source_target_pairs={{0,2},{1,3},{2,0},{3,1},{4,6},{5,7},{6,4},{7,5},{8,10},{9,11},{10,... | collective-permute-start | bytes 589832 | tf_op jit(solution)/shard_map/ppermute | solution.py:23
  11.2 0.0 collective-permute-done.4
  11.2 0.1 maximum_bitcast_fusion.spot_ref
  11.3 0.0 collective-permute-done.2.got_ref
  11.3 0.2 merge0.1
  11.5 1.0 %collective-permute-start.5 = (bf16[560,128]{1,0:T(8,128)(2,1)S(1)}, bf16[560,128]{1,0:T(8,128)(2,1)S(1)}, u32[]{:S(2)}, u32[]{:S(2)}) collective-permute-start(bf16[560,128]{1,0:T(8,128)(2,1)S(1)} %get-tuple-element.39.own_ref), channel_id=1, source_target_pairs={{0,2},{1,3},{2,0},{3,1},{4,6},{5,7},{6,4},{7,5},{8,10},{9,11},{10,... | collective-permute-start | bytes 430088 | tf_op jit(solution)/shard_map/ppermute | solution.py:23
  12.5 0.2 left16.1.left_ref
  12.7 0.0 copy-start.3
  12.7 0.0 copy-start.4
  12.7 0.1 collective-permute-start.1
  12.8 0.5 collective-permute-start
  13.3 6.4 %collective-permute-done.5.got_ref = bf16[560,128]{1,0:T(8,128)(2,1)S(1)} collective-permute-done((bf16[560,128]{1,0:T(8,128)(2,1)S(1)}, bf16[560,128]{1,0:T(8,128)(2,1)S(1)}, u32[]{:S(2)}, u32[]{:S(2)}) %collective-permute-start.5) | collective-permute-done | bytes 143392 | tf_op jit(solution)/shard_map/ppermute | solution.py:23
  19.8 0.0 collective-permute-done.6.rest_1_
  19.8 0.2 merge1.1
  20.0 1.9 %collective-permute-start.7 = (bf16[432,128]{1,0:T(8,128)(2,1)S(1)}, bf16[432,128]{1,0:T(8,128)(2,1)S(1)}, u32[]{:S(2)}, u32[]{:S(2)}) collective-permute-start(bf16[432,128]{1,0:T(8,128)(2,1)S(1)} %get-tuple-element.41.own_ref), channel_id=1, source_target_pairs={{0,4},{1,5},{2,6},{3,7},{4,0},{5,1},{6,2},{7,3},{8,12},{9,13},{10,... | collective-permute-start | bytes 331784 | tf_op jit(solution)/shard_map/ppermute | solution.py:23
  21.8 0.3 collective-permute-start.8
  22.2 4.8 %collective-permute-done.8.rest_1_ = bf16[384,128]{1,0:T(8,128)(2,1)S(1)} collective-permute-done((bf16[384,128]{1,0:T(8,128)(2,1)S(1)}, bf16[384,128]{1,0:T(8,128)(2,1)S(1)}, u32[]{:S(2)}, u32[]{:S(2)}) %collective-permute-start.8) | collective-permute-done | bytes 98336 | tf_op jit(solution)/shard_map/ppermute | solution.py:23
  26.9 0.2 merge2.1
  27.1 1.9 %collective-permute-start.9 = (bf16[432,128]{1,0:T(8,128)(2,1)S(1)}, bf16[432,128]{1,0:T(8,128)(2,1)S(1)}, u32[]{:S(2)}, u32[]{:S(2)}) collective-permute-start(bf16[432,128]{1,0:T(8,128)(2,1)S(1)} %get-tuple-element.42.own_ref), channel_id=1, source_target_pairs={{0,8},{1,9},{2,10},{3,11},{4,12},{5,13},{6,14},{7,15},{8,0},{9,1},... | collective-permute-start | bytes 331784 | tf_op jit(solution)/shard_map/ppermute | solution.py:23
  29.0 0.8 %dynamic-slice_bitcast_fusion.1 = (f32[4,128]{1,0:T(4,128)S(1)}, f32[4,128]{1,0:T(4,128)S(1)}) fusion(f32[16384]{0:T(1024)} %param.13, s32[]{:T(128)S(6)} %select_n.33, s32[]{:T(128)S(6)} %select_n.34), kind=kLoop, calls=%fused_computation.14 | loop fusion | bytes 8200 | tf_op jit(solution)/shard_map/reshape | solution.py:406
  29.8 0.0 collective-permute-start.12
  29.9 2.1 %collective-permute-done.9.got_ref = bf16[432,128]{1,0:T(8,128)(2,1)S(1)} collective-permute-done((bf16[432,128]{1,0:T(8,128)(2,1)S(1)}, bf16[432,128]{1,0:T(8,128)(2,1)S(1)}, u32[]{:S(2)}, u32[]{:S(2)}) %collective-permute-start.9) | collective-permute-done | bytes 110624 | tf_op jit(solution)/shard_map/ppermute | solution.py:23
  31.9 0.0 collective-permute-start.11
  31.9 0.2 merge3.1.own_ref
  32.1 0.0 collective-permute-done.other_ref
  32.1 0.6 collective-permute-start.10
  32.7 0.0 collective-permute-done.13.refs_7_
  32.7 2.8 %collective-permute-start.14 = (bf16[176,128]{1,0:T(8,128)(2,1)S(1)}, bf16[176,128]{1,0:T(8,128)(2,1)S(1)}, u32[]{:S(2)}, u32[]{:S(2)}) collective-permute-start(bf16[176,128]{1,0:T(8,128)(2,1)S(1)} %merge3.1.own_ref), channel_id=1, source_target_pairs={{0,16},{1,17},{2,18},{3,19},{4,20},{5,21},{6,22},{7,23},{8,24},{9,... | collective-permute-start | bytes 135176 | tf_op jit(solution)/shard_map/ppermute | solution.py:23
  35.5 0.2 dynamic-slice_reduce_fusion
  35.8 0.1 concatenate.16.info_ref
  35.8 1.5 %near.1 = (bf16[256,1024]{1,0:T(8,128)(2,1)S(1)}, bf16[256,1024]{1,0:T(8,128)(2,1)S(1)}, bf16[256,1024]{1,0:T(8,128)(2,1)S(1)}, bf16[256,1024]{1,0:T(8,128)(2,1)S(1)}) custom-call(s32[129]{0:T(256)S(1)} %concatenate.16.info_ref, bf16[176,128]{1,0:T(8,128)(2,1)S(1)} %merge3.1.own_ref, f32[8,128]{1,0:T(8,128)S(1)} %pad_maximum_fusion.point_ref), custom_call_target="tpu_custom_call" | custom-call | flops 10485760 | bytes 2097152 | tf_op jit(solution)/shard_map/near/pallas_call | solution.py:412
  37.4 0.0 collective-permute-done.12.refs_6_
  37.4 0.0 collective-permute-done.1.left_other_ref
  37.4 0.0 collective-permute-done.10.refs_4_
  37.4 0.6 partial.1
  38.0 0.1 collective-permute-done.14.got_ref
  38.1 0.2 coeffs.1
  38.3 1.2 %weigh3.1 = bf16[512,128]{1,0:T(8,128)(2,1)S(1)} custom-call(s32[129]{0:T(256)S(1)} %concatenate.16.info_ref, f32[128,8]{1,0:T(8,128)S(1)} %get-tuple-element.47.spot_ref, bf16[256,1024]{1,0:T(8,128)(2,1)S(1)} %get-tuple-element.48.near_ref, f32[8,128]{1,0:T(8,128)S(1)} %pad_maximum_fusion.point_ref, bf16[1024,128]{1,0:T(8,128)(2,1)S(1)} %get-tuple-element.60.coeff_ref), custom_call_target="tpu_custom_call" | custom-call | flops 268435456 | bytes 524288 | tf_op jit(solution)/shard_map/weigh3/pallas_call | solution.py:430
  39.6 1.2 %weigh2.1 = bf16[512,128]{1,0:T(8,128)(2,1)S(1)} custom-call(s32[129]{0:T(256)S(1)} %concatenate.16.info_ref, f32[128,8]{1,0:T(8,128)S(1)} %get-tuple-element.47.spot_ref, bf16[256,1024]{1,0:T(8,128)(2,1)S(1)} %get-tuple-element.50.near_ref, f32[8,128]{1,0:T(8,128)S(1)} %pad_maximum_fusion.point_ref, bf16[1024,128]{1,0:T(8,128)(2,1)S(1)} %get-tuple-element.60.coeff_ref), custom_call_target="tpu_custom_call" | custom-call | flops 268435456 | bytes 524288 | tf_op jit(solution)/shard_map/weigh2/pallas_call | solution.py:430
  40.8 1.7 %collective-permute-start.17 = (bf16[512,128]{1,0:T(8,128)(2,1)S(1)}, bf16[512,128]{1,0:T(8,128)(2,1)S(1)}, u32[]{:S(2)}, u32[]{:S(2)}) collective-permute-start(bf16[512,128]{1,0:T(8,128)(2,1)S(1)} %weigh2.1), channel_id=1, source_target_pairs={{0,4},{1,5},{2,6},{3,7},{4,0},{5,1},{6,2},{7,3},{8,12},{9,13},{10,... | collective-permute-start | bytes 393224 | tf_op jit(solution)/shard_map/ppermute | solution.py:23
  42.4 1.6 %collective-permute-start.16 = (bf16[512,128]{1,0:T(8,128)(2,1)S(1)}, bf16[512,128]{1,0:T(8,128)(2,1)S(1)}, u32[]{:S(2)}, u32[]{:S(2)}) collective-permute-start(bf16[512,128]{1,0:T(8,128)(2,1)S(1)} %weigh3.1), channel_id=1, source_target_pairs={{0,6},{1,7},{2,4},{3,5},{4,2},{5,3},{6,0},{7,1},{8,14},{9,15},{10,... | collective-permute-start | bytes 393224 | tf_op jit(solution)/shard_map/ppermute | solution.py:23
  44.0 0.0 collective-permute-done.15.share_ref
  44.0 1.2 %weigh1.1 = bf16[512,128]{1,0:T(8,128)(2,1)S(1)} custom-call(s32[129]{0:T(256)S(1)} %concatenate.16.info_ref, f32[128,8]{1,0:T(8,128)S(1)} %get-tuple-element.47.spot_ref, bf16[256,1024]{1,0:T(8,128)(2,1)S(1)} %get-tuple-element.53.near_ref, f32[8,128]{1,0:T(8,128)S(1)} %pad_maximum_fusion.point_ref, bf16[1024,128]{1,0:T(8,128)(2,1)S(1)} %get-tuple-element.60.coeff_ref), custom_call_target="tpu_custom_call" | custom-call | flops 268435456 | bytes 524288 | tf_op jit(solution)/shard_map/weigh1/pallas_call | solution.py:430
  45.2 0.4 collective-permute-start.18
  45.6 1.0 %solved.1 = f32[512,256]{1,0:T(8,128)} custom-call(s32[1]{0:T(128)} %bitcast.core_ref, f32[512,128]{1,0:T(8,128)S(1)} %get-tuple-element.55.mine_ref, f32[512,128]{1,0:T(8,128)S(1)} %get-tuple-element.56.rest_ref, bf16[512,640]{1,0:T(8,128)(2,1)S(1)} %left16.1.left_ref, bf16[128,128]{1,0:T(8,128)(2,1)S(1)} %collective-permute-done.15.share_ref), custom_call_target="tpu_custom_call" | custom-call | flops 16777216 | bytes 2097152 | tf_op jit(solution)/shard_map/solved/pallas_call | solution.py:448
  46.6 1.2 %weigh0.1 = f32[512,128]{1,0:T(8,128)S(1)} custom-call(s32[129]{0:T(256)S(1)} %concatenate.16.info_ref, f32[128,8]{1,0:T(8,128)S(1)} %get-tuple-element.47.spot_ref, bf16[256,1024]{1,0:T(8,128)(2,1)S(1)} %get-tuple-element.59.near_ref, f32[8,128]{1,0:T(8,128)S(1)} %pad_maximum_fusion.point_ref, bf16[1024,128]{1,0:T(8,128)(2,1)S(1)} %get-tuple-element.60.coeff_ref), custom_call_target="tpu_custom_call" | custom-call | flops 268435456 | bytes 524288 | tf_op jit(solution)/shard_map/weigh0/pallas_call | solution.py:430
  47.7 1.8 %collective-permute-done.17 = bf16[512,128]{1,0:T(8,128)(2,1)S(1)} collective-permute-done((bf16[512,128]{1,0:T(8,128)(2,1)S(1)}, bf16[512,128]{1,0:T(8,128)(2,1)S(1)}, u32[]{:S(2)}, u32[]{:S(2)}) %collective-permute-start.17) | collective-permute-done | bytes 131104 | tf_op jit(solution)/shard_map/ppermute | solution.py:23
  49.5 0.0 collective-permute-done.16
  49.5 1.2 %collective-permute-done.18 = bf16[512,128]{1,0:T(8,128)(2,1)S(1)} collective-permute-done((bf16[512,128]{1,0:T(8,128)(2,1)S(1)}, bf16[512,128]{1,0:T(8,128)(2,1)S(1)}, u32[]{:S(2)}, u32[]{:S(2)}) %collective-permute-start.18) | collective-permute-done | bytes 131104 | tf_op jit(solution)/shard_map/ppermute | solution.py:23
  50.8 0.1 fusion.3
  50.9 3.9 %collective-permute-start.21 = (bf16[128,128]{1,0:T(8,128)(2,1)S(1)}, bf16[128,128]{1,0:T(8,128)(2,1)S(1)}, u32[]{:S(2)}, u32[]{:S(2)}) collective-permute-start(bf16[128,128]{1,0:T(8,128)(2,1)S(1)} %get-tuple-element.71), channel_id=1, source_target_pairs={{0,24},{1,25},{2,26},{3,27},{4,28},{5,29},{6,30},{7,31},{8,16},{9,... | collective-permute-start | bytes 98312 | tf_op jit(solution)/shard_map/ppermute | solution.py:23
  54.7 0.6 %collective-permute-start.19 = (bf16[128,128]{1,0:T(8,128)(2,1)S(1)}, bf16[128,128]{1,0:T(8,128)(2,1)S(1)}, u32[]{:S(2)}, u32[]{:S(2)}) collective-permute-start(bf16[128,128]{1,0:T(8,128)(2,1)S(1)} %get-tuple-element.70), channel_id=1, source_target_pairs={{0,8},{1,9},{2,10},{3,11},{4,12},{5,13},{6,14},{7,15},{8,0},{9,1},... | collective-permute-start | bytes 98312 | tf_op jit(solution)/shard_map/ppermute | solution.py:23
  55.4 1.3 %collective-permute-done.21 = bf16[128,128]{1,0:T(8,128)(2,1)S(1)} collective-permute-done((bf16[128,128]{1,0:T(8,128)(2,1)S(1)}, bf16[128,128]{1,0:T(8,128)(2,1)S(1)}, u32[]{:S(2)}, u32[]{:S(2)}) %collective-permute-start.21) | collective-permute-done | bytes 32800 | tf_op jit(solution)/shard_map/ppermute | solution.py:23
  56.7 2.9 %collective-permute-done.20 = bf16[128,128]{1,0:T(8,128)(2,1)S(1)} collective-permute-done((bf16[128,128]{1,0:T(8,128)(2,1)S(1)}, bf16[128,128]{1,0:T(8,128)(2,1)S(1)}, u32[]{:S(2)}, u32[]{:S(2)}) %collective-permute-start.20) | collective-permute-done | bytes 32800 | tf_op jit(solution)/shard_map/ppermute | solution.py:23
  59.5 0.0 collective-permute-done.19
  59.6 0.1 collective-permute-start.22
  59.7 1.2 %collective-permute-done.22 = f32[64,128]{1,0:T(8,128)S(1)} collective-permute-done((f32[64,128]{1,0:T(8,128)S(1)}, f32[64,128]{1,0:T(8,128)S(1)}, u32[]{:S(2)}, u32[]{:S(2)}) %collective-permute-start.22) | collective-permute-done | bytes 32800 | tf_op jit(solution)/shard_map/ppermute | solution.py:23
  60.9 0.6 %fusion.2 = f32[64,256]{1,0:T(8,128)} fusion(f32[64,128]{1,0:T(8,128)S(1)} %collective-permute-done.22, f32[64,128]{1,0:T(8,128)S(1)} %get-tuple-element.73, bf16[64,256]{1,0:T(8,128)(2,1)S(1)} %copy-done.5, pred[]{:T(512)S(6)} %eq.5), kind=kLoop, calls=%fused_computation.7 | loop fusion | flops 81920 | bytes 163841 | tf_op jit(solution)/shard_map/add | solution.py:472
  (28 shorter events, 0.1 us)
Async XLA Ops:
  0.6 3.2 %copy-start.1 = (bf16[512,256]{1,0:T(8,128)(2,1)S(1)}, bf16[512,256]{1,0:T(8,128)(2,1)}, u32[]{:S(2)}) copy-start(bf16[512,256]{1,0:T(8,128)(2,1)} %residual_ref.1) | copy-start | bytes 786436
  0.6 3.2 %copy-start.2 = (bf16[512,128]{1,0:T(8,128)(2,1)S(1)}, bf16[512,128]{1,0:T(8,128)(2,1)}, u32[]{:S(2)}) copy-start(bf16[512,128]{1,0:T(8,128)(2,1)} %inverse_ref.1) | copy-start | bytes 393220
  3.3 5.2 %collective-permute-start.3 = (bf16[1280,128]{1,0:T(8,128)(2,1)S(1)}, bf16[1280,128]{1,0:T(8,128)(2,1)S(1)}, u32[]{:S(2)}, u32[]{:S(2)}) collective-permute-start(bf16[1280,128]{1,0:T(8,128)(2,1)S(1)} %small.1.small_ref), channel_id=1, source_target_pairs={{0,1},{1,0},{2,3},{3,2},{4,5},{5,4},{6,7},{7,6},{8,9},{9,8},{10,11... | collective-permute-start | bytes 983048 | tf_op jit(solution)/shard_map/ppermute | solution.py:23
  3.8 4.2 %copy-start.6 = (f32[64]{0:T(128)S(1)}, f32[64]{0:T(128)}, u32[]{:S(2)}) copy-start(f32[64]{0:T(128)} %param.14) | copy-start | bytes 772
  3.8 8.7 %copy-start = (f32[7,512,128]{2,1,0:T(8,128)S(1)}, f32[7,512,128]{2,1,0:T(8,128)}, u32[]{:S(2)}) copy-start(f32[7,512,128]{2,1,0:T(8,128)} %left_ref.5) | copy-start | bytes 5505028
  7.9 3.3 %collective-permute-start.2 = (bf16[640,128]{1,0:T(8,128)(2,1)S(1)}, bf16[640,128]{1,0:T(8,128)(2,1)S(1)}, u32[]{:S(2)}, u32[]{:S(2)}) collective-permute-start(bf16[640,128]{1,0:T(8,128)(2,1)S(1)} %get-tuple-element.36), channel_id=1, source_target_pairs={{0,1},{1,0},{2,3},{3,2},{4,5},{5,4},{6,7},{7,6},{8,9},{9,8},{10,11... | collective-permute-start | bytes 491528 | tf_op jit(solution)/shard_map/ppermute | solution.py:23
  8.0 3.2 %collective-permute-start.4 = (f32[64]{0:T(128)S(1)}, f32[64]{0:T(128)S(1)}, u32[]{:S(2)}, u32[]{:S(2)}) collective-permute-start(f32[64]{0:T(128)S(1)} %copy-done.6), channel_id=1, source_target_pairs={{0,1},{1,0},{2,3},{3,2},{4,5},{5,4},{6,7},{7,6},{8,9},{9,8},{10,11... | collective-permute-start | bytes 776 | tf_op jit(solution)/shard_map/ppermute | solution.py:23
  8.6 11.2 %collective-permute-start.6 = (bf16[768,128]{1,0:T(8,128)(2,1)S(1)}, bf16[768,128]{1,0:T(8,128)(2,1)S(1)}, u32[]{:S(2)}, u32[]{:S(2)}) collective-permute-start(bf16[768,128]{1,0:T(8,128)(2,1)S(1)} %add_convert_fusion.rest_0_), channel_id=1, source_target_pairs={{0,2},{1,3},{2,0},{3,1},{4,6},{5,7},{6,4},{7,5},{8,10},{9,11},{10,... | collective-permute-start | bytes 589832 | tf_op jit(solution)/shard_map/ppermute | solution.py:23
  11.5 8.3 %collective-permute-start.5 = (bf16[560,128]{1,0:T(8,128)(2,1)S(1)}, bf16[560,128]{1,0:T(8,128)(2,1)S(1)}, u32[]{:S(2)}, u32[]{:S(2)}) collective-permute-start(bf16[560,128]{1,0:T(8,128)(2,1)S(1)} %get-tuple-element.39.own_ref), channel_id=1, source_target_pairs={{0,2},{1,3},{2,0},{3,1},{4,6},{5,7},{6,4},{7,5},{8,10},{9,11},{10,... | collective-permute-start | bytes 430088 | tf_op jit(solution)/shard_map/ppermute | solution.py:23
  12.7 22.8 %copy-start.3 = (s32[32,32]{1,0:T(8,128)S(1)}, s32[32,32]{1,0:T(8,128)}, u32[]{:S(2)}) copy-start(s32[32,32]{1,0:T(8,128)} %param.17) | copy-start | bytes 12292
  12.7 22.8 %copy-start.4 = (s32[32,32]{1,0:T(8,128)S(1)}, s32[32,32]{1,0:T(8,128)}, u32[]{:S(2)}) copy-start(s32[32,32]{1,0:T(8,128)} %param.16) | copy-start | bytes 12292
  12.7 24.6 %collective-permute-start.1 = (bf16[512,640]{1,0:T(8,128)(2,1)S(1)}, bf16[512,640]{1,0:T(8,128)(2,1)S(1)}, u32[]{:S(2)}, u32[]{:S(2)}) collective-permute-start(bf16[512,640]{1,0:T(8,128)(2,1)S(1)} %left16.1.left_ref), channel_id=1, source_target_pairs={{0,1},{1,0},{2,3},{3,2},{4,5},{5,4},{6,7},{7,6},{8,9},{9,8},{10,11... | collective-permute-start | bytes 1966088 | tf_op jit(solution)/shard_map/ppermute | solution.py:23
  12.8 19.3 %collective-permute-start = (f32[512,128]{1,0:T(8,128)S(1)}, f32[512,128]{1,0:T(8,128)S(1)}, u32[]{:S(2)}, u32[]{:S(2)}) collective-permute-start(f32[512,128]{1,0:T(8,128)S(1)} %get-tuple-element.34.rest_ref), channel_id=1, source_target_pairs={{0,1},{1,0},{2,3},{3,2},{4,5},{5,4},{6,7},{7,6},{8,9},{9,8},{10,11... | collective-permute-start | bytes 786440 | tf_op jit(solution)/shard_map/ppermute | solution.py:23
  20.0 7.0 %collective-permute-start.7 = (bf16[432,128]{1,0:T(8,128)(2,1)S(1)}, bf16[432,128]{1,0:T(8,128)(2,1)S(1)}, u32[]{:S(2)}, u32[]{:S(2)}) collective-permute-start(bf16[432,128]{1,0:T(8,128)(2,1)S(1)} %get-tuple-element.41.own_ref), channel_id=1, source_target_pairs={{0,4},{1,5},{2,6},{3,7},{4,0},{5,1},{6,2},{7,3},{8,12},{9,13},{10,... | collective-permute-start | bytes 331784 | tf_op jit(solution)/shard_map/ppermute | solution.py:23
  21.8 5.1 %collective-permute-start.8 = (bf16[384,128]{1,0:T(8,128)(2,1)S(1)}, bf16[384,128]{1,0:T(8,128)(2,1)S(1)}, u32[]{:S(2)}, u32[]{:S(2)}) collective-permute-start(bf16[384,128]{1,0:T(8,128)(2,1)S(1)} %add_convert_fusion.1.rest_0_), channel_id=1, source_target_pairs={{0,4},{1,5},{2,6},{3,7},{4,0},{5,1},{6,2},{7,3},{8,12},{9,13},{10,... | collective-permute-start | bytes 294920 | tf_op jit(solution)/shard_map/ppermute | solution.py:23
  22.1 10.5 %collective-permute-start.13 = (bf16[128,128]{1,0:T(8,128)(2,1)S(1)}, bf16[128,128]{1,0:T(8,128)(2,1)S(1)}, u32[]{:S(2)}, u32[]{:S(2)}) collective-permute-start(bf16[128,128]{1,0:T(8,128)(2,1)S(1)} %get-tuple-element.37.last_ref), channel_id=1, source_target_pairs={{0,1},{1,0},{2,3},{3,2},{4,5},{5,4},{6,7},{7,6},{8,9},{9,8},{10,11... | collective-permute-start | bytes 98312 | tf_op jit(solution)/shard_map/ppermute | solution.py:23
  27.1 4.8 %collective-permute-start.9 = (bf16[432,128]{1,0:T(8,128)(2,1)S(1)}, bf16[432,128]{1,0:T(8,128)(2,1)S(1)}, u32[]{:S(2)}, u32[]{:S(2)}) collective-permute-start(bf16[432,128]{1,0:T(8,128)(2,1)S(1)} %get-tuple-element.42.own_ref), channel_id=1, source_target_pairs={{0,8},{1,9},{2,10},{3,11},{4,12},{5,13},{6,14},{7,15},{8,0},{9,1},... | collective-permute-start | bytes 331784 | tf_op jit(solution)/shard_map/ppermute | solution.py:23
  29.8 7.5 %collective-permute-start.12 = (bf16[128,128]{1,0:T(8,128)(2,1)S(1)}, bf16[128,128]{1,0:T(8,128)(2,1)S(1)}, u32[]{:S(2)}, u32[]{:S(2)}) collective-permute-start(bf16[128,128]{1,0:T(8,128)(2,1)S(1)} %slice.74.refs_2_), channel_id=1, source_target_pairs={{0,1},{1,0},{2,3},{3,2},{4,5},{5,4},{6,7},{7,6},{8,9},{9,8},{10,11... | collective-permute-start | bytes 98312 | tf_op jit(solution)/shard_map/ppermute | solution.py:23
  31.9 5.4 %collective-permute-start.11 = (bf16[128,128]{1,0:T(8,128)(2,1)S(1)}, bf16[128,128]{1,0:T(8,128)(2,1)S(1)}, u32[]{:S(2)}, u32[]{:S(2)}) collective-permute-start(bf16[128,128]{1,0:T(8,128)(2,1)S(1)} %slice.73.refs_1_), channel_id=1, source_target_pairs={{0,1},{1,0},{2,3},{3,2},{4,5},{5,4},{6,7},{7,6},{8,9},{9,8},{10,11... | collective-permute-start | bytes 98312 | tf_op jit(solution)/shard_map/ppermute | solution.py:23
  32.1 5.3 %collective-permute-start.10 = (bf16[128,128]{1,0:T(8,128)(2,1)S(1)}, bf16[128,128]{1,0:T(8,128)(2,1)S(1)}, u32[]{:S(2)}, u32[]{:S(2)}) collective-permute-start(bf16[128,128]{1,0:T(8,128)(2,1)S(1)} %slice.72.refs_0_), channel_id=1, source_target_pairs={{0,1},{1,0},{2,3},{3,2},{4,5},{5,4},{6,7},{7,6},{8,9},{9,8},{10,11... | collective-permute-start | bytes 98312 | tf_op jit(solution)/shard_map/ppermute | solution.py:23
  32.7 5.4 %collective-permute-start.14 = (bf16[176,128]{1,0:T(8,128)(2,1)S(1)}, bf16[176,128]{1,0:T(8,128)(2,1)S(1)}, u32[]{:S(2)}, u32[]{:S(2)}) collective-permute-start(bf16[176,128]{1,0:T(8,128)(2,1)S(1)} %merge3.1.own_ref), channel_id=1, source_target_pairs={{0,16},{1,17},{2,18},{3,19},{4,20},{5,21},{6,22},{7,23},{8,24},{9,... | collective-permute-start | bytes 135176 | tf_op jit(solution)/shard_map/ppermute | solution.py:23
  38.1 5.9 %collective-permute-start.15 = (bf16[128,128]{1,0:T(8,128)(2,1)S(1)}, bf16[128,128]{1,0:T(8,128)(2,1)S(1)}, u32[]{:S(2)}, u32[]{:S(2)}) collective-permute-start(bf16[128,128]{1,0:T(8,128)(2,1)S(1)} %slice.76), channel_id=1, source_target_pairs={{0,1},{1,0},{2,3},{3,2},{4,5},{5,4},{6,7},{7,6},{8,9},{9,8},{10,11... | collective-permute-start | bytes 98312 | tf_op jit(solution)/shard_map/ppermute | solution.py:23
  40.8 8.8 %collective-permute-start.17 = (bf16[512,128]{1,0:T(8,128)(2,1)S(1)}, bf16[512,128]{1,0:T(8,128)(2,1)S(1)}, u32[]{:S(2)}, u32[]{:S(2)}) collective-permute-start(bf16[512,128]{1,0:T(8,128)(2,1)S(1)} %weigh2.1), channel_id=1, source_target_pairs={{0,4},{1,5},{2,6},{3,7},{4,0},{5,1},{6,2},{7,3},{8,12},{9,13},{10,... | collective-permute-start | bytes 393224 | tf_op jit(solution)/shard_map/ppermute | solution.py:23
  42.4 7.1 %collective-permute-start.16 = (bf16[512,128]{1,0:T(8,128)(2,1)S(1)}, bf16[512,128]{1,0:T(8,128)(2,1)S(1)}, u32[]{:S(2)}, u32[]{:S(2)}) collective-permute-start(bf16[512,128]{1,0:T(8,128)(2,1)S(1)} %weigh3.1), channel_id=1, source_target_pairs={{0,6},{1,7},{2,4},{3,5},{4,2},{5,3},{6,0},{7,1},{8,14},{9,15},{10,... | collective-permute-start | bytes 393224 | tf_op jit(solution)/shard_map/ppermute | solution.py:23
  45.2 5.6 %collective-permute-start.18 = (bf16[512,128]{1,0:T(8,128)(2,1)S(1)}, bf16[512,128]{1,0:T(8,128)(2,1)S(1)}, u32[]{:S(2)}, u32[]{:S(2)}) collective-permute-start(bf16[512,128]{1,0:T(8,128)(2,1)S(1)} %weigh1.1), channel_id=1, source_target_pairs={{0,2},{1,3},{2,0},{3,1},{4,6},{5,7},{6,4},{7,5},{8,10},{9,11},{10,... | collective-permute-start | bytes 393224 | tf_op jit(solution)/shard_map/ppermute | solution.py:23
  45.6 15.3 %copy-start.5 = (bf16[64,256]{1,0:T(8,128)(2,1)S(1)}, bf16[64,256]{1,0:T(8,128)(2,1)}, u32[]{:S(2)}) copy-start(bf16[64,256]{1,0:T(8,128)(2,1)} %param.15) | copy-start | bytes 98308
  50.9 5.8 %collective-permute-start.21 = (bf16[128,128]{1,0:T(8,128)(2,1)S(1)}, bf16[128,128]{1,0:T(8,128)(2,1)S(1)}, u32[]{:S(2)}, u32[]{:S(2)}) collective-permute-start(bf16[128,128]{1,0:T(8,128)(2,1)S(1)} %get-tuple-element.71), channel_id=1, source_target_pairs={{0,24},{1,25},{2,26},{3,27},{4,28},{5,29},{6,30},{7,31},{8,16},{9,... | collective-permute-start | bytes 98312 | tf_op jit(solution)/shard_map/ppermute | solution.py:23
  54.7 4.8 %collective-permute-start.20 = (bf16[128,128]{1,0:T(8,128)(2,1)S(1)}, bf16[128,128]{1,0:T(8,128)(2,1)S(1)}, u32[]{:S(2)}, u32[]{:S(2)}) collective-permute-start(bf16[128,128]{1,0:T(8,128)(2,1)S(1)} %get-tuple-element.72), channel_id=1, source_target_pairs={{0,16},{1,17},{2,18},{3,19},{4,20},{5,21},{6,22},{7,23},{8,24},{9,... | collective-permute-start | bytes 98312 | tf_op jit(solution)/shard_map/ppermute | solution.py:23
  54.7 4.8 %collective-permute-start.19 = (bf16[128,128]{1,0:T(8,128)(2,1)S(1)}, bf16[128,128]{1,0:T(8,128)(2,1)S(1)}, u32[]{:S(2)}, u32[]{:S(2)}) collective-permute-start(bf16[128,128]{1,0:T(8,128)(2,1)S(1)} %get-tuple-element.70), channel_id=1, source_target_pairs={{0,8},{1,9},{2,10},{3,11},{4,12},{5,13},{6,14},{7,15},{8,0},{9,1},... | collective-permute-start | bytes 98312 | tf_op jit(solution)/shard_map/ppermute | solution.py:23
  59.6 1.3 %collective-permute-start.22 = (f32[64,128]{1,0:T(8,128)S(1)}, f32[64,128]{1,0:T(8,128)S(1)}, u32[]{:S(2)}, u32[]{:S(2)}) collective-permute-start(f32[64,128]{1,0:T(8,128)S(1)} %get-tuple-element.74), channel_id=1, source_target_pairs={{0,1},{1,0},{2,3},{3,2},{4,5},{5,4},{6,7},{7,6},{8,9},{9,8},{10,11... | collective-permute-start | bytes 98312 | tf_op jit(solution)/shard_map/ppermute | solution.py:23

commit v5 on v4

--- a/solution.py
+++ b/solution.py
@@ -194,22 +194,20 @@
     put_spots(message_ref, cut + inner, depths[1], spots)
 
 
-def partial_kernel(bits, rank, mine_ref, rest_ref, other_ref, left_ref, left_other_ref, last_ref, *refs):
-    shares, others, outs = refs[: bits - 1], refs[bits - 1 : 2 * bits - 2], refs[2 * bits - 2 :]
+def partial_kernel(bits, rank, mine_ref, other_ref, left_ref, left_other_ref, last_ref, *refs):
+    shares, outs = refs[: bits - 2], refs[bits - 2 :]
     top = [s[...] for s in shares[:-1]]
-    left = left_ref[:, rank:]
-    outs[0][...] = mine_ref[...] + dot(left, jnp.concatenate([s[...] for s in shares], 0))
-    outs[1][...] = rest_ref[...] + dot(left, jnp.concatenate([s[...] for s in others], 0))
-    outs[2][...] = other_ref[...] + dot(left_other_ref[:, rank:], jnp.concatenate(top + [last_ref[...]], 0))
-
-
-def coeff_kernel(rank, n, depth, scale, mine_ref, other_ref, left_ref, left_other_ref, got_ref, final_ref, coeff_ref, spot_ref):
+    outs[0][...] = mine_ref[...] + dot(left_ref[:, 2 * rank :], jnp.concatenate([s[...] for s in shares], 0))
+    outs[1][...] = other_ref[...] + dot(left_other_ref[:, 2 * rank :], jnp.concatenate(top + [last_ref[...]], 0))
+
+
+def coeff_kernel(rank, n, depth, scale, mine_ref, other_ref, left_ref, left_other_ref, share_ref, got_ref, final_ref, coeff_ref, spot_ref):
     rows = mine_ref.shape[0]
-    share = got_ref[:rank, :]
-    x = mine_ref[...] + dot(left_ref[:, :rank], share)
+    share = jnp.concatenate([got_ref[:rank, :], share_ref[...]], 0)
+    x = mine_ref[...] + dot(left_ref[:, : 2 * rank], share)
     final_ref[...] = x
     coeff_ref[:rows, :] = x.astype(bf16)
-    coeff_ref[rows:, :] = (other_ref[...] + dot(left_other_ref[:, :rank], share)).astype(bf16)
+    coeff_ref[rows:, :] = (other_ref[...] + dot(left_other_ref[:, : 2 * rank], share)).astype(bf16)
     spot_ref[...] = (gathered(got_ref, rank, depth)[:n, :] * scale).T
 
 
@@ -255,9 +253,10 @@
     out_ref[half:, :] = dot(weight_ref[...], coeff_ref[...]).astype(out_ref.dtype)
 
 
-def solved_kernel(rank, core_ref, mine_ref, rest_ref, left_ref, share_ref, out_ref):
+def solved_kernel(core_ref, mine_ref, rest_ref, left_ref, *refs):
+    others, out_ref = refs[:-1], refs[-1]
     half = mine_ref.shape[1]
-    x, y = mine_ref[...], rest_ref[...] + dot(left_ref[:, :rank], share_ref[...])
+    x, y = mine_ref[...], rest_ref[...] + dot(left_ref[...], jnp.concatenate([s[...] for s in others], 0))
     first = core_ref[0] == 0
     out_ref[:, :half] = jnp.where(first, x, y)
     out_ref[:, half:] = jnp.where(first, y, x)
@@ -371,12 +370,30 @@
         previous = small_own[bit], small_theirs[bit]
     shares[top] = got[top * rank :]
     others[top] = swapped(last, 1)
+    points = [lax.dynamic_slice_in_dim(point_pos, s * rows, rows).reshape(blocks, leaf) for s in (me, me ^ 1)]
+    points = jnp.concatenate(points, 0)
+    info = jnp.concatenate(
+        [me.reshape(1)]
+        + [lax.dynamic_index_in_dim(t, s, 1, keepdims=False) for t in (block_first, block_count) for s in (me, me ^ 1)]
+    )
     for bit in range(1, bits):
         level = top - bit
         arrived = swapped(message, 1 << bit)
         share = arrived[level * rank : (level + 1) * rank]
         shares[level] = share
-        others[level] = swapped(share, 1)
+        if level > 1:
+            others[level] = swapped(share, 1)
+        if level == 1:
+            part_mine, part_other = call(
+                functools.partial(partial_kernel, bits, rank),
+                [out((rows, half), f32)] * 2,
+                "partial",
+                4 * bits * rows * rank * half,
+                16 * rows * half,
+            )(solved_mine, solved_other, left16, left_other, last, *shares[2:])
+            arrived, part_mine, part_other, info, points, others[2:] = lax.optimization_barrier(
+                (arrived, part_mine, part_other, info, points, others[2:])
+            )
         if level:
             apart, along = bit in ahead, bit + 1 not in ahead
             inner_rows = pairs_below(level) if along else 0
@@ -392,23 +409,10 @@
             )(y, message, arrived, *((small_own[bit], small_theirs[bit]) if apart else ()))
             y = kept_y[0] if kept_y else None
 
-    part_mine, part_rest, part_other = call(
-        functools.partial(partial_kernel, bits, rank),
-        [out((rows, half), f32)] * 3,
-        "partial",
-        6 * bits * rows * rank * half,
-        24 * rows * half,
-    )(solved_mine, solved_send, solved_other, left16, left_other, last, *shares[1:], *others[1:])
     plane = 4
     near = devices // (4 * plane)
     depth = depth_of(bits - 1)
     chips = 1 << (bits - 2)
-    points = [lax.dynamic_slice_in_dim(point_pos, s * rows, rows).reshape(blocks, leaf) for s in (me, me ^ 1)]
-    points = jnp.concatenate(points, 0)
-    info = jnp.concatenate(
-        [me.reshape(1)]
-        + [lax.dynamic_index_in_dim(t, s, 1, keepdims=False) for t in (block_first, block_count) for s in (me, me ^ 1)]
-    )
     near_weights = call(
         functools.partial(near_kernel, plane, near, tile, leaf, blocks, devices, chips, depth, rank),
         [out((2 * near * tile, 2 * rows), bf16)] * plane,
@@ -424,7 +428,7 @@
         "coeffs",
         4 * rows * rank * half,
         16 * rows * half,
-    )(part_mine, part_other, left16, left_other, arrived)
+    )(part_mine, part_other, left16, left_other, shares[1], arrived)
 
     def weighed(mask, coeffs):
         return call(
@@ -441,18 +445,21 @@
     sent = []
     for mask in (3, 2, 1):
         if mask == 1:
-            coeffs, others[0] = lax.optimization_barrier((coeffs, others[0]))
+            coeffs, others[:2] = lax.optimization_barrier((coeffs, others[:2]))
         partial = weighed(mask, coeffs)
         coeffs, partial = lax.optimization_barrier((coeffs, partial))
+        if mask == 2:
+            share0, share1, _ = lax.optimization_barrier((shares[0], shares[1], coeffs))
+            others[:2] = swapped(share0, 1), swapped(share1, 1)
         sent.append(swapped(partial, mask << 1))
     solved_out = call(
-        functools.partial(solved_kernel, rank),
+        solved_kernel,
         out((rows, samples), f32),
         "solved",
-        2 * rows * rank * half,
+        2 * bits * rows * rank * half,
         16 * rows * samples,
-        ins=[SMEM, VMEM, VMEM, VMEM, VMEM],
-    )(core_s, final_mine, part_rest, left16, others[0])
+        ins=[SMEM] + [VMEM] * (3 + bits),
+    )(core_s, final_mine, solved_send, left16, *others)
     coeffs, solved_out = lax.optimization_barrier((coeffs, solved_out))
     total = weighed(0, coeffs)
     for partial in sent:

time: 61.7 us -> 62.1 us (level)
  Pallas kernels: 15.8 us -> 17.8 us
  starting transfers between devices: 20.9 us -> 19.7 us
  waiting for transfers between devices: 21.9 us -> 20.7 us
    ppermute x23, starting transfers between devices: 20.9 us -> 19.7 us  [swapped(): return lax.ppermute(value, 'pts', pairs)]
    ppermute x23, waiting for transfers between devices: 21.9 us -> 20.7 us  [swapped(): return lax.ppermute(value, 'pts', pairs)]
    pallas_call x1, Pallas kernels: 0.97 us -> 1.9 us  [body(): call(solved_kernel, out((rows, samples), f32), 'solved', 2 * bits * rows...]
  transfers between devices with their start and end apart: 23 -> 23, of which waited for: 9 -> 9; matrix products, arithmetic and copies ran while one was open for 2% -> 2% of each run, Pallas kernels for 21% -> 20%
where the time goes in v5:
time: 62.1 us; the launch traced here: 61.8 us
  waiting for transfers between devices  20.7 us (33%)
  starting transfers between devices  19.7 us (32%)
  Pallas kernels  17.8 us (29%)
  local copies, waits for them, and re-layouts  1.83 us (3%)
  other arithmetic  0.9 us (1%)
  between operations  0.9 us (1%)
    ppermute x23, waiting for transfers between devices, swapped(): return lax.ppermute(value, 'pts', pairs)  20.7 us
    ppermute x23, starting transfers between devices, swapped(): return lax.ppermute(value, 'pts', pairs)  19.7 us
    pallas_call x4, Pallas kernels, weighed(): call(functools.partial(far_kernel, mask, plane, near, tile, leaf, blocks,...  4.77 us
    pallas_call x1, Pallas kernels, body(): call(functools.partial(front_kernel, rows, leaf, bits, rank, inner, sizes...  4.11 us
    pallas_call x1, Pallas kernels, body(): call(functools.partial(small_kernel, bits, rank), out((pair_count * rank,...  2.62 us
    pallas_call x1, Pallas kernels, body(): call(solved_kernel, out((rows, samples), f32), 'solved', 2 * bits * rows...  1.9 us
    pallas_call x1, Pallas kernels, body(): call(functools.partial(near_kernel, plane, near, tile, leaf, blocks, devi...  1.5 us
  transfers between devices with their start and end apart: 23, of which 9 were waited for; matrix products, arithmetic and copies ran while one was open for 2% of the time, Pallas kernels for 20%

profile of v5, /device:TPU:0, one launch (start us, length us, event | category | flops | bytes accessed | tf_op | source)
XLA Modules:
  0.0 61.8 jit_solution(9041478672254841020)
XLA Ops:
  0.6 2.6 %small.1.small_ref = bf16[1280,128]{1,0:T(8,128)(2,1)S(1)} custom-call(f32[7,512,128]{2,1,0:T(8,128)} %right_ref.3, f32[7,512,128]{2,1,0:T(8,128)} %left_ref.5), custom_call_target="tpu_custom_call" | custom-call | flops 167772160 | bytes 2621440 | tf_op jit(solution)/shard_map/small/pallas_call | solution.py:293
  3.3 0.5 collective-permute-start.1
  3.8 4.1 %front.1 = (f32[512,128]{1,0:T(8,128)S(1)}, f32[512,128]{1,0:T(8,128)S(1)}, f32[640,128]{1,0:T(8,128)S(1)}, bf16[640,128]{1,0:T(8,128)(2,1)S(1)}) custom-call(s32[1]{0:T(128)} %bitcast.core_ref, bf16[512,256]{1,0:T(8,128)(2,1)S(1)} %copy-done.1, bf16[512,128]{1,0:T(8,128)(2,1)S(1)} %copy-done.2, f32[7,512,128]{2,1,0:T(8,128)} %right_ref.3, ...), custom_call_target="tpu_custom_call" | custom-call | flops 503316480 | bytes 3670016 | tf_op jit(solution)/shard_map/front/pallas_call | solution.py:309
  7.9 0.1 collective-permute-start
  8.0 0.5 collective-permute-start.2
  8.5 0.2 left16.1.left_ref
  8.7 0.0 copy-start.5
  8.8 0.0 copy-start.6
  8.8 0.2 collective-permute-start.9
  8.9 0.0 collective-permute-done.1.their_ref
  8.9 0.1 add_convert_fusion.rest_0_
  9.0 3.0 %collective-permute-start.4 = (bf16[768,128]{1,0:T(8,128)(2,1)S(1)}, bf16[768,128]{1,0:T(8,128)(2,1)S(1)}, u32[]{:S(2)}, u32[]{:S(2)}) collective-permute-start(bf16[768,128]{1,0:T(8,128)(2,1)S(1)} %add_convert_fusion.rest_0_), channel_id=1, source_target_pairs={{0,2},{1,3},{2,0},{3,1},{4,6},{5,7},{6,4},{7,5},{8,10},{9,11},{10,... | collective-permute-start | bytes 589832 | tf_op jit(solution)/shard_map/ppermute | solution.py:23
  11.9 0.0 collective-permute-done.2
  11.9 0.1 maximum_bitcast_fusion.spot_ref
  12.0 0.0 collective-permute-done.got_ref
  12.0 0.7 %merge0.1 = (f32[512,128]{1,0:T(8,128)S(1)}, bf16[560,128]{1,0:T(8,128)(2,1)S(1)}, bf16[128,128]{1,0:T(8,128)(2,1)}) custom-call(f32[640,128]{1,0:T(8,128)S(1)} %get-tuple-element.43.keep_ref, bf16[640,128]{1,0:T(8,128)(2,1)S(1)} %collective-permute-done.got_ref, bf16[1280,128]{1,0:T(8,128)(2,1)S(1)} %small.1.small_ref, ...), custom_call_target="tpu_custom_call" | custom-call | flops 33554432 | bytes 524288 | tf_op jit(solution)/shard_map/merge0/pallas_call | solution.py:351
  12.7 0.1 collective-permute-start.3
  12.9 7.3 %collective-permute-done.3.got_ref = bf16[560,128]{1,0:T(8,128)(2,1)S(1)} collective-permute-done((bf16[560,128]{1,0:T(8,128)(2,1)S(1)}, bf16[560,128]{1,0:T(8,128)(2,1)S(1)}, u32[]{:S(2)}, u32[]{:S(2)}) %collective-permute-start.3) | collective-permute-done | bytes 143392 | tf_op jit(solution)/shard_map/ppermute | solution.py:23
  20.2 0.0 collective-permute-done.4.rest_1_
  20.2 0.2 merge1.1
  20.4 1.8 %collective-permute-start.5 = (bf16[432,128]{1,0:T(8,128)(2,1)S(1)}, bf16[432,128]{1,0:T(8,128)(2,1)S(1)}, u32[]{:S(2)}, u32[]{:S(2)}) collective-permute-start(bf16[432,128]{1,0:T(8,128)(2,1)S(1)} %get-tuple-element.48.own_ref), channel_id=1, source_target_pairs={{0,4},{1,5},{2,6},{3,7},{4,0},{5,1},{6,2},{7,3},{8,12},{9,13},{10,... | collective-permute-start | bytes 331784 | tf_op jit(solution)/shard_map/ppermute | solution.py:23
  22.2 0.3 collective-permute-start.6
  22.6 0.8 %dynamic-slice_bitcast_fusion.1 = (f32[4,128]{1,0:T(4,128)S(1)}, f32[4,128]{1,0:T(4,128)S(1)}) fusion(f32[16384]{0:T(1024)} %param.13, s32[]{:T(128)S(6)} %select_n.33, s32[]{:T(128)S(6)} %select_n.34), kind=kLoop, calls=%fused_computation.14 | loop fusion | bytes 8200 | tf_op jit(solution)/shard_map/reshape | solution.py:373
  23.4 3.7 %collective-permute-done.6.rest_1_ = bf16[384,128]{1,0:T(8,128)(2,1)S(1)} collective-permute-done((bf16[384,128]{1,0:T(8,128)(2,1)S(1)}, bf16[384,128]{1,0:T(8,128)(2,1)S(1)}, u32[]{:S(2)}, u32[]{:S(2)}) %collective-permute-start.6) | collective-permute-done | bytes 98336 | tf_op jit(solution)/shard_map/ppermute | solution.py:23
  27.2 0.2 merge2.1
  27.3 1.6 %collective-permute-start.7 = (bf16[432,128]{1,0:T(8,128)(2,1)S(1)}, bf16[432,128]{1,0:T(8,128)(2,1)S(1)}, u32[]{:S(2)}, u32[]{:S(2)}) collective-permute-start(bf16[432,128]{1,0:T(8,128)(2,1)S(1)} %get-tuple-element.49.own_ref), channel_id=1, source_target_pairs={{0,8},{1,9},{2,10},{3,11},{4,12},{5,13},{6,14},{7,15},{8,0},{9,1},... | collective-permute-start | bytes 331784 | tf_op jit(solution)/shard_map/ppermute | solution.py:23
  29.0 0.2 collective-permute-start.10
  29.2 0.2 dynamic-slice_reduce_fusion
  29.5 0.1 concatenate.16.info_ref
  29.6 0.0 collective-permute-done.9.left_other_ref
  29.6 1.1 %partial.1 = (f32[512,128]{1,0:T(8,128)S(1)}, f32[512,128]{1,0:T(8,128)S(1)}) custom-call(f32[512,128]{1,0:T(8,128)S(1)} %get-tuple-element.50.mine_ref, f32[512,128]{1,0:T(8,128)S(1)} %collective-permute-done.8.other_ref, bf16[512,640]{1,0:T(8,128)(2,1)S(1)} %left16.1.left_ref, bf16[512,640]{1,0:T(8,128)(2,1)S(1)} %collective-permute-done.9.left_other_ref, ...), custom_call_target="tpu_custom_call" | custom-call | flops 167772160 | bytes 1048576 | tf_op jit(solution)/shard_map/partial/pallas_call | solution.py:387
  30.7 0.0 collective-permute-done.11.refs_3_
  30.7 0.0 copy-start.3
  30.7 0.6 copy-done.3
  31.3 0.0 collective-permute-done.10.refs_2_
  31.3 1.5 %collective-permute-done.7.got_ref = bf16[432,128]{1,0:T(8,128)(2,1)S(1)} collective-permute-done((bf16[432,128]{1,0:T(8,128)(2,1)S(1)}, bf16[432,128]{1,0:T(8,128)(2,1)S(1)}, u32[]{:S(2)}, u32[]{:S(2)}) %collective-permute-start.7) | collective-permute-done | bytes 110624 | tf_op jit(solution)/shard_map/ppermute | solution.py:23
  32.9 0.2 merge3.1.own_ref
  33.0 2.7 %collective-permute-start.13 = (bf16[176,128]{1,0:T(8,128)(2,1)S(1)}, bf16[176,128]{1,0:T(8,128)(2,1)S(1)}, u32[]{:S(2)}, u32[]{:S(2)}) collective-permute-start(bf16[176,128]{1,0:T(8,128)(2,1)S(1)} %merge3.1.own_ref), channel_id=1, source_target_pairs={{0,16},{1,17},{2,18},{3,19},{4,20},{5,21},{6,22},{7,23},{8,24},{9,... | collective-permute-start | bytes 135176 | tf_op jit(solution)/shard_map/ppermute | solution.py:23
  35.7 1.5 %near.1 = (bf16[256,1024]{1,0:T(8,128)(2,1)S(1)}, bf16[256,1024]{1,0:T(8,128)(2,1)S(1)}, bf16[256,1024]{1,0:T(8,128)(2,1)S(1)}, bf16[256,1024]{1,0:T(8,128)(2,1)S(1)}) custom-call(s32[129]{0:T(256)S(1)} %concatenate.16.info_ref, bf16[176,128]{1,0:T(8,128)(2,1)S(1)} %merge3.1.own_ref, f32[8,128]{1,0:T(8,128)S(1)} %pad_maximum_fusion.point_ref), custom_call_target="tpu_custom_call" | custom-call | flops 10485760 | bytes 2097152 | tf_op jit(solution)/shard_map/near/pallas_call | solution.py:416
  37.2 1.1 %collective-permute-done.13.got_ref = bf16[176,128]{1,0:T(8,128)(2,1)S(1)} collective-permute-done((bf16[176,128]{1,0:T(8,128)(2,1)S(1)}, bf16[176,128]{1,0:T(8,128)(2,1)S(1)}, u32[]{:S(2)}, u32[]{:S(2)}) %collective-permute-start.13) | collective-permute-done | bytes 45088 | tf_op jit(solution)/shard_map/ppermute | solution.py:23
  38.3 0.3 coeffs.1
  38.6 0.0 copy-start.4
  38.6 1.2 %weigh3.1 = bf16[512,128]{1,0:T(8,128)(2,1)S(1)} custom-call(s32[129]{0:T(256)S(1)} %concatenate.16.info_ref, f32[128,8]{1,0:T(8,128)S(1)} %get-tuple-element.61.spot_ref, bf16[256,1024]{1,0:T(8,128)(2,1)S(1)} %get-tuple-element.63.near_ref, f32[8,128]{1,0:T(8,128)S(1)} %pad_maximum_fusion.point_ref, bf16[1024,128]{1,0:T(8,128)(2,1)S(1)} %get-tuple-element.80.coeff_ref), custom_call_target="tpu_custom_call" | custom-call | flops 268435456 | bytes 524288 | tf_op jit(solution)/shard_map/weigh3/pallas_call | solution.py:434
  39.8 1.2 %weigh2.1 = bf16[512,128]{1,0:T(8,128)(2,1)S(1)} custom-call(s32[129]{0:T(256)S(1)} %concatenate.16.info_ref, f32[128,8]{1,0:T(8,128)S(1)} %get-tuple-element.61.spot_ref, bf16[256,1024]{1,0:T(8,128)(2,1)S(1)} %get-tuple-element.65.near_ref, f32[8,128]{1,0:T(8,128)S(1)} %pad_maximum_fusion.point_ref, bf16[1024,128]{1,0:T(8,128)(2,1)S(1)} %get-tuple-element.80.coeff_ref), custom_call_target="tpu_custom_call" | custom-call | flops 268435456 | bytes 524288 | tf_op jit(solution)/shard_map/weigh2/pallas_call | solution.py:434
  41.1 0.1 collective-permute-start.14
  41.1 0.5 collective-permute-start.15
  41.6 1.4 %collective-permute-start.17 = (bf16[512,128]{1,0:T(8,128)(2,1)S(1)}, bf16[512,128]{1,0:T(8,128)(2,1)S(1)}, u32[]{:S(2)}, u32[]{:S(2)}) collective-permute-start(bf16[512,128]{1,0:T(8,128)(2,1)S(1)} %weigh2.1), channel_id=1, source_target_pairs={{0,4},{1,5},{2,6},{3,7},{4,0},{5,1},{6,2},{7,3},{8,12},{9,13},{10,... | collective-permute-start | bytes 393224 | tf_op jit(solution)/shard_map/ppermute | solution.py:23
  43.0 1.6 %collective-permute-start.16 = (bf16[512,128]{1,0:T(8,128)(2,1)S(1)}, bf16[512,128]{1,0:T(8,128)(2,1)S(1)}, u32[]{:S(2)}, u32[]{:S(2)}) collective-permute-start(bf16[512,128]{1,0:T(8,128)(2,1)S(1)} %weigh3.1), channel_id=1, source_target_pairs={{0,6},{1,7},{2,4},{3,5},{4,2},{5,3},{6,0},{7,1},{8,14},{9,15},{10,... | collective-permute-start | bytes 393224 | tf_op jit(solution)/shard_map/ppermute | solution.py:23
  44.6 1.2 %weigh1.1 = bf16[512,128]{1,0:T(8,128)(2,1)S(1)} custom-call(s32[129]{0:T(256)S(1)} %concatenate.16.info_ref, f32[128,8]{1,0:T(8,128)S(1)} %get-tuple-element.61.spot_ref, bf16[256,1024]{1,0:T(8,128)(2,1)S(1)} %get-tuple-element.70.near_ref, f32[8,128]{1,0:T(8,128)S(1)} %pad_maximum_fusion.point_ref, bf16[1024,128]{1,0:T(8,128)(2,1)S(1)} %get-tuple-element.80.coeff_ref), custom_call_target="tpu_custom_call" | custom-call | flops 268435456 | bytes 524288 | tf_op jit(solution)/shard_map/weigh1/pallas_call | solution.py:434
  45.8 0.6 collective-permute-start.18
  46.4 1.9 %solved.1 = f32[512,256]{1,0:T(8,128)} custom-call(s32[1]{0:T(128)} %bitcast.core_ref, f32[512,128]{1,0:T(8,128)S(1)} %get-tuple-element.72.mine_ref, f32[512,128]{1,0:T(8,128)S(1)} %get-tuple-element.51.rest_ref, bf16[512,640]{1,0:T(8,128)(2,1)S(1)} %left16.1.left_ref, bf16[128,128]{1,0:T(8,128)(2,1)S(1)} %collective-permute-done.14.refs_0_, ...), custom_call_target="tpu_custom_call" | custom-call | flops 83886080 | bytes 2097152 | tf_op jit(solution)/shard_map/solved/pallas_call | solution.py:455
  48.3 1.2 %weigh0.1 = f32[512,128]{1,0:T(8,128)S(1)} custom-call(s32[129]{0:T(256)S(1)} %concatenate.16.info_ref, f32[128,8]{1,0:T(8,128)S(1)} %get-tuple-element.61.spot_ref, bf16[256,1024]{1,0:T(8,128)(2,1)S(1)} %get-tuple-element.79.near_ref, f32[8,128]{1,0:T(8,128)S(1)} %pad_maximum_fusion.point_ref, bf16[1024,128]{1,0:T(8,128)(2,1)S(1)} %get-tuple-element.80.coeff_ref), custom_call_target="tpu_custom_call" | custom-call | flops 268435456 | bytes 524288 | tf_op jit(solution)/shard_map/weigh0/pallas_call | solution.py:434
  49.5 0.5 collective-permute-done.17
  49.9 0.0 collective-permute-done.16
  49.9 1.2 %collective-permute-done.18 = bf16[512,128]{1,0:T(8,128)(2,1)S(1)} collective-permute-done((bf16[512,128]{1,0:T(8,128)(2,1)S(1)}, bf16[512,128]{1,0:T(8,128)(2,1)S(1)}, u32[]{:S(2)}, u32[]{:S(2)}) %collective-permute-start.18) | collective-permute-done | bytes 131104 | tf_op jit(solution)/shard_map/ppermute | solution.py:23
  51.1 0.1 fusion.3
  51.2 3.8 %collective-permute-start.21 = (bf16[128,128]{1,0:T(8,128)(2,1)S(1)}, bf16[128,128]{1,0:T(8,128)(2,1)S(1)}, u32[]{:S(2)}, u32[]{:S(2)}) collective-permute-start(bf16[128,128]{1,0:T(8,128)(2,1)S(1)} %get-tuple-element.91), channel_id=1, source_target_pairs={{0,24},{1,25},{2,26},{3,27},{4,28},{5,29},{6,30},{7,31},{8,16},{9,... | collective-permute-start | bytes 98312 | tf_op jit(solution)/shard_map/ppermute | solution.py:23
  55.0 0.7 %collective-permute-start.19 = (bf16[128,128]{1,0:T(8,128)(2,1)S(1)}, bf16[128,128]{1,0:T(8,128)(2,1)S(1)}, u32[]{:S(2)}, u32[]{:S(2)}) collective-permute-start(bf16[128,128]{1,0:T(8,128)(2,1)S(1)} %get-tuple-element.90), channel_id=1, source_target_pairs={{0,8},{1,9},{2,10},{3,11},{4,12},{5,13},{6,14},{7,15},{8,0},{9,1},... | collective-permute-start | bytes 98312 | tf_op jit(solution)/shard_map/ppermute | solution.py:23
  55.7 1.3 %collective-permute-done.21 = bf16[128,128]{1,0:T(8,128)(2,1)S(1)} collective-permute-done((bf16[128,128]{1,0:T(8,128)(2,1)S(1)}, bf16[128,128]{1,0:T(8,128)(2,1)S(1)}, u32[]{:S(2)}, u32[]{:S(2)}) %collective-permute-start.21) | collective-permute-done | bytes 32800 | tf_op jit(solution)/shard_map/ppermute | solution.py:23
  57.0 2.8 %collective-permute-done.20 = bf16[128,128]{1,0:T(8,128)(2,1)S(1)} collective-permute-done((bf16[128,128]{1,0:T(8,128)(2,1)S(1)}, bf16[128,128]{1,0:T(8,128)(2,1)S(1)}, u32[]{:S(2)}, u32[]{:S(2)}) %collective-permute-start.20) | collective-permute-done | bytes 32800 | tf_op jit(solution)/shard_map/ppermute | solution.py:23
  59.8 0.0 collective-permute-done.19
  59.9 0.1 collective-permute-start.22
  60.0 1.2 %collective-permute-done.22 = f32[64,128]{1,0:T(8,128)S(1)} collective-permute-done((f32[64,128]{1,0:T(8,128)S(1)}, f32[64,128]{1,0:T(8,128)S(1)}, u32[]{:S(2)}, u32[]{:S(2)}) %collective-permute-start.22) | collective-permute-done | bytes 32800 | tf_op jit(solution)/shard_map/ppermute | solution.py:23
  61.2 0.6 %fusion.2 = f32[64,256]{1,0:T(8,128)} fusion(f32[64,128]{1,0:T(8,128)S(1)} %collective-permute-done.22, f32[64,128]{1,0:T(8,128)S(1)} %get-tuple-element.93, bf16[64,256]{1,0:T(8,128)(2,1)S(1)} %copy-done.7, pred[]{:T(512)S(6)} %eq.5), kind=kLoop, calls=%fused_computation.7 | loop fusion | flops 81920 | bytes 163841 | tf_op jit(solution)/shard_map/add | solution.py:479
  (32 shorter events, 0.1 us)
Async XLA Ops:
  0.6 3.2 %copy-start.1 = (bf16[512,256]{1,0:T(8,128)(2,1)S(1)}, bf16[512,256]{1,0:T(8,128)(2,1)}, u32[]{:S(2)}) copy-start(bf16[512,256]{1,0:T(8,128)(2,1)} %residual_ref.1) | copy-start | bytes 786436
  0.6 3.2 %copy-start.2 = (bf16[512,128]{1,0:T(8,128)(2,1)S(1)}, bf16[512,128]{1,0:T(8,128)(2,1)}, u32[]{:S(2)}) copy-start(bf16[512,128]{1,0:T(8,128)(2,1)} %inverse_ref.1) | copy-start | bytes 393220
  3.3 5.6 %collective-permute-start.1 = (bf16[1280,128]{1,0:T(8,128)(2,1)S(1)}, bf16[1280,128]{1,0:T(8,128)(2,1)S(1)}, u32[]{:S(2)}, u32[]{:S(2)}) collective-permute-start(bf16[1280,128]{1,0:T(8,128)(2,1)S(1)} %small.1.small_ref), channel_id=1, source_target_pairs={{0,1},{1,0},{2,3},{3,2},{4,5},{5,4},{6,7},{7,6},{8,9},{9,8},{10,11... | collective-permute-start | bytes 983048 | tf_op jit(solution)/shard_map/ppermute | solution.py:23
  3.8 4.2 %copy-start.8 = (f32[64]{0:T(128)S(1)}, f32[64]{0:T(128)}, u32[]{:S(2)}) copy-start(f32[64]{0:T(128)} %param.14) | copy-start | bytes 772
  3.8 4.7 %copy-start = (f32[7,512,128]{2,1,0:T(8,128)S(1)}, f32[7,512,128]{2,1,0:T(8,128)}, u32[]{:S(2)}) copy-start(f32[7,512,128]{2,1,0:T(8,128)} %left_ref.5) | copy-start | bytes 5505028
  7.9 4.1 %collective-permute-start = (bf16[640,128]{1,0:T(8,128)(2,1)S(1)}, bf16[640,128]{1,0:T(8,128)(2,1)S(1)}, u32[]{:S(2)}, u32[]{:S(2)}) collective-permute-start(bf16[640,128]{1,0:T(8,128)(2,1)S(1)} %get-tuple-element.44), channel_id=1, source_target_pairs={{0,1},{1,0},{2,3},{3,2},{4,5},{5,4},{6,7},{7,6},{8,9},{9,8},{10,11... | collective-permute-start | bytes 491528 | tf_op jit(solution)/shard_map/ppermute | solution.py:23
  8.0 3.9 %collective-permute-start.2 = (f32[64]{0:T(128)S(1)}, f32[64]{0:T(128)S(1)}, u32[]{:S(2)}, u32[]{:S(2)}) collective-permute-start(f32[64]{0:T(128)S(1)} %copy-done.8), channel_id=1, source_target_pairs={{0,1},{1,0},{2,3},{3,2},{4,5},{5,4},{6,7},{7,6},{8,9},{9,8},{10,11... | collective-permute-start | bytes 776 | tf_op jit(solution)/shard_map/ppermute | solution.py:23
  8.7 20.5 %copy-start.5 = (s32[32,32]{1,0:T(8,128)S(1)}, s32[32,32]{1,0:T(8,128)}, u32[]{:S(2)}) copy-start(s32[32,32]{1,0:T(8,128)} %param.17) | copy-start | bytes 12292
  8.8 20.5 %copy-start.6 = (s32[32,32]{1,0:T(8,128)S(1)}, s32[32,32]{1,0:T(8,128)}, u32[]{:S(2)}) copy-start(s32[32,32]{1,0:T(8,128)} %param.16) | copy-start | bytes 12292
  8.8 20.8 %collective-permute-start.9 = (bf16[512,640]{1,0:T(8,128)(2,1)S(1)}, bf16[512,640]{1,0:T(8,128)(2,1)S(1)}, u32[]{:S(2)}, u32[]{:S(2)}) collective-permute-start(bf16[512,640]{1,0:T(8,128)(2,1)S(1)} %left16.1.left_ref), channel_id=1, source_target_pairs={{0,1},{1,0},{2,3},{3,2},{4,5},{5,4},{6,7},{7,6},{8,9},{9,8},{10,11... | collective-permute-start | bytes 1966088 | tf_op jit(solution)/shard_map/ppermute | solution.py:23
  9.0 11.2 %collective-permute-start.4 = (bf16[768,128]{1,0:T(8,128)(2,1)S(1)}, bf16[768,128]{1,0:T(8,128)(2,1)S(1)}, u32[]{:S(2)}, u32[]{:S(2)}) collective-permute-start(bf16[768,128]{1,0:T(8,128)(2,1)S(1)} %add_convert_fusion.rest_0_), channel_id=1, source_target_pairs={{0,2},{1,3},{2,0},{3,1},{4,6},{5,7},{6,4},{7,5},{8,10},{9,11},{10,... | collective-permute-start | bytes 589832 | tf_op jit(solution)/shard_map/ppermute | solution.py:23
  12.7 7.4 %collective-permute-start.3 = (bf16[560,128]{1,0:T(8,128)(2,1)S(1)}, bf16[560,128]{1,0:T(8,128)(2,1)S(1)}, u32[]{:S(2)}, u32[]{:S(2)}) collective-permute-start(bf16[560,128]{1,0:T(8,128)(2,1)S(1)} %get-tuple-element.46.own_ref), channel_id=1, source_target_pairs={{0,2},{1,3},{2,0},{3,1},{4,6},{5,7},{6,4},{7,5},{8,10},{9,11},{10,... | collective-permute-start | bytes 430088 | tf_op jit(solution)/shard_map/ppermute | solution.py:23
  12.9 16.1 %collective-permute-start.8 = (f32[512,128]{1,0:T(8,128)S(1)}, f32[512,128]{1,0:T(8,128)S(1)}, u32[]{:S(2)}, u32[]{:S(2)}) collective-permute-start(f32[512,128]{1,0:T(8,128)S(1)} %get-tuple-element.51.rest_ref), channel_id=1, source_target_pairs={{0,1},{1,0},{2,3},{3,2},{4,5},{5,4},{6,7},{7,6},{8,9},{9,8},{10,11... | collective-permute-start | bytes 786440 | tf_op jit(solution)/shard_map/ppermute | solution.py:23
  20.4 6.8 %collective-permute-start.5 = (bf16[432,128]{1,0:T(8,128)(2,1)S(1)}, bf16[432,128]{1,0:T(8,128)(2,1)S(1)}, u32[]{:S(2)}, u32[]{:S(2)}) collective-permute-start(bf16[432,128]{1,0:T(8,128)(2,1)S(1)} %get-tuple-element.48.own_ref), channel_id=1, source_target_pairs={{0,4},{1,5},{2,6},{3,7},{4,0},{5,1},{6,2},{7,3},{8,12},{9,13},{10,... | collective-permute-start | bytes 331784 | tf_op jit(solution)/shard_map/ppermute | solution.py:23
  22.2 4.9 %collective-permute-start.6 = (bf16[384,128]{1,0:T(8,128)(2,1)S(1)}, bf16[384,128]{1,0:T(8,128)(2,1)S(1)}, u32[]{:S(2)}, u32[]{:S(2)}) collective-permute-start(bf16[384,128]{1,0:T(8,128)(2,1)S(1)} %add_convert_fusion.1.rest_0_), channel_id=1, source_target_pairs={{0,4},{1,5},{2,6},{3,7},{4,0},{5,1},{6,2},{7,3},{8,12},{9,13},{10,... | collective-permute-start | bytes 294920 | tf_op jit(solution)/shard_map/ppermute | solution.py:23
  23.4 7.3 %collective-permute-start.12 = (bf16[128,128]{1,0:T(8,128)(2,1)}, bf16[128,128]{1,0:T(8,128)(2,1)}, u32[]{:S(2)}, u32[]{:S(2)}) collective-permute-start(bf16[128,128]{1,0:T(8,128)(2,1)} %get-tuple-element.52.last_ref), channel_id=1, source_target_pairs={{0,1},{1,0},{2,3},{3,2},{4,5},{5,4},{6,7},{7,6},{8,9},{9,8},{10,11... | collective-permute-start | bytes 98312 | tf_op jit(solution)/shard_map/ppermute | solution.py:23
  27.2 3.5 %collective-permute-start.11 = (bf16[128,128]{1,0:T(8,128)(2,1)S(1)}, bf16[128,128]{1,0:T(8,128)(2,1)S(1)}, u32[]{:S(2)}, u32[]{:S(2)}) collective-permute-start(bf16[128,128]{1,0:T(8,128)(2,1)S(1)} %slice.73.refs_1_), channel_id=1, source_target_pairs={{0,1},{1,0},{2,3},{3,2},{4,5},{5,4},{6,7},{7,6},{8,9},{9,8},{10,11... | collective-permute-start | bytes 98312 | tf_op jit(solution)/shard_map/ppermute | solution.py:23
  27.3 5.5 %collective-permute-start.7 = (bf16[432,128]{1,0:T(8,128)(2,1)S(1)}, bf16[432,128]{1,0:T(8,128)(2,1)S(1)}, u32[]{:S(2)}, u32[]{:S(2)}) collective-permute-start(bf16[432,128]{1,0:T(8,128)(2,1)S(1)} %get-tuple-element.49.own_ref), channel_id=1, source_target_pairs={{0,8},{1,9},{2,10},{3,11},{4,12},{5,13},{6,14},{7,15},{8,0},{9,1},... | collective-permute-start | bytes 331784 | tf_op jit(solution)/shard_map/ppermute | solution.py:23
  29.0 2.3 %collective-permute-start.10 = (bf16[128,128]{1,0:T(8,128)(2,1)S(1)}, bf16[128,128]{1,0:T(8,128)(2,1)S(1)}, u32[]{:S(2)}, u32[]{:S(2)}) collective-permute-start(bf16[128,128]{1,0:T(8,128)(2,1)S(1)} %slice.72.refs_0_), channel_id=1, source_target_pairs={{0,1},{1,0},{2,3},{3,2},{4,5},{5,4},{6,7},{7,6},{8,9},{9,8},{10,11... | collective-permute-start | bytes 98312 | tf_op jit(solution)/shard_map/ppermute | solution.py:23
  30.7 0.6 copy-start.3
  33.0 5.3 %collective-permute-start.13 = (bf16[176,128]{1,0:T(8,128)(2,1)S(1)}, bf16[176,128]{1,0:T(8,128)(2,1)S(1)}, u32[]{:S(2)}, u32[]{:S(2)}) collective-permute-start(bf16[176,128]{1,0:T(8,128)(2,1)S(1)} %merge3.1.own_ref), channel_id=1, source_target_pairs={{0,16},{1,17},{2,18},{3,19},{4,20},{5,21},{6,22},{7,23},{8,24},{9,... | collective-permute-start | bytes 135176 | tf_op jit(solution)/shard_map/ppermute | solution.py:23
  38.6 7.8 %copy-start.4 = (bf16[128,128]{1,0:T(8,128)(2,1)S(1)}, bf16[128,128]{1,0:T(8,128)(2,1)}, u32[]{:S(2)}) copy-start(bf16[128,128]{1,0:T(8,128)(2,1)} %copy-done.3) | copy-start | bytes 98308
  41.1 3.5 %collective-permute-start.14 = (bf16[128,128]{1,0:T(8,128)(2,1)S(1)}, bf16[128,128]{1,0:T(8,128)(2,1)S(1)}, u32[]{:S(2)}, u32[]{:S(2)}) collective-permute-start(bf16[128,128]{1,0:T(8,128)(2,1)S(1)} %slice.76), channel_id=1, source_target_pairs={{0,1},{1,0},{2,3},{3,2},{4,5},{5,4},{6,7},{7,6},{8,9},{9,8},{10,11... | collective-permute-start | bytes 98312 | tf_op jit(solution)/shard_map/ppermute | solution.py:23
  41.1 3.5 %collective-permute-start.15 = (bf16[128,128]{1,0:T(8,128)(2,1)S(1)}, bf16[128,128]{1,0:T(8,128)(2,1)S(1)}, u32[]{:S(2)}, u32[]{:S(2)}) collective-permute-start(bf16[128,128]{1,0:T(8,128)(2,1)S(1)} %slice.75.share_ref), channel_id=1, source_target_pairs={{0,1},{1,0},{2,3},{3,2},{4,5},{5,4},{6,7},{7,6},{8,9},{9,8},{10,11... | collective-permute-start | bytes 98312 | tf_op jit(solution)/shard_map/ppermute | solution.py:23
  41.6 8.3 %collective-permute-start.17 = (bf16[512,128]{1,0:T(8,128)(2,1)S(1)}, bf16[512,128]{1,0:T(8,128)(2,1)S(1)}, u32[]{:S(2)}, u32[]{:S(2)}) collective-permute-start(bf16[512,128]{1,0:T(8,128)(2,1)S(1)} %weigh2.1), channel_id=1, source_target_pairs={{0,4},{1,5},{2,6},{3,7},{4,0},{5,1},{6,2},{7,3},{8,12},{9,13},{10,... | collective-permute-start | bytes 393224 | tf_op jit(solution)/shard_map/ppermute | solution.py:23
  43.0 6.9 %collective-permute-start.16 = (bf16[512,128]{1,0:T(8,128)(2,1)S(1)}, bf16[512,128]{1,0:T(8,128)(2,1)S(1)}, u32[]{:S(2)}, u32[]{:S(2)}) collective-permute-start(bf16[512,128]{1,0:T(8,128)(2,1)S(1)} %weigh3.1), channel_id=1, source_target_pairs={{0,6},{1,7},{2,4},{3,5},{4,2},{5,3},{6,0},{7,1},{8,14},{9,15},{10,... | collective-permute-start | bytes 393224 | tf_op jit(solution)/shard_map/ppermute | solution.py:23
  45.8 5.4 %collective-permute-start.18 = (bf16[512,128]{1,0:T(8,128)(2,1)S(1)}, bf16[512,128]{1,0:T(8,128)(2,1)S(1)}, u32[]{:S(2)}, u32[]{:S(2)}) collective-permute-start(bf16[512,128]{1,0:T(8,128)(2,1)S(1)} %weigh1.1), channel_id=1, source_target_pairs={{0,2},{1,3},{2,0},{3,1},{4,6},{5,7},{6,4},{7,5},{8,10},{9,11},{10,... | collective-permute-start | bytes 393224 | tf_op jit(solution)/shard_map/ppermute | solution.py:23
  48.3 12.9 %copy-start.7 = (bf16[64,256]{1,0:T(8,128)(2,1)S(1)}, bf16[64,256]{1,0:T(8,128)(2,1)}, u32[]{:S(2)}) copy-start(bf16[64,256]{1,0:T(8,128)(2,1)} %param.15) | copy-start | bytes 98308
  51.2 5.8 %collective-permute-start.21 = (bf16[128,128]{1,0:T(8,128)(2,1)S(1)}, bf16[128,128]{1,0:T(8,128)(2,1)S(1)}, u32[]{:S(2)}, u32[]{:S(2)}) collective-permute-start(bf16[128,128]{1,0:T(8,128)(2,1)S(1)} %get-tuple-element.91), channel_id=1, source_target_pairs={{0,24},{1,25},{2,26},{3,27},{4,28},{5,29},{6,30},{7,31},{8,16},{9,... | collective-permute-start | bytes 98312 | tf_op jit(solution)/shard_map/ppermute | solution.py:23
  55.0 4.8 %collective-permute-start.20 = (bf16[128,128]{1,0:T(8,128)(2,1)S(1)}, bf16[128,128]{1,0:T(8,128)(2,1)S(1)}, u32[]{:S(2)}, u32[]{:S(2)}) collective-permute-start(bf16[128,128]{1,0:T(8,128)(2,1)S(1)} %get-tuple-element.92), channel_id=1, source_target_pairs={{0,16},{1,17},{2,18},{3,19},{4,20},{5,21},{6,22},{7,23},{8,24},{9,... | collective-permute-start | bytes 98312 | tf_op jit(solution)/shard_map/ppermute | solution.py:23
  55.0 4.8 %collective-permute-start.19 = (bf16[128,128]{1,0:T(8,128)(2,1)S(1)}, bf16[128,128]{1,0:T(8,128)(2,1)S(1)}, u32[]{:S(2)}, u32[]{:S(2)}) collective-permute-start(bf16[128,128]{1,0:T(8,128)(2,1)S(1)} %get-tuple-element.90), channel_id=1, source_target_pairs={{0,8},{1,9},{2,10},{3,11},{4,12},{5,13},{6,14},{7,15},{8,0},{9,1},... | collective-permute-start | bytes 98312 | tf_op jit(solution)/shard_map/ppermute | solution.py:23
  59.9 1.3 %collective-permute-start.22 = (f32[64,128]{1,0:T(8,128)S(1)}, f32[64,128]{1,0:T(8,128)S(1)}, u32[]{:S(2)}, u32[]{:S(2)}) collective-permute-start(f32[64,128]{1,0:T(8,128)S(1)} %get-tuple-element.94), channel_id=1, source_target_pairs={{0,1},{1,0},{2,3},{3,2},{4,5},{5,4},{6,7},{7,6},{8,9},{9,8},{10,11... | collective-permute-start | bytes 98312 | tf_op jit(solution)/shard_map/ppermute | solution.py:23

commit v6 on v5

--- a/solution.py
+++ b/solution.py
@@ -162,14 +162,13 @@
     return slice(at, at + level * rank)
 
 
-def first_merge(level, rank, depth, keep_ref, got_ref, small_ref, their_ref, spot_ref, y_ref, message_ref, last_ref):
+def first_merge(level, rank, depth, keep_ref, got_ref, small_ref, their_ref, spot_ref, y_ref, message_ref):
     at = small_at(level, rank)
     y = linked(level, rank, keep_ref[...], got_ref[...], small_ref[at, :], their_ref[at, :])
     y_ref[...] = y
     cut = level * rank
     message_ref[:cut, :] = y.astype(bf16)
     put_spots(message_ref, cut, depth, spot_ref[...])
-    last_ref[...] = keep_ref[cut : cut + rank, :].astype(bf16)
 
 
 def merge(level, rank, apart, along, n, depths, y_in, own_ref, got_ref, *rest):
@@ -348,12 +347,11 @@
     depth_of = lambda bit: max(16, 1 << (bit - 1))
     pairs_below = lambda level: level * (level - 1) // 2 * rank
     spot_rows = jnp.concatenate([map_pos, spot_other]).reshape(1, 2 * tile)
-    y, message, last = call(
+    y, message = call(
         functools.partial(first_merge, top, rank, depth_of(1)),
         [
             out((top * rank, half), f32),
             out((top * rank + 3 * depth_of(1), half), bf16),
-            out((rank, half), bf16),
         ],
         "merge0",
         4 * top * rank * rank * half,
@@ -369,6 +367,7 @@
         small_theirs[bit] = swapped(both, 1 << bit)
         previous = small_own[bit], small_theirs[bit]
     shares[top] = got[top * rank :]
+    last = keep[top * rank :].astype(bf16)
     others[top] = swapped(last, 1)
     points = [lax.dynamic_slice_in_dim(point_pos, s * rows, rows).reshape(blocks, leaf) for s in (me, me ^ 1)]
     points = jnp.concatenate(points, 0)
@@ -391,8 +390,8 @@
                 4 * bits * rows * rank * half,
                 16 * rows * half,
             )(solved_mine, solved_other, left16, left_other, last, *shares[2:])
-            arrived, part_mine, part_other, info, points, others[2:] = lax.optimization_barrier(
-                (arrived, part_mine, part_other, info, points, others[2:])
+            arrived, part_mine, part_other, info, points = lax.optimization_barrier(
+                (arrived, part_mine, part_other, info, points)
             )
         if level:
             apart, along = bit in ahead, bit + 1 not in ahead
@@ -445,7 +444,7 @@
     sent = []
     for mask in (3, 2, 1):
         if mask == 1:
-            coeffs, others[:2] = lax.optimization_barrier((coeffs, others[:2]))
+            coeffs, others = lax.optimization_barrier((coeffs, others))
         partial = weighed(mask, coeffs)
         coeffs, partial = lax.optimization_barrier((coeffs, partial))
         if mask == 2:

time: 62.1 us -> 61.3 us (0.987)
  Pallas kernels: 17.8 us -> 15.8 us
  waiting for transfers between devices: 20.7 us -> 22.1 us
    ppermute x23, waiting for transfers between devices: 20.7 us -> 22.1 us  [swapped(): return lax.ppermute(value, 'pts', pairs)]
    pallas_call x1, Pallas kernels: 1.9 us -> 1.13 us  [body(): call(solved_kernel, out((rows, samples), f32), 'solved', 2 * bits * rows...]
    pallas_call x1, Pallas kernels: 1.12 us -> 0.36 us  [body(): call(functools.partial(partial_kernel, bits, rank), [out((rows, half), f3...]
  transfers between devices with their start and end apart: 23 -> 23, of which waited for: 9 -> 9; matrix products, arithmetic and copies ran while one was open for 2% -> 2% of each run, Pallas kernels for 20% -> 21%
where the time goes in v6:
time: 61.3 us; the launch traced here: 61.1 us
  waiting for transfers between devices  22.1 us (36%)
  starting transfers between devices  20.2 us (33%)
  Pallas kernels  15.8 us (26%)
  local copies, waits for them, and re-layouts  1.22 us (2%)
  between operations  0.91 us (1%)
  other arithmetic  0.89 us (1%)
    ppermute x23, waiting for transfers between devices, swapped(): return lax.ppermute(value, 'pts', pairs)  22.1 us
    ppermute x23, starting transfers between devices, swapped(): return lax.ppermute(value, 'pts', pairs)  20.2 us
    pallas_call x4, Pallas kernels, weighed(): call(functools.partial(far_kernel, mask, plane, near, tile, leaf, blocks,...  4.77 us
    pallas_call x1, Pallas kernels, body(): call(functools.partial(front_kernel, rows, leaf, bits, rank, inner, sizes...  4.11 us
    pallas_call x1, Pallas kernels, body(): call(functools.partial(small_kernel, bits, rank), out((pair_count * rank,...  2.62 us
    pallas_call x1, Pallas kernels, body(): call(functools.partial(near_kernel, plane, near, tile, leaf, blocks, devi...  1.51 us
  transfers between devices with their start and end apart: 23, of which 9 were waited for; matrix products, arithmetic and copies ran while one was open for 2% of the time, Pallas kernels for 21%

profile of v6, /device:TPU:0, one launch (start us, length us, event | category | flops | bytes accessed | tf_op | source)
XLA Modules:
  0.0 61.1 jit_solution(11753604674557047547)
XLA Ops:
  0.6 2.6 %small.1.small_ref = bf16[1280,128]{1,0:T(8,128)(2,1)S(1)} custom-call(f32[7,512,128]{2,1,0:T(8,128)} %right_ref.3, f32[7,512,128]{2,1,0:T(8,128)} %left_ref.5), custom_call_target="tpu_custom_call" | custom-call | flops 167772160 | bytes 2621440 | tf_op jit(solution)/shard_map/small/pallas_call | solution.py:292
  3.3 0.5 collective-permute-start.1
  3.8 4.1 %front.1 = (f32[512,128]{1,0:T(8,128)S(1)}, f32[512,128]{1,0:T(8,128)S(1)}, f32[640,128]{1,0:T(8,128)S(1)}, bf16[640,128]{1,0:T(8,128)(2,1)S(1)}) custom-call(s32[1]{0:T(128)} %bitcast.core_ref, bf16[512,256]{1,0:T(8,128)(2,1)S(1)} %copy-done.1, bf16[512,128]{1,0:T(8,128)(2,1)S(1)} %copy-done.2, f32[7,512,128]{2,1,0:T(8,128)} %right_ref.3, ...), custom_call_target="tpu_custom_call" | custom-call | flops 503316480 | bytes 3670016 | tf_op jit(solution)/shard_map/front/pallas_call | solution.py:308
  7.9 0.0 copy-start.3
  7.9 0.0 copy-start.4
  7.9 0.1 collective-permute-start
  8.1 0.5 collective-permute-start.2
  8.5 0.2 left16.1.left_ref
  8.8 0.2 collective-permute-start.9
  8.9 0.0 collective-permute-done.1.their_ref
  8.9 0.1 add_convert_fusion.rest_0_
  9.0 3.0 %collective-permute-start.4 = (bf16[768,128]{1,0:T(8,128)(2,1)S(1)}, bf16[768,128]{1,0:T(8,128)(2,1)S(1)}, u32[]{:S(2)}, u32[]{:S(2)}) collective-permute-start(bf16[768,128]{1,0:T(8,128)(2,1)S(1)} %add_convert_fusion.rest_0_), channel_id=1, source_target_pairs={{0,2},{1,3},{2,0},{3,1},{4,6},{5,7},{6,4},{7,5},{8,10},{9,11},{10,... | collective-permute-start | bytes 589832 | tf_op jit(solution)/shard_map/ppermute | solution.py:23
  11.9 0.0 collective-permute-done.2
  11.9 0.1 maximum_bitcast_fusion.spot_ref
  12.0 0.0 collective-permute-done.got_ref
  12.0 0.2 merge0.1
  12.3 0.2 collective-permute-start.3
  12.5 0.0 collective-permute-start.8
  12.5 0.2 dynamic-slice_reduce_fusion
  12.8 0.1 concatenate.16.info_ref
  12.8 7.3 %collective-permute-done.3.got_ref = bf16[560,128]{1,0:T(8,128)(2,1)S(1)} collective-permute-done((bf16[560,128]{1,0:T(8,128)(2,1)S(1)}, bf16[560,128]{1,0:T(8,128)(2,1)S(1)}, u32[]{:S(2)}, u32[]{:S(2)}) %collective-permute-start.3) | collective-permute-done | bytes 143392 | tf_op jit(solution)/shard_map/ppermute | solution.py:23
  20.2 0.2 merge1.1
  20.4 1.8 %collective-permute-start.5 = (bf16[432,128]{1,0:T(8,128)(2,1)S(1)}, bf16[432,128]{1,0:T(8,128)(2,1)S(1)}, u32[]{:S(2)}, u32[]{:S(2)}) collective-permute-start(bf16[432,128]{1,0:T(8,128)(2,1)S(1)} %get-tuple-element.47.own_ref), channel_id=1, source_target_pairs={{0,4},{1,5},{2,6},{3,7},{4,0},{5,1},{6,2},{7,3},{8,12},{9,13},{10,... | collective-permute-start | bytes 331784 | tf_op jit(solution)/shard_map/ppermute | solution.py:23
  22.2 0.3 collective-permute-start.6
  22.6 0.8 %dynamic-slice_bitcast_fusion.1 = (f32[4,128]{1,0:T(4,128)S(1)}, f32[4,128]{1,0:T(4,128)S(1)}) fusion(f32[16384]{0:T(1024)} %param.13, s32[]{:T(128)S(6)} %select_n.33, s32[]{:T(128)S(6)} %select_n.34), kind=kLoop, calls=%fused_computation.15 | loop fusion | bytes 8200 | tf_op jit(solution)/shard_map/reshape | solution.py:372
  23.4 3.8 %collective-permute-done.6.rest_1_ = bf16[384,128]{1,0:T(8,128)(2,1)S(1)} collective-permute-done((bf16[384,128]{1,0:T(8,128)(2,1)S(1)}, bf16[384,128]{1,0:T(8,128)(2,1)S(1)}, u32[]{:S(2)}, u32[]{:S(2)}) %collective-permute-start.6) | collective-permute-done | bytes 98336 | tf_op jit(solution)/shard_map/ppermute | solution.py:23
  27.2 0.0 collective-permute-done.5.got_ref
  27.2 0.2 merge2.1
  27.3 1.6 %collective-permute-start.7 = (bf16[432,128]{1,0:T(8,128)(2,1)S(1)}, bf16[432,128]{1,0:T(8,128)(2,1)S(1)}, u32[]{:S(2)}, u32[]{:S(2)}) collective-permute-start(bf16[432,128]{1,0:T(8,128)(2,1)S(1)} %get-tuple-element.48.own_ref), channel_id=1, source_target_pairs={{0,8},{1,9},{2,10},{3,11},{4,12},{5,13},{6,14},{7,15},{8,0},{9,1},... | collective-permute-start | bytes 331784 | tf_op jit(solution)/shard_map/ppermute | solution.py:23
  29.0 0.0 collective-permute-done.8.other_ref
  29.1 0.4 partial.1
  29.4 2.7 %collective-permute-done.7.got_ref = bf16[432,128]{1,0:T(8,128)(2,1)S(1)} collective-permute-done((bf16[432,128]{1,0:T(8,128)(2,1)S(1)}, bf16[432,128]{1,0:T(8,128)(2,1)S(1)}, u32[]{:S(2)}, u32[]{:S(2)}) %collective-permute-start.7) | collective-permute-done | bytes 110624 | tf_op jit(solution)/shard_map/ppermute | solution.py:23
  32.2 0.2 merge3.1.own_ref
  32.3 2.7 %collective-permute-start.10 = (bf16[176,128]{1,0:T(8,128)(2,1)S(1)}, bf16[176,128]{1,0:T(8,128)(2,1)S(1)}, u32[]{:S(2)}, u32[]{:S(2)}) collective-permute-start(bf16[176,128]{1,0:T(8,128)(2,1)S(1)} %merge3.1.own_ref), channel_id=1, source_target_pairs={{0,16},{1,17},{2,18},{3,19},{4,20},{5,21},{6,22},{7,23},{8,24},{9,... | collective-permute-start | bytes 135176 | tf_op jit(solution)/shard_map/ppermute | solution.py:23
  35.0 0.5 collective-permute-start.14
  35.5 0.0 collective-permute-start.13
  35.5 1.5 %near.1 = (bf16[256,1024]{1,0:T(8,128)(2,1)S(1)}, bf16[256,1024]{1,0:T(8,128)(2,1)S(1)}, bf16[256,1024]{1,0:T(8,128)(2,1)S(1)}, bf16[256,1024]{1,0:T(8,128)(2,1)S(1)}) custom-call(s32[129]{0:T(256)S(1)} %concatenate.16.info_ref, bf16[176,128]{1,0:T(8,128)(2,1)S(1)} %merge3.1.own_ref, f32[8,128]{1,0:T(8,128)S(1)} %pad_maximum_fusion.point_ref), custom_call_target="tpu_custom_call" | custom-call | flops 10485760 | bytes 2097152 | tf_op jit(solution)/shard_map/near/pallas_call | solution.py:415
  37.0 0.3 collective-permute-done.10.got_ref
  37.3 0.3 coeffs.1
  37.6 1.2 %weigh3.1 = bf16[512,128]{1,0:T(8,128)(2,1)S(1)} custom-call(s32[129]{0:T(256)S(1)} %concatenate.16.info_ref, f32[128,8]{1,0:T(8,128)S(1)} %get-tuple-element.59.spot_ref, bf16[256,1024]{1,0:T(8,128)(2,1)S(1)} %get-tuple-element.61.near_ref, f32[8,128]{1,0:T(8,128)S(1)} %pad_maximum_fusion.point_ref, bf16[1024,128]{1,0:T(8,128)(2,1)S(1)} %get-tuple-element.78.coeff_ref), custom_call_target="tpu_custom_call" | custom-call | flops 268435456 | bytes 524288 | tf_op jit(solution)/shard_map/weigh3/pallas_call | solution.py:433
  38.8 1.2 %weigh2.1 = bf16[512,128]{1,0:T(8,128)(2,1)S(1)} custom-call(s32[129]{0:T(256)S(1)} %concatenate.16.info_ref, f32[128,8]{1,0:T(8,128)S(1)} %get-tuple-element.59.spot_ref, bf16[256,1024]{1,0:T(8,128)(2,1)S(1)} %get-tuple-element.63.near_ref, f32[8,128]{1,0:T(8,128)S(1)} %pad_maximum_fusion.point_ref, bf16[1024,128]{1,0:T(8,128)(2,1)S(1)} %get-tuple-element.78.coeff_ref), custom_call_target="tpu_custom_call" | custom-call | flops 268435456 | bytes 524288 | tf_op jit(solution)/shard_map/weigh2/pallas_call | solution.py:433
  40.1 0.3 collective-permute-start.11
  40.3 0.3 collective-permute-start.12
  40.6 1.4 %collective-permute-start.17 = (bf16[512,128]{1,0:T(8,128)(2,1)S(1)}, bf16[512,128]{1,0:T(8,128)(2,1)S(1)}, u32[]{:S(2)}, u32[]{:S(2)}) collective-permute-start(bf16[512,128]{1,0:T(8,128)(2,1)S(1)} %weigh2.1), channel_id=1, source_target_pairs={{0,4},{1,5},{2,6},{3,7},{4,0},{5,1},{6,2},{7,3},{8,12},{9,13},{10,... | collective-permute-start | bytes 393224 | tf_op jit(solution)/shard_map/ppermute | solution.py:23
  42.0 0.0 collective-permute-done.14.refs_3_
  42.0 1.6 %collective-permute-start.16 = (bf16[512,128]{1,0:T(8,128)(2,1)S(1)}, bf16[512,128]{1,0:T(8,128)(2,1)S(1)}, u32[]{:S(2)}, u32[]{:S(2)}) collective-permute-start(bf16[512,128]{1,0:T(8,128)(2,1)S(1)} %weigh3.1), channel_id=1, source_target_pairs={{0,6},{1,7},{2,4},{3,5},{4,2},{5,3},{6,0},{7,1},{8,14},{9,15},{10,... | collective-permute-start | bytes 393224 | tf_op jit(solution)/shard_map/ppermute | solution.py:23
  43.6 0.0 collective-permute-done.13.refs_2_
  43.6 0.0 collective-permute-done.11.refs_0_
  43.6 0.0 collective-permute-done.12.refs_1_
  43.6 1.2 %weigh1.1 = bf16[512,128]{1,0:T(8,128)(2,1)S(1)} custom-call(s32[129]{0:T(256)S(1)} %concatenate.16.info_ref, f32[128,8]{1,0:T(8,128)S(1)} %get-tuple-element.59.spot_ref, bf16[256,1024]{1,0:T(8,128)(2,1)S(1)} %get-tuple-element.68.near_ref, f32[8,128]{1,0:T(8,128)S(1)} %pad_maximum_fusion.point_ref, bf16[1024,128]{1,0:T(8,128)(2,1)S(1)} %get-tuple-element.78.coeff_ref), custom_call_target="tpu_custom_call" | custom-call | flops 268435456 | bytes 524288 | tf_op jit(solution)/shard_map/weigh1/pallas_call | solution.py:433
  44.8 0.6 collective-permute-start.18
  45.4 1.1 %solved.1 = f32[512,256]{1,0:T(8,128)} custom-call(s32[1]{0:T(128)} %bitcast.core_ref, f32[512,128]{1,0:T(8,128)S(1)} %get-tuple-element.70.mine_ref, f32[512,128]{1,0:T(8,128)S(1)} %get-tuple-element.50.rest_ref, bf16[512,640]{1,0:T(8,128)(2,1)S(1)} %left16.1.left_ref, bf16[128,128]{1,0:T(8,128)(2,1)S(1)} %collective-permute-done.11.refs_0_, ...), custom_call_target="tpu_custom_call" | custom-call | flops 83886080 | bytes 2097152 | tf_op jit(solution)/shard_map/solved/pallas_call | solution.py:454
  46.5 1.2 %weigh0.1 = f32[512,128]{1,0:T(8,128)S(1)} custom-call(s32[129]{0:T(256)S(1)} %concatenate.16.info_ref, f32[128,8]{1,0:T(8,128)S(1)} %get-tuple-element.59.spot_ref, bf16[256,1024]{1,0:T(8,128)(2,1)S(1)} %get-tuple-element.77.near_ref, f32[8,128]{1,0:T(8,128)S(1)} %pad_maximum_fusion.point_ref, bf16[1024,128]{1,0:T(8,128)(2,1)S(1)} %get-tuple-element.78.coeff_ref), custom_call_target="tpu_custom_call" | custom-call | flops 268435456 | bytes 524288 | tf_op jit(solution)/shard_map/weigh0/pallas_call | solution.py:433
  47.7 1.3 %collective-permute-done.17 = bf16[512,128]{1,0:T(8,128)(2,1)S(1)} collective-permute-done((bf16[512,128]{1,0:T(8,128)(2,1)S(1)}, bf16[512,128]{1,0:T(8,128)(2,1)S(1)}, u32[]{:S(2)}, u32[]{:S(2)}) %collective-permute-start.17) | collective-permute-done | bytes 131104 | tf_op jit(solution)/shard_map/ppermute | solution.py:23
  49.1 1.2 %collective-permute-done.18 = bf16[512,128]{1,0:T(8,128)(2,1)S(1)} collective-permute-done((bf16[512,128]{1,0:T(8,128)(2,1)S(1)}, bf16[512,128]{1,0:T(8,128)(2,1)S(1)}, u32[]{:S(2)}, u32[]{:S(2)}) %collective-permute-start.18) | collective-permute-done | bytes 131104 | tf_op jit(solution)/shard_map/ppermute | solution.py:23
  50.3 0.1 fusion.3
  50.4 3.9 %collective-permute-start.21 = (bf16[128,128]{1,0:T(8,128)(2,1)S(1)}, bf16[128,128]{1,0:T(8,128)(2,1)S(1)}, u32[]{:S(2)}, u32[]{:S(2)}) collective-permute-start(bf16[128,128]{1,0:T(8,128)(2,1)S(1)} %get-tuple-element.89), channel_id=1, source_target_pairs={{0,24},{1,25},{2,26},{3,27},{4,28},{5,29},{6,30},{7,31},{8,16},{9,... | collective-permute-start | bytes 98312 | tf_op jit(solution)/shard_map/ppermute | solution.py:23
  54.3 0.6 %collective-permute-start.19 = (bf16[128,128]{1,0:T(8,128)(2,1)S(1)}, bf16[128,128]{1,0:T(8,128)(2,1)S(1)}, u32[]{:S(2)}, u32[]{:S(2)}) collective-permute-start(bf16[128,128]{1,0:T(8,128)(2,1)S(1)} %get-tuple-element.88), channel_id=1, source_target_pairs={{0,8},{1,9},{2,10},{3,11},{4,12},{5,13},{6,14},{7,15},{8,0},{9,1},... | collective-permute-start | bytes 98312 | tf_op jit(solution)/shard_map/ppermute | solution.py:23
  54.9 1.3 %collective-permute-done.21 = bf16[128,128]{1,0:T(8,128)(2,1)S(1)} collective-permute-done((bf16[128,128]{1,0:T(8,128)(2,1)S(1)}, bf16[128,128]{1,0:T(8,128)(2,1)S(1)}, u32[]{:S(2)}, u32[]{:S(2)}) %collective-permute-start.21) | collective-permute-done | bytes 32800 | tf_op jit(solution)/shard_map/ppermute | solution.py:23
  56.3 2.8 %collective-permute-done.20 = bf16[128,128]{1,0:T(8,128)(2,1)S(1)} collective-permute-done((bf16[128,128]{1,0:T(8,128)(2,1)S(1)}, bf16[128,128]{1,0:T(8,128)(2,1)S(1)}, u32[]{:S(2)}, u32[]{:S(2)}) %collective-permute-start.20) | collective-permute-done | bytes 32800 | tf_op jit(solution)/shard_map/ppermute | solution.py:23
  59.1 0.0 collective-permute-done.19
  59.1 0.1 collective-permute-start.22
  59.2 1.2 %collective-permute-done.22 = f32[64,128]{1,0:T(8,128)S(1)} collective-permute-done((f32[64,128]{1,0:T(8,128)S(1)}, f32[64,128]{1,0:T(8,128)S(1)}, u32[]{:S(2)}, u32[]{:S(2)}) %collective-permute-start.22) | collective-permute-done | bytes 32800 | tf_op jit(solution)/shard_map/ppermute | solution.py:23
  60.4 0.6 %fusion.2 = f32[64,256]{1,0:T(8,128)} fusion(f32[64,128]{1,0:T(8,128)S(1)} %collective-permute-done.22, f32[64,128]{1,0:T(8,128)S(1)} %get-tuple-element.91, bf16[64,256]{1,0:T(8,128)(2,1)S(1)} %copy-done.5, pred[]{:T(512)S(6)} %eq.5), kind=kLoop, calls=%fused_computation.8 | loop fusion | flops 81920 | bytes 163841 | tf_op jit(solution)/shard_map/add | solution.py:478
  (29 shorter events, 0.1 us)
Async XLA Ops:
  0.6 3.2 %copy-start.1 = (bf16[512,256]{1,0:T(8,128)(2,1)S(1)}, bf16[512,256]{1,0:T(8,128)(2,1)}, u32[]{:S(2)}) copy-start(bf16[512,256]{1,0:T(8,128)(2,1)} %residual_ref.1) | copy-start | bytes 786436
  0.6 3.2 %copy-start.2 = (bf16[512,128]{1,0:T(8,128)(2,1)S(1)}, bf16[512,128]{1,0:T(8,128)(2,1)}, u32[]{:S(2)}) copy-start(bf16[512,128]{1,0:T(8,128)(2,1)} %inverse_ref.1) | copy-start | bytes 393220
  3.3 5.6 %collective-permute-start.1 = (bf16[1280,128]{1,0:T(8,128)(2,1)S(1)}, bf16[1280,128]{1,0:T(8,128)(2,1)S(1)}, u32[]{:S(2)}, u32[]{:S(2)}) collective-permute-start(bf16[1280,128]{1,0:T(8,128)(2,1)S(1)} %small.1.small_ref), channel_id=1, source_target_pairs={{0,1},{1,0},{2,3},{3,2},{4,5},{5,4},{6,7},{7,6},{8,9},{9,8},{10,11... | collective-permute-start | bytes 983048 | tf_op jit(solution)/shard_map/ppermute | solution.py:23
  3.8 4.3 %copy-start.6 = (f32[64]{0:T(128)S(1)}, f32[64]{0:T(128)}, u32[]{:S(2)}) copy-start(f32[64]{0:T(128)} %param.14) | copy-start | bytes 772
  3.8 4.7 %copy-start = (f32[7,512,128]{2,1,0:T(8,128)S(1)}, f32[7,512,128]{2,1,0:T(8,128)}, u32[]{:S(2)}) copy-start(f32[7,512,128]{2,1,0:T(8,128)} %left_ref.5) | copy-start | bytes 5505028
  7.9 4.6 %copy-start.3 = (s32[32,32]{1,0:T(8,128)S(1)}, s32[32,32]{1,0:T(8,128)}, u32[]{:S(2)}) copy-start(s32[32,32]{1,0:T(8,128)} %param.17) | copy-start | bytes 12292
  7.9 4.6 %copy-start.4 = (s32[32,32]{1,0:T(8,128)S(1)}, s32[32,32]{1,0:T(8,128)}, u32[]{:S(2)}) copy-start(s32[32,32]{1,0:T(8,128)} %param.16) | copy-start | bytes 12292
  7.9 4.1 %collective-permute-start = (bf16[640,128]{1,0:T(8,128)(2,1)S(1)}, bf16[640,128]{1,0:T(8,128)(2,1)S(1)}, u32[]{:S(2)}, u32[]{:S(2)}) collective-permute-start(bf16[640,128]{1,0:T(8,128)(2,1)S(1)} %get-tuple-element.43), channel_id=1, source_target_pairs={{0,1},{1,0},{2,3},{3,2},{4,5},{5,4},{6,7},{7,6},{8,9},{9,8},{10,11... | collective-permute-start | bytes 491528 | tf_op jit(solution)/shard_map/ppermute | solution.py:23
  8.1 3.9 %collective-permute-start.2 = (f32[64]{0:T(128)S(1)}, f32[64]{0:T(128)S(1)}, u32[]{:S(2)}, u32[]{:S(2)}) collective-permute-start(f32[64]{0:T(128)S(1)} %copy-done.6), channel_id=1, source_target_pairs={{0,1},{1,0},{2,3},{3,2},{4,5},{5,4},{6,7},{7,6},{8,9},{9,8},{10,11... | collective-permute-start | bytes 776 | tf_op jit(solution)/shard_map/ppermute | solution.py:23
  8.8 20.3 %collective-permute-start.9 = (bf16[512,640]{1,0:T(8,128)(2,1)S(1)}, bf16[512,640]{1,0:T(8,128)(2,1)S(1)}, u32[]{:S(2)}, u32[]{:S(2)}) collective-permute-start(bf16[512,640]{1,0:T(8,128)(2,1)S(1)} %left16.1.left_ref), channel_id=1, source_target_pairs={{0,1},{1,0},{2,3},{3,2},{4,5},{5,4},{6,7},{7,6},{8,9},{9,8},{10,11... | collective-permute-start | bytes 1966088 | tf_op jit(solution)/shard_map/ppermute | solution.py:23
  9.0 11.2 %collective-permute-start.4 = (bf16[768,128]{1,0:T(8,128)(2,1)S(1)}, bf16[768,128]{1,0:T(8,128)(2,1)S(1)}, u32[]{:S(2)}, u32[]{:S(2)}) collective-permute-start(bf16[768,128]{1,0:T(8,128)(2,1)S(1)} %add_convert_fusion.rest_0_), channel_id=1, source_target_pairs={{0,2},{1,3},{2,0},{3,1},{4,6},{5,7},{6,4},{7,5},{8,10},{9,11},{10,... | collective-permute-start | bytes 589832 | tf_op jit(solution)/shard_map/ppermute | solution.py:23
  12.3 7.9 %collective-permute-start.3 = (bf16[560,128]{1,0:T(8,128)(2,1)S(1)}, bf16[560,128]{1,0:T(8,128)(2,1)S(1)}, u32[]{:S(2)}, u32[]{:S(2)}) collective-permute-start(bf16[560,128]{1,0:T(8,128)(2,1)S(1)} %get-tuple-element.45.own_ref), channel_id=1, source_target_pairs={{0,2},{1,3},{2,0},{3,1},{4,6},{5,7},{6,4},{7,5},{8,10},{9,11},{10,... | collective-permute-start | bytes 430088 | tf_op jit(solution)/shard_map/ppermute | solution.py:23
  12.5 16.5 %collective-permute-start.8 = (f32[512,128]{1,0:T(8,128)S(1)}, f32[512,128]{1,0:T(8,128)S(1)}, u32[]{:S(2)}, u32[]{:S(2)}) collective-permute-start(f32[512,128]{1,0:T(8,128)S(1)} %get-tuple-element.50.rest_ref), channel_id=1, source_target_pairs={{0,1},{1,0},{2,3},{3,2},{4,5},{5,4},{6,7},{7,6},{8,9},{9,8},{10,11... | collective-permute-start | bytes 786440 | tf_op jit(solution)/shard_map/ppermute | solution.py:23
  20.4 6.8 %collective-permute-start.5 = (bf16[432,128]{1,0:T(8,128)(2,1)S(1)}, bf16[432,128]{1,0:T(8,128)(2,1)S(1)}, u32[]{:S(2)}, u32[]{:S(2)}) collective-permute-start(bf16[432,128]{1,0:T(8,128)(2,1)S(1)} %get-tuple-element.47.own_ref), channel_id=1, source_target_pairs={{0,4},{1,5},{2,6},{3,7},{4,0},{5,1},{6,2},{7,3},{8,12},{9,13},{10,... | collective-permute-start | bytes 331784 | tf_op jit(solution)/shard_map/ppermute | solution.py:23
  22.2 4.9 %collective-permute-start.6 = (bf16[384,128]{1,0:T(8,128)(2,1)S(1)}, bf16[384,128]{1,0:T(8,128)(2,1)S(1)}, u32[]{:S(2)}, u32[]{:S(2)}) collective-permute-start(bf16[384,128]{1,0:T(8,128)(2,1)S(1)} %add_convert_fusion.1.rest_0_), channel_id=1, source_target_pairs={{0,4},{1,5},{2,6},{3,7},{4,0},{5,1},{6,2},{7,3},{8,12},{9,13},{10,... | collective-permute-start | bytes 294920 | tf_op jit(solution)/shard_map/ppermute | solution.py:23
  27.3 4.8 %collective-permute-start.7 = (bf16[432,128]{1,0:T(8,128)(2,1)S(1)}, bf16[432,128]{1,0:T(8,128)(2,1)S(1)}, u32[]{:S(2)}, u32[]{:S(2)}) collective-permute-start(bf16[432,128]{1,0:T(8,128)(2,1)S(1)} %get-tuple-element.48.own_ref), channel_id=1, source_target_pairs={{0,8},{1,9},{2,10},{3,11},{4,12},{5,13},{6,14},{7,15},{8,0},{9,1},... | collective-permute-start | bytes 331784 | tf_op jit(solution)/shard_map/ppermute | solution.py:23
  32.3 5.0 %collective-permute-start.10 = (bf16[176,128]{1,0:T(8,128)(2,1)S(1)}, bf16[176,128]{1,0:T(8,128)(2,1)S(1)}, u32[]{:S(2)}, u32[]{:S(2)}) collective-permute-start(bf16[176,128]{1,0:T(8,128)(2,1)S(1)} %merge3.1.own_ref), channel_id=1, source_target_pairs={{0,16},{1,17},{2,18},{3,19},{4,20},{5,21},{6,22},{7,23},{8,24},{9,... | collective-permute-start | bytes 135176 | tf_op jit(solution)/shard_map/ppermute | solution.py:23
  35.0 5.7 %collective-permute-start.15 = (bf16[128,128]{1,0:T(8,128)(2,1)S(1)}, bf16[128,128]{1,0:T(8,128)(2,1)S(1)}, u32[]{:S(2)}, u32[]{:S(2)}) collective-permute-start(bf16[128,128]{1,0:T(8,128)(2,1)S(1)} %slice.99.last_ref), channel_id=1, source_target_pairs={{0,1},{1,0},{2,3},{3,2},{4,5},{5,4},{6,7},{7,6},{8,9},{9,8},{10,11... | collective-permute-start | bytes 98312 | tf_op jit(solution)/shard_map/ppermute | solution.py:23
  35.0 7.0 %collective-permute-start.14 = (bf16[128,128]{1,0:T(8,128)(2,1)S(1)}, bf16[128,128]{1,0:T(8,128)(2,1)S(1)}, u32[]{:S(2)}, u32[]{:S(2)}) collective-permute-start(bf16[128,128]{1,0:T(8,128)(2,1)S(1)} %slice.79.refs_1_), channel_id=1, source_target_pairs={{0,1},{1,0},{2,3},{3,2},{4,5},{5,4},{6,7},{7,6},{8,9},{9,8},{10,11... | collective-permute-start | bytes 98312 | tf_op jit(solution)/shard_map/ppermute | solution.py:23
  35.5 8.1 %collective-permute-start.13 = (bf16[128,128]{1,0:T(8,128)(2,1)S(1)}, bf16[128,128]{1,0:T(8,128)(2,1)S(1)}, u32[]{:S(2)}, u32[]{:S(2)}) collective-permute-start(bf16[128,128]{1,0:T(8,128)(2,1)S(1)} %slice.78.refs_0_), channel_id=1, source_target_pairs={{0,1},{1,0},{2,3},{3,2},{4,5},{5,4},{6,7},{7,6},{8,9},{9,8},{10,11... | collective-permute-start | bytes 98312 | tf_op jit(solution)/shard_map/ppermute | solution.py:23
  40.1 3.5 %collective-permute-start.11 = (bf16[128,128]{1,0:T(8,128)(2,1)S(1)}, bf16[128,128]{1,0:T(8,128)(2,1)S(1)}, u32[]{:S(2)}, u32[]{:S(2)}) collective-permute-start(bf16[128,128]{1,0:T(8,128)(2,1)S(1)} %slice.82), channel_id=1, source_target_pairs={{0,1},{1,0},{2,3},{3,2},{4,5},{5,4},{6,7},{7,6},{8,9},{9,8},{10,11... | collective-permute-start | bytes 98312 | tf_op jit(solution)/shard_map/ppermute | solution.py:23
  40.3 3.3 %collective-permute-start.12 = (bf16[128,128]{1,0:T(8,128)(2,1)S(1)}, bf16[128,128]{1,0:T(8,128)(2,1)S(1)}, u32[]{:S(2)}, u32[]{:S(2)}) collective-permute-start(bf16[128,128]{1,0:T(8,128)(2,1)S(1)} %slice.81.share_ref), channel_id=1, source_target_pairs={{0,1},{1,0},{2,3},{3,2},{4,5},{5,4},{6,7},{7,6},{8,9},{9,8},{10,11... | collective-permute-start | bytes 98312 | tf_op jit(solution)/shard_map/ppermute | solution.py:23
  40.6 8.4 %collective-permute-start.17 = (bf16[512,128]{1,0:T(8,128)(2,1)S(1)}, bf16[512,128]{1,0:T(8,128)(2,1)S(1)}, u32[]{:S(2)}, u32[]{:S(2)}) collective-permute-start(bf16[512,128]{1,0:T(8,128)(2,1)S(1)} %weigh2.1), channel_id=1, source_target_pairs={{0,4},{1,5},{2,6},{3,7},{4,0},{5,1},{6,2},{7,3},{8,12},{9,13},{10,... | collective-permute-start | bytes 393224 | tf_op jit(solution)/shard_map/ppermute | solution.py:23
  42.0 7.1 %collective-permute-start.16 = (bf16[512,128]{1,0:T(8,128)(2,1)S(1)}, bf16[512,128]{1,0:T(8,128)(2,1)S(1)}, u32[]{:S(2)}, u32[]{:S(2)}) collective-permute-start(bf16[512,128]{1,0:T(8,128)(2,1)S(1)} %weigh3.1), channel_id=1, source_target_pairs={{0,6},{1,7},{2,4},{3,5},{4,2},{5,3},{6,0},{7,1},{8,14},{9,15},{10,... | collective-permute-start | bytes 393224 | tf_op jit(solution)/shard_map/ppermute | solution.py:23
  44.8 5.5 %collective-permute-start.18 = (bf16[512,128]{1,0:T(8,128)(2,1)S(1)}, bf16[512,128]{1,0:T(8,128)(2,1)S(1)}, u32[]{:S(2)}, u32[]{:S(2)}) collective-permute-start(bf16[512,128]{1,0:T(8,128)(2,1)S(1)} %weigh1.1), channel_id=1, source_target_pairs={{0,2},{1,3},{2,0},{3,1},{4,6},{5,7},{6,4},{7,5},{8,10},{9,11},{10,... | collective-permute-start | bytes 393224 | tf_op jit(solution)/shard_map/ppermute | solution.py:23
  46.5 13.9 %copy-start.5 = (bf16[64,256]{1,0:T(8,128)(2,1)S(1)}, bf16[64,256]{1,0:T(8,128)(2,1)}, u32[]{:S(2)}) copy-start(bf16[64,256]{1,0:T(8,128)(2,1)} %param.15) | copy-start | bytes 98308
  50.4 5.9 %collective-permute-start.21 = (bf16[128,128]{1,0:T(8,128)(2,1)S(1)}, bf16[128,128]{1,0:T(8,128)(2,1)S(1)}, u32[]{:S(2)}, u32[]{:S(2)}) collective-permute-start(bf16[128,128]{1,0:T(8,128)(2,1)S(1)} %get-tuple-element.89), channel_id=1, source_target_pairs={{0,24},{1,25},{2,26},{3,27},{4,28},{5,29},{6,30},{7,31},{8,16},{9,... | collective-permute-start | bytes 98312 | tf_op jit(solution)/shard_map/ppermute | solution.py:23
  54.3 4.8 %collective-permute-start.20 = (bf16[128,128]{1,0:T(8,128)(2,1)S(1)}, bf16[128,128]{1,0:T(8,128)(2,1)S(1)}, u32[]{:S(2)}, u32[]{:S(2)}) collective-permute-start(bf16[128,128]{1,0:T(8,128)(2,1)S(1)} %get-tuple-element.90), channel_id=1, source_target_pairs={{0,16},{1,17},{2,18},{3,19},{4,20},{5,21},{6,22},{7,23},{8,24},{9,... | collective-permute-start | bytes 98312 | tf_op jit(solution)/shard_map/ppermute | solution.py:23
  54.3 4.8 %collective-permute-start.19 = (bf16[128,128]{1,0:T(8,128)(2,1)S(1)}, bf16[128,128]{1,0:T(8,128)(2,1)S(1)}, u32[]{:S(2)}, u32[]{:S(2)}) collective-permute-start(bf16[128,128]{1,0:T(8,128)(2,1)S(1)} %get-tuple-element.88), channel_id=1, source_target_pairs={{0,8},{1,9},{2,10},{3,11},{4,12},{5,13},{6,14},{7,15},{8,0},{9,1},... | collective-permute-start | bytes 98312 | tf_op jit(solution)/shard_map/ppermute | solution.py:23
  59.1 1.3 %collective-permute-start.22 = (f32[64,128]{1,0:T(8,128)S(1)}, f32[64,128]{1,0:T(8,128)S(1)}, u32[]{:S(2)}, u32[]{:S(2)}) collective-permute-start(f32[64,128]{1,0:T(8,128)S(1)} %get-tuple-element.92), channel_id=1, source_target_pairs={{0,1},{1,0},{2,3},{3,2},{4,5},{5,4},{6,7},{7,6},{8,9},{9,8},{10,11... | collective-permute-start | bytes 98312 | tf_op jit(solution)/shard_map/ppermute | solution.py:23

commit v7 on v6

--- a/solution.py
+++ b/solution.py
@@ -250,6 +250,15 @@
     half = 2 * near * tile
     out_ref[:half, :] = dot(near_ref[...], coeff_ref[...]).astype(out_ref.dtype)
     out_ref[half:, :] = dot(weight_ref[...], coeff_ref[...]).astype(out_ref.dtype)
+
+
+def first_kernel(rank, n, depth, scale, masks, shape, info_ref, point_ref, *refs):
+    count = len(masks)
+    inputs, near_refs, outs = refs[:6], refs[6 : 6 + count], refs[6 + count :]
+    final_ref, coeff_ref, spot_ref = outs[:3]
+    coeff_kernel(rank, n, depth, scale, *inputs, final_ref, coeff_ref, spot_ref)
+    for k, mask in enumerate(masks):
+        far_kernel(mask, *shape, info_ref, spot_ref, near_refs[k], point_ref, coeff_ref, outs[3 + k], outs[-1])
 
 
 def solved_kernel(core_ref, mine_ref, rest_ref, left_ref, *refs):
@@ -421,17 +430,26 @@
         room=8 if near <= 4 else 24,
         ins=[SMEM, VMEM, VMEM],
     )(info, message, points)
-    final_mine, coeffs, spots = call(
-        functools.partial(coeff_kernel, rank, chips, depth, 2.0 * leaf),
-        [out((rows, half), f32), out((2 * rows, half), bf16), out((2 * tile, chips), f32)],
-        "coeffs",
-        4 * rows * rank * half,
-        16 * rows * half,
-    )(part_mine, part_other, left16, left_other, shares[1], arrived)
+    early_masks = (3, 2)
+    shape = plane, near, tile, leaf, blocks, devices
+    final_mine, coeffs, spots, *partials = call(
+        functools.partial(first_kernel, rank, chips, depth, 2.0 * leaf, early_masks, shape),
+        [out((rows, half), f32), out((2 * rows, half), bf16), out((2 * tile, chips), f32)]
+        + [out((4 * near * tile, half), bf16)] * len(early_masks),
+        "first",
+        64 * near * tile * rows * half,
+        64 * near * tile * half,
+        room=10 if near <= 4 else 24,
+        ins=[SMEM] + [VMEM] * (7 + len(early_masks)),
+        scratch=[pltpu.VMEM((2 * near * tile, 2 * rows), bf16)],
+    )(
+        info, points, part_mine, part_other, left16, left_other, shares[1], arrived,
+        *[near_weights[mask] for mask in early_masks],
+    )
 
     def weighed(mask, coeffs):
         return call(
-            functools.partial(far_kernel, mask, plane, near, tile, leaf, blocks, devices),
+            functools.partial(far_kernel, mask, *shape),
             out((4 * near * tile, half), bf16 if mask else f32),
             f"weigh{mask}",
             32 * near * tile * rows * half,
@@ -441,16 +459,11 @@
             scratch=[pltpu.VMEM((2 * near * tile, 2 * rows), bf16)],
         )(info, spots, near_weights[mask], points, coeffs)
 
-    sent = []
-    for mask in (3, 2, 1):
-        if mask == 1:
-            coeffs, others = lax.optimization_barrier((coeffs, others))
-        partial = weighed(mask, coeffs)
-        coeffs, partial = lax.optimization_barrier((coeffs, partial))
-        if mask == 2:
-            share0, share1, _ = lax.optimization_barrier((shares[0], shares[1], coeffs))
-            others[:2] = swapped(share0, 1), swapped(share1, 1)
-        sent.append(swapped(partial, mask << 1))
+    sent = [swapped(partial, mask << 1) for mask, partial in zip(early_masks, partials)]
+    share0, share1, _ = lax.optimization_barrier((shares[0], shares[1], coeffs))
+    others[:2] = swapped(share0, 1), swapped(share1, 1)
+    coeffs, others = lax.optimization_barrier((coeffs, others))
+    sent.append(swapped(weighed(1, coeffs), 1 << 1))
     solved_out = call(
         solved_kernel,
         out((rows, samples), f32),
@@ -466,7 +479,7 @@
     far = 2 * near
     total = total.reshape(far, 2 * tile, half)
     result = total[0]
-    for mask in range(1, far):
+    for mask in reversed(range(1, far)):
         result = result + swapped(total[mask].astype(bf16), mask << 3).astype(f32)
     rest = swapped(result[tile:], 1)
 

time: 61.3 us -> 60.3 us (0.984)
  Pallas kernels: 15.8 us -> 15 us
    pallas_call x5 -> x3, Pallas kernels: 5.06 us -> 4.31 us  [the longest x2 2.36 us: weighed(): call(functools.partial(far_kernel, mask, *shape), out((4 * near * tile, h...]
  transfers between devices with their start and end apart: 23 -> 23, of which waited for: 9 -> 8; matrix products, arithmetic and copies ran while one was open for 2% -> 2% of each run, Pallas kernels for 21% -> 20%
where the time goes in v7:
time: 60.3 us; the launch traced here: 60 us
  waiting for transfers between devices  21.8 us (36%)
  starting transfers between devices  20.2 us (33%)
  Pallas kernels  15 us (25%)
  local copies, waits for them, and re-layouts  1.22 us (2%)
  between operations  0.9 us (1%)
  other arithmetic  0.89 us (1%)
    ppermute x23, waiting for transfers between devices, swapped(): return lax.ppermute(value, 'pts', pairs)  21.8 us
    ppermute x23, starting transfers between devices, swapped(): return lax.ppermute(value, 'pts', pairs)  20.2 us
    pallas_call x1, Pallas kernels, body(): call(functools.partial(front_kernel, rows, leaf, bits, rank, inner, sizes...  4.1 us
    pallas_call x1, Pallas kernels, body(): call(functools.partial(small_kernel, bits, rank), out((pair_count * rank,...  2.62 us
    pallas_call x2, Pallas kernels, weighed(): call(functools.partial(far_kernel, mask, *shape), out((4 * near * tile, h...  2.36 us
    pallas_call x1, Pallas kernels, body(): call(functools.partial(first_kernel, rank, chips, depth, 2.0 * leaf, earl...  1.95 us
    pallas_call x1, Pallas kernels, body(): call(functools.partial(near_kernel, plane, near, tile, leaf, blocks, devi...  1.51 us
  transfers between devices with their start and end apart: 23, of which 8 were waited for; matrix products, arithmetic and copies ran while one was open for 2% of the time, Pallas kernels for 20%

profile of v7, /device:TPU:0, one launch (start us, length us, event | category | flops | bytes accessed | tf_op | source)
XLA Modules:
  0.0 60.0 jit_solution(16943943057256264063)
XLA Ops:
  0.6 2.6 %small.1.small_ref = bf16[1280,128]{1,0:T(8,128)(2,1)S(1)} custom-call(f32[7,512,128]{2,1,0:T(8,128)} %right_ref.3, f32[7,512,128]{2,1,0:T(8,128)} %left_ref.5), custom_call_target="tpu_custom_call" | custom-call | flops 167772160 | bytes 2621440 | tf_op jit(solution)/shard_map/small/pallas_call | solution.py:301
  3.3 0.5 collective-permute-start.1
  3.8 4.1 %front.1 = (f32[512,128]{1,0:T(8,128)S(1)}, f32[512,128]{1,0:T(8,128)S(1)}, f32[640,128]{1,0:T(8,128)S(1)}, bf16[640,128]{1,0:T(8,128)(2,1)S(1)}) custom-call(s32[1]{0:T(128)} %bitcast.core_ref, bf16[512,256]{1,0:T(8,128)(2,1)S(1)} %copy-done.1, bf16[512,128]{1,0:T(8,128)(2,1)S(1)} %copy-done.2, f32[7,512,128]{2,1,0:T(8,128)} %right_ref.3, ...), custom_call_target="tpu_custom_call" | custom-call | flops 503316480 | bytes 3670016 | tf_op jit(solution)/shard_map/front/pallas_call | solution.py:317
  7.9 0.0 copy-start.3
  7.9 0.0 copy-start.4
  7.9 0.1 collective-permute-start
  8.1 0.5 collective-permute-start.2
  8.5 0.2 left16.1.left_ref.refs_2_
  8.8 0.2 collective-permute-start.9
  8.9 0.0 collective-permute-done.1.their_ref
  8.9 0.1 add_convert_fusion.rest_0_
  9.0 3.0 %collective-permute-start.4 = (bf16[768,128]{1,0:T(8,128)(2,1)S(1)}, bf16[768,128]{1,0:T(8,128)(2,1)S(1)}, u32[]{:S(2)}, u32[]{:S(2)}) collective-permute-start(bf16[768,128]{1,0:T(8,128)(2,1)S(1)} %add_convert_fusion.rest_0_), channel_id=1, source_target_pairs={{0,2},{1,3},{2,0},{3,1},{4,6},{5,7},{6,4},{7,5},{8,10},{9,11},{10,... | collective-permute-start | bytes 589832 | tf_op jit(solution)/shard_map/ppermute | solution.py:23
  12.0 0.0 collective-permute-done.2
  12.0 0.1 maximum_bitcast_fusion.spot_ref
  12.0 0.2 merge0.1
  12.3 0.2 collective-permute-start.3
  12.5 0.2 dynamic-slice_reduce_fusion
  12.8 0.1 concatenate.16.info_ref
  12.8 7.3 %collective-permute-done.3.got_ref = bf16[560,128]{1,0:T(8,128)(2,1)S(1)} collective-permute-done((bf16[560,128]{1,0:T(8,128)(2,1)S(1)}, bf16[560,128]{1,0:T(8,128)(2,1)S(1)}, u32[]{:S(2)}, u32[]{:S(2)}) %collective-permute-start.3) | collective-permute-done | bytes 143392 | tf_op jit(solution)/shard_map/ppermute | solution.py:23
  20.2 0.0 collective-permute-done.4.rest_1_
  20.2 0.2 merge1.1
  20.4 1.8 %collective-permute-start.5 = (bf16[432,128]{1,0:T(8,128)(2,1)S(1)}, bf16[432,128]{1,0:T(8,128)(2,1)S(1)}, u32[]{:S(2)}, u32[]{:S(2)}) collective-permute-start(bf16[432,128]{1,0:T(8,128)(2,1)S(1)} %get-tuple-element.43.own_ref), channel_id=1, source_target_pairs={{0,4},{1,5},{2,6},{3,7},{4,0},{5,1},{6,2},{7,3},{8,12},{9,13},{10,... | collective-permute-start | bytes 331784 | tf_op jit(solution)/shard_map/ppermute | solution.py:23
  22.2 0.3 collective-permute-start.6
  22.6 0.8 %dynamic-slice_bitcast_fusion.1 = (f32[4,128]{1,0:T(4,128)S(1)}, f32[4,128]{1,0:T(4,128)S(1)}) fusion(f32[16384]{0:T(1024)} %param.13, s32[]{:T(128)S(6)} %select_n.33, s32[]{:T(128)S(6)} %select_n.34), kind=kLoop, calls=%fused_computation.15 | loop fusion | bytes 8200 | tf_op jit(solution)/shard_map/reshape | solution.py:381
  23.4 3.7 %collective-permute-done.6.rest_1_ = bf16[384,128]{1,0:T(8,128)(2,1)S(1)} collective-permute-done((bf16[384,128]{1,0:T(8,128)(2,1)S(1)}, bf16[384,128]{1,0:T(8,128)(2,1)S(1)}, u32[]{:S(2)}, u32[]{:S(2)}) %collective-permute-start.6) | collective-permute-done | bytes 98336 | tf_op jit(solution)/shard_map/ppermute | solution.py:23
  27.2 0.0 collective-permute-done.5.got_ref
  27.2 0.2 merge2.1
  27.3 1.6 %collective-permute-start.7 = (bf16[432,128]{1,0:T(8,128)(2,1)S(1)}, bf16[432,128]{1,0:T(8,128)(2,1)S(1)}, u32[]{:S(2)}, u32[]{:S(2)}) collective-permute-start(bf16[432,128]{1,0:T(8,128)(2,1)S(1)} %get-tuple-element.44.own_ref), channel_id=1, source_target_pairs={{0,8},{1,9},{2,10},{3,11},{4,12},{5,13},{6,14},{7,15},{8,0},{9,1},... | collective-permute-start | bytes 331784 | tf_op jit(solution)/shard_map/ppermute | solution.py:23
  29.0 0.0 collective-permute-done.8.other_ref
  29.1 0.4 partial.1
  29.4 2.7 %collective-permute-done.7.got_ref = bf16[432,128]{1,0:T(8,128)(2,1)S(1)} collective-permute-done((bf16[432,128]{1,0:T(8,128)(2,1)S(1)}, bf16[432,128]{1,0:T(8,128)(2,1)S(1)}, u32[]{:S(2)}, u32[]{:S(2)}) %collective-permute-start.7) | collective-permute-done | bytes 110624 | tf_op jit(solution)/shard_map/ppermute | solution.py:23
  32.2 0.2 merge3.1.own_ref
  32.3 2.7 %collective-permute-start.10 = (bf16[176,128]{1,0:T(8,128)(2,1)S(1)}, bf16[176,128]{1,0:T(8,128)(2,1)S(1)}, u32[]{:S(2)}, u32[]{:S(2)}) collective-permute-start(bf16[176,128]{1,0:T(8,128)(2,1)S(1)} %merge3.1.own_ref), channel_id=1, source_target_pairs={{0,16},{1,17},{2,18},{3,19},{4,20},{5,21},{6,22},{7,23},{8,24},{9,... | collective-permute-start | bytes 135176 | tf_op jit(solution)/shard_map/ppermute | solution.py:23
  35.0 0.0 collective-permute-start.15
  35.0 0.5 collective-permute-start.14
  35.5 0.0 collective-permute-start.13
  35.5 1.5 %near.1 = (bf16[256,1024]{1,0:T(8,128)(2,1)S(1)}, bf16[256,1024]{1,0:T(8,128)(2,1)S(1)}, bf16[256,1024]{1,0:T(8,128)(2,1)S(1)}, bf16[256,1024]{1,0:T(8,128)(2,1)S(1)}) custom-call(s32[129]{0:T(256)S(1)} %concatenate.16.info_ref, bf16[176,128]{1,0:T(8,128)(2,1)S(1)} %merge3.1.own_ref, f32[8,128]{1,0:T(8,128)S(1)} %pad_maximum_fusion.point_ref), custom_call_target="tpu_custom_call" | custom-call | flops 10485760 | bytes 2097152 | tf_op jit(solution)/shard_map/near/pallas_call | solution.py:424
  37.0 0.3 collective-permute-done.10.refs_5_
  37.3 1.9 %first.1 = (f32[512,128]{1,0:T(8,128)S(1)}, bf16[1024,128]{1,0:T(8,128)(2,1)S(1)}, f32[128,8]{1,0:T(8,128)S(1)}, bf16[512,128]{1,0:T(8,128)(2,1)S(1)}, bf16[512,128]{1,0:T(8,128)(2,1)S(1)}) custom-call(s32[129]{0:T(256)S(1)} %concatenate.16.info_ref, f32[8,128]{1,0:T(8,128)S(1)} %pad_maximum_fusion.point_ref, f32[512,128]{1,0:T(8,128)S(1)} %get-tuple-element.51.refs_0_, ...), custom_call_target="tpu_custom_call" | custom-call | flops 536870912 | bytes 1048576 | tf_op jit(solution)/shard_map/first/pallas_call | solution.py:435
  39.3 0.3 collective-permute-start.11
  39.6 0.3 collective-permute-start.12
  39.9 0.0 collective-permute-done.15.refs_4_
  39.9 2.3 %collective-permute-start.16 = (bf16[512,128]{1,0:T(8,128)(2,1)S(1)}, bf16[512,128]{1,0:T(8,128)(2,1)S(1)}, u32[]{:S(2)}, u32[]{:S(2)}) collective-permute-start(bf16[512,128]{1,0:T(8,128)(2,1)S(1)} %get-tuple-element.71), channel_id=1, source_target_pairs={{0,6},{1,7},{2,4},{3,5},{4,2},{5,3},{6,0},{7,1},{8,14},{9,15},{10,... | collective-permute-start | bytes 393224 | tf_op jit(solution)/shard_map/ppermute | solution.py:23
  42.2 0.0 collective-permute-done.14.refs_3_
  42.2 0.7 %collective-permute-start.17 = (bf16[512,128]{1,0:T(8,128)(2,1)S(1)}, bf16[512,128]{1,0:T(8,128)(2,1)S(1)}, u32[]{:S(2)}, u32[]{:S(2)}) collective-permute-start(bf16[512,128]{1,0:T(8,128)(2,1)S(1)} %get-tuple-element.72), channel_id=1, source_target_pairs={{0,4},{1,5},{2,6},{3,7},{4,0},{5,1},{6,2},{7,3},{8,12},{9,13},{10,... | collective-permute-start | bytes 393224 | tf_op jit(solution)/shard_map/ppermute | solution.py:23
  42.8 0.0 collective-permute-done.11.refs_0_
  42.9 0.0 collective-permute-done.12.refs_1_
  42.9 1.2 %weigh1.1 = bf16[512,128]{1,0:T(8,128)(2,1)S(1)} custom-call(s32[129]{0:T(256)S(1)} %concatenate.16.info_ref, f32[128,8]{1,0:T(8,128)S(1)} %get-tuple-element.68.spot_ref, bf16[256,1024]{1,0:T(8,128)(2,1)S(1)} %get-tuple-element.73.near_ref, f32[8,128]{1,0:T(8,128)S(1)} %pad_maximum_fusion.point_ref, bf16[1024,128]{1,0:T(8,128)(2,1)S(1)} %get-tuple-element.70.coeff_ref), custom_call_target="tpu_custom_call" | custom-call | flops 268435456 | bytes 524288 | tf_op jit(solution)/shard_map/weigh1/pallas_call | solution.py:451
  44.1 0.6 collective-permute-start.18
  44.7 1.1 %solved.1 = f32[512,256]{1,0:T(8,128)} custom-call(s32[1]{0:T(128)} %bitcast.core_ref, f32[512,128]{1,0:T(8,128)S(1)} %get-tuple-element.61.mine_ref, f32[512,128]{1,0:T(8,128)S(1)} %get-tuple-element.46.rest_ref, bf16[512,640]{1,0:T(8,128)(2,1)S(1)} %left16.1.left_ref.refs_2_, bf16[128,128]{1,0:T(8,128)(2,1)S(1)} %collective-permute-done.11.refs_0_, ...), custom_call_target="tpu_custom_call" | custom-call | flops 83886080 | bytes 2097152 | tf_op jit(solution)/shard_map/solved/pallas_call | solution.py:467
  45.8 1.2 %weigh0.1 = f32[512,128]{1,0:T(8,128)S(1)} custom-call(s32[129]{0:T(256)S(1)} %concatenate.16.info_ref, f32[128,8]{1,0:T(8,128)S(1)} %get-tuple-element.68.spot_ref, bf16[256,1024]{1,0:T(8,128)(2,1)S(1)} %get-tuple-element.69.near_ref, f32[8,128]{1,0:T(8,128)S(1)} %pad_maximum_fusion.point_ref, bf16[1024,128]{1,0:T(8,128)(2,1)S(1)} %get-tuple-element.70.coeff_ref), custom_call_target="tpu_custom_call" | custom-call | flops 268435456 | bytes 524288 | tf_op jit(solution)/shard_map/weigh0/pallas_call | solution.py:451
  47.0 0.0 collective-permute-done.16
  47.0 2.2 %collective-permute-done.17 = bf16[512,128]{1,0:T(8,128)(2,1)S(1)} collective-permute-done((bf16[512,128]{1,0:T(8,128)(2,1)S(1)}, bf16[512,128]{1,0:T(8,128)(2,1)S(1)}, u32[]{:S(2)}, u32[]{:S(2)}) %collective-permute-start.17) | collective-permute-done | bytes 131104 | tf_op jit(solution)/shard_map/ppermute | solution.py:23
  49.2 0.0 collective-permute-done.18
  49.2 0.1 fusion.3
  49.3 3.9 %collective-permute-start.19 = (bf16[128,128]{1,0:T(8,128)(2,1)S(1)}, bf16[128,128]{1,0:T(8,128)(2,1)S(1)}, u32[]{:S(2)}, u32[]{:S(2)}) collective-permute-start(bf16[128,128]{1,0:T(8,128)(2,1)S(1)} %get-tuple-element.80), channel_id=1, source_target_pairs={{0,24},{1,25},{2,26},{3,27},{4,28},{5,29},{6,30},{7,31},{8,16},{9,... | collective-permute-start | bytes 98312 | tf_op jit(solution)/shard_map/ppermute | solution.py:23
  53.3 0.0 collective-permute-start.20
  53.3 0.6 %collective-permute-start.21 = (bf16[128,128]{1,0:T(8,128)(2,1)S(1)}, bf16[128,128]{1,0:T(8,128)(2,1)S(1)}, u32[]{:S(2)}, u32[]{:S(2)}) collective-permute-start(bf16[128,128]{1,0:T(8,128)(2,1)S(1)} %get-tuple-element.81), channel_id=1, source_target_pairs={{0,8},{1,9},{2,10},{3,11},{4,12},{5,13},{6,14},{7,15},{8,0},{9,1},... | collective-permute-start | bytes 98312 | tf_op jit(solution)/shard_map/ppermute | solution.py:23
  53.9 1.3 %collective-permute-done.19 = bf16[128,128]{1,0:T(8,128)(2,1)S(1)} collective-permute-done((bf16[128,128]{1,0:T(8,128)(2,1)S(1)}, bf16[128,128]{1,0:T(8,128)(2,1)S(1)}, u32[]{:S(2)}, u32[]{:S(2)}) %collective-permute-start.19) | collective-permute-done | bytes 32800 | tf_op jit(solution)/shard_map/ppermute | solution.py:23
  55.2 2.9 %collective-permute-done.20 = bf16[128,128]{1,0:T(8,128)(2,1)S(1)} collective-permute-done((bf16[128,128]{1,0:T(8,128)(2,1)S(1)}, bf16[128,128]{1,0:T(8,128)(2,1)S(1)}, u32[]{:S(2)}, u32[]{:S(2)}) %collective-permute-start.20) | collective-permute-done | bytes 32800 | tf_op jit(solution)/shard_map/ppermute | solution.py:23
  58.1 0.0 collective-permute-done.21
  58.1 0.1 collective-permute-start.22
  58.2 1.2 %collective-permute-done.22 = f32[64,128]{1,0:T(8,128)S(1)} collective-permute-done((f32[64,128]{1,0:T(8,128)S(1)}, f32[64,128]{1,0:T(8,128)S(1)}, u32[]{:S(2)}, u32[]{:S(2)}) %collective-permute-start.22) | collective-permute-done | bytes 32800 | tf_op jit(solution)/shard_map/ppermute | solution.py:23
  59.4 0.6 %fusion.2 = f32[64,256]{1,0:T(8,128)} fusion(f32[64,128]{1,0:T(8,128)S(1)} %collective-permute-done.22, f32[64,128]{1,0:T(8,128)S(1)} %get-tuple-element.83, bf16[64,256]{1,0:T(8,128)(2,1)S(1)} %copy-done.5, pred[]{:T(512)S(6)} %eq.5), kind=kLoop, calls=%fused_computation.8 | loop fusion | flops 81920 | bytes 163841 | tf_op jit(solution)/shard_map/add | solution.py:491
  (27 shorter events, 0.1 us)
Async XLA Ops:
  0.6 3.2 %copy-start.2 = (bf16[512,128]{1,0:T(8,128)(2,1)S(1)}, bf16[512,128]{1,0:T(8,128)(2,1)}, u32[]{:S(2)}) copy-start(bf16[512,128]{1,0:T(8,128)(2,1)} %inverse_ref.1) | copy-start | bytes 393220
  0.6 3.2 %copy-start.1 = (bf16[512,256]{1,0:T(8,128)(2,1)S(1)}, bf16[512,256]{1,0:T(8,128)(2,1)}, u32[]{:S(2)}) copy-start(bf16[512,256]{1,0:T(8,128)(2,1)} %residual_ref.1) | copy-start | bytes 786436
  3.3 5.6 %collective-permute-start.1 = (bf16[1280,128]{1,0:T(8,128)(2,1)S(1)}, bf16[1280,128]{1,0:T(8,128)(2,1)S(1)}, u32[]{:S(2)}, u32[]{:S(2)}) collective-permute-start(bf16[1280,128]{1,0:T(8,128)(2,1)S(1)} %small.1.small_ref), channel_id=1, source_target_pairs={{0,1},{1,0},{2,3},{3,2},{4,5},{5,4},{6,7},{7,6},{8,9},{9,8},{10,11... | collective-permute-start | bytes 983048 | tf_op jit(solution)/shard_map/ppermute | solution.py:23
  3.8 4.3 %copy-start.6 = (f32[64]{0:T(128)S(1)}, f32[64]{0:T(128)}, u32[]{:S(2)}) copy-start(f32[64]{0:T(128)} %param.14) | copy-start | bytes 772
  3.8 4.7 %copy-start = (f32[7,512,128]{2,1,0:T(8,128)S(1)}, f32[7,512,128]{2,1,0:T(8,128)}, u32[]{:S(2)}) copy-start(f32[7,512,128]{2,1,0:T(8,128)} %left_ref.5) | copy-start | bytes 5505028
  7.9 4.6 %copy-start.3 = (s32[32,32]{1,0:T(8,128)S(1)}, s32[32,32]{1,0:T(8,128)}, u32[]{:S(2)}) copy-start(s32[32,32]{1,0:T(8,128)} %param.17) | copy-start | bytes 12292
  7.9 4.6 %copy-start.4 = (s32[32,32]{1,0:T(8,128)S(1)}, s32[32,32]{1,0:T(8,128)}, u32[]{:S(2)}) copy-start(s32[32,32]{1,0:T(8,128)} %param.16) | copy-start | bytes 12292
  7.9 4.1 %collective-permute-start = (bf16[640,128]{1,0:T(8,128)(2,1)S(1)}, bf16[640,128]{1,0:T(8,128)(2,1)S(1)}, u32[]{:S(2)}, u32[]{:S(2)}) collective-permute-start(bf16[640,128]{1,0:T(8,128)(2,1)S(1)} %get-tuple-element.39), channel_id=1, source_target_pairs={{0,1},{1,0},{2,3},{3,2},{4,5},{5,4},{6,7},{7,6},{8,9},{9,8},{10,11... | collective-permute-start | bytes 491528 | tf_op jit(solution)/shard_map/ppermute | solution.py:23
  8.1 3.9 %collective-permute-start.2 = (f32[64]{0:T(128)S(1)}, f32[64]{0:T(128)S(1)}, u32[]{:S(2)}, u32[]{:S(2)}) collective-permute-start(f32[64]{0:T(128)S(1)} %copy-done.6), channel_id=1, source_target_pairs={{0,1},{1,0},{2,3},{3,2},{4,5},{5,4},{6,7},{7,6},{8,9},{9,8},{10,11... | collective-permute-start | bytes 776 | tf_op jit(solution)/shard_map/ppermute | solution.py:23
  8.8 20.3 %collective-permute-start.9 = (bf16[512,640]{1,0:T(8,128)(2,1)S(1)}, bf16[512,640]{1,0:T(8,128)(2,1)S(1)}, u32[]{:S(2)}, u32[]{:S(2)}) collective-permute-start(bf16[512,640]{1,0:T(8,128)(2,1)S(1)} %left16.1.left_ref.refs_2_), channel_id=1, source_target_pairs={{0,1},{1,0},{2,3},{3,2},{4,5},{5,4},{6,7},{7,6},{8,9},{9,8},{10,11... | collective-permute-start | bytes 1966088 | tf_op jit(solution)/shard_map/ppermute | solution.py:23
  9.0 11.2 %collective-permute-start.4 = (bf16[768,128]{1,0:T(8,128)(2,1)S(1)}, bf16[768,128]{1,0:T(8,128)(2,1)S(1)}, u32[]{:S(2)}, u32[]{:S(2)}) collective-permute-start(bf16[768,128]{1,0:T(8,128)(2,1)S(1)} %add_convert_fusion.rest_0_), channel_id=1, source_target_pairs={{0,2},{1,3},{2,0},{3,1},{4,6},{5,7},{6,4},{7,5},{8,10},{9,11},{10,... | collective-permute-start | bytes 589832 | tf_op jit(solution)/shard_map/ppermute | solution.py:23
  12.3 7.9 %collective-permute-start.3 = (bf16[560,128]{1,0:T(8,128)(2,1)S(1)}, bf16[560,128]{1,0:T(8,128)(2,1)S(1)}, u32[]{:S(2)}, u32[]{:S(2)}) collective-permute-start(bf16[560,128]{1,0:T(8,128)(2,1)S(1)} %get-tuple-element.41.own_ref), channel_id=1, source_target_pairs={{0,2},{1,3},{2,0},{3,1},{4,6},{5,7},{6,4},{7,5},{8,10},{9,11},{10,... | collective-permute-start | bytes 430088 | tf_op jit(solution)/shard_map/ppermute | solution.py:23
  12.5 16.5 %collective-permute-start.8 = (f32[512,128]{1,0:T(8,128)S(1)}, f32[512,128]{1,0:T(8,128)S(1)}, u32[]{:S(2)}, u32[]{:S(2)}) collective-permute-start(f32[512,128]{1,0:T(8,128)S(1)} %get-tuple-element.46.rest_ref), channel_id=1, source_target_pairs={{0,1},{1,0},{2,3},{3,2},{4,5},{5,4},{6,7},{7,6},{8,9},{9,8},{10,11... | collective-permute-start | bytes 786440 | tf_op jit(solution)/shard_map/ppermute | solution.py:23
  20.4 6.8 %collective-permute-start.5 = (bf16[432,128]{1,0:T(8,128)(2,1)S(1)}, bf16[432,128]{1,0:T(8,128)(2,1)S(1)}, u32[]{:S(2)}, u32[]{:S(2)}) collective-permute-start(bf16[432,128]{1,0:T(8,128)(2,1)S(1)} %get-tuple-element.43.own_ref), channel_id=1, source_target_pairs={{0,4},{1,5},{2,6},{3,7},{4,0},{5,1},{6,2},{7,3},{8,12},{9,13},{10,... | collective-permute-start | bytes 331784 | tf_op jit(solution)/shard_map/ppermute | solution.py:23
  22.2 4.9 %collective-permute-start.6 = (bf16[384,128]{1,0:T(8,128)(2,1)S(1)}, bf16[384,128]{1,0:T(8,128)(2,1)S(1)}, u32[]{:S(2)}, u32[]{:S(2)}) collective-permute-start(bf16[384,128]{1,0:T(8,128)(2,1)S(1)} %add_convert_fusion.1.rest_0_), channel_id=1, source_target_pairs={{0,4},{1,5},{2,6},{3,7},{4,0},{5,1},{6,2},{7,3},{8,12},{9,13},{10,... | collective-permute-start | bytes 294920 | tf_op jit(solution)/shard_map/ppermute | solution.py:23
  27.3 4.8 %collective-permute-start.7 = (bf16[432,128]{1,0:T(8,128)(2,1)S(1)}, bf16[432,128]{1,0:T(8,128)(2,1)S(1)}, u32[]{:S(2)}, u32[]{:S(2)}) collective-permute-start(bf16[432,128]{1,0:T(8,128)(2,1)S(1)} %get-tuple-element.44.own_ref), channel_id=1, source_target_pairs={{0,8},{1,9},{2,10},{3,11},{4,12},{5,13},{6,14},{7,15},{8,0},{9,1},... | collective-permute-start | bytes 331784 | tf_op jit(solution)/shard_map/ppermute | solution.py:23
  32.3 5.0 %collective-permute-start.10 = (bf16[176,128]{1,0:T(8,128)(2,1)S(1)}, bf16[176,128]{1,0:T(8,128)(2,1)S(1)}, u32[]{:S(2)}, u32[]{:S(2)}) collective-permute-start(bf16[176,128]{1,0:T(8,128)(2,1)S(1)} %merge3.1.own_ref), channel_id=1, source_target_pairs={{0,16},{1,17},{2,18},{3,19},{4,20},{5,21},{6,22},{7,23},{8,24},{9,... | collective-permute-start | bytes 135176 | tf_op jit(solution)/shard_map/ppermute | solution.py:23
  35.0 4.9 %collective-permute-start.15 = (bf16[128,128]{1,0:T(8,128)(2,1)S(1)}, bf16[128,128]{1,0:T(8,128)(2,1)S(1)}, u32[]{:S(2)}, u32[]{:S(2)}) collective-permute-start(bf16[128,128]{1,0:T(8,128)(2,1)S(1)} %slice.99.last_ref), channel_id=1, source_target_pairs={{0,1},{1,0},{2,3},{3,2},{4,5},{5,4},{6,7},{7,6},{8,9},{9,8},{10,11... | collective-permute-start | bytes 98312 | tf_op jit(solution)/shard_map/ppermute | solution.py:23
  35.0 7.2 %collective-permute-start.14 = (bf16[128,128]{1,0:T(8,128)(2,1)S(1)}, bf16[128,128]{1,0:T(8,128)(2,1)S(1)}, u32[]{:S(2)}, u32[]{:S(2)}) collective-permute-start(bf16[128,128]{1,0:T(8,128)(2,1)S(1)} %slice.79.refs_1_), channel_id=1, source_target_pairs={{0,1},{1,0},{2,3},{3,2},{4,5},{5,4},{6,7},{7,6},{8,9},{9,8},{10,11... | collective-permute-start | bytes 98312 | tf_op jit(solution)/shard_map/ppermute | solution.py:23
  35.5 7.4 %collective-permute-start.13 = (bf16[128,128]{1,0:T(8,128)(2,1)S(1)}, bf16[128,128]{1,0:T(8,128)(2,1)S(1)}, u32[]{:S(2)}, u32[]{:S(2)}) collective-permute-start(bf16[128,128]{1,0:T(8,128)(2,1)S(1)} %slice.78.refs_0_), channel_id=1, source_target_pairs={{0,1},{1,0},{2,3},{3,2},{4,5},{5,4},{6,7},{7,6},{8,9},{9,8},{10,11... | collective-permute-start | bytes 98312 | tf_op jit(solution)/shard_map/ppermute | solution.py:23
  39.3 3.6 %collective-permute-start.11 = (bf16[128,128]{1,0:T(8,128)(2,1)S(1)}, bf16[128,128]{1,0:T(8,128)(2,1)S(1)}, u32[]{:S(2)}, u32[]{:S(2)}) collective-permute-start(bf16[128,128]{1,0:T(8,128)(2,1)S(1)} %slice.82), channel_id=1, source_target_pairs={{0,1},{1,0},{2,3},{3,2},{4,5},{5,4},{6,7},{7,6},{8,9},{9,8},{10,11... | collective-permute-start | bytes 98312 | tf_op jit(solution)/shard_map/ppermute | solution.py:23
  39.6 3.3 %collective-permute-start.12 = (bf16[128,128]{1,0:T(8,128)(2,1)S(1)}, bf16[128,128]{1,0:T(8,128)(2,1)S(1)}, u32[]{:S(2)}, u32[]{:S(2)}) collective-permute-start(bf16[128,128]{1,0:T(8,128)(2,1)S(1)} %slice.81.refs_4_), channel_id=1, source_target_pairs={{0,1},{1,0},{2,3},{3,2},{4,5},{5,4},{6,7},{7,6},{8,9},{9,8},{10,11... | collective-permute-start | bytes 98312 | tf_op jit(solution)/shard_map/ppermute | solution.py:23
  39.9 7.1 %collective-permute-start.16 = (bf16[512,128]{1,0:T(8,128)(2,1)S(1)}, bf16[512,128]{1,0:T(8,128)(2,1)S(1)}, u32[]{:S(2)}, u32[]{:S(2)}) collective-permute-start(bf16[512,128]{1,0:T(8,128)(2,1)S(1)} %get-tuple-element.71), channel_id=1, source_target_pairs={{0,6},{1,7},{2,4},{3,5},{4,2},{5,3},{6,0},{7,1},{8,14},{9,15},{10,... | collective-permute-start | bytes 393224 | tf_op jit(solution)/shard_map/ppermute | solution.py:23
  42.2 7.0 %collective-permute-start.17 = (bf16[512,128]{1,0:T(8,128)(2,1)S(1)}, bf16[512,128]{1,0:T(8,128)(2,1)S(1)}, u32[]{:S(2)}, u32[]{:S(2)}) collective-permute-start(bf16[512,128]{1,0:T(8,128)(2,1)S(1)} %get-tuple-element.72), channel_id=1, source_target_pairs={{0,4},{1,5},{2,6},{3,7},{4,0},{5,1},{6,2},{7,3},{8,12},{9,13},{10,... | collective-permute-start | bytes 393224 | tf_op jit(solution)/shard_map/ppermute | solution.py:23
  44.1 5.2 %collective-permute-start.18 = (bf16[512,128]{1,0:T(8,128)(2,1)S(1)}, bf16[512,128]{1,0:T(8,128)(2,1)S(1)}, u32[]{:S(2)}, u32[]{:S(2)}) collective-permute-start(bf16[512,128]{1,0:T(8,128)(2,1)S(1)} %weigh1.1), channel_id=1, source_target_pairs={{0,2},{1,3},{2,0},{3,1},{4,6},{5,7},{6,4},{7,5},{8,10},{9,11},{10,... | collective-permute-start | bytes 393224 | tf_op jit(solution)/shard_map/ppermute | solution.py:23
  45.8 13.6 %copy-start.5 = (bf16[64,256]{1,0:T(8,128)(2,1)S(1)}, bf16[64,256]{1,0:T(8,128)(2,1)}, u32[]{:S(2)}) copy-start(bf16[64,256]{1,0:T(8,128)(2,1)} %param.15) | copy-start | bytes 98308
  49.3 5.9 %collective-permute-start.19 = (bf16[128,128]{1,0:T(8,128)(2,1)S(1)}, bf16[128,128]{1,0:T(8,128)(2,1)S(1)}, u32[]{:S(2)}, u32[]{:S(2)}) collective-permute-start(bf16[128,128]{1,0:T(8,128)(2,1)S(1)} %get-tuple-element.80), channel_id=1, source_target_pairs={{0,24},{1,25},{2,26},{3,27},{4,28},{5,29},{6,30},{7,31},{8,16},{9,... | collective-permute-start | bytes 98312 | tf_op jit(solution)/shard_map/ppermute | solution.py:23
  53.3 4.8 %collective-permute-start.20 = (bf16[128,128]{1,0:T(8,128)(2,1)S(1)}, bf16[128,128]{1,0:T(8,128)(2,1)S(1)}, u32[]{:S(2)}, u32[]{:S(2)}) collective-permute-start(bf16[128,128]{1,0:T(8,128)(2,1)S(1)} %get-tuple-element.82), channel_id=1, source_target_pairs={{0,16},{1,17},{2,18},{3,19},{4,20},{5,21},{6,22},{7,23},{8,24},{9,... | collective-permute-start | bytes 98312 | tf_op jit(solution)/shard_map/ppermute | solution.py:23
  53.3 4.8 %collective-permute-start.21 = (bf16[128,128]{1,0:T(8,128)(2,1)S(1)}, bf16[128,128]{1,0:T(8,128)(2,1)S(1)}, u32[]{:S(2)}, u32[]{:S(2)}) collective-permute-start(bf16[128,128]{1,0:T(8,128)(2,1)S(1)} %get-tuple-element.81), channel_id=1, source_target_pairs={{0,8},{1,9},{2,10},{3,11},{4,12},{5,13},{6,14},{7,15},{8,0},{9,1},... | collective-permute-start | bytes 98312 | tf_op jit(solution)/shard_map/ppermute | solution.py:23
  58.1 1.3 %collective-permute-start.22 = (f32[64,128]{1,0:T(8,128)S(1)}, f32[64,128]{1,0:T(8,128)S(1)}, u32[]{:S(2)}, u32[]{:S(2)}) collective-permute-start(f32[64,128]{1,0:T(8,128)S(1)} %get-tuple-element.84), channel_id=1, source_target_pairs={{0,1},{1,0},{2,3},{3,2},{4,5},{5,4},{6,7},{7,6},{8,9},{9,8},{10,11... | collective-permute-start | bytes 98312 | tf_op jit(solution)/shard_map/ppermute | solution.py:23

commit v8 on v7

--- a/solution.py
+++ b/solution.py
@@ -430,7 +430,7 @@
         room=8 if near <= 4 else 24,
         ins=[SMEM, VMEM, VMEM],
     )(info, message, points)
-    early_masks = (3, 2)
+    early_masks = (3, 2, 1)
     shape = plane, near, tile, leaf, blocks, devices
     final_mine, coeffs, spots, *partials = call(
         functools.partial(first_kernel, rank, chips, depth, 2.0 * leaf, early_masks, shape),
@@ -439,7 +439,7 @@
         "first",
         64 * near * tile * rows * half,
         64 * near * tile * half,
-        room=10 if near <= 4 else 24,
+        room=12 if near <= 4 else 28,
         ins=[SMEM] + [VMEM] * (7 + len(early_masks)),
         scratch=[pltpu.VMEM((2 * near * tile, 2 * rows), bf16)],
     )(
@@ -462,8 +462,6 @@
     sent = [swapped(partial, mask << 1) for mask, partial in zip(early_masks, partials)]
     share0, share1, _ = lax.optimization_barrier((shares[0], shares[1], coeffs))
     others[:2] = swapped(share0, 1), swapped(share1, 1)
-    coeffs, others = lax.optimization_barrier((coeffs, others))
-    sent.append(swapped(weighed(1, coeffs), 1 << 1))
     solved_out = call(
         solved_kernel,
         out((rows, samples), f32),

time: 60.3 us -> 59.4 us (0.985)
    pallas_call x2 -> x1, Pallas kernels: 2.36 us -> 1.16 us  [weighed(): call(functools.partial(far_kernel, mask, *shape), out((4 * near * tile, h...]
  transfers between devices with their start and end apart: 23 -> 23, of which waited for: 8 -> 11; matrix products, arithmetic and copies ran while one was open for 2% -> 2% of each run, Pallas kernels for 20% -> 20%
where the time goes in v8:
time: 59.4 us; the launch traced here: 59.2 us
  waiting for transfers between devices  21.8 us (37%)
  starting transfers between devices  20 us (34%)
  Pallas kernels  14.4 us (24%)
  local copies, waits for them, and re-layouts  1.21 us (2%)
  other arithmetic  0.89 us (1%)
  between operations  0.89 us (1%)
    ppermute x23, waiting for transfers between devices, swapped(): return lax.ppermute(value, 'pts', pairs)  21.8 us
    ppermute x23, starting transfers between devices, swapped(): return lax.ppermute(value, 'pts', pairs)  20 us
    pallas_call x1, Pallas kernels, body(): call(functools.partial(front_kernel, rows, leaf, bits, rank, inner, sizes...  4.1 us
    pallas_call x1, Pallas kernels, body(): call(functools.partial(small_kernel, bits, rank), out((pair_count * rank,...  2.62 us
    pallas_call x1, Pallas kernels, body(): call(functools.partial(first_kernel, rank, chips, depth, 2.0 * leaf, earl...  2.48 us
    pallas_call x1, Pallas kernels, body(): call(functools.partial(near_kernel, plane, near, tile, leaf, blocks, devi...  1.51 us
  transfers between devices with their start and end apart: 23, of which 11 were waited for; matrix products, arithmetic and copies ran while one was open for 2% of the time, Pallas kernels for 20%

profile of v8, /device:TPU:0, one launch (start us, length us, event | category | flops | bytes accessed | tf_op | source)
XLA Modules:
  0.0 59.2 jit_solution(9396379149956712621)
XLA Ops:
  0.6 2.6 %small.1.small_ref = bf16[1280,128]{1,0:T(8,128)(2,1)S(1)} custom-call(f32[7,512,128]{2,1,0:T(8,128)} %right_ref.3, f32[7,512,128]{2,1,0:T(8,128)} %left_ref.5), custom_call_target="tpu_custom_call" | custom-call | flops 167772160 | bytes 2621440 | tf_op jit(solution)/shard_map/small/pallas_call | solution.py:301
  3.3 0.5 collective-permute-start.1
  3.8 4.1 %front.1 = (f32[512,128]{1,0:T(8,128)S(1)}, f32[512,128]{1,0:T(8,128)S(1)}, f32[640,128]{1,0:T(8,128)S(1)}, bf16[640,128]{1,0:T(8,128)(2,1)S(1)}) custom-call(s32[1]{0:T(128)} %bitcast.core_ref, bf16[512,256]{1,0:T(8,128)(2,1)S(1)} %copy-done.1, bf16[512,128]{1,0:T(8,128)(2,1)S(1)} %copy-done.2, f32[7,512,128]{2,1,0:T(8,128)} %right_ref.3, ...), custom_call_target="tpu_custom_call" | custom-call | flops 503316480 | bytes 3670016 | tf_op jit(solution)/shard_map/front/pallas_call | solution.py:317
  7.9 0.0 copy-start.3
  7.9 0.0 copy-start.4
  7.9 0.1 collective-permute-start
  8.1 0.5 collective-permute-start.2
  8.5 0.2 left16.1.left_ref.refs_2_
  8.8 0.2 collective-permute-start.9
  8.9 0.0 collective-permute-done.1.their_ref
  8.9 0.1 add_convert_fusion.rest_0_
  9.0 3.0 %collective-permute-start.4 = (bf16[768,128]{1,0:T(8,128)(2,1)S(1)}, bf16[768,128]{1,0:T(8,128)(2,1)S(1)}, u32[]{:S(2)}, u32[]{:S(2)}) collective-permute-start(bf16[768,128]{1,0:T(8,128)(2,1)S(1)} %add_convert_fusion.rest_0_), channel_id=1, source_target_pairs={{0,2},{1,3},{2,0},{3,1},{4,6},{5,7},{6,4},{7,5},{8,10},{9,11},{10,... | collective-permute-start | bytes 589832 | tf_op jit(solution)/shard_map/ppermute | solution.py:23
  12.0 0.0 collective-permute-done.2
  12.0 0.1 maximum_bitcast_fusion.spot_ref
  12.0 0.0 collective-permute-done.got_ref
  12.0 0.2 merge0.1
  12.3 0.2 collective-permute-start.3
  12.5 0.0 collective-permute-start.8
  12.5 0.2 dynamic-slice_reduce_fusion
  12.8 0.1 concatenate.16.info_ref
  12.8 7.3 %collective-permute-done.3.got_ref = bf16[560,128]{1,0:T(8,128)(2,1)S(1)} collective-permute-done((bf16[560,128]{1,0:T(8,128)(2,1)S(1)}, bf16[560,128]{1,0:T(8,128)(2,1)S(1)}, u32[]{:S(2)}, u32[]{:S(2)}) %collective-permute-start.3) | collective-permute-done | bytes 143392 | tf_op jit(solution)/shard_map/ppermute | solution.py:23
  20.2 0.0 collective-permute-done.4.rest_1_
  20.2 0.2 merge1.1
  20.4 1.8 %collective-permute-start.5 = (bf16[432,128]{1,0:T(8,128)(2,1)S(1)}, bf16[432,128]{1,0:T(8,128)(2,1)S(1)}, u32[]{:S(2)}, u32[]{:S(2)}) collective-permute-start(bf16[432,128]{1,0:T(8,128)(2,1)S(1)} %get-tuple-element.38.own_ref), channel_id=1, source_target_pairs={{0,4},{1,5},{2,6},{3,7},{4,0},{5,1},{6,2},{7,3},{8,12},{9,13},{10,... | collective-permute-start | bytes 331784 | tf_op jit(solution)/shard_map/ppermute | solution.py:23
  22.2 0.3 collective-permute-start.6
  22.6 0.8 %dynamic-slice_bitcast_fusion.1 = (f32[4,128]{1,0:T(4,128)S(1)}, f32[4,128]{1,0:T(4,128)S(1)}) fusion(f32[16384]{0:T(1024)} %param.13, s32[]{:T(128)S(6)} %select_n.33, s32[]{:T(128)S(6)} %select_n.34), kind=kLoop, calls=%fused_computation.15 | loop fusion | bytes 8200 | tf_op jit(solution)/shard_map/reshape | solution.py:381
  23.4 3.7 %collective-permute-done.6.rest_1_ = bf16[384,128]{1,0:T(8,128)(2,1)S(1)} collective-permute-done((bf16[384,128]{1,0:T(8,128)(2,1)S(1)}, bf16[384,128]{1,0:T(8,128)(2,1)S(1)}, u32[]{:S(2)}, u32[]{:S(2)}) %collective-permute-start.6) | collective-permute-done | bytes 98336 | tf_op jit(solution)/shard_map/ppermute | solution.py:23
  27.2 0.0 collective-permute-done.5.got_ref
  27.2 0.2 merge2.1
  27.3 1.6 %collective-permute-start.7 = (bf16[432,128]{1,0:T(8,128)(2,1)S(1)}, bf16[432,128]{1,0:T(8,128)(2,1)S(1)}, u32[]{:S(2)}, u32[]{:S(2)}) collective-permute-start(bf16[432,128]{1,0:T(8,128)(2,1)S(1)} %get-tuple-element.39.own_ref), channel_id=1, source_target_pairs={{0,8},{1,9},{2,10},{3,11},{4,12},{5,13},{6,14},{7,15},{8,0},{9,1},... | collective-permute-start | bytes 331784 | tf_op jit(solution)/shard_map/ppermute | solution.py:23
  29.1 0.4 partial.1
  29.4 2.7 %collective-permute-done.7.got_ref = bf16[432,128]{1,0:T(8,128)(2,1)S(1)} collective-permute-done((bf16[432,128]{1,0:T(8,128)(2,1)S(1)}, bf16[432,128]{1,0:T(8,128)(2,1)S(1)}, u32[]{:S(2)}, u32[]{:S(2)}) %collective-permute-start.7) | collective-permute-done | bytes 110624 | tf_op jit(solution)/shard_map/ppermute | solution.py:23
  32.2 0.2 merge3.1.own_ref
  32.3 2.7 %collective-permute-start.10 = (bf16[176,128]{1,0:T(8,128)(2,1)S(1)}, bf16[176,128]{1,0:T(8,128)(2,1)S(1)}, u32[]{:S(2)}, u32[]{:S(2)}) collective-permute-start(bf16[176,128]{1,0:T(8,128)(2,1)S(1)} %merge3.1.own_ref), channel_id=1, source_target_pairs={{0,16},{1,17},{2,18},{3,19},{4,20},{5,21},{6,22},{7,23},{8,24},{9,... | collective-permute-start | bytes 135176 | tf_op jit(solution)/shard_map/ppermute | solution.py:23
  35.0 0.0 collective-permute-start.15
  35.0 1.5 %near.1 = (bf16[256,1024]{1,0:T(8,128)(2,1)S(1)}, bf16[256,1024]{1,0:T(8,128)(2,1)S(1)}, bf16[256,1024]{1,0:T(8,128)(2,1)S(1)}, bf16[256,1024]{1,0:T(8,128)(2,1)S(1)}) custom-call(s32[129]{0:T(256)S(1)} %concatenate.16.info_ref, bf16[176,128]{1,0:T(8,128)(2,1)S(1)} %merge3.1.own_ref, f32[8,128]{1,0:T(8,128)S(1)} %pad_maximum_fusion.point_ref), custom_call_target="tpu_custom_call" | custom-call | flops 10485760 | bytes 2097152 | tf_op jit(solution)/shard_map/near/pallas_call | solution.py:424
  36.5 0.8 %collective-permute-done.10.refs_5_ = bf16[176,128]{1,0:T(8,128)(2,1)S(1)} collective-permute-done((bf16[176,128]{1,0:T(8,128)(2,1)S(1)}, bf16[176,128]{1,0:T(8,128)(2,1)S(1)}, u32[]{:S(2)}, u32[]{:S(2)}) %collective-permute-start.10) | collective-permute-done | bytes 45088 | tf_op jit(solution)/shard_map/ppermute | solution.py:23
  37.3 2.5 %first.1 = (f32[512,128]{1,0:T(8,128)S(1)}, bf16[1024,128]{1,0:T(8,128)(2,1)S(1)}, f32[128,8]{1,0:T(8,128)S(1)}, bf16[512,128]{1,0:T(8,128)(2,1)S(1)}, bf16[512,...) custom-call(s32[129]{0:T(256)S(1)} %concatenate.16.info_ref, f32[8,128]{1,0:T(8,128)S(1)} %pad_maximum_fusion.point_ref, ...), custom_call_target="tpu_custom_call" | custom-call | flops 536870912 | bytes 1048576 | tf_op jit(solution)/shard_map/first/pallas_call | solution.py:435
  39.8 2.4 %collective-permute-start.16 = (bf16[512,128]{1,0:T(8,128)(2,1)S(1)}, bf16[512,128]{1,0:T(8,128)(2,1)S(1)}, u32[]{:S(2)}, u32[]{:S(2)}) collective-permute-start(bf16[512,128]{1,0:T(8,128)(2,1)S(1)} %get-tuple-element.61), channel_id=1, source_target_pairs={{0,6},{1,7},{2,4},{3,5},{4,2},{5,3},{6,0},{7,1},{8,14},{9,15},{10,... | collective-permute-start | bytes 393224 | tf_op jit(solution)/shard_map/ppermute | solution.py:23
  42.2 0.7 %collective-permute-start.17 = (bf16[512,128]{1,0:T(8,128)(2,1)S(1)}, bf16[512,128]{1,0:T(8,128)(2,1)S(1)}, u32[]{:S(2)}, u32[]{:S(2)}) collective-permute-start(bf16[512,128]{1,0:T(8,128)(2,1)S(1)} %get-tuple-element.62), channel_id=1, source_target_pairs={{0,4},{1,5},{2,6},{3,7},{4,0},{5,1},{6,2},{7,3},{8,12},{9,13},{10,... | collective-permute-start | bytes 393224 | tf_op jit(solution)/shard_map/ppermute | solution.py:23
  42.8 0.5 collective-permute-start.18
  43.4 0.0 collective-permute-start.14
  43.4 0.0 collective-permute-done.15.refs_4_
  43.4 0.5 collective-permute-start.13
  43.9 0.7 %collective-permute-done.14.refs_3_ = bf16[128,128]{1,0:T(8,128)(2,1)S(1)} collective-permute-done((bf16[128,128]{1,0:T(8,128)(2,1)S(1)}, bf16[128,128]{1,0:T(8,128)(2,1)S(1)}, u32[]{:S(2)}, u32[]{:S(2)}) %collective-permute-start.14) | collective-permute-done | bytes 32800 | tf_op jit(solution)/shard_map/ppermute | solution.py:23
  44.6 0.2 collective-permute-start.11
  44.7 0.0 collective-permute-done.13.refs_2_
  44.7 0.3 collective-permute-start.12
  45.1 0.7 %collective-permute-done.11.refs_0_ = bf16[128,128]{1,0:T(8,128)(2,1)S(1)} collective-permute-done((bf16[128,128]{1,0:T(8,128)(2,1)S(1)}, bf16[128,128]{1,0:T(8,128)(2,1)S(1)}, u32[]{:S(2)}, u32[]{:S(2)}) %collective-permute-start.11) | collective-permute-done | bytes 32800 | tf_op jit(solution)/shard_map/ppermute | solution.py:23
  45.8 0.2 collective-permute-done.12.refs_1_
  45.9 1.1 %solved.1 = f32[512,256]{1,0:T(8,128)} custom-call(s32[1]{0:T(128)} %bitcast.core_ref, f32[512,128]{1,0:T(8,128)S(1)} %get-tuple-element.54.mine_ref, f32[512,128]{1,0:T(8,128)S(1)} %get-tuple-element.41.rest_ref, bf16[512,640]{1,0:T(8,128)(2,1)S(1)} %left16.1.left_ref.refs_2_, bf16[128,128]{1,0:T(8,128)(2,1)S(1)} %collective-permute-done.11.refs_0_, ...), custom_call_target="tpu_custom_call" | custom-call | flops 83886080 | bytes 2097152 | tf_op jit(solution)/shard_map/solved/pallas_call | solution.py:465
  47.1 1.2 %weigh0.1 = f32[512,128]{1,0:T(8,128)S(1)} custom-call(s32[129]{0:T(256)S(1)} %concatenate.16.info_ref, f32[128,8]{1,0:T(8,128)S(1)} %get-tuple-element.58.spot_ref, bf16[256,1024]{1,0:T(8,128)(2,1)S(1)} %get-tuple-element.59.near_ref, f32[8,128]{1,0:T(8,128)S(1)} %pad_maximum_fusion.point_ref, bf16[1024,128]{1,0:T(8,128)(2,1)S(1)} %get-tuple-element.60.coeff_ref), custom_call_target="tpu_custom_call" | custom-call | flops 268435456 | bytes 524288 | tf_op jit(solution)/shard_map/weigh0/pallas_call | solution.py:451
  48.3 0.0 collective-permute-done.16
  48.3 0.4 collective-permute-done.17
  48.7 0.0 collective-permute-done.18
  48.7 0.1 fusion.3
  48.8 3.6 %collective-permute-start.19 = (bf16[128,128]{1,0:T(8,128)(2,1)S(1)}, bf16[128,128]{1,0:T(8,128)(2,1)S(1)}, u32[]{:S(2)}, u32[]{:S(2)}) collective-permute-start(bf16[128,128]{1,0:T(8,128)(2,1)S(1)} %get-tuple-element.70), channel_id=1, source_target_pairs={{0,24},{1,25},{2,26},{3,27},{4,28},{5,29},{6,30},{7,31},{8,16},{9,... | collective-permute-start | bytes 98312 | tf_op jit(solution)/shard_map/ppermute | solution.py:23
  52.4 0.8 %collective-permute-start.21 = (bf16[128,128]{1,0:T(8,128)(2,1)S(1)}, bf16[128,128]{1,0:T(8,128)(2,1)S(1)}, u32[]{:S(2)}, u32[]{:S(2)}) collective-permute-start(bf16[128,128]{1,0:T(8,128)(2,1)S(1)} %get-tuple-element.71), channel_id=1, source_target_pairs={{0,8},{1,9},{2,10},{3,11},{4,12},{5,13},{6,14},{7,15},{8,0},{9,1},... | collective-permute-start | bytes 98312 | tf_op jit(solution)/shard_map/ppermute | solution.py:23
  53.3 1.3 %collective-permute-done.19 = bf16[128,128]{1,0:T(8,128)(2,1)S(1)} collective-permute-done((bf16[128,128]{1,0:T(8,128)(2,1)S(1)}, bf16[128,128]{1,0:T(8,128)(2,1)S(1)}, u32[]{:S(2)}, u32[]{:S(2)}) %collective-permute-start.19) | collective-permute-done | bytes 32800 | tf_op jit(solution)/shard_map/ppermute | solution.py:23
  54.6 2.7 %collective-permute-done.20 = bf16[128,128]{1,0:T(8,128)(2,1)S(1)} collective-permute-done((bf16[128,128]{1,0:T(8,128)(2,1)S(1)}, bf16[128,128]{1,0:T(8,128)(2,1)S(1)}, u32[]{:S(2)}, u32[]{:S(2)}) %collective-permute-start.20) | collective-permute-done | bytes 32800 | tf_op jit(solution)/shard_map/ppermute | solution.py:23
  57.2 0.0 collective-permute-done.21
  57.3 0.1 collective-permute-start.22
  57.4 1.2 %collective-permute-done.22 = f32[64,128]{1,0:T(8,128)S(1)} collective-permute-done((f32[64,128]{1,0:T(8,128)S(1)}, f32[64,128]{1,0:T(8,128)S(1)}, u32[]{:S(2)}, u32[]{:S(2)}) %collective-permute-start.22) | collective-permute-done | bytes 32800 | tf_op jit(solution)/shard_map/ppermute | solution.py:23
  58.6 0.6 %fusion.2 = f32[64,256]{1,0:T(8,128)} fusion(f32[64,128]{1,0:T(8,128)S(1)} %collective-permute-done.22, f32[64,128]{1,0:T(8,128)S(1)} %get-tuple-element.73, bf16[64,256]{1,0:T(8,128)(2,1)S(1)} %copy-done.5, pred[]{:T(512)S(6)} %eq.5), kind=kLoop, calls=%fused_computation.8 | loop fusion | flops 81920 | bytes 163841 | tf_op jit(solution)/shard_map/add | solution.py:489
  (26 shorter events, 0.1 us)
Async XLA Ops:
  0.6 3.2 %copy-start.2 = (bf16[512,128]{1,0:T(8,128)(2,1)S(1)}, bf16[512,128]{1,0:T(8,128)(2,1)}, u32[]{:S(2)}) copy-start(bf16[512,128]{1,0:T(8,128)(2,1)} %inverse_ref.1) | copy-start | bytes 393220
  0.6 3.2 %copy-start.1 = (bf16[512,256]{1,0:T(8,128)(2,1)S(1)}, bf16[512,256]{1,0:T(8,128)(2,1)}, u32[]{:S(2)}) copy-start(bf16[512,256]{1,0:T(8,128)(2,1)} %residual_ref.1) | copy-start | bytes 786436
  3.3 5.6 %collective-permute-start.1 = (bf16[1280,128]{1,0:T(8,128)(2,1)S(1)}, bf16[1280,128]{1,0:T(8,128)(2,1)S(1)}, u32[]{:S(2)}, u32[]{:S(2)}) collective-permute-start(bf16[1280,128]{1,0:T(8,128)(2,1)S(1)} %small.1.small_ref), channel_id=1, source_target_pairs={{0,1},{1,0},{2,3},{3,2},{4,5},{5,4},{6,7},{7,6},{8,9},{9,8},{10,11... | collective-permute-start | bytes 983048 | tf_op jit(solution)/shard_map/ppermute | solution.py:23
  3.8 4.3 %copy-start.6 = (f32[64]{0:T(128)S(1)}, f32[64]{0:T(128)}, u32[]{:S(2)}) copy-start(f32[64]{0:T(128)} %param.14) | copy-start | bytes 772
  3.8 4.7 %copy-start = (f32[7,512,128]{2,1,0:T(8,128)S(1)}, f32[7,512,128]{2,1,0:T(8,128)}, u32[]{:S(2)}) copy-start(f32[7,512,128]{2,1,0:T(8,128)} %left_ref.5) | copy-start | bytes 5505028
  7.9 4.6 %copy-start.3 = (s32[32,32]{1,0:T(8,128)S(1)}, s32[32,32]{1,0:T(8,128)}, u32[]{:S(2)}) copy-start(s32[32,32]{1,0:T(8,128)} %param.17) | copy-start | bytes 12292
  7.9 4.6 %copy-start.4 = (s32[32,32]{1,0:T(8,128)S(1)}, s32[32,32]{1,0:T(8,128)}, u32[]{:S(2)}) copy-start(s32[32,32]{1,0:T(8,128)} %param.16) | copy-start | bytes 12292
  7.9 4.1 %collective-permute-start = (bf16[640,128]{1,0:T(8,128)(2,1)S(1)}, bf16[640,128]{1,0:T(8,128)(2,1)S(1)}, u32[]{:S(2)}, u32[]{:S(2)}) collective-permute-start(bf16[640,128]{1,0:T(8,128)(2,1)S(1)} %get-tuple-element.34), channel_id=1, source_target_pairs={{0,1},{1,0},{2,3},{3,2},{4,5},{5,4},{6,7},{7,6},{8,9},{9,8},{10,11... | collective-permute-start | bytes 491528 | tf_op jit(solution)/shard_map/ppermute | solution.py:23
  8.1 3.9 %collective-permute-start.2 = (f32[64]{0:T(128)S(1)}, f32[64]{0:T(128)S(1)}, u32[]{:S(2)}, u32[]{:S(2)}) collective-permute-start(f32[64]{0:T(128)S(1)} %copy-done.6), channel_id=1, source_target_pairs={{0,1},{1,0},{2,3},{3,2},{4,5},{5,4},{6,7},{7,6},{8,9},{9,8},{10,11... | collective-permute-start | bytes 776 | tf_op jit(solution)/shard_map/ppermute | solution.py:23
  8.8 20.3 %collective-permute-start.9 = (bf16[512,640]{1,0:T(8,128)(2,1)S(1)}, bf16[512,640]{1,0:T(8,128)(2,1)S(1)}, u32[]{:S(2)}, u32[]{:S(2)}) collective-permute-start(bf16[512,640]{1,0:T(8,128)(2,1)S(1)} %left16.1.left_ref.refs_2_), channel_id=1, source_target_pairs={{0,1},{1,0},{2,3},{3,2},{4,5},{5,4},{6,7},{7,6},{8,9},{9,8},{10,11... | collective-permute-start | bytes 1966088 | tf_op jit(solution)/shard_map/ppermute | solution.py:23
  9.0 11.2 %collective-permute-start.4 = (bf16[768,128]{1,0:T(8,128)(2,1)S(1)}, bf16[768,128]{1,0:T(8,128)(2,1)S(1)}, u32[]{:S(2)}, u32[]{:S(2)}) collective-permute-start(bf16[768,128]{1,0:T(8,128)(2,1)S(1)} %add_convert_fusion.rest_0_), channel_id=1, source_target_pairs={{0,2},{1,3},{2,0},{3,1},{4,6},{5,7},{6,4},{7,5},{8,10},{9,11},{10,... | collective-permute-start | bytes 589832 | tf_op jit(solution)/shard_map/ppermute | solution.py:23
  12.3 7.9 %collective-permute-start.3 = (bf16[560,128]{1,0:T(8,128)(2,1)S(1)}, bf16[560,128]{1,0:T(8,128)(2,1)S(1)}, u32[]{:S(2)}, u32[]{:S(2)}) collective-permute-start(bf16[560,128]{1,0:T(8,128)(2,1)S(1)} %get-tuple-element.36.own_ref), channel_id=1, source_target_pairs={{0,2},{1,3},{2,0},{3,1},{4,6},{5,7},{6,4},{7,5},{8,10},{9,11},{10,... | collective-permute-start | bytes 430088 | tf_op jit(solution)/shard_map/ppermute | solution.py:23
  12.5 16.5 %collective-permute-start.8 = (f32[512,128]{1,0:T(8,128)S(1)}, f32[512,128]{1,0:T(8,128)S(1)}, u32[]{:S(2)}, u32[]{:S(2)}) collective-permute-start(f32[512,128]{1,0:T(8,128)S(1)} %get-tuple-element.41.rest_ref), channel_id=1, source_target_pairs={{0,1},{1,0},{2,3},{3,2},{4,5},{5,4},{6,7},{7,6},{8,9},{9,8},{10,11... | collective-permute-start | bytes 786440 | tf_op jit(solution)/shard_map/ppermute | solution.py:23
  20.4 6.8 %collective-permute-start.5 = (bf16[432,128]{1,0:T(8,128)(2,1)S(1)}, bf16[432,128]{1,0:T(8,128)(2,1)S(1)}, u32[]{:S(2)}, u32[]{:S(2)}) collective-permute-start(bf16[432,128]{1,0:T(8,128)(2,1)S(1)} %get-tuple-element.38.own_ref), channel_id=1, source_target_pairs={{0,4},{1,5},{2,6},{3,7},{4,0},{5,1},{6,2},{7,3},{8,12},{9,13},{10,... | collective-permute-start | bytes 331784 | tf_op jit(solution)/shard_map/ppermute | solution.py:23
  22.2 4.9 %collective-permute-start.6 = (bf16[384,128]{1,0:T(8,128)(2,1)S(1)}, bf16[384,128]{1,0:T(8,128)(2,1)S(1)}, u32[]{:S(2)}, u32[]{:S(2)}) collective-permute-start(bf16[384,128]{1,0:T(8,128)(2,1)S(1)} %add_convert_fusion.1.rest_0_), channel_id=1, source_target_pairs={{0,4},{1,5},{2,6},{3,7},{4,0},{5,1},{6,2},{7,3},{8,12},{9,13},{10,... | collective-permute-start | bytes 294920 | tf_op jit(solution)/shard_map/ppermute | solution.py:23
  27.3 4.8 %collective-permute-start.7 = (bf16[432,128]{1,0:T(8,128)(2,1)S(1)}, bf16[432,128]{1,0:T(8,128)(2,1)S(1)}, u32[]{:S(2)}, u32[]{:S(2)}) collective-permute-start(bf16[432,128]{1,0:T(8,128)(2,1)S(1)} %get-tuple-element.39.own_ref), channel_id=1, source_target_pairs={{0,8},{1,9},{2,10},{3,11},{4,12},{5,13},{6,14},{7,15},{8,0},{9,1},... | collective-permute-start | bytes 331784 | tf_op jit(solution)/shard_map/ppermute | solution.py:23
  32.3 5.0 %collective-permute-start.10 = (bf16[176,128]{1,0:T(8,128)(2,1)S(1)}, bf16[176,128]{1,0:T(8,128)(2,1)S(1)}, u32[]{:S(2)}, u32[]{:S(2)}) collective-permute-start(bf16[176,128]{1,0:T(8,128)(2,1)S(1)} %merge3.1.own_ref), channel_id=1, source_target_pairs={{0,16},{1,17},{2,18},{3,19},{4,20},{5,21},{6,22},{7,23},{8,24},{9,... | collective-permute-start | bytes 135176 | tf_op jit(solution)/shard_map/ppermute | solution.py:23
  35.0 8.4 %collective-permute-start.15 = (bf16[128,128]{1,0:T(8,128)(2,1)S(1)}, bf16[128,128]{1,0:T(8,128)(2,1)S(1)}, u32[]{:S(2)}, u32[]{:S(2)}) collective-permute-start(bf16[128,128]{1,0:T(8,128)(2,1)S(1)} %slice.99.last_ref), channel_id=1, source_target_pairs={{0,1},{1,0},{2,3},{3,2},{4,5},{5,4},{6,7},{7,6},{8,9},{9,8},{10,11... | collective-permute-start | bytes 98312 | tf_op jit(solution)/shard_map/ppermute | solution.py:23
  39.8 8.4 %collective-permute-start.16 = (bf16[512,128]{1,0:T(8,128)(2,1)S(1)}, bf16[512,128]{1,0:T(8,128)(2,1)S(1)}, u32[]{:S(2)}, u32[]{:S(2)}) collective-permute-start(bf16[512,128]{1,0:T(8,128)(2,1)S(1)} %get-tuple-element.61), channel_id=1, source_target_pairs={{0,6},{1,7},{2,4},{3,5},{4,2},{5,3},{6,0},{7,1},{8,14},{9,15},{10,... | collective-permute-start | bytes 393224 | tf_op jit(solution)/shard_map/ppermute | solution.py:23
  42.2 6.5 %collective-permute-start.17 = (bf16[512,128]{1,0:T(8,128)(2,1)S(1)}, bf16[512,128]{1,0:T(8,128)(2,1)S(1)}, u32[]{:S(2)}, u32[]{:S(2)}) collective-permute-start(bf16[512,128]{1,0:T(8,128)(2,1)S(1)} %get-tuple-element.62), channel_id=1, source_target_pairs={{0,4},{1,5},{2,6},{3,7},{4,0},{5,1},{6,2},{7,3},{8,12},{9,13},{10,... | collective-permute-start | bytes 393224 | tf_op jit(solution)/shard_map/ppermute | solution.py:23
  42.8 5.9 %collective-permute-start.18 = (bf16[512,128]{1,0:T(8,128)(2,1)S(1)}, bf16[512,128]{1,0:T(8,128)(2,1)S(1)}, u32[]{:S(2)}, u32[]{:S(2)}) collective-permute-start(bf16[512,128]{1,0:T(8,128)(2,1)S(1)} %get-tuple-element.63), channel_id=1, source_target_pairs={{0,2},{1,3},{2,0},{3,1},{4,6},{5,7},{6,4},{7,5},{8,10},{9,11},{10,... | collective-permute-start | bytes 393224 | tf_op jit(solution)/shard_map/ppermute | solution.py:23
  43.4 1.2 %collective-permute-start.14 = (bf16[128,128]{1,0:T(8,128)(2,1)S(1)}, bf16[128,128]{1,0:T(8,128)(2,1)S(1)}, u32[]{:S(2)}, u32[]{:S(2)}) collective-permute-start(bf16[128,128]{1,0:T(8,128)(2,1)S(1)} %slice.79.refs_1_), channel_id=1, source_target_pairs={{0,1},{1,0},{2,3},{3,2},{4,5},{5,4},{6,7},{7,6},{8,9},{9,8},{10,11... | collective-permute-start | bytes 98312 | tf_op jit(solution)/shard_map/ppermute | solution.py:23
  43.4 1.4 %collective-permute-start.13 = (bf16[128,128]{1,0:T(8,128)(2,1)S(1)}, bf16[128,128]{1,0:T(8,128)(2,1)S(1)}, u32[]{:S(2)}, u32[]{:S(2)}) collective-permute-start(bf16[128,128]{1,0:T(8,128)(2,1)S(1)} %slice.78.refs_0_), channel_id=1, source_target_pairs={{0,1},{1,0},{2,3},{3,2},{4,5},{5,4},{6,7},{7,6},{8,9},{9,8},{10,11... | collective-permute-start | bytes 98312 | tf_op jit(solution)/shard_map/ppermute | solution.py:23
  44.6 1.2 %collective-permute-start.11 = (bf16[128,128]{1,0:T(8,128)(2,1)S(1)}, bf16[128,128]{1,0:T(8,128)(2,1)S(1)}, u32[]{:S(2)}, u32[]{:S(2)}) collective-permute-start(bf16[128,128]{1,0:T(8,128)(2,1)S(1)} %slice.82), channel_id=1, source_target_pairs={{0,1},{1,0},{2,3},{3,2},{4,5},{5,4},{6,7},{7,6},{8,9},{9,8},{10,11... | collective-permute-start | bytes 98312 | tf_op jit(solution)/shard_map/ppermute | solution.py:23
  44.7 1.2 %collective-permute-start.12 = (bf16[128,128]{1,0:T(8,128)(2,1)S(1)}, bf16[128,128]{1,0:T(8,128)(2,1)S(1)}, u32[]{:S(2)}, u32[]{:S(2)}) collective-permute-start(bf16[128,128]{1,0:T(8,128)(2,1)S(1)} %slice.81.refs_4_), channel_id=1, source_target_pairs={{0,1},{1,0},{2,3},{3,2},{4,5},{5,4},{6,7},{7,6},{8,9},{9,8},{10,11... | collective-permute-start | bytes 98312 | tf_op jit(solution)/shard_map/ppermute | solution.py:23
  47.1 11.5 %copy-start.5 = (bf16[64,256]{1,0:T(8,128)(2,1)S(1)}, bf16[64,256]{1,0:T(8,128)(2,1)}, u32[]{:S(2)}) copy-start(bf16[64,256]{1,0:T(8,128)(2,1)} %param.15) | copy-start | bytes 98308
  48.8 5.8 %collective-permute-start.19 = (bf16[128,128]{1,0:T(8,128)(2,1)S(1)}, bf16[128,128]{1,0:T(8,128)(2,1)S(1)}, u32[]{:S(2)}, u32[]{:S(2)}) collective-permute-start(bf16[128,128]{1,0:T(8,128)(2,1)S(1)} %get-tuple-element.70), channel_id=1, source_target_pairs={{0,24},{1,25},{2,26},{3,27},{4,28},{5,29},{6,30},{7,31},{8,16},{9,... | collective-permute-start | bytes 98312 | tf_op jit(solution)/shard_map/ppermute | solution.py:23
  52.4 4.8 %collective-permute-start.20 = (bf16[128,128]{1,0:T(8,128)(2,1)S(1)}, bf16[128,128]{1,0:T(8,128)(2,1)S(1)}, u32[]{:S(2)}, u32[]{:S(2)}) collective-permute-start(bf16[128,128]{1,0:T(8,128)(2,1)S(1)} %get-tuple-element.72), channel_id=1, source_target_pairs={{0,16},{1,17},{2,18},{3,19},{4,20},{5,21},{6,22},{7,23},{8,24},{9,... | collective-permute-start | bytes 98312 | tf_op jit(solution)/shard_map/ppermute | solution.py:23
  52.4 4.8 %collective-permute-start.21 = (bf16[128,128]{1,0:T(8,128)(2,1)S(1)}, bf16[128,128]{1,0:T(8,128)(2,1)S(1)}, u32[]{:S(2)}, u32[]{:S(2)}) collective-permute-start(bf16[128,128]{1,0:T(8,128)(2,1)S(1)} %get-tuple-element.71), channel_id=1, source_target_pairs={{0,8},{1,9},{2,10},{3,11},{4,12},{5,13},{6,14},{7,15},{8,0},{9,1},... | collective-permute-start | bytes 98312 | tf_op jit(solution)/shard_map/ppermute | solution.py:23
  57.3 1.3 %collective-permute-start.22 = (f32[64,128]{1,0:T(8,128)S(1)}, f32[64,128]{1,0:T(8,128)S(1)}, u32[]{:S(2)}, u32[]{:S(2)}) collective-permute-start(f32[64,128]{1,0:T(8,128)S(1)} %get-tuple-element.74), channel_id=1, source_target_pairs={{0,1},{1,0},{2,3},{3,2},{4,5},{5,4},{6,7},{7,6},{8,9},{9,8},{10,11... | collective-permute-start | bytes 98312 | tf_op jit(solution)/shard_map/ppermute | solution.py:23

commit v9 on v8

--- a/solution.py
+++ b/solution.py
@@ -430,7 +430,7 @@
         room=8 if near <= 4 else 24,
         ins=[SMEM, VMEM, VMEM],
     )(info, message, points)
-    early_masks = (3, 2, 1)
+    early_masks = (2, 3, 1)
     shape = plane, near, tile, leaf, blocks, devices
     final_mine, coeffs, spots, *partials = call(
         functools.partial(first_kernel, rank, chips, depth, 2.0 * leaf, early_masks, shape),

time: 59.4 us -> 59.4 us (level)
  transfers between devices with their start and end apart: 23 -> 23, of which waited for: 11 -> 12; matrix products, arithmetic and copies ran while one was open for 2% -> 2% of each run, Pallas kernels for 20% -> 20%
where the time goes in v9:
time: 59.4 us; the launch traced here: 59.2 us
  waiting for transfers between devices  21.9 us (37%)
  starting transfers between devices  20 us (34%)
  Pallas kernels  14.4 us (24%)
  local copies, waits for them, and re-layouts  1.21 us (2%)
  other arithmetic  0.89 us (1%)
  between operations  0.89 us (1%)
    ppermute x23, waiting for transfers between devices, swapped(): return lax.ppermute(value, 'pts', pairs)  21.9 us
    ppermute x23, starting transfers between devices, swapped(): return lax.ppermute(value, 'pts', pairs)  20 us
    pallas_call x1, Pallas kernels, body(): call(functools.partial(front_kernel, rows, leaf, bits, rank, inner, sizes...  4.1 us
    pallas_call x1, Pallas kernels, body(): call(functools.partial(small_kernel, bits, rank), out((pair_count * rank,...  2.62 us
    pallas_call x1, Pallas kernels, body(): call(functools.partial(first_kernel, rank, chips, depth, 2.0 * leaf, earl...  2.48 us
    pallas_call x1, Pallas kernels, body(): call(functools.partial(near_kernel, plane, near, tile, leaf, blocks, devi...  1.51 us
  transfers between devices with their start and end apart: 23, of which 12 were waited for; matrix products, arithmetic and copies ran while one was open for 2% of the time, Pallas kernels for 20%

profile of v9, /device:TPU:0, one launch (start us, length us, event | category | flops | bytes accessed | tf_op | source)
XLA Modules:
  0.0 59.2 jit_solution(6383180461330696385)
XLA Ops:
  0.6 2.6 %small.1.small_ref = bf16[1280,128]{1,0:T(8,128)(2,1)S(1)} custom-call(f32[7,512,128]{2,1,0:T(8,128)} %right_ref.3, f32[7,512,128]{2,1,0:T(8,128)} %left_ref.5), custom_call_target="tpu_custom_call" | custom-call | flops 167772160 | bytes 2621440 | tf_op jit(solution)/shard_map/small/pallas_call | solution.py:301
  3.3 0.5 collective-permute-start.1
  3.8 4.1 %front.1 = (f32[512,128]{1,0:T(8,128)S(1)}, f32[512,128]{1,0:T(8,128)S(1)}, f32[640,128]{1,0:T(8,128)S(1)}, bf16[640,128]{1,0:T(8,128)(2,1)S(1)}) custom-call(s32[1]{0:T(128)} %bitcast.core_ref, bf16[512,256]{1,0:T(8,128)(2,1)S(1)} %copy-done.1, bf16[512,128]{1,0:T(8,128)(2,1)S(1)} %copy-done.2, f32[7,512,128]{2,1,0:T(8,128)} %right_ref.3, ...), custom_call_target="tpu_custom_call" | custom-call | flops 503316480 | bytes 3670016 | tf_op jit(solution)/shard_map/front/pallas_call | solution.py:317
  7.9 0.0 copy-start.3
  7.9 0.0 copy-start.4
  7.9 0.1 collective-permute-start
  8.1 0.5 collective-permute-start.2
  8.5 0.2 left16.1.left_ref.refs_2_
  8.8 0.2 collective-permute-start.9
  8.9 0.0 collective-permute-done.1.their_ref
  8.9 0.1 add_convert_fusion.rest_0_
  9.0 3.0 %collective-permute-start.4 = (bf16[768,128]{1,0:T(8,128)(2,1)S(1)}, bf16[768,128]{1,0:T(8,128)(2,1)S(1)}, u32[]{:S(2)}, u32[]{:S(2)}) collective-permute-start(bf16[768,128]{1,0:T(8,128)(2,1)S(1)} %add_convert_fusion.rest_0_), channel_id=1, source_target_pairs={{0,2},{1,3},{2,0},{3,1},{4,6},{5,7},{6,4},{7,5},{8,10},{9,11},{10,... | collective-permute-start | bytes 589832 | tf_op jit(solution)/shard_map/ppermute | solution.py:23
  12.0 0.0 collective-permute-done.2
  12.0 0.1 maximum_bitcast_fusion.spot_ref
  12.0 0.0 collective-permute-done.got_ref
  12.0 0.2 merge0.1
  12.3 0.2 collective-permute-start.3
  12.5 0.0 collective-permute-start.8
  12.5 0.2 dynamic-slice_reduce_fusion
  12.8 0.1 concatenate.16.info_ref
  12.8 7.3 %collective-permute-done.3.got_ref = bf16[560,128]{1,0:T(8,128)(2,1)S(1)} collective-permute-done((bf16[560,128]{1,0:T(8,128)(2,1)S(1)}, bf16[560,128]{1,0:T(8,128)(2,1)S(1)}, u32[]{:S(2)}, u32[]{:S(2)}) %collective-permute-start.3) | collective-permute-done | bytes 143392 | tf_op jit(solution)/shard_map/ppermute | solution.py:23
  20.2 0.0 collective-permute-done.4.rest_1_
  20.2 0.2 merge1.1
  20.4 1.8 %collective-permute-start.5 = (bf16[432,128]{1,0:T(8,128)(2,1)S(1)}, bf16[432,128]{1,0:T(8,128)(2,1)S(1)}, u32[]{:S(2)}, u32[]{:S(2)}) collective-permute-start(bf16[432,128]{1,0:T(8,128)(2,1)S(1)} %get-tuple-element.38.own_ref), channel_id=1, source_target_pairs={{0,4},{1,5},{2,6},{3,7},{4,0},{5,1},{6,2},{7,3},{8,12},{9,13},{10,... | collective-permute-start | bytes 331784 | tf_op jit(solution)/shard_map/ppermute | solution.py:23
  22.2 0.3 collective-permute-start.6
  22.6 0.8 %dynamic-slice_bitcast_fusion.1 = (f32[4,128]{1,0:T(4,128)S(1)}, f32[4,128]{1,0:T(4,128)S(1)}) fusion(f32[16384]{0:T(1024)} %param.13, s32[]{:T(128)S(6)} %select_n.33, s32[]{:T(128)S(6)} %select_n.34), kind=kLoop, calls=%fused_computation.15 | loop fusion | bytes 8200 | tf_op jit(solution)/shard_map/reshape | solution.py:381
  23.4 3.7 %collective-permute-done.6.rest_1_ = bf16[384,128]{1,0:T(8,128)(2,1)S(1)} collective-permute-done((bf16[384,128]{1,0:T(8,128)(2,1)S(1)}, bf16[384,128]{1,0:T(8,128)(2,1)S(1)}, u32[]{:S(2)}, u32[]{:S(2)}) %collective-permute-start.6) | collective-permute-done | bytes 98336 | tf_op jit(solution)/shard_map/ppermute | solution.py:23
  27.2 0.0 collective-permute-done.5.got_ref
  27.2 0.2 merge2.1
  27.3 1.6 %collective-permute-start.7 = (bf16[432,128]{1,0:T(8,128)(2,1)S(1)}, bf16[432,128]{1,0:T(8,128)(2,1)S(1)}, u32[]{:S(2)}, u32[]{:S(2)}) collective-permute-start(bf16[432,128]{1,0:T(8,128)(2,1)S(1)} %get-tuple-element.39.own_ref), channel_id=1, source_target_pairs={{0,8},{1,9},{2,10},{3,11},{4,12},{5,13},{6,14},{7,15},{8,0},{9,1},... | collective-permute-start | bytes 331784 | tf_op jit(solution)/shard_map/ppermute | solution.py:23
  29.0 0.0 collective-permute-done.8.other_ref
  29.0 0.0 collective-permute-done.9.left_other_ref.refs_3_
  29.1 0.4 partial.1
  29.4 2.7 %collective-permute-done.7.got_ref = bf16[432,128]{1,0:T(8,128)(2,1)S(1)} collective-permute-done((bf16[432,128]{1,0:T(8,128)(2,1)S(1)}, bf16[432,128]{1,0:T(8,128)(2,1)S(1)}, u32[]{:S(2)}, u32[]{:S(2)}) %collective-permute-start.7) | collective-permute-done | bytes 110624 | tf_op jit(solution)/shard_map/ppermute | solution.py:23
  32.2 0.2 merge3.1.own_ref
  32.3 2.7 %collective-permute-start.10 = (bf16[176,128]{1,0:T(8,128)(2,1)S(1)}, bf16[176,128]{1,0:T(8,128)(2,1)S(1)}, u32[]{:S(2)}, u32[]{:S(2)}) collective-permute-start(bf16[176,128]{1,0:T(8,128)(2,1)S(1)} %merge3.1.own_ref), channel_id=1, source_target_pairs={{0,16},{1,17},{2,18},{3,19},{4,20},{5,21},{6,22},{7,23},{8,24},{9,... | collective-permute-start | bytes 135176 | tf_op jit(solution)/shard_map/ppermute | solution.py:23
  35.0 1.5 %near.1 = (bf16[256,1024]{1,0:T(8,128)(2,1)S(1)}, bf16[256,1024]{1,0:T(8,128)(2,1)S(1)}, bf16[256,1024]{1,0:T(8,128)(2,1)S(1)}, bf16[256,1024]{1,0:T(8,128)(2,1)S(1)}) custom-call(s32[129]{0:T(256)S(1)} %concatenate.16.info_ref, bf16[176,128]{1,0:T(8,128)(2,1)S(1)} %merge3.1.own_ref, f32[8,128]{1,0:T(8,128)S(1)} %pad_maximum_fusion.point_ref), custom_call_target="tpu_custom_call" | custom-call | flops 10485760 | bytes 2097152 | tf_op jit(solution)/shard_map/near/pallas_call | solution.py:424
  36.5 0.8 %collective-permute-done.10.refs_5_ = bf16[176,128]{1,0:T(8,128)(2,1)S(1)} collective-permute-done((bf16[176,128]{1,0:T(8,128)(2,1)S(1)}, bf16[176,128]{1,0:T(8,128)(2,1)S(1)}, u32[]{:S(2)}, u32[]{:S(2)}) %collective-permute-start.10) | collective-permute-done | bytes 45088 | tf_op jit(solution)/shard_map/ppermute | solution.py:23
  37.3 2.5 %first.1 = (f32[512,128]{1,0:T(8,128)S(1)}, bf16[1024,128]{1,0:T(8,128)(2,1)S(1)}, f32[128,8]{1,0:T(8,128)S(1)}, bf16[512,128]{1,0:T(8,128)(2,1)S(1)}, bf16[512,...) custom-call(s32[129]{0:T(256)S(1)} %concatenate.16.info_ref, f32[8,128]{1,0:T(8,128)S(1)} %pad_maximum_fusion.point_ref, ...), custom_call_target="tpu_custom_call" | custom-call | flops 536870912 | bytes 1048576 | tf_op jit(solution)/shard_map/first/pallas_call | solution.py:435
  39.8 1.4 %collective-permute-start.16 = (bf16[512,128]{1,0:T(8,128)(2,1)S(1)}, bf16[512,128]{1,0:T(8,128)(2,1)S(1)}, u32[]{:S(2)}, u32[]{:S(2)}) collective-permute-start(bf16[512,128]{1,0:T(8,128)(2,1)S(1)} %get-tuple-element.61), channel_id=1, source_target_pairs={{0,4},{1,5},{2,6},{3,7},{4,0},{5,1},{6,2},{7,3},{8,12},{9,13},{10,... | collective-permute-start | bytes 393224 | tf_op jit(solution)/shard_map/ppermute | solution.py:23
  41.2 1.6 %collective-permute-start.17 = (bf16[512,128]{1,0:T(8,128)(2,1)S(1)}, bf16[512,128]{1,0:T(8,128)(2,1)S(1)}, u32[]{:S(2)}, u32[]{:S(2)}) collective-permute-start(bf16[512,128]{1,0:T(8,128)(2,1)S(1)} %get-tuple-element.62), channel_id=1, source_target_pairs={{0,6},{1,7},{2,4},{3,5},{4,2},{5,3},{6,0},{7,1},{8,14},{9,15},{10,... | collective-permute-start | bytes 393224 | tf_op jit(solution)/shard_map/ppermute | solution.py:23
  42.8 0.5 collective-permute-start.18
  43.4 0.0 collective-permute-start.14
  43.4 0.0 collective-permute-done.15.refs_4_
  43.4 0.5 collective-permute-start.13
  43.9 0.7 %collective-permute-done.14.refs_3_ = bf16[128,128]{1,0:T(8,128)(2,1)S(1)} collective-permute-done((bf16[128,128]{1,0:T(8,128)(2,1)S(1)}, bf16[128,128]{1,0:T(8,128)(2,1)S(1)}, u32[]{:S(2)}, u32[]{:S(2)}) %collective-permute-start.14) | collective-permute-done | bytes 32800 | tf_op jit(solution)/shard_map/ppermute | solution.py:23
  44.6 0.2 collective-permute-start.11
  44.7 0.0 collective-permute-done.13.refs_2_
  44.7 0.3 collective-permute-start.12
  45.1 0.7 %collective-permute-done.11.refs_0_ = bf16[128,128]{1,0:T(8,128)(2,1)S(1)} collective-permute-done((bf16[128,128]{1,0:T(8,128)(2,1)S(1)}, bf16[128,128]{1,0:T(8,128)(2,1)S(1)}, u32[]{:S(2)}, u32[]{:S(2)}) %collective-permute-start.11) | collective-permute-done | bytes 32800 | tf_op jit(solution)/shard_map/ppermute | solution.py:23
  45.8 0.2 collective-permute-done.12.refs_1_
  45.9 1.1 %solved.1 = f32[512,256]{1,0:T(8,128)} custom-call(s32[1]{0:T(128)} %bitcast.core_ref, f32[512,128]{1,0:T(8,128)S(1)} %get-tuple-element.54.mine_ref, f32[512,128]{1,0:T(8,128)S(1)} %get-tuple-element.41.rest_ref, bf16[512,640]{1,0:T(8,128)(2,1)S(1)} %left16.1.left_ref.refs_2_, bf16[128,128]{1,0:T(8,128)(2,1)S(1)} %collective-permute-done.11.refs_0_, ...), custom_call_target="tpu_custom_call" | custom-call | flops 83886080 | bytes 2097152 | tf_op jit(solution)/shard_map/solved/pallas_call | solution.py:465
  47.1 1.2 %weigh0.1 = f32[512,128]{1,0:T(8,128)S(1)} custom-call(s32[129]{0:T(256)S(1)} %concatenate.16.info_ref, f32[128,8]{1,0:T(8,128)S(1)} %get-tuple-element.58.spot_ref, bf16[256,1024]{1,0:T(8,128)(2,1)S(1)} %get-tuple-element.59.near_ref, f32[8,128]{1,0:T(8,128)S(1)} %pad_maximum_fusion.point_ref, bf16[1024,128]{1,0:T(8,128)(2,1)S(1)} %get-tuple-element.60.coeff_ref), custom_call_target="tpu_custom_call" | custom-call | flops 268435456 | bytes 524288 | tf_op jit(solution)/shard_map/weigh0/pallas_call | solution.py:451
  48.3 0.3 collective-permute-done.17
  48.5 0.5 collective-permute-done.18
  49.0 0.1 fusion.3
  49.1 3.3 %collective-permute-start.19 = (bf16[128,128]{1,0:T(8,128)(2,1)S(1)}, bf16[128,128]{1,0:T(8,128)(2,1)S(1)}, u32[]{:S(2)}, u32[]{:S(2)}) collective-permute-start(bf16[128,128]{1,0:T(8,128)(2,1)S(1)} %get-tuple-element.70), channel_id=1, source_target_pairs={{0,24},{1,25},{2,26},{3,27},{4,28},{5,29},{6,30},{7,31},{8,16},{9,... | collective-permute-start | bytes 98312 | tf_op jit(solution)/shard_map/ppermute | solution.py:23
  52.4 1.1 %collective-permute-start.21 = (bf16[128,128]{1,0:T(8,128)(2,1)S(1)}, bf16[128,128]{1,0:T(8,128)(2,1)S(1)}, u32[]{:S(2)}, u32[]{:S(2)}) collective-permute-start(bf16[128,128]{1,0:T(8,128)(2,1)S(1)} %get-tuple-element.71), channel_id=1, source_target_pairs={{0,8},{1,9},{2,10},{3,11},{4,12},{5,13},{6,14},{7,15},{8,0},{9,1},... | collective-permute-start | bytes 98312 | tf_op jit(solution)/shard_map/ppermute | solution.py:23
  53.6 1.6 %collective-permute-done.19 = bf16[128,128]{1,0:T(8,128)(2,1)S(1)} collective-permute-done((bf16[128,128]{1,0:T(8,128)(2,1)S(1)}, bf16[128,128]{1,0:T(8,128)(2,1)S(1)}, u32[]{:S(2)}, u32[]{:S(2)}) %collective-permute-start.19) | collective-permute-done | bytes 32800 | tf_op jit(solution)/shard_map/ppermute | solution.py:23
  55.1 2.1 %collective-permute-done.20 = bf16[128,128]{1,0:T(8,128)(2,1)S(1)} collective-permute-done((bf16[128,128]{1,0:T(8,128)(2,1)S(1)}, bf16[128,128]{1,0:T(8,128)(2,1)S(1)}, u32[]{:S(2)}, u32[]{:S(2)}) %collective-permute-start.20) | collective-permute-done | bytes 32800 | tf_op jit(solution)/shard_map/ppermute | solution.py:23
  57.2 0.0 collective-permute-done.21
  57.3 0.1 collective-permute-start.22
  57.4 1.2 %collective-permute-done.22 = f32[64,128]{1,0:T(8,128)S(1)} collective-permute-done((f32[64,128]{1,0:T(8,128)S(1)}, f32[64,128]{1,0:T(8,128)S(1)}, u32[]{:S(2)}, u32[]{:S(2)}) %collective-permute-start.22) | collective-permute-done | bytes 32800 | tf_op jit(solution)/shard_map/ppermute | solution.py:23
  58.6 0.6 %fusion.2 = f32[64,256]{1,0:T(8,128)} fusion(f32[64,128]{1,0:T(8,128)S(1)} %collective-permute-done.22, f32[64,128]{1,0:T(8,128)S(1)} %get-tuple-element.73, bf16[64,256]{1,0:T(8,128)(2,1)S(1)} %copy-done.5, pred[]{:T(512)S(6)} %eq.5), kind=kLoop, calls=%fused_computation.8 | loop fusion | flops 81920 | bytes 163841 | tf_op jit(solution)/shard_map/add | solution.py:489
  (26 shorter events, 0.1 us)
Async XLA Ops:
  0.6 3.2 %copy-start.2 = (bf16[512,128]{1,0:T(8,128)(2,1)S(1)}, bf16[512,128]{1,0:T(8,128)(2,1)}, u32[]{:S(2)}) copy-start(bf16[512,128]{1,0:T(8,128)(2,1)} %inverse_ref.1) | copy-start | bytes 393220
  0.6 3.2 %copy-start.1 = (bf16[512,256]{1,0:T(8,128)(2,1)S(1)}, bf16[512,256]{1,0:T(8,128)(2,1)}, u32[]{:S(2)}) copy-start(bf16[512,256]{1,0:T(8,128)(2,1)} %residual_ref.1) | copy-start | bytes 786436
  3.3 5.6 %collective-permute-start.1 = (bf16[1280,128]{1,0:T(8,128)(2,1)S(1)}, bf16[1280,128]{1,0:T(8,128)(2,1)S(1)}, u32[]{:S(2)}, u32[]{:S(2)}) collective-permute-start(bf16[1280,128]{1,0:T(8,128)(2,1)S(1)} %small.1.small_ref), channel_id=1, source_target_pairs={{0,1},{1,0},{2,3},{3,2},{4,5},{5,4},{6,7},{7,6},{8,9},{9,8},{10,11... | collective-permute-start | bytes 983048 | tf_op jit(solution)/shard_map/ppermute | solution.py:23
  3.8 4.3 %copy-start.6 = (f32[64]{0:T(128)S(1)}, f32[64]{0:T(128)}, u32[]{:S(2)}) copy-start(f32[64]{0:T(128)} %param.14) | copy-start | bytes 772
  3.8 4.7 %copy-start = (f32[7,512,128]{2,1,0:T(8,128)S(1)}, f32[7,512,128]{2,1,0:T(8,128)}, u32[]{:S(2)}) copy-start(f32[7,512,128]{2,1,0:T(8,128)} %left_ref.5) | copy-start | bytes 5505028
  7.9 4.6 %copy-start.3 = (s32[32,32]{1,0:T(8,128)S(1)}, s32[32,32]{1,0:T(8,128)}, u32[]{:S(2)}) copy-start(s32[32,32]{1,0:T(8,128)} %param.17) | copy-start | bytes 12292
  7.9 4.6 %copy-start.4 = (s32[32,32]{1,0:T(8,128)S(1)}, s32[32,32]{1,0:T(8,128)}, u32[]{:S(2)}) copy-start(s32[32,32]{1,0:T(8,128)} %param.16) | copy-start | bytes 12292
  7.9 4.1 %collective-permute-start = (bf16[640,128]{1,0:T(8,128)(2,1)S(1)}, bf16[640,128]{1,0:T(8,128)(2,1)S(1)}, u32[]{:S(2)}, u32[]{:S(2)}) collective-permute-start(bf16[640,128]{1,0:T(8,128)(2,1)S(1)} %get-tuple-element.34), channel_id=1, source_target_pairs={{0,1},{1,0},{2,3},{3,2},{4,5},{5,4},{6,7},{7,6},{8,9},{9,8},{10,11... | collective-permute-start | bytes 491528 | tf_op jit(solution)/shard_map/ppermute | solution.py:23
  8.1 3.9 %collective-permute-start.2 = (f32[64]{0:T(128)S(1)}, f32[64]{0:T(128)S(1)}, u32[]{:S(2)}, u32[]{:S(2)}) collective-permute-start(f32[64]{0:T(128)S(1)} %copy-done.6), channel_id=1, source_target_pairs={{0,1},{1,0},{2,3},{3,2},{4,5},{5,4},{6,7},{7,6},{8,9},{9,8},{10,11... | collective-permute-start | bytes 776 | tf_op jit(solution)/shard_map/ppermute | solution.py:23
  8.8 20.3 %collective-permute-start.9 = (bf16[512,640]{1,0:T(8,128)(2,1)S(1)}, bf16[512,640]{1,0:T(8,128)(2,1)S(1)}, u32[]{:S(2)}, u32[]{:S(2)}) collective-permute-start(bf16[512,640]{1,0:T(8,128)(2,1)S(1)} %left16.1.left_ref.refs_2_), channel_id=1, source_target_pairs={{0,1},{1,0},{2,3},{3,2},{4,5},{5,4},{6,7},{7,6},{8,9},{9,8},{10,11... | collective-permute-start | bytes 1966088 | tf_op jit(solution)/shard_map/ppermute | solution.py:23
  9.0 11.2 %collective-permute-start.4 = (bf16[768,128]{1,0:T(8,128)(2,1)S(1)}, bf16[768,128]{1,0:T(8,128)(2,1)S(1)}, u32[]{:S(2)}, u32[]{:S(2)}) collective-permute-start(bf16[768,128]{1,0:T(8,128)(2,1)S(1)} %add_convert_fusion.rest_0_), channel_id=1, source_target_pairs={{0,2},{1,3},{2,0},{3,1},{4,6},{5,7},{6,4},{7,5},{8,10},{9,11},{10,... | collective-permute-start | bytes 589832 | tf_op jit(solution)/shard_map/ppermute | solution.py:23
  12.3 7.9 %collective-permute-start.3 = (bf16[560,128]{1,0:T(8,128)(2,1)S(1)}, bf16[560,128]{1,0:T(8,128)(2,1)S(1)}, u32[]{:S(2)}, u32[]{:S(2)}) collective-permute-start(bf16[560,128]{1,0:T(8,128)(2,1)S(1)} %get-tuple-element.36.own_ref), channel_id=1, source_target_pairs={{0,2},{1,3},{2,0},{3,1},{4,6},{5,7},{6,4},{7,5},{8,10},{9,11},{10,... | collective-permute-start | bytes 430088 | tf_op jit(solution)/shard_map/ppermute | solution.py:23
  12.5 16.5 %collective-permute-start.8 = (f32[512,128]{1,0:T(8,128)S(1)}, f32[512,128]{1,0:T(8,128)S(1)}, u32[]{:S(2)}, u32[]{:S(2)}) collective-permute-start(f32[512,128]{1,0:T(8,128)S(1)} %get-tuple-element.41.rest_ref), channel_id=1, source_target_pairs={{0,1},{1,0},{2,3},{3,2},{4,5},{5,4},{6,7},{7,6},{8,9},{9,8},{10,11... | collective-permute-start | bytes 786440 | tf_op jit(solution)/shard_map/ppermute | solution.py:23
  20.4 6.8 %collective-permute-start.5 = (bf16[432,128]{1,0:T(8,128)(2,1)S(1)}, bf16[432,128]{1,0:T(8,128)(2,1)S(1)}, u32[]{:S(2)}, u32[]{:S(2)}) collective-permute-start(bf16[432,128]{1,0:T(8,128)(2,1)S(1)} %get-tuple-element.38.own_ref), channel_id=1, source_target_pairs={{0,4},{1,5},{2,6},{3,7},{4,0},{5,1},{6,2},{7,3},{8,12},{9,13},{10,... | collective-permute-start | bytes 331784 | tf_op jit(solution)/shard_map/ppermute | solution.py:23
  22.2 4.9 %collective-permute-start.6 = (bf16[384,128]{1,0:T(8,128)(2,1)S(1)}, bf16[384,128]{1,0:T(8,128)(2,1)S(1)}, u32[]{:S(2)}, u32[]{:S(2)}) collective-permute-start(bf16[384,128]{1,0:T(8,128)(2,1)S(1)} %add_convert_fusion.1.rest_0_), channel_id=1, source_target_pairs={{0,4},{1,5},{2,6},{3,7},{4,0},{5,1},{6,2},{7,3},{8,12},{9,13},{10,... | collective-permute-start | bytes 294920 | tf_op jit(solution)/shard_map/ppermute | solution.py:23
  27.3 4.8 %collective-permute-start.7 = (bf16[432,128]{1,0:T(8,128)(2,1)S(1)}, bf16[432,128]{1,0:T(8,128)(2,1)S(1)}, u32[]{:S(2)}, u32[]{:S(2)}) collective-permute-start(bf16[432,128]{1,0:T(8,128)(2,1)S(1)} %get-tuple-element.39.own_ref), channel_id=1, source_target_pairs={{0,8},{1,9},{2,10},{3,11},{4,12},{5,13},{6,14},{7,15},{8,0},{9,1},... | collective-permute-start | bytes 331784 | tf_op jit(solution)/shard_map/ppermute | solution.py:23
  32.3 5.0 %collective-permute-start.10 = (bf16[176,128]{1,0:T(8,128)(2,1)S(1)}, bf16[176,128]{1,0:T(8,128)(2,1)S(1)}, u32[]{:S(2)}, u32[]{:S(2)}) collective-permute-start(bf16[176,128]{1,0:T(8,128)(2,1)S(1)} %merge3.1.own_ref), channel_id=1, source_target_pairs={{0,16},{1,17},{2,18},{3,19},{4,20},{5,21},{6,22},{7,23},{8,24},{9,... | collective-permute-start | bytes 135176 | tf_op jit(solution)/shard_map/ppermute | solution.py:23
  35.0 8.4 %collective-permute-start.15 = (bf16[128,128]{1,0:T(8,128)(2,1)S(1)}, bf16[128,128]{1,0:T(8,128)(2,1)S(1)}, u32[]{:S(2)}, u32[]{:S(2)}) collective-permute-start(bf16[128,128]{1,0:T(8,128)(2,1)S(1)} %slice.99.last_ref), channel_id=1, source_target_pairs={{0,1},{1,0},{2,3},{3,2},{4,5},{5,4},{6,7},{7,6},{8,9},{9,8},{10,11... | collective-permute-start | bytes 98312 | tf_op jit(solution)/shard_map/ppermute | solution.py:23
  39.8 8.4 %collective-permute-start.16 = (bf16[512,128]{1,0:T(8,128)(2,1)S(1)}, bf16[512,128]{1,0:T(8,128)(2,1)S(1)}, u32[]{:S(2)}, u32[]{:S(2)}) collective-permute-start(bf16[512,128]{1,0:T(8,128)(2,1)S(1)} %get-tuple-element.61), channel_id=1, source_target_pairs={{0,4},{1,5},{2,6},{3,7},{4,0},{5,1},{6,2},{7,3},{8,12},{9,13},{10,... | collective-permute-start | bytes 393224 | tf_op jit(solution)/shard_map/ppermute | solution.py:23
  41.2 7.3 %collective-permute-start.17 = (bf16[512,128]{1,0:T(8,128)(2,1)S(1)}, bf16[512,128]{1,0:T(8,128)(2,1)S(1)}, u32[]{:S(2)}, u32[]{:S(2)}) collective-permute-start(bf16[512,128]{1,0:T(8,128)(2,1)S(1)} %get-tuple-element.62), channel_id=1, source_target_pairs={{0,6},{1,7},{2,4},{3,5},{4,2},{5,3},{6,0},{7,1},{8,14},{9,15},{10,... | collective-permute-start | bytes 393224 | tf_op jit(solution)/shard_map/ppermute | solution.py:23
  42.8 6.2 %collective-permute-start.18 = (bf16[512,128]{1,0:T(8,128)(2,1)S(1)}, bf16[512,128]{1,0:T(8,128)(2,1)S(1)}, u32[]{:S(2)}, u32[]{:S(2)}) collective-permute-start(bf16[512,128]{1,0:T(8,128)(2,1)S(1)} %get-tuple-element.63), channel_id=1, source_target_pairs={{0,2},{1,3},{2,0},{3,1},{4,6},{5,7},{6,4},{7,5},{8,10},{9,11},{10,... | collective-permute-start | bytes 393224 | tf_op jit(solution)/shard_map/ppermute | solution.py:23
  43.4 1.2 %collective-permute-start.14 = (bf16[128,128]{1,0:T(8,128)(2,1)S(1)}, bf16[128,128]{1,0:T(8,128)(2,1)S(1)}, u32[]{:S(2)}, u32[]{:S(2)}) collective-permute-start(bf16[128,128]{1,0:T(8,128)(2,1)S(1)} %slice.79.refs_1_), channel_id=1, source_target_pairs={{0,1},{1,0},{2,3},{3,2},{4,5},{5,4},{6,7},{7,6},{8,9},{9,8},{10,11... | collective-permute-start | bytes 98312 | tf_op jit(solution)/shard_map/ppermute | solution.py:23
  43.4 1.4 %collective-permute-start.13 = (bf16[128,128]{1,0:T(8,128)(2,1)S(1)}, bf16[128,128]{1,0:T(8,128)(2,1)S(1)}, u32[]{:S(2)}, u32[]{:S(2)}) collective-permute-start(bf16[128,128]{1,0:T(8,128)(2,1)S(1)} %slice.78.refs_0_), channel_id=1, source_target_pairs={{0,1},{1,0},{2,3},{3,2},{4,5},{5,4},{6,7},{7,6},{8,9},{9,8},{10,11... | collective-permute-start | bytes 98312 | tf_op jit(solution)/shard_map/ppermute | solution.py:23
  44.6 1.2 %collective-permute-start.11 = (bf16[128,128]{1,0:T(8,128)(2,1)S(1)}, bf16[128,128]{1,0:T(8,128)(2,1)S(1)}, u32[]{:S(2)}, u32[]{:S(2)}) collective-permute-start(bf16[128,128]{1,0:T(8,128)(2,1)S(1)} %slice.82), channel_id=1, source_target_pairs={{0,1},{1,0},{2,3},{3,2},{4,5},{5,4},{6,7},{7,6},{8,9},{9,8},{10,11... | collective-permute-start | bytes 98312 | tf_op jit(solution)/shard_map/ppermute | solution.py:23
  44.7 1.2 %collective-permute-start.12 = (bf16[128,128]{1,0:T(8,128)(2,1)S(1)}, bf16[128,128]{1,0:T(8,128)(2,1)S(1)}, u32[]{:S(2)}, u32[]{:S(2)}) collective-permute-start(bf16[128,128]{1,0:T(8,128)(2,1)S(1)} %slice.81.refs_4_), channel_id=1, source_target_pairs={{0,1},{1,0},{2,3},{3,2},{4,5},{5,4},{6,7},{7,6},{8,9},{9,8},{10,11... | collective-permute-start | bytes 98312 | tf_op jit(solution)/shard_map/ppermute | solution.py:23
  47.1 11.5 %copy-start.5 = (bf16[64,256]{1,0:T(8,128)(2,1)S(1)}, bf16[64,256]{1,0:T(8,128)(2,1)}, u32[]{:S(2)}) copy-start(bf16[64,256]{1,0:T(8,128)(2,1)} %param.15) | copy-start | bytes 98308
  49.1 6.0 %collective-permute-start.19 = (bf16[128,128]{1,0:T(8,128)(2,1)S(1)}, bf16[128,128]{1,0:T(8,128)(2,1)S(1)}, u32[]{:S(2)}, u32[]{:S(2)}) collective-permute-start(bf16[128,128]{1,0:T(8,128)(2,1)S(1)} %get-tuple-element.70), channel_id=1, source_target_pairs={{0,24},{1,25},{2,26},{3,27},{4,28},{5,29},{6,30},{7,31},{8,16},{9,... | collective-permute-start | bytes 98312 | tf_op jit(solution)/shard_map/ppermute | solution.py:23
  52.4 4.8 %collective-permute-start.20 = (bf16[128,128]{1,0:T(8,128)(2,1)S(1)}, bf16[128,128]{1,0:T(8,128)(2,1)S(1)}, u32[]{:S(2)}, u32[]{:S(2)}) collective-permute-start(bf16[128,128]{1,0:T(8,128)(2,1)S(1)} %get-tuple-element.72), channel_id=1, source_target_pairs={{0,16},{1,17},{2,18},{3,19},{4,20},{5,21},{6,22},{7,23},{8,24},{9,... | collective-permute-start | bytes 98312 | tf_op jit(solution)/shard_map/ppermute | solution.py:23
  52.4 4.8 %collective-permute-start.21 = (bf16[128,128]{1,0:T(8,128)(2,1)S(1)}, bf16[128,128]{1,0:T(8,128)(2,1)S(1)}, u32[]{:S(2)}, u32[]{:S(2)}) collective-permute-start(bf16[128,128]{1,0:T(8,128)(2,1)S(1)} %get-tuple-element.71), channel_id=1, source_target_pairs={{0,8},{1,9},{2,10},{3,11},{4,12},{5,13},{6,14},{7,15},{8,0},{9,1},... | collective-permute-start | bytes 98312 | tf_op jit(solution)/shard_map/ppermute | solution.py:23
  57.3 1.3 %collective-permute-start.22 = (f32[64,128]{1,0:T(8,128)S(1)}, f32[64,128]{1,0:T(8,128)S(1)}, u32[]{:S(2)}, u32[]{:S(2)}) collective-permute-start(f32[64,128]{1,0:T(8,128)S(1)} %get-tuple-element.74), channel_id=1, source_target_pairs={{0,1},{1,0},{2,3},{3,2},{4,5},{5,4},{6,7},{7,6},{8,9},{9,8},{10,11... | collective-permute-start | bytes 98312 | tf_op jit(solution)/shard_map/ppermute | solution.py:23
